TPU v7x, 32 devices: a whole 2x2x4 slice. The times are simulated.
32 devices in a mesh: ctx: 8 (over z, core), tp: 4 (over y, x).
Axes of the slice: x: 2, y: 2, z: 4, core: 2. Of those that a mesh axis runs over, the one named last changes fastest.
Arguments:
- tokens: bfloat16 [8, 1536, 2048], P('ctx', 'tp'), may hold values from -6 to 6
- counts: int32 [8, 6, 2], replicated, may hold values from 32 to 128, as said below
- norm_gain: bfloat16 [2048], replicated, may hold values from 0.25 to 1.75
- w_query: bfloat16 [2048, 2048], P(None, 'tp'), may hold values from -0.1875 to 0.1875
- w_key: bfloat16 [2048, 2048], P(None, 'tp'), may hold values from -0.1875 to 0.1875
- w_value: bfloat16 [2048, 2048], P(None, 'tp'), may hold values from -0.125 to 0.125
- w_output: bfloat16 [2048, 2048], P('tp'), may hold values from -0.1875 to 0.1875
- mlp_gain: bfloat16 [2048], replicated, may hold values from 0.25 to 1.75
- w_gate: bfloat16 [2048, 8192], P(None, 'tp'), may hold values from -0.125 to 0.125
- w_up: bfloat16 [2048, 8192], P(None, 'tp'), may hold values from -0.125 to 0.125
- w_down: bfloat16 [8192, 2048], P('tp'), may hold values from -0.0625 to 0.0625
- cotangent: bfloat16 [8, 1536, 2048], P('ctx', 'tp'), may hold values from -6 to 6
Outputs:
- output: bfloat16 [8, 1536, 2048], P('ctx', 'tp')
- input_grad: bfloat16 [8, 1536, 2048], P('ctx', 'tp')
- grad_norm_gain: float32 [2048], replicated
- grad_query: float32 [2048, 2048], P(None, 'tp')
- grad_key: float32 [2048, 2048], P(None, 'tp')
- grad_value: float32 [2048, 2048], P(None, 'tp')
- grad_output_w: float32 [2048, 2048], P('tp')
- grad_mlp_gain: float32 [2048], replicated
- grad_gate: float32 [2048, 8192], P(None, 'tp')
- grad_up: float32 [2048, 8192], P(None, 'tp')
- grad_down: float32 [8192, 2048], P('tp')
Inputs may be any that keep to these rules, and one draw needn't show every extreme that they name: `counts`: each block's valid tokens are its first ones; every draw has a block with 128 valid tokens and one with 32.
All inputs are finite; a program needn't handle non-finite values.
Results may differ from a plain program's by a relative error of at most 0.015.
Values may be sent and summed in bfloat16 or wider, within the bound.
A program may use at most 448 MiB of HBM per device.

v0:
```python
import math

import jax
import jax.numpy as jnp
from jax import lax
from jax.sharding import PartitionSpec as P

HD = 128
BLOCK = 128


EPS = 1e-05
THETA = 10000.0


def norm_rows(values, gain_vec):
    return values * lax.rsqrt(jnp.mean(values * values, axis=-1, keepdims=True) + EPS) * gain_vec


def rotate_pairs(values, cos_tab, sin_tab):
    half_dim = values.shape[-1] // 2
    first_half = values[..., :half_dim]
    second_half = values[..., half_dim:]
    return jnp.concatenate(
        [
            first_half * cos_tab - second_half * sin_tab,
            second_half * cos_tab + first_half * sin_tab,
        ],
        axis=-1,
    )


def block_positions(devices, groups):
    offsets = jnp.arange(2 * BLOCK, dtype=jnp.int32)
    inner_pos = offsets % BLOCK
    front_pos = devices[:, None] * BLOCK + inner_pos[None, :]
    back_pos = (2 * groups - 1 - devices[:, None]) * BLOCK + inner_pos[None, :]
    return jnp.where((offsets // BLOCK)[None, :] == 0, front_pos, back_pos)


def rotation_tables(positions):
    inverse = THETA ** (-(jnp.arange(HD // 2, dtype=jnp.float32) * (2.0 / HD)))
    angles = positions.astype(jnp.float32)[:, None] * inverse[None, :]
    return (jnp.cos(angles)[:, None, :], jnp.sin(angles)[:, None, :])


def swiglu(gate_pre, up_pre):
    return jax.nn.silu(gate_pre) * up_pre


def contract_rows(left, right):
    return lax.dot_general(
        left, right, (((0,), (0,)), ((), ())), preferred_element_type=jnp.float32
    )


def times_transposed(left, right):
    return lax.dot_general(
        left, right, (((1,), (1,)), ((), ())), preferred_element_type=jnp.float32
    )


def body(
    tokens,
    counts,
    norm_gain,
    w_query,
    w_key,
    w_value,
    w_output,
    mlp_gain,
    w_gate,
    w_up,
    w_down,
    cotangent,
):
    groups = lax.axis_size("ctx")
    ctx_index = lax.axis_index("ctx")
    seq_count = counts.shape[1]
    seq_rows = 2 * BLOCK
    local_rows = seq_count * seq_rows
    local_width = w_query.shape[1]
    head_count = local_width // HD
    score_scale = HD ** (-0.5)
    offset_bias = math.log(seq_rows * groups)
    own_positions = block_positions(jnp.reshape(ctx_index, (1,)), groups)[0]
    own_counts = lax.dynamic_index_in_dim(counts, ctx_index, 0, keepdims=False)
    validity = (
        (jnp.arange(BLOCK, dtype=jnp.int32)[None, None, :] < own_counts[:, :, None])
        .astype(jnp.float32)
        .reshape(local_rows)
    )
    row_positions = jnp.broadcast_to(own_positions[None, :], (seq_count, seq_rows)).reshape(
        local_rows
    )
    cos_tab, sin_tab = rotation_tables(row_positions)

    def head_grid(flat):
        return flat.reshape(flat.shape[0] // local_rows, seq_count, seq_rows, head_count, HD)

    def key_mask(piece_count):
        devices = jnp.arange(piece_count, dtype=jnp.int32)
        key_pos = block_positions(devices, groups)
        return (own_positions[:, None, None] >= key_pos[None, :, :]).astype(jnp.float32)

    x_rows = tokens[0].astype(jnp.float32)
    gain_one = norm_gain.astype(jnp.float32)
    normed = norm_rows(x_rows, gain_one).astype(jnp.bfloat16)
    normed_all = lax.all_gather(normed, "tp", axis=0, tiled=True)
    queries = jnp.dot(normed_all, w_query, preferred_element_type=jnp.float32).reshape(
        local_rows, head_count, HD
    )
    keys_pre = jnp.dot(normed_all, w_key, preferred_element_type=jnp.float32).reshape(
        local_rows, head_count, HD
    )
    values_pre = jnp.dot(normed_all, w_value, preferred_element_type=jnp.float32)
    query_rot = (
        rotate_pairs(queries, cos_tab, sin_tab)
        .astype(jnp.bfloat16)
        .reshape(local_rows, local_width)
    )
    key_rot = (
        rotate_pairs(keys_pre, cos_tab, sin_tab)
        .astype(jnp.bfloat16)
        .reshape(local_rows, local_width)
    )
    value_kept = (values_pre * validity[:, None]).astype(jnp.bfloat16)
    query_grid = head_grid(query_rot)[0]
    pieces = (
        lax.all_gather(key_rot, "ctx", axis=0, tiled=True),
        lax.all_gather(value_kept, "ctx", axis=0, tiled=True),
    )
    key_piece = pieces[0]
    piece_count = key_piece.shape[0] // local_rows
    key_grid = head_grid(key_piece)
    value_grid = head_grid(pieces[1])
    causal = key_mask(piece_count)
    scores = (
        jnp.einsum("sqhd,psKhd->shqpK", query_grid, key_grid, preferred_element_type=jnp.float32)
        * score_scale
        - offset_bias
    )
    attn_prob = (jax.nn.sigmoid(scores) * causal).astype(jnp.bfloat16)
    update = jnp.einsum(
        "shqpK,psKhd->sqhd", attn_prob, value_grid, preferred_element_type=jnp.float32
    )
    heads_out = (update.reshape(local_rows, local_width) * validity[:, None]).astype(jnp.bfloat16)
    attn_rows = lax.psum_scatter(
        jnp.dot(heads_out, w_output, preferred_element_type=jnp.float32),
        "tp",
        scatter_dimension=0,
        tiled=True,
    )
    residual = x_rows + attn_rows
    gain_two = mlp_gain.astype(jnp.float32)
    normed_two = norm_rows(residual, gain_two).astype(jnp.bfloat16)
    normed_two_all = lax.all_gather(normed_two, "tp", axis=0, tiled=True)
    gate_pre = jnp.dot(normed_two_all, w_gate, preferred_element_type=jnp.float32)
    up_pre = jnp.dot(normed_two_all, w_up, preferred_element_type=jnp.float32)
    hidden = swiglu(gate_pre, up_pre).astype(jnp.bfloat16)
    mlp_rows_out = lax.psum_scatter(
        jnp.dot(hidden, w_down, preferred_element_type=jnp.float32),
        "tp",
        scatter_dimension=0,
        tiled=True,
    )
    output = (residual + mlp_rows_out).astype(jnp.bfloat16)
    grad_rows = cotangent[0]
    piece = lax.all_gather(grad_rows, "tp", axis=0, tiled=True)
    hidden_grad = times_transposed(piece, w_down)
    hidden_grad, grad_down = (hidden_grad, contract_rows(hidden, piece))
    swiglu_back = jax.vjp(swiglu, gate_pre, up_pre)[1]
    gate_grad, up_grad = swiglu_back(hidden_grad)
    gate_grad = gate_grad.astype(jnp.bfloat16)
    up_grad = up_grad.astype(jnp.bfloat16)
    grad_gate = contract_rows(normed_two_all, gate_grad)
    grad_up = contract_rows(normed_two_all, up_grad)
    normed_two_grad = lax.psum_scatter(
        times_transposed(gate_grad, w_gate) + times_transposed(up_grad, w_up),
        "tp",
        scatter_dimension=0,
        tiled=True,
    )
    norm_two_back = jax.vjp(norm_rows, residual, gain_two)[1]
    residual_part, grad_mlp_gain = norm_two_back(normed_two_grad)
    residual_grad = grad_rows.astype(jnp.float32) + residual_part
    attn_grad = residual_grad.astype(jnp.bfloat16)
    piece = lax.all_gather(attn_grad, "tp", axis=0, tiled=True)
    heads_grad = times_transposed(piece, w_output)
    heads_grad, grad_output_w = (heads_grad, contract_rows(heads_out, piece))
    heads_grad_low = heads_grad.astype(jnp.bfloat16) * validity[:, None].astype(jnp.bfloat16)
    grad_grid = head_grid(heads_grad_low)[0]
    pieces = (
        lax.all_gather(key_rot, "ctx", axis=0, tiled=True),
        lax.all_gather(value_kept, "ctx", axis=0, tiled=True),
    )
    piece_count = pieces[0].shape[0] // local_rows
    piece_rows = piece_count * local_rows
    key_grid = head_grid(pieces[0])
    value_grid = head_grid(pieces[1])
    causal = key_mask(piece_count)
    scores = (
        jnp.einsum("sqhd,psKhd->shqpK", query_grid, key_grid, preferred_element_type=jnp.float32)
        * score_scale
        - offset_bias
    )
    sigmoid_s = jax.nn.sigmoid(scores)
    prob_grad = jnp.einsum(
        "sqhd,psKhd->shqpK", grad_grid, value_grid, preferred_element_type=jnp.float32
    )
    score_grad = (prob_grad * sigmoid_s * (1.0 - sigmoid_s) * causal).astype(jnp.bfloat16)
    sigmoid_s, causal, score_grad = (sigmoid_s, causal, score_grad)
    attn_prob = (sigmoid_s * causal).astype(jnp.bfloat16)
    query_part = jnp.einsum(
        "shqpK,psKhd->sqhd", score_grad, key_grid, preferred_element_type=jnp.float32
    )
    key_part = jnp.einsum(
        "shqpK,sqhd->psKhd", score_grad, query_grid, preferred_element_type=jnp.float32
    )
    value_part = jnp.einsum(
        "shqpK,sqhd->psKhd", attn_prob, grad_grid, preferred_element_type=jnp.float32
    )
    key_rows = key_part.reshape(piece_rows, local_width) * score_scale
    value_rows = value_part.reshape(piece_rows, local_width)
    query_grad = query_part.reshape(local_rows, local_width) * score_scale
    key_grad, value_grad = (
        lax.psum_scatter(key_rows, "ctx", scatter_dimension=0, tiled=True),
        lax.psum_scatter(value_rows, "ctx", scatter_dimension=0, tiled=True),
    )
    query_back = (
        rotate_pairs(query_grad.reshape(local_rows, head_count, HD), cos_tab, -sin_tab)
        .reshape(local_rows, local_width)
        .astype(jnp.bfloat16)
    )
    key_back = (
        rotate_pairs(key_grad.reshape(local_rows, head_count, HD), cos_tab, -sin_tab)
        .reshape(local_rows, local_width)
        .astype(jnp.bfloat16)
    )
    value_back = (value_grad * validity[:, None]).astype(jnp.bfloat16)
    grad_query = contract_rows(normed_all, query_back)
    grad_key = contract_rows(normed_all, key_back)
    grad_value = contract_rows(normed_all, value_back)
    key_rows = key_back
    value_rows = value_back
    normed_grad = lax.psum_scatter(
        times_transposed(query_back, w_query)
        + times_transposed(key_rows, w_key)
        + times_transposed(value_rows, w_value),
        "tp",
        scatter_dimension=0,
        tiled=True,
    )
    norm_one_back = jax.vjp(norm_rows, x_rows, gain_one)[1]
    input_part, grad_norm_gain = norm_one_back(normed_grad)
    input_grad = (residual_grad + input_part).astype(jnp.bfloat16)
    weight_sums = lax.psum(
        (grad_query, grad_key, grad_value, grad_output_w, grad_gate, grad_up, grad_down), "ctx"
    )
    gain_sums = lax.psum((grad_norm_gain, grad_mlp_gain), ("ctx", "tp"))
    return (
        output[None],
        input_grad[None],
        gain_sums[0],
        weight_sums[0],
        weight_sums[1],
        weight_sums[2],
        weight_sums[3],
        gain_sums[1],
        weight_sums[4],
        weight_sums[5],
        weight_sums[6],
    )


def solution(mesh):
    placed = (
        P("ctx", "tp", None),
        P(),
        P(),
        P(None, "tp"),
        P(None, "tp"),
        P(None, "tp"),
        P("tp", None),
        P(),
        P(None, "tp"),
        P(None, "tp"),
        P("tp", None),
        P("ctx", "tp", None),
    )
    return jax.shard_map(
        body,
        mesh=mesh,
        in_specs=placed,
        out_specs=(
            P("ctx", "tp", None),
            P("ctx", "tp", None),
            P(),
            P(None, "tp"),
            P(None, "tp"),
            P(None, "tp"),
            P("tp", None),
            P(),
            P(None, "tp"),
            P(None, "tp"),
            P("tp", None),
        ),
        check_vma=False,
    )
```

profile of v0, /device:TPU:1, one launch (start us, length us, event | category | flops | bytes accessed | tf_op | source)
XLA Modules:
  0.0 3136.7 jit_solution(8609453494525290435)
XLA Ops:
  16.4 70.0 %all-gather.8.cloned.1.call-done = bf16[1536,2048]{1,0:T(8,128)(2,1)} async-done(((bf16[384,2048]{1,0:T(8,128)(2,1)}), bf16[1536,2048]{1,0:T(8,128)(2,1)}) %all-gather.8.cloned.1.call-update) | async-done | bytes 6291472 | tf_op jit(solution)/shard_map/all_gather | solution.py:109
  117.9 99.4 %all-gather.12.cloned.1.call-done = bf16[12288,512]{0,1:T(8,128)(2,1)} async-done(((bf16[1536,512]{0,1:T(8,128)(2,1)}), bf16[12288,512]{0,1:T(8,128)(2,1)}) %all-gather.12.cloned.1.call-update) | async-done | bytes 12582928 | tf_op jit(solution)/shard_map/all_gather | solution.py:130
  217.4 26.5 reshape.388
  243.9 32.2 %add_divide_fusion = f32[6,4,256,8,256]{4,2,3,1,0:T(8,128)} fusion(bf16[8,6,256,4,128]{2,1,0,4,3:T(8,128)(2,1)} %reshape.388, bf16[6,256,4,64]{3,1,2,0:T(8,128)(2,1)} %copy.57, bf16[6,256,4,64]{3,1,2,0:T(8,128)(2,1)} %copy.56), kind=kOutput, calls=%fused_computation.2 | convolution fusion | flops 3287285760 | bytes 64487424 | tf_op jit(solution)/shard_map/sqhd,psKhd->shqpK/dot_general | solution.py:139
  276.1 58.5 %all-gather.10.cloned.1.call-done = bf16[12288,512]{1,0:T(8,128)(2,1)} async-done(((bf16[1536,512]{1,0:T(8,128)(2,1)}), bf16[12288,512]{1,0:T(8,128)(2,1)}) %all-gather.10.cloned.1.call-update) | async-done | bytes 12582928 | tf_op jit(solution)/shard_map/all_gather | solution.py:131
  352.6 23.6 fusion.29
  390.7 118.0 %reduce-scatter.7.cloned.1.call-done = f32[384,2048]{1,0:T(8,128)} async-done(((f32[1536,2048]{1,0:T(8,128)}), f32[384,2048]{1,0:T(8,128)}) %reduce-scatter.7.cloned.1.call-update) | async-done | bytes 3145744 | tf_op jit(solution)/shard_map/reduce_scatter | solution.py:148
  515.4 69.7 %all-gather.14.cloned.1.call-done = bf16[1536,2048]{1,0:T(8,128)(2,1)} async-done(((bf16[384,2048]{1,0:T(8,128)(2,1)}), bf16[1536,2048]{1,0:T(8,128)(2,1)}) %all-gather.14.cloned.1.call-update) | async-done | bytes 6291472 | tf_op jit(solution)/shard_map/all_gather | solution.py:157
  585.0 19.4 fusion.54
  621.5 35.4 %all-gather.18.cloned.1.call-done = bf16[1,1536,2048]{2,1,0:T(8,128)(2,1)} async-done(((bf16[1,384,2048]{2,1,0:T(8,128)(2,1)}), bf16[1,1536,2048]{2,1,0:T(8,128)(2,1)}) %all-gather.18.cloned.1.call-update) | async-done | bytes 6291472 | tf_op jit(solution)/shard_map/all_gather | solution.py:169
  656.9 27.6 multiply_convert_fusion.2
  684.5 19.0 fusion.57
  703.5 22.1 convolution_add_fusion
  725.7 120.8 %reduce-scatter.11.cloned.1.call-done = f32[384,2048]{1,0:T(8,128)} async-done(((f32[1536,2048]{1,0:T(8,128)}), f32[384,2048]{1,0:T(8,128)}) %reduce-scatter.11.cloned.1.call-update) | async-done | bytes 3145744 | tf_op jit(solution)/shard_map/reduce_scatter | solution.py:178
  855.2 70.2 %all-gather.16.cloned.1.call-done = bf16[1536,2048]{1,0:T(8,128)(2,1)} async-done(((bf16[384,2048]{1,0:T(8,128)(2,1)}), bf16[1536,2048]{1,0:T(8,128)(2,1)}) %all-gather.16.cloned.1.call-update) | async-done | bytes 6291472 | tf_op jit(solution)/shard_map/all_gather | solution.py:188
  940.4 29.6 multiply_convert_fusion
  986.7 28.5 copy.69
  1015.3 19.0 copy.112
  1034.3 27.8 fusion.11
  1062.1 28.7 copy.72
  1090.7 19.2 copy.111
  1110.0 20.2 fusion.26
  1145.8 133.6 %reduce-scatter.13.cloned.1.call-done = f32[1536,512]{1,0:T(8,128)} async-done(((f32[12288,512]{1,0:T(8,128)}), f32[1536,512]{1,0:T(8,128)}) %reduce-scatter.13.cloned.1.call-update) | async-done | bytes 3145744 | tf_op jit(solution)/shard_map/reduce_scatter | solution.py:227
  1302.5 224.7 %reduce-scatter.15.cloned.1.call-done = f32[1536,512]{1,0:T(8,128)} async-done(((f32[12288,512]{1,0:T(8,128)}), f32[1536,512]{1,0:T(8,128)}) %reduce-scatter.15.cloned.1.call-update) | async-done | bytes 3145744 | tf_op jit(solution)/shard_map/reduce_scatter | solution.py:228
  1542.8 18.9 fusion.56
  1561.9 20.9 fusion.62
  1582.8 21.2 fusion.63
  1604.1 19.4 fusion.12
  1645.2 19.0 reduce-scatter.17.cloned.1.call-done
  1667.0 40.6 %all-reduce = (f32[2048]{0:T(1024)}, f32[2048]{0:T(1024)}) all-reduce(f32[2048]{0:T(1024)S(1)} %get-tuple-element.13, f32[2048]{0:T(1024)S(1)} %copy-done.31), channel_id=1, replica_groups=mesh['ctx'=8,'tp'=4] {'ctx','tp'}, use_global_device_ids=true, to_apply=%region_11.12 | all-reduce | flops 4096 | bytes 32768 | tf_op jit(solution)/shard_map/psum | solution.py:260
  1707.6 81.2 %reduce-scatter.9.cloned.1.call-done = f32[384,2048]{1,0:T(8,128)} async-done(((f32[1536,2048]{1,0:T(8,128)}), f32[384,2048]{1,0:T(8,128)}) %reduce-scatter.9.cloned.1.call-update) | async-done | bytes 3145744 | tf_op jit(solution)/shard_map/reduce_scatter | solution.py:161
  1796.5 1285.6 %all-reduce.4.cloned.1.call-done = (f32[2048,512]{1,0:T(8,128)}, f32[2048,512]{1,0:T(8,128)}, f32[2048,512]{1,0:T(8,128)}, f32[512,2048]{1,0:T(8,128)}, f32[2048...) async-done(((f32[2048,512]{1,0:T(8,128)}, f32[2048,512]{1,0:T(8,128)}, f32[2048,512]{1,0:T(8,128)}, f32[512,2048]{1,0:T(8,128)}, f32[2048,2048]{1,0:T(8,128)}, ...) | async-done | bytes 67108880 | tf_op jit(solution)/shard_map/psum | solution.py:257
  (225 shorter events, 271.2 us)
Async XLA Ops:
  7.2 373.9 %copy-start = (bf16[512,2048]{1,0:T(8,128)(2,1)S(1)}, bf16[512,2048]{1,0:T(8,128)(2,1)}, u32[]{:S(2)}) copy-start(bf16[512,2048]{1,0:T(8,128)(2,1)} %param.18) | copy-start | bytes 6291460
  7.2 79.3 %all-gather.8.cloned.1.call-start = ((), (), s32[]{:S(2)}) async-start(), calls=%async_computation.6 | async-start | bytes 7864320 | tf_op jit(solution)/shard_map/all_gather | solution.py:109
  14.1 203.3 %all-gather.12.cloned.1.call-start = ((), (), s32[]{:S(2)}) async-start(), calls=%async_computation.8 | async-start | bytes 14155776 | tf_op jit(solution)/shard_map/all_gather | solution.py:130
  16.4 80.1 %copy-start.11 = (f32[1536,64]{0,1:T(8,128)}, f32[1536,64]{0,1:T(8,128)S(1)}, u32[]{:S(2)}) copy-start(f32[1536,64]{0,1:T(8,128)S(1)} %get-tuple-element.47) | copy-start | bytes 1179652
  100.1 234.5 %all-gather.10.cloned.1.call-start = ((), (), s32[]{:S(2)}) async-start(), calls=%async_computation.7 | async-start | bytes 14155776 | tf_op jit(solution)/shard_map/all_gather | solution.py:131
  100.5 280.6 %copy-start.20 = (f32[1536]{0:T(1024)}, f32[1536]{0:T(1024)S(1)}, u32[]{:S(2)}) copy-start(f32[1536]{0:T(1024)S(1)} %reshape.379) | copy-start | bytes 18436
  108.5 400.2 %reduce-scatter.7.cloned.1.call-start = ((), (), s32[]{:S(2)}) async-start(), calls=%async_computation.9 | async-start | bytes 15728640 | tf_op jit(solution)/shard_map/reduce_scatter | solution.py:148
  390.1 195.0 %all-gather.14.cloned.1.call-start = ((), (), s32[]{:S(2)}) async-start(), calls=%async_computation.10 | async-start | bytes 7864320 | tf_op jit(solution)/shard_map/all_gather | solution.py:157
  390.7 121.5 %copy-start.23 = (f32[2048]{0:T(1024)}, f32[2048]{0:T(1024)S(1)}, u32[]{:S(2)}) copy-start(f32[2048]{0:T(1024)S(1)} %convert_element_type.127) | copy-start | bytes 24580
  514.7 142.2 %all-gather.18.cloned.1.call-start = ((), (), s32[]{:S(2)}) async-start(), calls=%async_computation.17 | async-start | bytes 7864320 | tf_op jit(solution)/shard_map/all_gather | solution.py:169
  515.3 331.2 %reduce-scatter.11.cloned.1.call-start = ((), (), s32[]{:S(2)}) async-start(), calls=%async_computation.12 | async-start | bytes 15728640 | tf_op jit(solution)/shard_map/reduce_scatter | solution.py:178
  725.6 120.9 %copy-start.24 = (f32[2048]{0:T(1024)S(1)}, f32[2048]{0:T(1024)}, u32[]{:S(2)}) copy-start(f32[2048]{0:T(1024)} %copy-done.23) | copy-start | bytes 24580
  725.6 120.9 %copy-start.29 = (f32[384]{0:T(512)S(1)}, f32[384]{0:T(512)}, u32[]{:S(2)}) copy-start(f32[384]{0:T(512)} %copy-done.28) | copy-start | bytes 4612
  725.6 125.3 %copy-start.39 = (f32[384]{0:T(512)S(1)}, f32[384]{0:T(512)}, u32[]{:S(2)}) copy-start(f32[384]{0:T(512)} %copy-done.38) | copy-start | bytes 4612
  725.6 199.8 %all-gather.16.cloned.1.call-start = ((), (), s32[]{:S(2)}) async-start(), calls=%async_computation.13 | async-start | bytes 7864320 | tf_op jit(solution)/shard_map/all_gather | solution.py:188
  855.2 424.3 %reduce-scatter.13.cloned.1.call-start = ((), (), s32[]{:S(2)}) async-start(), calls=%async_computation.14 | async-start | bytes 28311552 | tf_op jit(solution)/shard_map/reduce_scatter | solution.py:227
  1034.3 492.9 %reduce-scatter.15.cloned.1.call-start = ((), (), s32[]{:S(2)}) async-start(), calls=%async_computation.15 | async-start | bytes 28311552 | tf_op jit(solution)/shard_map/reduce_scatter | solution.py:228
  1110.0 554.2 %reduce-scatter.17.cloned.1.call-start = ((), (), s32[]{:S(2)}) async-start(), calls=%async_computation.16 | async-start | bytes 15728640 | tf_op jit(solution)/shard_map/reduce_scatter | solution.py:246
  1145.8 137.2 %copy-start.12 = (f32[1536,64]{0,1:T(8,128)S(1)}, f32[1536,64]{0,1:T(8,128)}, u32[]{:S(2)}) copy-start(f32[1536,64]{0,1:T(8,128)} %copy-done.11) | copy-start | bytes 1179652
  1145.8 137.2 %copy-start.15 = (f32[1536,64]{0,1:T(8,128)S(1)}, f32[1536,64]{0,1:T(8,128)}, u32[]{:S(2)}) copy-start(f32[1536,64]{0,1:T(8,128)} %get-tuple-element.45) | copy-start | bytes 1179652
  1295.8 231.4 %copy-start.14 = (bf16[2048,512]{1,0:T(8,128)(2,1)S(1)}, bf16[2048,512]{1,0:T(8,128)(2,1)}, u32[]{:S(2)}) copy-start(bf16[2048,512]{1,0:T(8,128)(2,1)} %param.17) | copy-start | bytes 6291460
  1295.8 231.4 %copy-start.22 = (f32[1536]{0:T(1024)S(1)}, f32[1536]{0:T(1024)}, u32[]{:S(2)}) copy-start(f32[1536]{0:T(1024)} %copy-done.20) | copy-start | bytes 18436
  1542.8 246.0 %reduce-scatter.9.cloned.1.call-start = ((), (), s32[]{:S(2)}) async-start(), calls=%async_computation.11 | async-start | bytes 15728640 | tf_op jit(solution)/shard_map/reduce_scatter | solution.py:161
  1561.8 1520.3 %all-reduce.4.cloned.1.call-start = ((), (), s32[]{:S(2)}) async-start(), calls=%async_computation.18 | async-start | bytes 134217728 | tf_op jit(solution)/shard_map/psum | solution.py:257
  1561.8 42.2 %slice-start.12 = ((s8[6291456]{0:T(1024)(128)(4,1)}), s8[4194304]{0:T(1024)(128)(4,1)S(1)}, s32[]{:S(2)}) async-start(s8[6291456]{0:T(1024)(128)(4,1)} %bitcast.153), calls=%async_computation.31 | async-start | bytes 8388608
  1582.8 40.6 %slice-start = ((s8[6291456]{0:T(1024)(128)(4,1)}), s8[4194304]{0:T(1024)(128)(4,1)S(1)}, s32[]{:S(2)}) async-start(s8[6291456]{0:T(1024)(128)(4,1)} %bitcast.135), calls=%async_computation.19 | async-start | bytes 8388608
  1582.8 45.9 %slice-start.10 = ((s8[6291456]{0:T(1024)(128)(4,1)}), s8[4194304]{0:T(1024)(128)(4,1)S(1)}, s32[]{:S(2)}) async-start(s8[6291456]{0:T(1024)(128)(4,1)} %bitcast.151), calls=%async_computation.29 | async-start | bytes 8388608
  1604.0 24.6 slice-start.11
  1645.1 62.5 %copy-start.37 = (f32[384]{0:T(512)S(1)}, f32[384]{0:T(512)}, u32[]{:S(2)}) copy-start(f32[384]{0:T(512)} %copy-done.36) | copy-start | bytes 4612
  1645.1 143.7 %copy-start.25 = (f32[2048]{0:T(1024)S(1)}, f32[2048]{0:T(1024)}, u32[]{:S(2)}) copy-start(f32[2048]{0:T(1024)} %copy-done.23) | copy-start | bytes 24580
  1645.1 143.7 %copy-start.30 = (f32[384]{0:T(512)S(1)}, f32[384]{0:T(512)}, u32[]{:S(2)}) copy-start(f32[384]{0:T(512)} %copy-done.28) | copy-start | bytes 4612
  1645.2 143.7 %copy-start.35 = (f32[384]{0:T(512)S(1)}, f32[384]{0:T(512)}, u32[]{:S(2)}) copy-start(f32[384]{0:T(512)} %copy-done.34) | copy-start | bytes 4612
  (43 other events, 411.3 us)
Sparse Core Ops, SparseCore 0:
  14.2 72.2 all-gather.7
  100.2 117.1 all-gather.11
  219.6 114.9 all-gather.9
  390.2 118.5 reduce-scatter.6
  514.9 70.1 all-gather.13
  586.7 70.1 all-gather.17
  725.7 120.7 reduce-scatter.10
  855.3 70.1 all-gather.15
  1034.4 245.0 reduce-scatter.12
  1281.6 245.5 reduce-scatter.14
  1542.9 121.2 reduce-scatter.16
  1667.1 121.6 reduce-scatter.8
  1793.4 1288.6 all-reduce.3
where the time goes:
time: 3150 us; the launch traced here: 3140 us
  waiting for transfers between devices  2390 us (76%)
  matrix products  421 us (13%)
  local copies, waits for them, and re-layouts  233 us (7%)
  blocking collectives  40.6 us (1%)
  other arithmetic  39.5 us (1%)
    psum x1, waiting for transfers between devices, body(): lax.psum((grad_query, grad_key, grad_value, grad_output_w, grad_gate, gra...  1290 us
    reduce_scatter x1, waiting for transfers between devices, body(): lax.psum_scatter(value_rows, 'ctx', scatter_dimension=0, tiled=True)  225 us
    reduce_scatter x1, waiting for transfers between devices, body(): lax.psum_scatter(key_rows, 'ctx', scatter_dimension=0, tiled=True)  134 us
    reduce_scatter x1, waiting for transfers between devices, body(): lax.psum_scatter(times_transposed(gate_grad, w_gate) + times_transposed(u...  121 us
    reduce_scatter x1, waiting for transfers between devices, body(): lax.psum_scatter(jnp.dot(heads_out, w_output, preferred_element_type=jnp....  118 us
    dot_general x7, matrix products, times_transposed(): lax.dot_general(left, right, (((1,), (1,)), ((), ())), preferred_element_...  105 us
    all_gather x1, waiting for transfers between devices, body(): lax.all_gather(key_rot, 'ctx', axis=0, tiled=True)  99.4 us
    unnamed x135, local copies, waits for them, and re-layouts  98 us
  transfers between devices with their start and end apart: 13, of which 13 were waited for; matrix products, arithmetic and copies ran while one was open for 11% of the time, Pallas kernels for 0%

commit v1 on v0

v1 whole, which is shorter than its diff:
```python
import functools
import math

import jax
import jax.numpy as jnp
from jax import lax
from jax.experimental import pallas as pl
from jax.experimental.pallas import tpu as pltpu
from jax.sharding import PartitionSpec as P

HD = 128
BLOCK = 128
PAIR = 2 * BLOCK
EPS = 1e-05
THETA = 10000.0
LOG2E = 1.4426950408889634
BF = jnp.bfloat16
F32 = jnp.float32
VMEM_LIMIT = 58 * 1024 * 1024

X_SWAP = [(i, i ^ 1) for i in range(4)]
Y_SWAP = [(i, i ^ 2) for i in range(4)]


def dot(left, right):
    return jnp.dot(left, right, preferred_element_type=F32)


def contract_rows(left, right):
    return lax.dot_general(left, right, (((0,), (0,)), ((), ())), preferred_element_type=F32)


def times_transposed(left, right):
    return lax.dot_general(left, right, (((1,), (1,)), ((), ())), preferred_element_type=F32)


def send_x(values):
    return lax.ppermute(values, "tp", X_SWAP)


def send_y(values):
    return lax.ppermute(values, "tp", Y_SWAP)


def gather_rows(own):
    if lax.axis_size("tp") != 4:
        return lax.all_gather(own, "tp", axis=0, tiled=True)
    half = own.shape[0] // 2
    from_x = send_x(own)
    from_y = send_y(own)
    diag_low = send_x(from_y[:half])
    diag_high = send_y(from_x[half:])
    return jnp.concatenate([own, from_x, from_y, diag_low, diag_high])


def scatter_rows(partial):
    if lax.axis_size("tp") != 4:
        return lax.psum_scatter(partial, "tp", scatter_dimension=0, tiled=True).astype(F32)
    rows = partial.shape[0] // 4
    half = rows // 2
    mine = partial[:rows]
    from_x = send_x(jnp.concatenate([partial[rows : rows + half], partial[3 * rows : 3 * rows + half]]))
    from_y = send_y(jnp.concatenate([partial[2 * rows + half : 3 * rows], partial[3 * rows + half :]]))
    for_y = partial[2 * rows : 2 * rows + half].astype(F32) + from_x[half:].astype(F32)
    for_x = partial[rows + half : 2 * rows].astype(F32) + from_y[half:].astype(F32)
    low_rest = send_y(for_y.astype(BF))
    high_rest = send_x(for_x.astype(BF))
    low = mine[:half].astype(F32) + from_x[:half].astype(F32) + low_rest.astype(F32)
    high = mine[half:].astype(F32) + from_y[:half].astype(F32) + high_rest.astype(F32)
    return jnp.concatenate([low, high])


def exchange(pieces, n_ctx):
    got = [pieces[0]]
    for k in range(1, n_ctx):
        got.append(lax.ppermute(pieces[k], "ctx", [(i, i ^ k) for i in range(n_ctx)]))
    return jnp.stack(got)


def qkv_kernel(swap_ref, n_ref, wq_ref, wk_ref, wv_ref, cos_ref, sin_ref, valid_ref, out_ref):
    rows = n_ref[...]
    swap = swap_ref[0]
    first = pl.multiple_of(swap * BLOCK, BLOCK)
    second = pl.multiple_of((1 - swap) * BLOCK, BLOCK)
    cos_tab = cos_ref[...]
    sin_tab = sin_ref[...]
    for which, w_ref in enumerate((wq_ref, wk_ref, wv_ref)):
        product = dot(rows, w_ref[...])
        for head in range(product.shape[1] // HD):
            part = product[:, head * HD : (head + 1) * HD]
            if which < 2:
                part = part * cos_tab + pltpu.roll(part, HD // 2, 1) * sin_tab
            else:
                part = part * valid_ref[...]
            part = part.astype(BF)
            out_ref[head, which, pl.ds(first, BLOCK), :] = part[:BLOCK]
            out_ref[head, which, pl.ds(second, BLOCK), :] = part[BLOCK:]


def project_qkv(swap, normed, wq, wk, wv, cos_tab, sin_tab, valid):
    rows, depth = normed.shape
    width = wq.shape[1]
    heads = width // HD
    steps = rows // PAIR
    row_block = pl.BlockSpec((PAIR, HD), lambda i, s: (i, 0))
    weight = pl.BlockSpec((depth, width), lambda i, s: (0, 0))
    return pl.pallas_call(
        qkv_kernel,
        out_shape=jax.ShapeDtypeStruct((steps * heads, 3, PAIR, HD), BF),
        grid_spec=pltpu.PrefetchScalarGridSpec(
            num_scalar_prefetch=1,
            grid=(steps,),
            in_specs=[
                pl.BlockSpec((PAIR, depth), lambda i, s: (i, 0)),
                weight,
                weight,
                weight,
                row_block,
                row_block,
                row_block,
            ],
            out_specs=pl.BlockSpec((heads, 3, PAIR, HD), lambda i, s: (i, 0, 0, 0)),
        ),
        compiler_params=pltpu.CompilerParams(vmem_limit_bytes=VMEM_LIMIT),
        cost_estimate=pl.CostEstimate(
            flops=6 * rows * depth * width, bytes_accessed=rows * depth * 2 + 6 * depth * width, transcendentals=0
        ),
    )(swap, normed, wq, wk, wv, cos_tab, sin_tab, valid)


def ordered_blocks(n_ctx):
    for block in range(2 * n_ctx):
        if block < n_ctx:
            yield block, block, 0
        else:
            yield block, 2 * n_ctx - 1 - block, 1


def attention_kernel(n_ctx, tile, me_ref, x_ref, o_ref, qs, ks, vs):
    me = me_ref[0]
    length = 2 * n_ctx * BLOCK
    for block, source, half in ordered_blocks(n_ctx):
        place = jnp.bitwise_xor(me, source)
        for which, dest in enumerate((qs, ks, vs)):
            dest[block * BLOCK : (block + 1) * BLOCK, :] = x_ref[place, 0, which, half * BLOCK : (half + 1) * BLOCK, :]
    factor = -(HD ** (-0.5)) * LOG2E
    shift = math.log(length) * LOG2E
    count = length // tile
    per_tile = tile // BLOCK
    row_at = lax.broadcasted_iota(jnp.int32, (tile, tile), 0)
    col_at = lax.broadcasted_iota(jnp.int32, (tile, tile), 1)
    order = list(ordered_blocks(n_ctx))
    for i in range(count):
        query = qs[i * tile : (i + 1) * tile, :]

        def part(j, masked):
            at = pl.ds(pl.multiple_of(j * tile, tile), tile)
            raw = times_transposed(query, ks[at, :])
            prob = 1.0 / (1.0 + jnp.exp2(raw * factor + shift))
            if masked:
                prob = jnp.where(row_at >= col_at, prob, 0.0)
            return dot(prob.astype(BF), vs[at, :])

        total = part(i, True)
        if i > 0:
            total = lax.fori_loop(0, i, lambda j, acc: acc + part(j, False), total)
        low = total.astype(BF)
        for b in range(per_tile):
            _, source, half = order[i * per_tile + b]
            place = jnp.bitwise_xor(me, source)
            o_ref[place, 0, half * BLOCK : (half + 1) * BLOCK, :] = low[b * BLOCK : (b + 1) * BLOCK]


def attention_forward(me, qkv, n_ctx):
    pairs = qkv.shape[1]
    length = 2 * n_ctx * BLOCK
    tile = min(512, length)
    flops = pairs * length * length * HD * 2
    return pl.pallas_call(
        functools.partial(attention_kernel, n_ctx, tile),
        out_shape=jax.ShapeDtypeStruct((n_ctx, pairs, PAIR, HD), BF),
        grid_spec=pltpu.PrefetchScalarGridSpec(
            num_scalar_prefetch=1,
            grid=(pairs,),
            in_specs=[pl.BlockSpec((n_ctx, 1, 3, PAIR, HD), lambda i, s: (0, i, 0, 0, 0))],
            out_specs=pl.BlockSpec((n_ctx, 1, PAIR, HD), lambda i, s: (0, i, 0, 0)),
            scratch_shapes=[pltpu.VMEM((length, HD), BF)] * 3,
        ),
        compiler_params=pltpu.CompilerParams(vmem_limit_bytes=VMEM_LIMIT),
        cost_estimate=pl.CostEstimate(
            flops=flops * 3, bytes_accessed=pairs * length * HD * 8, transcendentals=pairs * length * length
        ),
    )(me, qkv)


def attention_back_kernel(n_ctx, tile, me_ref, x_ref, g_ref, cos_ref, sin_ref, out_ref, qs, ks, vs, gs, dqs):
    me = me_ref[0]
    length = 2 * n_ctx * BLOCK
    for block, source, half in ordered_blocks(n_ctx):
        place = jnp.bitwise_xor(me, source)
        at = slice(block * BLOCK, (block + 1) * BLOCK)
        part_at = slice(half * BLOCK, (half + 1) * BLOCK)
        for which, dest in enumerate((qs, ks, vs)):
            dest[at, :] = x_ref[place, 0, which, part_at, :]
        gs[at, :] = g_ref[place, 0, part_at, :]
    scale = HD ** (-0.5)
    factor = -scale * LOG2E
    shift = math.log(length) * LOG2E
    count = length // tile
    per_tile = tile // BLOCK
    key_at = lax.broadcasted_iota(jnp.int32, (tile, tile), 0)
    query_at = lax.broadcasted_iota(jnp.int32, (tile, tile), 1)
    order = list(ordered_blocks(n_ctx))
    dqs[...] = jnp.zeros_like(dqs)

    def unrotate(values, tile_index):
        at = slice(tile_index * tile, (tile_index + 1) * tile)
        return (values * cos_ref[at, :] - pltpu.roll(values, HD // 2, 1) * sin_ref[at, :]).astype(BF)

    def put(which, tile_index, low):
        for b in range(per_tile):
            _, source, half = order[tile_index * per_tile + b]
            place = jnp.bitwise_xor(me, source)
            out_ref[place, 0, which, half * BLOCK : (half + 1) * BLOCK, :] = low[b * BLOCK : (b + 1) * BLOCK]

    for j in range(count):
        keys = ks[j * tile : (j + 1) * tile, :]
        values = vs[j * tile : (j + 1) * tile, :]

        def part(i, masked):
            at = pl.ds(pl.multiple_of(i * tile, tile), tile)
            query = qs[at, :]
            grad = gs[at, :]
            raw = times_transposed(keys, query)
            prob = 1.0 / (1.0 + jnp.exp2(raw * factor + shift))
            if masked:
                prob = jnp.where(query_at >= key_at, prob, 0.0)
            prob_grad = times_transposed(values, grad)
            score_grad = (prob_grad * prob * (1.0 - prob)).astype(BF)
            dqs[at, :] += contract_rows(score_grad, keys)
            return dot(score_grad, query), dot(prob.astype(BF), grad)

        total = part(j, True)
        if j + 1 < count:

            def step(i, acc):
                more = part(i, False)
                return acc[0] + more[0], acc[1] + more[1]

            total = lax.fori_loop(j + 1, count, step, total)
        put(1, j, unrotate(total[0] * scale, j))
        put(2, j, total[1].astype(BF))
    for i in range(count):
        put(0, i, unrotate(dqs[i * tile : (i + 1) * tile, :] * scale, i))


def attention_backward(me, qkv, grads, cos_tab, sin_tab, n_ctx):
    pairs = qkv.shape[1]
    length = 2 * n_ctx * BLOCK
    tile = min(512, length)
    table = pl.BlockSpec((length, HD), lambda i, s: (0, 0))
    return pl.pallas_call(
        functools.partial(attention_back_kernel, n_ctx, tile),
        out_shape=jax.ShapeDtypeStruct((n_ctx, pairs, 3, PAIR, HD), BF),
        grid_spec=pltpu.PrefetchScalarGridSpec(
            num_scalar_prefetch=1,
            grid=(pairs,),
            in_specs=[
                pl.BlockSpec((n_ctx, 1, 3, PAIR, HD), lambda i, s: (0, i, 0, 0, 0)),
                pl.BlockSpec((n_ctx, 1, PAIR, HD), lambda i, s: (0, i, 0, 0)),
                table,
                table,
            ],
            out_specs=pl.BlockSpec((n_ctx, 1, 3, PAIR, HD), lambda i, s: (0, i, 0, 0, 0)),
            scratch_shapes=[pltpu.VMEM((length, HD), BF)] * 4 + [pltpu.VMEM((length, HD), F32)],
        ),
        compiler_params=pltpu.CompilerParams(vmem_limit_bytes=VMEM_LIMIT),
        cost_estimate=pl.CostEstimate(
            flops=pairs * length * length * HD * 2 * 6,
            bytes_accessed=pairs * length * HD * 14,
            transcendentals=pairs * length * length,
        ),
    )(me, qkv, grads, cos_tab, sin_tab)


def mlp_kernel(n_ref, g_ref, wg_ref, wu_ref, wd_ref, h_ref, dgp_ref, dup_ref):
    rows = n_ref[...]
    gate_pre = dot(rows, wg_ref[...])
    up_pre = dot(rows, wu_ref[...])
    hidden_grad = times_transposed(g_ref[...], wd_ref[...])
    gate_sig = 1.0 / (1.0 + jnp.exp2(gate_pre * (-LOG2E)))
    gate_act = gate_pre * gate_sig
    h_ref[...] = (gate_act * up_pre).astype(BF)
    dup_ref[...] = (hidden_grad * gate_act).astype(BF)
    dgp_ref[...] = (hidden_grad * up_pre * (gate_sig * (1.0 + gate_pre * (1.0 - gate_sig)))).astype(BF)


def mlp_core(normed, grads, wg, wu, wd):
    rows, depth = normed.shape
    hidden = wg.shape[1]
    row_tile, tile = 512, 512
    row_block = pl.BlockSpec((row_tile, depth), lambda j, i: (i, 0))
    out_block = pl.BlockSpec((row_tile, tile), lambda j, i: (i, j))
    out = jax.ShapeDtypeStruct((rows, hidden), BF)
    return pl.pallas_call(
        mlp_kernel,
        out_shape=(out, out, out),
        grid=(hidden // tile, rows // row_tile),
        in_specs=[
            row_block,
            row_block,
            pl.BlockSpec((depth, tile), lambda j, i: (0, j)),
            pl.BlockSpec((depth, tile), lambda j, i: (0, j)),
            pl.BlockSpec((tile, depth), lambda j, i: (j, 0)),
        ],
        out_specs=(out_block, out_block, out_block),
        compiler_params=pltpu.CompilerParams(vmem_limit_bytes=VMEM_LIMIT),
        cost_estimate=pl.CostEstimate(
            flops=6 * rows * depth * hidden,
            bytes_accessed=rows * depth * 4 + 6 * depth * hidden + 6 * rows * hidden,
            transcendentals=rows * hidden,
        ),
    )(normed, grads, wg, wu, wd)


def inverse_rms(values):
    return lax.rsqrt(jnp.mean(values * values, axis=-1, keepdims=True) + EPS)


def norm_back(values, gain, grad):
    inv = inverse_rms(values)
    unit = values * inv
    scaled = grad * gain
    back = (scaled - unit * jnp.mean(scaled * unit, axis=-1, keepdims=True)) * inv
    return back, jnp.sum(grad * unit, axis=0)


def core_swap(values, n_ctx):
    return lax.ppermute(values, "ctx", [(i, i ^ 1) for i in range(n_ctx)])


def chain_pairs(n_ctx):
    chips = n_ctx // 2
    mid = chips // 2
    inward = []
    for hop in range(mid - 1):
        pairs = [(hop, hop + 1), (chips - 1 - hop, chips - 2 - hop)]
        inward.append([(2 * a + core, 2 * b + core) for a, b in pairs for core in range(2)])
    across = [(2 * a + core, 2 * b + core) for a, b in ((mid - 1, mid), (mid, mid - 1)) for core in range(2)]
    outward = [[(b, a) for a, b in hop] for hop in reversed(inward)]
    return inward, across, outward


def chain_sum(parts, n_ctx):
    inward, across, outward = chain_pairs(n_ctx)
    stages = [("add", hop) for hop in inward] + [("across", across)] + [("take", hop) for hop in outward]
    chip = lax.axis_index("ctx") // 2
    total = len(parts)
    state = list(parts)
    for slot in range(total + len(stages) - 1):
        moving = []
        for k, (kind, hop) in enumerate(stages):
            at = slot - k
            if 0 <= at < total:
                moving.append((at, k, kind, hop))
        sent = [lax.ppermute(state[at], "ctx", hop) for at, _, _, hop in moving]
        following = slot + 1 if slot + 1 < total else None
        held = lax.optimization_barrier(tuple(sent) + ((state[following],) if following is not None else ()))
        if following is not None:
            state[following] = held[-1]
        for (at, k, kind, hop), got in zip(moving, held):
            if kind == "take":
                edge = len(outward) - (k - len(inward) - 1)
                chips = n_ctx // 2
                receives = (chip == edge - 1) | (chip == chips - edge)
                state[at] = jnp.where(receives, got, state[at])
            else:
                state[at] = (state[at].astype(F32) + got.astype(F32)).astype(BF)
    return state


def body(
    tokens,
    counts,
    norm_gain,
    w_query,
    w_key,
    w_value,
    w_output,
    mlp_gain,
    w_gate,
    w_up,
    w_down,
    cotangent,
):
    n_ctx = lax.axis_size("ctx")
    me = lax.axis_index("ctx")
    rank = lax.axis_index("tp")
    odd = rank & 1
    core = me & 1
    length = 2 * BLOCK * n_ctx
    heads = w_query.shape[1] // HD
    me_ref = jnp.reshape(me, (1,)).astype(jnp.int32)
    gain_one = norm_gain.astype(F32)
    gain_two = mlp_gain.astype(F32)

    inverse = THETA ** (-(jnp.arange(HD // 2, dtype=F32) * (2.0 / HD)))
    angles = jnp.arange(length, dtype=jnp.int32).astype(F32)[:, None] * inverse[None, :]
    cos_half, sin_half = jnp.cos(angles), jnp.sin(angles)
    cos_full = jnp.concatenate([cos_half, cos_half], axis=1)
    sin_full = jnp.concatenate([-sin_half, sin_half], axis=1)

    def own_blocks(table):
        front = lax.dynamic_slice_in_dim(table, me * BLOCK, BLOCK, 0)
        back = lax.dynamic_slice_in_dim(table, (2 * n_ctx - 1 - me) * BLOCK, BLOCK, 0)
        return front, back

    cos_front, cos_back = own_blocks(cos_full)
    sin_front, sin_back = own_blocks(sin_full)
    own_counts = lax.dynamic_index_in_dim(counts, me, 0, keepdims=False)
    offsets = jnp.arange(BLOCK, dtype=jnp.int32)

    def valid_of(sequence, half):
        return (offsets < own_counts[sequence, half]).astype(F32)

    cos_own = jnp.concatenate([cos_front, cos_back])
    sin_own = jnp.concatenate([sin_front, sin_back])
    sequences = counts.shape[1]
    paired = lax.axis_size("tp") == 4 and sequences == 6
    if paired:
        ranks = [rank ^ k for k in range(4)]
        seq_a = [3 * (r >> 1) + 2 * (r & 1) for r in ranks]
        seq_b = [1 + 3 * (r >> 1) for r in ranks]
        valids = {
            "b": jnp.concatenate([valid_of(s, r & 1) for s, r in zip(seq_b, ranks)]),
            "a": jnp.concatenate([valid_of(s, half) for s in seq_a for half in range(2)]),
        }
        flip_back = lambda own: jnp.where(odd == 1, jnp.roll(own, BLOCK, axis=0), own)
        tables = {
            "b": (jnp.tile(flip_back(cos_own), (2, 1)), jnp.tile(flip_back(sin_own), (2, 1))),
            "a": (jnp.tile(cos_own, (4, 1)), jnp.tile(sin_own, (4, 1))),
        }
        swaps = {"b": jnp.reshape(odd, (1,)).astype(jnp.int32), "a": jnp.zeros((1,), jnp.int32)}
        n_pairs = {"b": 2 * heads, "a": 4 * heads}
    else:
        valids = {"a": jnp.concatenate([valid_of(s, half) for s in range(sequences) for half in range(2)])}
        tables = {"a": (jnp.tile(cos_own, (sequences, 1)), jnp.tile(sin_own, (sequences, 1)))}
        swaps = {"a": jnp.zeros((1,), jnp.int32)}
        n_pairs = {"a": sequences * heads}
    names = tuple(n_pairs)

    def own_rows(array):
        if not paired:
            return {"a": array}
        return {
            "b": lax.dynamic_slice_in_dim(array, (1 - odd) * PAIR, BLOCK, 0),
            "a": lax.dynamic_slice_in_dim(array, odd * BLOCK, PAIR, 0),
        }

    def whole_rows(part):
        if not paired:
            return part["a"]
        return jnp.where(odd == 1, jnp.concatenate([part["b"], part["a"]]), jnp.concatenate([part["a"], part["b"]]))

    x_own = {name: rows.astype(F32) for name, rows in own_rows(tokens[0]).items()}
    g_own = own_rows(cotangent[0])

    def to_dest(array, name):
        per = -(-n_pairs[name] // n_ctx)
        short = per * n_ctx - n_pairs[name]
        if short:
            array = jnp.concatenate([array, jnp.zeros((short,) + array.shape[1:], array.dtype)])
        return [lax.dynamic_slice_in_dim(array, (me ^ k) * per, per, 0) for k in range(n_ctx)]

    def from_dest(array, name):
        places = jnp.arange(n_ctx, dtype=jnp.int32) ^ me
        ordered = jnp.take(array, places, axis=0)
        return ordered.reshape((-1,) + array.shape[2:])[: n_pairs[name]]

    def flip(array, name):
        if name != "b":
            return array
        return jnp.where(odd == 1, array[:, ::-1], array)

    def rows_to_pairs(array, name):
        count = n_pairs[name] // heads
        array = flip(array.reshape(count, 2, BLOCK, heads, HD), name)
        return array.reshape(count, PAIR, heads, HD).transpose(0, 2, 1, 3).reshape(-1, PAIR, HD)

    def pairs_to_rows(array, name):
        count = n_pairs[name] // heads
        array = array.reshape(count, heads, PAIR, HD).transpose(0, 2, 1, 3)
        array = flip(array.reshape(count, 2, BLOCK, heads, HD), name)
        return array.reshape(count * PAIR, heads * HD)

    def forward_attention(name, x_rows):
        normed = (x_rows * inverse_rms(x_rows) * gain_one).astype(BF)
        normed_all = gather_rows(normed)
        cos_tab, sin_tab = tables[name]
        valid = jnp.broadcast_to(valids[name][:, None], cos_tab.shape)
        qkv = project_qkv(swaps[name], normed_all, w_query, w_key, w_value, cos_tab, sin_tab, valid)
        got = exchange(to_dest(qkv, name), n_ctx)
        mixed = attention_forward(me_ref, got, n_ctx)
        back = exchange([mixed[k] for k in range(n_ctx)], n_ctx)
        heads_out = pairs_to_rows(from_dest(back, name), name) * valids[name][:, None].astype(BF)
        attn_rows = scatter_rows(dot(heads_out, w_output).astype(BF))
        residual = x_rows + attn_rows
        normed_two = (residual * inverse_rms(residual) * gain_two).astype(BF)
        return normed_all, got, heads_out, residual, gather_rows(normed_two)

    n1, got, heads_out, residual, n2 = ({} for _ in range(5))
    for name in names:
        n1[name], got[name], heads_out[name], residual[name], n2[name] = forward_attention(name, x_own[name])
    cot = {name: gather_rows(g_own[name]) for name in names}

    h, dgp, dup = ({} for _ in range(3))
    for name in names:
        h[name], dgp[name], dup[name] = mlp_core(n2[name], cot[name], w_gate, w_up, w_down)

    def joined(part):
        return jnp.concatenate([part[name] for name in names]) if len(names) > 1 else part[names[0]]

    def halves(left, right):
        left, right = joined(left), joined(right)
        size = left.shape[1] // 2
        mine = lax.dynamic_slice_in_dim(left, core * size, size, 1)
        other = lax.dynamic_slice_in_dim(left, (1 - core) * size, size, 1)
        sent = core_swap(contract_rows(other, right).astype(BF), n_ctx)
        return (contract_rows(mine, right) + sent.astype(F32)).astype(BF)

    sum_down = halves(h, cot)
    sum_gate = halves(n2, dgp)
    sum_up = halves(n2, dup)

    def feed_back(name, dgp, dup, residual, g_rows):
        partial = (times_transposed(dgp, w_gate) + times_transposed(dup, w_up)).astype(BF)
        normed_grad = scatter_rows(partial)
        back, gain_grad = norm_back(residual, gain_two, normed_grad)
        res_grad = g_rows.astype(F32) + back
        return res_grad, gain_grad, gather_rows(res_grad.astype(BF))

    res_grad, gain_two_grad, da = ({} for _ in range(3))
    for name in names:
        res_grad[name], gain_two_grad[name], da[name] = feed_back(
            name, dgp[name], dup[name], residual[name], g_own[name]
        )

    def attention_back(name, da, got):
        heads_grad = times_transposed(da, w_output).astype(BF) * valids[name][:, None].astype(BF)
        there = exchange(to_dest(rows_to_pairs(heads_grad, name), name), n_ctx)
        grads = attention_backward(me_ref, got, there, cos_full, sin_full, n_ctx)
        back = exchange([grads[k] for k in range(n_ctx)], n_ctx)
        back = from_dest(back, name)
        dq, dk, dv = (pairs_to_rows(back[:, which], name) for which in range(3))
        return dq, dk, dv * valids[name][:, None].astype(BF)

    dq, dk, dv = ({} for _ in range(3))
    for name in names:
        dq[name], dk[name], dv[name] = attention_back(name, da[name], got[name])
    sum_out = halves(heads_out, da)
    sum_q = halves(n1, dq)
    sum_k = halves(n1, dk)
    sum_v = halves(n1, dv)

    def input_back(x_rows, res_grad, dq, dk, dv):
        partial = times_transposed(dq, w_query) + times_transposed(dk, w_key) + times_transposed(dv, w_value)
        back, gain_grad = norm_back(x_rows, gain_one, scatter_rows(partial.astype(BF)))
        return (res_grad + back).astype(BF), gain_grad

    input_grad, gain_one_grad = ({} for _ in range(2))
    for name in names:
        input_grad[name], gain_one_grad[name] = input_back(
            x_own[name], res_grad[name], dq[name], dk[name], dv[name]
        )

    def output_rows(h, residual):
        return (residual + scatter_rows(dot(h, w_down).astype(BF))).astype(BF)

    output = {name: output_rows(h[name], residual[name]) for name in names}

    split = lambda array, count: [
        array[k * (array.shape[0] // count) : (k + 1) * (array.shape[0] // count)] for k in range(count)
    ]
    first = chain_sum(split(sum_down, 2) + split(sum_gate, 2) + split(sum_up, 2), n_ctx)
    second = chain_sum([sum_out, sum_q, sum_k, sum_v], n_ctx)

    def join(parts):
        mine = jnp.concatenate(parts) if len(parts) > 1 else parts[0]
        other = core_swap(mine, n_ctx)
        low = jnp.where(core == 0, mine, other).astype(F32)
        high = jnp.where(core == 0, other, mine).astype(F32)
        return jnp.concatenate([low, high])

    gain_sums = lax.psum(jnp.stack([sum(gain_one_grad.values()), sum(gain_two_grad.values())]), ("ctx", "tp"))
    return (
        whole_rows(output)[None],
        whole_rows(input_grad)[None],
        gain_sums[0],
        join(second[1:2]),
        join(second[2:3]),
        join(second[3:4]),
        join(second[0:1]),
        gain_sums[1],
        join(first[2:4]),
        join(first[4:6]),
        join(first[0:2]),
    )


def solution(mesh):
    placed = (
        P("ctx", "tp", None),
        P(),
        P(),
        P(None, "tp"),
        P(None, "tp"),
        P(None, "tp"),
        P("tp", None),
        P(),
        P(None, "tp"),
        P(None, "tp"),
        P("tp", None),
        P("ctx", "tp", None),
    )
    return jax.shard_map(
        body,
        mesh=mesh,
        in_specs=placed,
        out_specs=(
            P("ctx", "tp", None),
            P("ctx", "tp", None),
            P(),
            P(None, "tp"),
            P(None, "tp"),
            P(None, "tp"),
            P("tp", None),
            P(),
            P(None, "tp"),
            P(None, "tp"),
            P("tp", None),
        ),
        check_vma=False,
    )
```

time: 3150 us -> 1690 us (0.54)
  waiting for transfers between devices: 2390 us -> 647 us
  starting transfers between devices: 0.75 us -> 254 us
  matrix products: 421 us -> 192 us
  other arithmetic: 39.5 us -> 194 us
  Pallas kernels: 0 us -> 136 us
  local copies, waits for them, and re-layouts: 233 us -> 169 us
  blocking collectives: 40.6 us -> 81.8 us
    psum x1 -> x0, waiting for transfers between devices: 1290 us -> none  [body(): lax.psum((grad_query, grad_key, grad_value, grad_output_w, grad_gate, gra...]
    reduce_scatter x6 -> x0, waiting for transfers between devices: 697 us -> none  [the longest x1 225 us: body(): lax.psum_scatter(value_rows, 'ctx', scatter_dimension=0, tiled=True)]
    ppermute x0 -> x164, waiting for transfers between devices: none -> 647 us  [the longest x30 295 us: chain_sum(): sent = [lax.ppermute(state[at], 'ctx', hop) for at, _, _, hop in moving]]
    all_gather x6 -> x0, waiting for transfers between devices: 403 us -> none  [the longest x1 99.4 us: body(): lax.all_gather(key_rot, 'ctx', axis=0, tiled=True)]
    ppermute x0 -> x164, starting transfers between devices: none -> 254 us  [the longest x56 108 us: exchange(): lax.ppermute(pieces[k], 'ctx', [(i, i ^ k) for i in range(n_ctx)])]
    dot_general x13 -> x4, matrix products: 233 us -> 23.7 us  [dot(): return jnp.dot(left, right, preferred_element_type=F32)]
    pallas_call x0 -> x8, Pallas kernels: none -> 136 us  [the longest x2 56.7 us: mlp_core(): pl.pallas_call(mlp_kernel, out_shape=(out, out, out), grid=(hidden // til...]
    concatenate x3 -> x34, other arithmetic: 1.45 us -> 72.2 us  [the longest x7 46.4 us: join(): return jnp.concatenate([low, high])]
  transfers between devices with their start and end apart: 13 -> 164, of which waited for: 13 -> 61; matrix products, arithmetic and copies ran while one was open for 11% -> 29% of each run, Pallas kernels for 0% -> 6%
where the time goes in v1:
time: 1690 us; the launch traced here: 1680 us
  waiting for transfers between devices  647 us (38%)
  starting transfers between devices  254 us (15%)
  other arithmetic  194 us (11%)
  matrix products  192 us (11%)
  local copies, waits for them, and re-layouts  169 us (10%)
  Pallas kernels  136 us (8%)
  blocking collectives  81.8 us (5%)
    ppermute x30, waiting for transfers between devices, chain_sum(): sent = [lax.ppermute(state[at], 'ctx', hop) for at, _, _, hop in moving]  295 us
    ppermute x56, waiting for transfers between devices, exchange(): lax.ppermute(pieces[k], 'ctx', [(i, i ^ k) for i in range(n_ctx)])  189 us
    ppermute x32, waiting for transfers between devices, send_y(): return lax.ppermute(values, 'tp', Y_SWAP)  118 us
    ppermute x56, starting transfers between devices, exchange(): lax.ppermute(pieces[k], 'ctx', [(i, i ^ k) for i in range(n_ctx)])  108 us
    dot_general x14, matrix products, contract_rows(): lax.dot_general(left, right, (((0,), (0,)), ((), ())), preferred_element_...  101 us
    unnamed x355, local copies, waits for them, and re-layouts  89.8 us
    psum x1, blocking collectives, body(): lax.psum(jnp.stack([sum(gain_one_grad.values()), sum(gain_two_grad.values...  81.8 us
    ppermute x30, starting transfers between devices, chain_sum(): sent = [lax.ppermute(state[at], 'ctx', hop) for at, _, _, hop in moving]  73.8 us
  transfers between devices with their start and end apart: 164, of which 61 were waited for; matrix products, arithmetic and copies ran while one was open for 29% of the time, Pallas kernels for 6%

profile of v1, /device:TPU:1, one launch (start us, length us, event | category | flops | bytes accessed | tf_op | source)
XLA Modules:
  0.0 1678.6 jit_solution(7834667883109318428)
XLA Ops:
  110.6 11.5 collective-permute-done.8
  196.9 26.5 %collective-permute-done.19 = bf16[64,2048]{1,0:T(8,128)(2,1)S(1)} collective-permute-done((bf16[64,2048]{1,0:T(8,128)(2,1)S(1)}, bf16[64,2048]{1,0:T(8,128)(2,1)S(1)}, u32[]{:S(2)}, u32[]{:S(2)}) %collective-permute-start.19) | collective-permute-done | bytes 262176 | tf_op jit(solution)/shard_map/ppermute | solution.py:42
  249.4 11.6 shard_map.206
  304.3 22.6 %collective-permute-done.42 = bf16[2,3,256,128]{3,2,1,0:T(8,128)(2,1)S(1)} collective-permute-done((bf16[2,3,256,128]{3,2,1,0:T(8,128)(2,1)S(1)}, bf16[2,3,256,128]{3,2,1,0:T(8,128)(2,1)S(1)}, u32[]{:S(2)}, u32[]{:S(2)}) %collective-permute-start.42) | collective-permute-done | bytes 393248 | tf_op jit(solution)/shard_map/ppermute | solution.py:76
  329.2 12.6 shard_map.207
  343.9 15.0 collective-permute-start.46
  363.8 19.7 %shard_map.205 = (bf16[512,2048]{1,0:T(8,128)(2,1)}, bf16[512,2048]{1,0:T(8,128)(2,1)}, bf16[512,2048]{1,0:T(8,128)(2,1)}) custom-call(bf16[512,2048]{1,0:T(8,128)(2,1)} %get-tuple-element.321.n_ref, bf16[512,2048]{1,0:T(8,128)(2,1)} %get-tuple-element.317.g_ref, bf16[2048,2048]{1,0:T(8,128)(2,1)} %wg_ref.3, bf16[2048,2048]{1,0:T(8,128)(2,1)} %wu_ref.3, ...), custom_call_target="tpu_custom_call" | custom-call | flops 12884901888 | bytes 35651584 | tf_op jit(solution)/shard_map/pallas_call | solution.py:305
  450.8 27.0 %collective-permute-done.69 = bf16[64,2048]{1,0:T(8,128)(2,1)S(1)} collective-permute-done((bf16[64,2048]{1,0:T(8,128)(2,1)S(1)}, bf16[64,2048]{1,0:T(8,128)(2,1)S(1)}, u32[]{:S(2)}, u32[]{:S(2)}) %collective-permute-start.69) | collective-permute-done | bytes 262176 | tf_op jit(solution)/shard_map/ppermute | solution.py:42
  542.0 14.6 shard_map.209
  634.3 19.2 %collective-permute-done.57 = bf16[256,2048]{1,0:T(8,128)(2,1)S(1)} collective-permute-done((bf16[256,2048]{1,0:T(8,128)(2,1)S(1)}, bf16[256,2048]{1,0:T(8,128)(2,1)S(1)}, u32[]{:S(2)}, u32[]{:S(2)}) %collective-permute-start.57) | collective-permute-done | bytes 1048608 | tf_op jit(solution)/shard_map/ppermute | solution.py:42
  670.3 37.0 %shard_map.208 = (bf16[1024,2048]{1,0:T(8,128)(2,1)}, bf16[1024,2048]{1,0:T(8,128)(2,1)}, bf16[1024,2048]{1,0:T(8,128)(2,1)}) custom-call(bf16[1024,2048]{1,0:T(8,128)(2,1)} %copy-done.87, bf16[1024,2048]{1,0:T(8,128)(2,1)} %get-tuple-element.271.g_ref, bf16[2048,2048]{1,0:T(8,128)(2,1)} %wg_ref.3, bf16[2048,2048]{1,0:T(8,128)(2,1)} %wu_ref.3, ...), custom_call_target="tpu_custom_call" | custom-call | flops 25769803776 | bytes 46137344 | tf_op jit(solution)/shard_map/pallas_call | solution.py:305
  707.3 14.7 fusion.135
  721.9 12.8 add_convert_fusion.4
  737.7 11.4 convolution_convert_fusion.3
  753.8 11.6 convolution_convert_fusion.2
  771.0 11.9 convolution_convert_fusion.1
  890.7 25.4 %shard_map.210 = bf16[8,2,3,256,128]{4,3,2,1,0:T(8,128)(2,1)} custom-call(s32[1]{0:T(128)} %bitcast.me_ref, bf16[8,2,3,256,128]{4,3,2,1,0:T(8,128)(2,1)} %bitcast_dynamic-update-slice_fusion.11.x_ref, bf16[8,2,256,128]{3,2,1,0:T(8,128)(2,1)} %copy-done.105, f32[2048,128]{1,0:T(8,128)} %get-tuple-element.356.cos_ref, f32[2048,128]{1,0:T(8,128)} %get-tuple-element.357.sin_ref), custom_call_target="tpu_custom_call" | custom-call | flops 12884901888 | bytes 7340032 | tf_op jit(solution)/shard_map/pallas_call | solution.py:262
  934.0 13.2 collective-permute-done.111
  961.4 17.1 %collective-permute-done.113 = bf16[2,3,256,128]{3,2,1,0:T(8,128)(2,1)S(1)} collective-permute-done((bf16[2,3,256,128]{3,2,1,0:T(8,128)(2,1)S(1)}, bf16[2,3,256,128]{3,2,1,0:T(8,128)(2,1)S(1)}, u32[]{:S(2)}, u32[]{:S(2)}) %collective-permute-start.113) | collective-permute-done | bytes 393248 | tf_op jit(solution)/shard_map/ppermute | solution.py:76
  1033.6 15.0 collective-permute-start.141
  1118.1 45.3 %collective-permute-done.121 = bf16[256,2048]{1,0:T(8,128)(2,1)S(1)} collective-permute-done((bf16[256,2048]{1,0:T(8,128)(2,1)S(1)}, bf16[256,2048]{1,0:T(8,128)(2,1)S(1)}, u32[]{:S(2)}, u32[]{:S(2)}) %collective-permute-start.121) | collective-permute-done | bytes 1048608 | tf_op jit(solution)/shard_map/ppermute | solution.py:366
  1194.3 38.1 %collective-permute-done.123 = bf16[1024,512]{1,0:T(8,128)(2,1)S(1)} collective-permute-done((bf16[1024,512]{1,0:T(8,128)(2,1)S(1)}, bf16[1024,512]{1,0:T(8,128)(2,1)S(1)}, u32[]{:S(2)}, u32[]{:S(2)}) %collective-permute-start.123) | collective-permute-done | bytes 1048608 | tf_op jit(solution)/shard_map/ppermute | solution.py:366
  1265.9 46.7 %collective-permute-done.128 = bf16[256,2048]{1,0:T(8,128)(2,1)S(1)} collective-permute-done((bf16[256,2048]{1,0:T(8,128)(2,1)S(1)}, bf16[256,2048]{1,0:T(8,128)(2,1)S(1)}, u32[]{:S(2)}, u32[]{:S(2)}) %collective-permute-start.128) | collective-permute-done | bytes 1048608 | tf_op jit(solution)/shard_map/ppermute | solution.py:366
  1334.1 81.8 %psum.7 = f32[2,2048]{1,0:T(2,128)S(1)} all-reduce(f32[2,2048]{1,0:T(2,128)S(1)} %pad_maximum_fusion.30), channel_id=1, replica_groups=mesh['ctx'=8,'tp'=4] {'ctx','tp'}, use_global_device_ids=true, to_apply=%region_12.13 | all-reduce | flops 4096 | bytes 32768 | tf_op jit(solution)/shard_map/psum | solution.py:594
  1452.1 20.0 %collective-permute-done.155 = bf16[512,2048]{1,0:T(8,128)(2,1)S(1)} collective-permute-done((bf16[512,2048]{1,0:T(8,128)(2,1)S(1)}, bf16[512,2048]{1,0:T(8,128)(2,1)S(1)}, u32[]{:S(2)}, u32[]{:S(2)}) %collective-permute-start.155) | collective-permute-done | bytes 2097184 | tf_op jit(solution)/shard_map/ppermute | solution.py:366
  1472.0 21.5 %collective-permute-done.157 = bf16[512,2048]{1,0:T(8,128)(2,1)S(1)} collective-permute-done((bf16[512,2048]{1,0:T(8,128)(2,1)S(1)}, bf16[512,2048]{1,0:T(8,128)(2,1)S(1)}, u32[]{:S(2)}, u32[]{:S(2)}) %collective-permute-start.157) | collective-permute-done | bytes 2097184 | tf_op jit(solution)/shard_map/ppermute | solution.py:366
  1502.6 13.4 collective-permute-done.137
  1518.7 42.4 %collective-permute-done.160 = bf16[512,2048]{1,0:T(8,128)(2,1)} collective-permute-done((bf16[512,2048]{1,0:T(8,128)(2,1)S(1)}, bf16[512,2048]{1,0:T(8,128)(2,1)}, u32[]{:S(2)}, u32[]{:S(2)}) %collective-permute-start.160) | collective-permute-done | bytes 2097184 | tf_op jit(solution)/shard_map/ppermute | solution.py:366
  1575.0 36.8 %collective-permute-done.161 = bf16[512,2048]{1,0:T(8,128)(2,1)} collective-permute-done((bf16[512,2048]{1,0:T(8,128)(2,1)S(1)}, bf16[512,2048]{1,0:T(8,128)(2,1)}, u32[]{:S(2)}, u32[]{:S(2)}) %collective-permute-start.161) | collective-permute-done | bytes 2097184 | tf_op jit(solution)/shard_map/ppermute | solution.py:366
  1629.6 12.0 maximum_convert_fusion.2
  1648.1 12.0 maximum_convert_fusion
  1666.5 12.0 maximum_convert_fusion.1
  (937 shorter events, 942.3 us)
Async XLA Ops:
  53.2 96.9 %collective-permute-start.28 = (bf16[64,2048]{1,0:T(8,128)(2,1)S(1)}, bf16[64,2048]{1,0:T(8,128)(2,1)S(1)}, u32[]{:S(2)}, u32[]{:S(2)}) collective-permute-start(bf16[64,2048]{1,0:T(8,128)(2,1)S(1)} %slice.694), channel_id=1, source_target_pairs={{0,1},{1,0},{2,3},{3,2},{4,5},{5,4},{6,7},{7,6},{8,9},{9,8},{10,11... | collective-permute-start | bytes 786440 | tf_op jit(solution)/shard_map/ppermute | solution.py:38
  55.2 126.6 %collective-permute-start.29 = (bf16[64,2048]{1,0:T(8,128)(2,1)}, bf16[64,2048]{1,0:T(8,128)(2,1)}, u32[]{:S(2)}, u32[]{:S(2)}) collective-permute-start(bf16[64,2048]{1,0:T(8,128)(2,1)} %slice.695), channel_id=1, source_target_pairs={{0,2},{1,3},{2,0},{3,1},{4,6},{5,7},{6,4},{7,5},{8,10},{9,11},{10,... | collective-permute-start | bytes 786440 | tf_op jit(solution)/shard_map/ppermute | solution.py:42
  81.0 146.1 %collective-permute-start.34 = (bf16[256,2048]{1,0:T(8,128)(2,1)S(1)}, bf16[256,2048]{1,0:T(8,128)(2,1)}, u32[]{:S(2)}, u32[]{:S(2)}) collective-permute-start(bf16[256,2048]{1,0:T(8,128)(2,1)S(1)} %get-tuple-element.112), channel_id=1, source_target_pairs={{0,1},{1,0},{2,3},{3,2},{4,5},{5,4},{6,7},{7,6},{8,9},{9,8},{10,11... | collective-permute-start | bytes 3145736 | tf_op jit(solution)/shard_map/ppermute | solution.py:38
  82.7 143.1 %collective-permute-start.35 = (bf16[256,2048]{1,0:T(8,128)(2,1)S(1)}, bf16[256,2048]{1,0:T(8,128)(2,1)}, u32[]{:S(2)}, u32[]{:S(2)}) collective-permute-start(bf16[256,2048]{1,0:T(8,128)(2,1)S(1)} %get-tuple-element.112), channel_id=1, source_target_pairs={{0,2},{1,3},{2,0},{3,1},{4,6},{5,7},{6,4},{7,5},{8,10},{9,11},{10,... | collective-permute-start | bytes 3145736 | tf_op jit(solution)/shard_map/ppermute | solution.py:42
  343.9 75.0 %collective-permute-start.45 = (bf16[2,256,128]{2,1,0:T(8,128)(2,1)S(1)}, bf16[2,256,128]{2,1,0:T(8,128)(2,1)S(1)}, u32[]{:S(2)}, u32[]{:S(2)}) collective-permute-start(bf16[2,256,128]{2,1,0:T(8,128)(2,1)S(1)} %get-tuple-element.262), channel_id=1, source_target_pairs={{0,4},{4,0},{8,12},{12,8},{16,20},{20,16},{24,28},{28,24},{1,5},{5... | collective-permute-start | bytes 393224 | tf_op jit(solution)/shard_map/ppermute | solution.py:76
  343.9 77.1 %collective-permute-start.46 = (bf16[2,256,128]{2,1,0:T(8,128)(2,1)S(1)}, bf16[2,256,128]{2,1,0:T(8,128)(2,1)S(1)}, u32[]{:S(2)}, u32[]{:S(2)}) collective-permute-start(bf16[2,256,128]{2,1,0:T(8,128)(2,1)S(1)} %get-tuple-element.261), channel_id=1, source_target_pairs={{0,8},{4,12},{8,0},{12,4},{16,24},{20,28},{24,16},{28,20},{1,9},{5... | collective-permute-start | bytes 393224 | tf_op jit(solution)/shard_map/ppermute | solution.py:76
  359.3 66.2 %collective-permute-start.48 = (bf16[2,256,128]{2,1,0:T(8,128)(2,1)S(1)}, bf16[2,256,128]{2,1,0:T(8,128)(2,1)S(1)}, u32[]{:S(2)}, u32[]{:S(2)}) collective-permute-start(bf16[2,256,128]{2,1,0:T(8,128)(2,1)S(1)} %get-tuple-element.259), channel_id=1, source_target_pairs={{0,16},{4,20},{8,24},{12,28},{16,0},{20,4},{24,8},{28,12},{1,17},{... | collective-permute-start | bytes 393224 | tf_op jit(solution)/shard_map/ppermute | solution.py:76
  440.3 119.0 %collective-permute-start.54 = (bf16[256,2048]{1,0:T(8,128)(2,1)}, bf16[256,2048]{1,0:T(8,128)(2,1)}, u32[]{:S(2)}, u32[]{:S(2)}) collective-permute-start(bf16[256,2048]{1,0:T(8,128)(2,1)} %pad_maximum_fusion.7), channel_id=1, source_target_pairs={{0,2},{1,3},{2,0},{3,1},{4,6},{5,7},{6,4},{7,5},{8,10},{9,11},{10,... | collective-permute-start | bytes 3145736 | tf_op jit(solution)/shard_map/ppermute | solution.py:42
  750.5 67.5 %collective-permute-start.66 = (bf16[256,2048]{1,0:T(8,128)(2,1)S(1)}, bf16[256,2048]{1,0:T(8,128)(2,1)S(1)}, u32[]{:S(2)}, u32[]{:S(2)}) collective-permute-start(bf16[256,2048]{1,0:T(8,128)(2,1)S(1)} %pad_maximum_fusion.9), channel_id=1, source_target_pairs={{0,2},{1,3},{2,0},{3,1},{4,6},{5,7},{6,4},{7,5},{8,10},{9,11},{10,... | collective-permute-start | bytes 3145736 | tf_op jit(solution)/shard_map/ppermute | solution.py:42
  765.4 258.7 %collective-permute-start.140 = (bf16[1024,2048]{1,0:T(8,128)(2,1)}, bf16[1024,2048]{1,0:T(8,128)(2,1)}, u32[]{:S(2)}, u32[]{:S(2)}) collective-permute-start(bf16[1024,2048]{1,0:T(8,128)(2,1)} %convolution_convert_fusion.2), channel_id=1, source_target_pairs={{0,4},{4,0},{8,12},{12,8},{16,20},{20,16},{24,28},{28,24},{1,5},{5... | collective-permute-start | bytes 12582920 | tf_op jit(solution)/shard_map/ppermute | solution.py:339
  818.0 215.6 %collective-permute-start.144 = (bf16[1024,2048]{1,0:T(8,128)(2,1)}, bf16[1024,2048]{1,0:T(8,128)(2,1)}, u32[]{:S(2)}, u32[]{:S(2)}) collective-permute-start(bf16[1024,2048]{1,0:T(8,128)(2,1)} %convolution_convert_fusion.1), channel_id=1, source_target_pairs={{0,4},{4,0},{8,12},{12,8},{16,20},{20,16},{24,28},{28,24},{1,5},{5... | collective-permute-start | bytes 12582920 | tf_op jit(solution)/shard_map/ppermute | solution.py:339
  822.4 237.2 %collective-permute-start.151 = (bf16[1024,2048]{1,0:T(8,128)(2,1)}, bf16[1024,2048]{1,0:T(8,128)(2,1)}, u32[]{:S(2)}, u32[]{:S(2)}) collective-permute-start(bf16[1024,2048]{1,0:T(8,128)(2,1)} %convolution_convert_fusion), channel_id=1, source_target_pairs={{0,4},{4,0},{8,12},{12,8},{16,20},{20,16},{24,28},{28,24},{1,5},{5... | collective-permute-start | bytes 12582920 | tf_op jit(solution)/shard_map/ppermute | solution.py:339
  979.3 120.0 %collective-permute-start.120 = (bf16[256,2048]{1,0:T(8,128)(2,1)}, bf16[256,2048]{1,0:T(8,128)(2,1)}, u32[]{:S(2)}, u32[]{:S(2)}) collective-permute-start(bf16[256,2048]{1,0:T(8,128)(2,1)} %convolution_convert_fusion.7), channel_id=1, source_target_pairs={{0,4},{4,0},{8,12},{12,8},{16,20},{20,16},{24,28},{28,24},{1,5},{5... | collective-permute-start | bytes 3145736 | tf_op jit(solution)/shard_map/ppermute | solution.py:339
  1017.2 99.5 %collective-permute-start.116 = (bf16[256,2048]{1,0:T(8,128)(2,1)}, bf16[256,2048]{1,0:T(8,128)(2,1)}, u32[]{:S(2)}, u32[]{:S(2)}) collective-permute-start(bf16[256,2048]{1,0:T(8,128)(2,1)} %pad_maximum_fusion.14), channel_id=1, source_target_pairs={{0,1},{1,0},{2,3},{3,2},{4,5},{5,4},{6,7},{7,6},{8,9},{9,8},{10,11... | collective-permute-start | bytes 3145736 | tf_op jit(solution)/shard_map/ppermute | solution.py:38
  1024.1 82.4 %collective-permute-start.122 = (bf16[1024,512]{1,0:T(8,128)(2,1)}, bf16[1024,512]{1,0:T(8,128)(2,1)}, u32[]{:S(2)}, u32[]{:S(2)}) collective-permute-start(bf16[1024,512]{1,0:T(8,128)(2,1)} %fusion.47), channel_id=1, source_target_pairs={{0,4},{4,0},{8,12},{12,8},{16,20},{20,16},{24,28},{28,24},{1,5},{5... | collective-permute-start | bytes 3145736 | tf_op jit(solution)/shard_map/ppermute | solution.py:339
  1093.0 70.4 %collective-permute-start.142 = (bf16[512,2048]{1,0:T(8,128)(2,1)S(1)}, bf16[512,2048]{1,0:T(8,128)(2,1)S(1)}, u32[]{:S(2)}, u32[]{:S(2)}) collective-permute-start(bf16[512,2048]{1,0:T(8,128)(2,1)S(1)} %get-tuple-element.73), channel_id=1, source_target_pairs={{0,8},{4,12},{24,16},{28,20},{1,9},{5,13},{25,17},{29,21},{2,10},{... | collective-permute-start | bytes 6291464 | tf_op jit(solution)/shard_map/ppermute | solution.py:366
  1163.4 75.4 %collective-permute-start.145 = (bf16[512,2048]{1,0:T(8,128)(2,1)S(1)}, bf16[512,2048]{1,0:T(8,128)(2,1)S(1)}, u32[]{:S(2)}, u32[]{:S(2)}) collective-permute-start(bf16[512,2048]{1,0:T(8,128)(2,1)S(1)} %get-tuple-element.75), channel_id=1, source_target_pairs={{0,8},{4,12},{24,16},{28,20},{1,9},{5,13},{25,17},{29,21},{2,10},{... | collective-permute-start | bytes 6291464 | tf_op jit(solution)/shard_map/ppermute | solution.py:366
  1168.4 70.4 %collective-permute-start.146 = (bf16[512,2048]{1,0:T(8,128)(2,1)S(1)}, bf16[512,2048]{1,0:T(8,128)(2,1)S(1)}, u32[]{:S(2)}, u32[]{:S(2)}) collective-permute-start(bf16[512,2048]{1,0:T(8,128)(2,1)S(1)} %add_convert_fusion.15), channel_id=1, source_target_pairs={{8,16},{12,20},{16,8},{20,12},{9,17},{13,21},{17,9},{21,13},{10,18... | collective-permute-start | bytes 6291464 | tf_op jit(solution)/shard_map/ppermute | solution.py:366
  1170.1 68.8 %collective-permute-start.147 = (bf16[512,2048]{1,0:T(8,128)(2,1)S(1)}, bf16[512,2048]{1,0:T(8,128)(2,1)S(1)}, u32[]{:S(2)}, u32[]{:S(2)}) collective-permute-start(bf16[512,2048]{1,0:T(8,128)(2,1)S(1)} %add_convert_fusion.14), channel_id=1, source_target_pairs={{8,0},{12,4},{16,24},{20,28},{9,1},{13,5},{17,25},{21,29},{10,2},{... | collective-permute-start | bytes 6291464 | tf_op jit(solution)/shard_map/ppermute | solution.py:366
  1240.2 75.7 %collective-permute-start.148 = (bf16[512,2048]{1,0:T(8,128)(2,1)S(1)}, bf16[512,2048]{1,0:T(8,128)(2,1)S(1)}, u32[]{:S(2)}, u32[]{:S(2)}) collective-permute-start(bf16[512,2048]{1,0:T(8,128)(2,1)S(1)} %get-tuple-element.78), channel_id=1, source_target_pairs={{0,8},{4,12},{24,16},{28,20},{1,9},{5,13},{25,17},{29,21},{2,10},{... | collective-permute-start | bytes 6291464 | tf_op jit(solution)/shard_map/ppermute | solution.py:366
  1242.6 73.3 %collective-permute-start.149 = (bf16[512,2048]{1,0:T(8,128)(2,1)S(1)}, bf16[512,2048]{1,0:T(8,128)(2,1)S(1)}, u32[]{:S(2)}, u32[]{:S(2)}) collective-permute-start(bf16[512,2048]{1,0:T(8,128)(2,1)S(1)} %add_convert_fusion.13), channel_id=1, source_target_pairs={{8,16},{12,20},{16,8},{20,12},{9,17},{13,21},{17,9},{21,13},{10,18... | collective-permute-start | bytes 6291464 | tf_op jit(solution)/shard_map/ppermute | solution.py:366
  1244.3 71.6 %collective-permute-start.150 = (bf16[512,2048]{1,0:T(8,128)(2,1)S(1)}, bf16[512,2048]{1,0:T(8,128)(2,1)S(1)}, u32[]{:S(2)}, u32[]{:S(2)}) collective-permute-start(bf16[512,2048]{1,0:T(8,128)(2,1)S(1)} %add_convert_fusion.12), channel_id=1, source_target_pairs={{8,0},{12,4},{16,24},{20,28},{9,1},{13,5},{17,25},{21,29},{10,2},{... | collective-permute-start | bytes 6291464 | tf_op jit(solution)/shard_map/ppermute | solution.py:366
  1314.2 103.8 %collective-permute-start.131 = (bf16[1024,512]{1,0:T(8,128)(2,1)S(1)}, bf16[1024,512]{1,0:T(8,128)(2,1)}, u32[]{:S(2)}, u32[]{:S(2)}) collective-permute-start(bf16[1024,512]{1,0:T(8,128)(2,1)S(1)} %add_convert_fusion.23), channel_id=1, source_target_pairs={{8,16},{12,20},{16,8},{20,12},{9,17},{13,21},{17,9},{21,13},{10,18... | collective-permute-start | bytes 3145736 | tf_op jit(solution)/shard_map/ppermute | solution.py:366
  1315.9 106.2 %collective-permute-start.152 = (bf16[512,2048]{1,0:T(8,128)(2,1)}, bf16[512,2048]{1,0:T(8,128)(2,1)}, u32[]{:S(2)}, u32[]{:S(2)}) collective-permute-start(bf16[512,2048]{1,0:T(8,128)(2,1)} %get-tuple-element.81), channel_id=1, source_target_pairs={{0,8},{4,12},{24,16},{28,20},{1,9},{5,13},{25,17},{29,21},{2,10},{... | collective-permute-start | bytes 6291464 | tf_op jit(solution)/shard_map/ppermute | solution.py:366
  1321.5 101.9 %collective-permute-start.153 = (bf16[512,2048]{1,0:T(8,128)(2,1)}, bf16[512,2048]{1,0:T(8,128)(2,1)}, u32[]{:S(2)}, u32[]{:S(2)}) collective-permute-start(bf16[512,2048]{1,0:T(8,128)(2,1)} %add_convert_fusion.11), channel_id=1, source_target_pairs={{8,16},{12,20},{16,8},{20,12},{9,17},{13,21},{17,9},{21,13},{10,18... | collective-permute-start | bytes 6291464 | tf_op jit(solution)/shard_map/ppermute | solution.py:366
  1324.3 99.1 %collective-permute-start.154 = (bf16[512,2048]{1,0:T(8,128)(2,1)S(1)}, bf16[512,2048]{1,0:T(8,128)(2,1)}, u32[]{:S(2)}, u32[]{:S(2)}) collective-permute-start(bf16[512,2048]{1,0:T(8,128)(2,1)S(1)} %add_convert_fusion.10), channel_id=1, source_target_pairs={{8,0},{12,4},{16,24},{20,28},{9,1},{13,5},{17,25},{21,29},{10,2},{... | collective-permute-start | bytes 6291464 | tf_op jit(solution)/shard_map/ppermute | solution.py:366
  1332.8 86.7 %collective-permute-start.132 = (bf16[1024,512]{1,0:T(8,128)(2,1)}, bf16[1024,512]{1,0:T(8,128)(2,1)}, u32[]{:S(2)}, u32[]{:S(2)}) collective-permute-start(bf16[1024,512]{1,0:T(8,128)(2,1)} %add_convert_fusion.22), channel_id=1, source_target_pairs={{8,0},{12,4},{16,24},{20,28},{9,1},{13,5},{17,25},{21,29},{10,2},{... | collective-permute-start | bytes 3145736 | tf_op jit(solution)/shard_map/ppermute | solution.py:366
  1448.7 123.0 %collective-permute-start.136 = (bf16[1024,512]{1,0:T(8,128)(2,1)S(1)}, bf16[1024,512]{1,0:T(8,128)(2,1)}, u32[]{:S(2)}, u32[]{:S(2)}) collective-permute-start(bf16[1024,512]{1,0:T(8,128)(2,1)S(1)} %broadcast_select_fusion.17), channel_id=1, source_target_pairs={{0,4},{4,0},{8,12},{12,8},{16,20},{20,16},{24,28},{28,24},{1,5},{5... | collective-permute-start | bytes 3145736 | tf_op jit(solution)/shard_map/ppermute | solution.py:339
  1450.6 65.4 %collective-permute-start.137 = (bf16[1024,512]{1,0:T(8,128)(2,1)S(1)}, bf16[1024,512]{1,0:T(8,128)(2,1)S(1)}, u32[]{:S(2)}, u32[]{:S(2)}) collective-permute-start(bf16[1024,512]{1,0:T(8,128)(2,1)S(1)} %add_convert_fusion.19), channel_id=1, source_target_pairs={{8,0},{12,4},{16,24},{20,28},{9,1},{13,5},{17,25},{21,29},{10,2},{... | collective-permute-start | bytes 3145736 | tf_op jit(solution)/shard_map/ppermute | solution.py:366
  1516.1 104.5 %collective-permute-start.138 = (bf16[1024,512]{1,0:T(8,128)(2,1)S(1)}, bf16[1024,512]{1,0:T(8,128)(2,1)}, u32[]{:S(2)}, u32[]{:S(2)}) collective-permute-start(bf16[1024,512]{1,0:T(8,128)(2,1)S(1)} %broadcast_select_fusion.16), channel_id=1, source_target_pairs={{0,4},{4,0},{8,12},{12,8},{16,20},{20,16},{24,28},{28,24},{1,5},{5... | collective-permute-start | bytes 3145736 | tf_op jit(solution)/shard_map/ppermute | solution.py:339
  1518.6 106.0 %collective-permute-start.163 = (bf16[1024,2048]{1,0:T(8,128)(2,1)S(1)}, bf16[1024,2048]{1,0:T(8,128)(2,1)S(1)}, u32[]{:S(2)}, u32[]{:S(2)}) collective-permute-start(bf16[1024,2048]{1,0:T(8,128)(2,1)S(1)} %pad_maximum_fusion.2), channel_id=1, source_target_pairs={{0,4},{4,0},{8,12},{12,8},{16,20},{20,16},{24,28},{28,24},{1,5},{5... | collective-permute-start | bytes 12582920 | tf_op jit(solution)/shard_map/ppermute | solution.py:339
  1570.8 70.8 %collective-permute-start.158 = (bf16[1024,2048]{1,0:T(8,128)(2,1)}, bf16[1024,2048]{1,0:T(8,128)(2,1)}, u32[]{:S(2)}, u32[]{:S(2)}) collective-permute-start(bf16[1024,2048]{1,0:T(8,128)(2,1)} %pad_maximum_fusion), channel_id=1, source_target_pairs={{0,4},{4,0},{8,12},{12,8},{16,20},{20,16},{24,28},{28,24},{1,5},{5... | collective-permute-start | bytes 12582920 | tf_op jit(solution)/shard_map/ppermute | solution.py:339
  (260 other events, 5681.9 us)

commit v2 on v1

v2 whole, which is shorter than its diff:
```python
import functools
import math

import jax
import jax.numpy as jnp
from jax import lax
from jax.experimental import pallas as pl
from jax.experimental.pallas import tpu as pltpu
from jax.sharding import PartitionSpec as P

HD = 128
BLOCK = 128
PAIR = 2 * BLOCK
EPS = 1e-05
THETA = 10000.0
LOG2E = 1.4426950408889634
BF = jnp.bfloat16
F32 = jnp.float32
VMEM_LIMIT = 58 * 1024 * 1024

X_SWAP = [(i, i ^ 1) for i in range(4)]
Y_SWAP = [(i, i ^ 2) for i in range(4)]


def dot(left, right):
    return jnp.dot(left, right, preferred_element_type=F32)


def contract_rows(left, right):
    return lax.dot_general(left, right, (((0,), (0,)), ((), ())), preferred_element_type=F32)


def times_transposed(left, right):
    return lax.dot_general(left, right, (((1,), (1,)), ((), ())), preferred_element_type=F32)


def send_x(values):
    return lax.ppermute(values, "tp", X_SWAP)


def send_y(values):
    return lax.ppermute(values, "tp", Y_SWAP)


def by_four():
    return lax.axis_size("tp") == 4


def gather_first(own):
    if not by_four():
        return (lax.all_gather(own, "tp", axis=0, tiled=True),)
    return own, send_x(own), send_y(own)


def gather_second(held):
    if len(held) == 1:
        return held
    own, from_x, from_y = held
    half = own.shape[0] // 2
    return own, from_x, from_y, send_x(from_y[:half]), send_y(from_x[half:])


def gathered(held):
    return jnp.concatenate(held) if len(held) > 1 else held[0]


def scatter_parts(partial):
    if not by_four():
        return (partial,)
    rows = partial.shape[0] // 4
    half = rows // 2
    at = lambda first: partial[first * half : (first + 1) * half]
    return (
        jnp.concatenate([at(2), at(6)]),
        jnp.concatenate([at(5), at(7)]),
        jnp.concatenate([at(0), at(1), at(4), at(3)]),
    )


def scatter_first(parts):
    if len(parts) == 1:
        return (lax.psum_scatter(parts[0], "tp", scatter_dimension=0, tiled=True),)
    return send_x(parts[0]), send_y(parts[1]), parts[2]


def add_low(left, right):
    return (left.astype(F32) + right.astype(F32)).astype(BF)


def scatter_second(held):
    if len(held) == 1:
        return held
    from_x, from_y, stay = held
    half = from_x.shape[0] // 2
    low_rest = send_y(add_low(stay[2 * half : 3 * half], from_x[half:]))
    high_rest = send_x(add_low(stay[3 * half :], from_y[half:]))
    return from_x, from_y, stay, low_rest, high_rest


def scattered(held):
    if len(held) == 1:
        return held[0].astype(F32)
    from_x, from_y, stay, low_rest, high_rest = (part.astype(F32) for part in held)
    half = low_rest.shape[0]
    low = stay[:half] + from_x[:half] + low_rest
    high = stay[half : 2 * half] + from_y[:half] + high_rest
    return jnp.concatenate([low, high])


def exchange(pieces, places, n_ctx):
    got = {}
    for k in places:
        got[k] = pieces[k] if k == 0 else lax.ppermute(pieces[k], "ctx", [(i, i ^ k) for i in range(n_ctx)])
    return got


def params():
    return pltpu.CompilerParams(vmem_limit_bytes=VMEM_LIMIT)


def whole(shape):
    return pl.BlockSpec(shape, lambda *_: (0,) * len(shape))


def put_partial(refs, first, value, rows):
    if len(refs) == 1:
        refs[0][first : first + value.shape[0], :] = value
        return
    to_x, to_y, stay = refs
    half = rows // 2
    homes = {
        0: (stay, 0), 1: (stay, 1), 2: (to_x, 0), 3: (stay, 3), 4: (stay, 2), 5: (to_y, 0), 6: (to_x, 1), 7: (to_y, 1)
    }
    for part in range(value.shape[0] // half):
        ref, place = homes[first // half + part]
        ref[place * half : (place + 1) * half, :] = value[part * half : (part + 1) * half]


def partial_shapes(rows, width, split):
    if not split:
        return [jax.ShapeDtypeStruct((rows, width), BF)]
    return [jax.ShapeDtypeStruct((rows // 4, width), BF)] * 2 + [jax.ShapeDtypeStruct((rows // 2, width), BF)]


def per_device(pairs, n_ctx):
    return -(-pairs // n_ctx)


def halves_at(swap):
    first = pl.multiple_of(swap * BLOCK, BLOCK)
    second = pl.multiple_of((1 - swap) * BLOCK, BLOCK)
    return pl.ds(first, BLOCK), pl.ds(second, BLOCK)


def qkv_kernel(n_ctx, pairs, scalar_ref, n_ref, wq_ref, wk_ref, wv_ref, cos_ref, sin_ref, valid_ref, *rest):
    out_refs, buffer = rest[:n_ctx], rest[n_ctx]
    rows = n_ref[...]
    first, second = halves_at(scalar_ref[1])
    me = scalar_ref[0]
    cos_tab = cos_ref[...]
    sin_tab = sin_ref[...]
    heads = wq_ref.shape[1] // HD
    step = pl.program_id(0)
    per = out_refs[0].shape[0]
    for pair in range(pairs, per * n_ctx):
        buffer[pair] = jnp.zeros(buffer.shape[1:], BF)
    for which, w_ref in enumerate((wq_ref, wk_ref, wv_ref)):
        product = dot(rows, w_ref[...])
        for head in range(heads):
            part = product[:, head * HD : (head + 1) * HD]
            if which < 2:
                part = part * cos_tab + pltpu.roll(part, HD // 2, 1) * sin_tab
            else:
                part = part * valid_ref[...]
            part = part.astype(BF)
            buffer[step * heads + head, which, first, :] = part[:BLOCK]
            buffer[step * heads + head, which, second, :] = part[BLOCK:]

    @pl.when(step == pl.num_programs(0) - 1)
    def _():
        for k in range(n_ctx):
            source = jnp.bitwise_xor(me, k)
            for p in range(per):
                out_refs[k][p] = buffer[source * per + p]


def project_qkv(scalars, normed, wq, wk, wv, cos_tab, sin_tab, valid, n_ctx):
    rows, depth = normed.shape
    width = wq.shape[1]
    heads = width // HD
    steps = rows // PAIR
    per = per_device(steps * heads, n_ctx)
    row_block = pl.BlockSpec((PAIR, HD), lambda i, s: (i, 0))
    weight = whole((depth, width))
    piece = (per, 3, PAIR, HD)
    return pl.pallas_call(
        functools.partial(qkv_kernel, n_ctx, steps * heads),
        out_shape=[jax.ShapeDtypeStruct(piece, BF)] * n_ctx,
        grid_spec=pltpu.PrefetchScalarGridSpec(
            num_scalar_prefetch=1,
            grid=(steps,),
            in_specs=[
                pl.BlockSpec((PAIR, depth), lambda i, s: (i, 0)),
                weight,
                weight,
                weight,
                row_block,
                row_block,
                row_block,
            ],
            out_specs=[whole(piece)] * n_ctx,
            scratch_shapes=[pltpu.VMEM((per * n_ctx, 3, PAIR, HD), BF)],
        ),
        compiler_params=params(),
        cost_estimate=pl.CostEstimate(
            flops=6 * rows * depth * width, bytes_accessed=rows * depth * 2 + 6 * depth * width, transcendentals=0
        ),
    )(scalars, normed, wq, wk, wv, cos_tab, sin_tab, valid)


def out_kernel(n_ctx, pairs, scalar_ref, *refs):
    piece_refs, (w_ref, valid_ref), (heads_ref, *partial_refs), buffer = (
        refs[:n_ctx],
        refs[n_ctx : n_ctx + 2],
        refs[n_ctx + 2 : -1],
        refs[-1],
    )
    me = scalar_ref[0]
    first, second = halves_at(scalar_ref[1])
    per = piece_refs[0].shape[0]
    heads = w_ref.shape[0] // HD
    for k in range(n_ctx):
        source = jnp.bitwise_xor(me, k)
        for p in range(per):
            buffer[source * per + p] = piece_refs[k][p]
    weight = w_ref[...]
    for sequence in range(pairs // heads):
        at = slice(sequence * PAIR, (sequence + 1) * PAIR)
        rows = jnp.concatenate(
            [
                jnp.concatenate(
                    [buffer[sequence * heads + head, first, :], buffer[sequence * heads + head, second, :]], axis=0
                )
                for head in range(heads)
            ],
            axis=1,
        )
        rows = rows * valid_ref[at, :]
        heads_ref[at, :] = rows
        put_partial(partial_refs, sequence * PAIR, dot(rows, weight).astype(BF), pairs // heads * PAIR // 4)


def project_out(scalars, pieces, weight, valid, pairs, n_ctx, split):
    width, depth = weight.shape
    rows = valid.shape[0]
    per = pieces[0].shape[0]
    shapes = [jax.ShapeDtypeStruct((rows, width), BF)] + partial_shapes(rows, depth, split)
    return pl.pallas_call(
        functools.partial(out_kernel, n_ctx, pairs),
        out_shape=shapes,
        grid_spec=pltpu.PrefetchScalarGridSpec(
            num_scalar_prefetch=1,
            grid=(1,),
            in_specs=[whole(piece.shape) for piece in pieces] + [whole(weight.shape), whole(valid.shape)],
            out_specs=[whole(shape.shape) for shape in shapes],
            scratch_shapes=[pltpu.VMEM((per * n_ctx, PAIR, HD), BF)],
        ),
        compiler_params=params(),
        cost_estimate=pl.CostEstimate(
            flops=2 * rows * depth * width, bytes_accessed=rows * depth * 2 + 2 * depth * width, transcendentals=0
        ),
    )(scalars, *pieces, weight, valid)


def heads_back_kernel(n_ctx, scalar_ref, da_ref, w_ref, valid_ref, *rest):
    out_refs, buffer = rest[:n_ctx], rest[n_ctx]
    me = scalar_ref[0]
    first, second = halves_at(scalar_ref[1])
    per = out_refs[0].shape[0]
    heads = w_ref.shape[0] // HD
    weight = w_ref[...]
    for pair in range(da_ref.shape[0] // PAIR * heads, per * n_ctx):
        buffer[pair] = jnp.zeros(buffer.shape[1:], BF)
    for sequence in range(da_ref.shape[0] // PAIR):
        at = slice(sequence * PAIR, (sequence + 1) * PAIR)
        grad = times_transposed(da_ref[at, :], weight).astype(BF) * valid_ref[at, :]
        for head in range(heads):
            part = grad[:, head * HD : (head + 1) * HD]
            buffer[sequence * heads + head, first, :] = part[:BLOCK]
            buffer[sequence * heads + head, second, :] = part[BLOCK:]
    for k in range(n_ctx):
        source = jnp.bitwise_xor(me, k)
        for p in range(per):
            out_refs[k][p] = buffer[source * per + p]


def heads_back(scalars, da, weight, valid, n_ctx):
    rows, depth = da.shape
    width = weight.shape[0]
    per = per_device(rows // PAIR * (width // HD), n_ctx)
    piece = (per, PAIR, HD)
    return pl.pallas_call(
        functools.partial(heads_back_kernel, n_ctx),
        out_shape=[jax.ShapeDtypeStruct(piece, BF)] * n_ctx,
        grid_spec=pltpu.PrefetchScalarGridSpec(
            num_scalar_prefetch=1,
            grid=(1,),
            in_specs=[whole(da.shape), whole(weight.shape), whole(valid.shape)],
            out_specs=[whole(piece)] * n_ctx,
            scratch_shapes=[pltpu.VMEM((per * n_ctx, PAIR, HD), BF)],
        ),
        compiler_params=params(),
        cost_estimate=pl.CostEstimate(
            flops=2 * rows * depth * width, bytes_accessed=rows * depth * 2 + 2 * depth * width, transcendentals=0
        ),
    )(scalars, da, weight, valid)


def in_kernel(n_ctx, pairs, scalar_ref, *refs):
    piece_refs, weight_refs, valid_ref = refs[:n_ctx], refs[n_ctx : n_ctx + 3], refs[n_ctx + 3]
    grad_refs, partial_refs, buffer = refs[n_ctx + 4 : n_ctx + 7], refs[n_ctx + 7 : -1], refs[-1]
    me = scalar_ref[0]
    first, second = halves_at(scalar_ref[1])
    per = piece_refs[0].shape[0]
    heads = weight_refs[0].shape[1] // HD
    for k in range(n_ctx):
        source = jnp.bitwise_xor(me, k)
        for p in range(per):
            buffer[source * per + p] = piece_refs[k][p]
    for sequence in range(pairs // heads):
        at = slice(sequence * PAIR, (sequence + 1) * PAIR)
        total = None
        for which in range(3):
            rows = jnp.concatenate(
                [
                    jnp.concatenate([buffer[pair, which, first, :], buffer[pair, which, second, :]], axis=0)
                    for pair in range(sequence * heads, (sequence + 1) * heads)
                ],
                axis=1,
            )
            if which == 2:
                rows = rows * valid_ref[at, :]
            grad_refs[which][at, :] = rows
            product = times_transposed(rows, weight_refs[which][...])
            total = product if total is None else total + product
        put_partial(partial_refs, sequence * PAIR, total.astype(BF), pairs // heads * PAIR // 4)


def project_in(scalars, pieces, weights, valid, pairs, n_ctx, split):
    depth, width = weights[0].shape
    rows = valid.shape[0]
    per = pieces[0].shape[0]
    shapes = [jax.ShapeDtypeStruct((rows, width), BF)] * 3 + partial_shapes(rows, depth, split)
    return pl.pallas_call(
        functools.partial(in_kernel, n_ctx, pairs),
        out_shape=shapes,
        grid_spec=pltpu.PrefetchScalarGridSpec(
            num_scalar_prefetch=1,
            grid=(1,),
            in_specs=[whole(piece.shape) for piece in pieces]
            + [whole(weight.shape) for weight in weights]
            + [whole(valid.shape)],
            out_specs=[whole(shape.shape) for shape in shapes],
            scratch_shapes=[pltpu.VMEM((per * n_ctx, 3, PAIR, HD), BF)],
        ),
        compiler_params=params(),
        cost_estimate=pl.CostEstimate(
            flops=6 * rows * depth * width, bytes_accessed=rows * depth * 2 + 6 * depth * width, transcendentals=0
        ),
    )(scalars, *pieces, *weights, valid)


def both_places(me, k, n_ctx):
    source = jnp.bitwise_xor(me, k)
    front = pl.multiple_of(source * BLOCK, BLOCK)
    back = pl.multiple_of((2 * n_ctx - 1 - source) * BLOCK, BLOCK)
    return pl.ds(front, BLOCK), pl.ds(back, BLOCK)


def attention_kernel(n_ctx, tile, scalar_ref, *refs):
    x_refs, o_refs, (qs, ks, vs, os) = refs[:n_ctx], refs[n_ctx : 2 * n_ctx], refs[2 * n_ctx :]
    me = scalar_ref[0]
    length = 2 * n_ctx * BLOCK
    for k in range(n_ctx):
        front, back = both_places(me, k, n_ctx)
        for which, dest in enumerate((qs, ks, vs)):
            dest[front, :] = x_refs[k][0, which, :BLOCK, :]
            dest[back, :] = x_refs[k][0, which, BLOCK:, :]
    factor = -(HD ** (-0.5)) * LOG2E
    shift = math.log(length) * LOG2E
    row_at = lax.broadcasted_iota(jnp.int32, (tile, tile), 0)
    col_at = lax.broadcasted_iota(jnp.int32, (tile, tile), 1)
    for i in range(length // tile):
        query = qs[i * tile : (i + 1) * tile, :]

        def part(j, masked):
            at = pl.ds(pl.multiple_of(j * tile, tile), tile)
            raw = times_transposed(query, ks[at, :])
            prob = 1.0 / (1.0 + jnp.exp2(raw * factor + shift))
            if masked:
                prob = jnp.where(row_at >= col_at, prob, 0.0)
            return dot(prob.astype(BF), vs[at, :])

        total = part(i, True)
        if i > 0:
            total = lax.fori_loop(0, i, lambda j, acc: acc + part(j, False), total)
        os[i * tile : (i + 1) * tile, :] = total.astype(BF)
    for k in range(n_ctx):
        front, back = both_places(me, k, n_ctx)
        o_refs[k][0, :BLOCK, :] = os[front, :]
        o_refs[k][0, BLOCK:, :] = os[back, :]


def attention_forward(scalars, pieces, n_ctx):
    pairs = pieces[0].shape[0]
    length = 2 * n_ctx * BLOCK
    tile = min(512, length)
    return pl.pallas_call(
        functools.partial(attention_kernel, n_ctx, tile),
        out_shape=[jax.ShapeDtypeStruct((pairs, PAIR, HD), BF)] * n_ctx,
        grid_spec=pltpu.PrefetchScalarGridSpec(
            num_scalar_prefetch=1,
            grid=(pairs,),
            in_specs=[pl.BlockSpec((1, 3, PAIR, HD), lambda i, s: (i, 0, 0, 0))] * n_ctx,
            out_specs=[pl.BlockSpec((1, PAIR, HD), lambda i, s: (i, 0, 0))] * n_ctx,
            scratch_shapes=[pltpu.VMEM((length, HD), BF)] * 4,
        ),
        compiler_params=params(),
        cost_estimate=pl.CostEstimate(
            flops=pairs * length * length * HD * 6,
            bytes_accessed=pairs * length * HD * 8,
            transcendentals=pairs * length * length,
        ),
    )(scalars, *pieces)


def attention_back_kernel(n_ctx, tile, scalar_ref, *refs):
    x_refs, g_refs, (cos_ref, sin_ref) = refs[:n_ctx], refs[n_ctx : 2 * n_ctx], refs[2 * n_ctx : 2 * n_ctx + 2]
    out_refs = refs[2 * n_ctx + 2 : 3 * n_ctx + 2]
    qs, ks, vs, gs, os, dqs = refs[3 * n_ctx + 2 :]
    me = scalar_ref[0]
    length = 2 * n_ctx * BLOCK
    for k in range(n_ctx):
        front, back = both_places(me, k, n_ctx)
        for which, dest in enumerate((qs, ks, vs)):
            dest[front, :] = x_refs[k][0, which, :BLOCK, :]
            dest[back, :] = x_refs[k][0, which, BLOCK:, :]
        gs[front, :] = g_refs[k][0, :BLOCK, :]
        gs[back, :] = g_refs[k][0, BLOCK:, :]
    scale = HD ** (-0.5)
    factor = -scale * LOG2E
    shift = math.log(length) * LOG2E
    count = length // tile
    key_at = lax.broadcasted_iota(jnp.int32, (tile, tile), 0)
    query_at = lax.broadcasted_iota(jnp.int32, (tile, tile), 1)
    dqs[...] = jnp.zeros_like(dqs)

    def unrotate(values, at):
        return (values * cos_ref[at, :] - pltpu.roll(values, HD // 2, 1) * sin_ref[at, :]).astype(BF)

    for j in range(count):
        own = slice(j * tile, (j + 1) * tile)
        keys = ks[own, :]
        values = vs[own, :]

        def part(i, masked):
            at = pl.ds(pl.multiple_of(i * tile, tile), tile)
            query = qs[at, :]
            grad = gs[at, :]
            raw = times_transposed(keys, query)
            prob = 1.0 / (1.0 + jnp.exp2(raw * factor + shift))
            if masked:
                prob = jnp.where(query_at >= key_at, prob, 0.0)
            prob_grad = times_transposed(values, grad)
            score_grad = (prob_grad * prob * (1.0 - prob)).astype(BF)
            dqs[at, :] += contract_rows(score_grad, keys)
            return dot(score_grad, query), dot(prob.astype(BF), grad)

        total = part(j, True)
        if j + 1 < count:

            def step(i, acc):
                more = part(i, False)
                return acc[0] + more[0], acc[1] + more[1]

            total = lax.fori_loop(j + 1, count, step, total)
        os[1, own, :] = unrotate(total[0] * scale, own)
        os[2, own, :] = total[1].astype(BF)
    for i in range(count):
        at = slice(i * tile, (i + 1) * tile)
        os[0, at, :] = unrotate(dqs[at, :] * scale, at)
    for k in range(n_ctx):
        front, back = both_places(me, k, n_ctx)
        for which in range(3):
            out_refs[k][0, which, :BLOCK, :] = os[which, front, :]
            out_refs[k][0, which, BLOCK:, :] = os[which, back, :]


def attention_backward(scalars, pieces, grads, cos_tab, sin_tab, n_ctx):
    pairs = pieces[0].shape[0]
    length = 2 * n_ctx * BLOCK
    tile = min(512, length)
    three = pl.BlockSpec((1, 3, PAIR, HD), lambda i, s: (i, 0, 0, 0))
    one = pl.BlockSpec((1, PAIR, HD), lambda i, s: (i, 0, 0))
    return pl.pallas_call(
        functools.partial(attention_back_kernel, n_ctx, tile),
        out_shape=[jax.ShapeDtypeStruct((pairs, 3, PAIR, HD), BF)] * n_ctx,
        grid_spec=pltpu.PrefetchScalarGridSpec(
            num_scalar_prefetch=1,
            grid=(pairs,),
            in_specs=[three] * n_ctx + [one] * n_ctx + [whole((length, HD))] * 2,
            out_specs=[three] * n_ctx,
            scratch_shapes=[pltpu.VMEM((length, HD), BF)] * 4
            + [pltpu.VMEM((3, length, HD), BF), pltpu.VMEM((length, HD), F32)],
        ),
        compiler_params=params(),
        cost_estimate=pl.CostEstimate(
            flops=pairs * length * length * HD * 12,
            bytes_accessed=pairs * length * HD * 14,
            transcendentals=pairs * length * length,
        ),
    )(scalars, *pieces, *grads, cos_tab, sin_tab)


def mlp_kernel(n_ref, g_ref, wg_ref, wu_ref, wd_ref, *rest):
    h_ref, dgp_ref, dup_ref = rest[-3:]
    rows = n_ref[...]
    gate_pre = dot(rows, wg_ref[...])
    up_pre = dot(rows, wu_ref[...])
    hidden_grad = times_transposed(g_ref[...], wd_ref[...])
    gate_sig = 1.0 / (1.0 + jnp.exp2(gate_pre * (-LOG2E)))
    gate_act = gate_pre * gate_sig
    h_ref[...] = (gate_act * up_pre).astype(BF)
    dup_ref[...] = (hidden_grad * gate_act).astype(BF)
    dgp_ref[...] = (hidden_grad * up_pre * (gate_sig * (1.0 + gate_pre * (1.0 - gate_sig)))).astype(BF)


def mlp_core(normed, grads, wg, wu, wd, total, first, held=()):
    rows, depth = normed.shape
    hidden = wg.shape[1]
    row_tile, tile = 512, 512
    skip = first // row_tile
    row_block = pl.BlockSpec((row_tile, depth), lambda j, i: (i, 0))
    out_block = pl.BlockSpec((row_tile, tile), lambda j, i: (i + skip, j))
    out = jax.ShapeDtypeStruct((total, hidden), BF)
    return pl.pallas_call(
        mlp_kernel,
        out_shape=(out, out, out),
        grid=(hidden // tile, rows // row_tile),
        in_specs=[
            row_block,
            row_block,
            pl.BlockSpec((depth, tile), lambda j, i: (0, j)),
            pl.BlockSpec((depth, tile), lambda j, i: (0, j)),
            pl.BlockSpec((tile, depth), lambda j, i: (j, 0)),
        ]
        + [pl.BlockSpec(memory_space=pl.ANY)] * len(held),
        out_specs=(out_block, out_block, out_block),
        input_output_aliases={5 + k: k for k in range(len(held))},
        compiler_params=params(),
        cost_estimate=pl.CostEstimate(
            flops=6 * rows * depth * hidden,
            bytes_accessed=rows * depth * 4 + 6 * depth * hidden + 6 * rows * hidden,
            transcendentals=rows * hidden,
        ),
    )(normed, grads, wg, wu, wd, *held)


def inverse_rms(values):
    return lax.rsqrt(jnp.mean(values * values, axis=-1, keepdims=True) + EPS)


def neighbours():
    index, rank = lax.axis_index("ctx"), lax.axis_index("tp")
    return (index, jnp.bitwise_xor(rank, 1)), (index, jnp.bitwise_xor(rank, 2))


def remote(source, dest, send_sem, recv_sem, device):
    return pltpu.make_async_remote_copy(
        src_ref=source,
        dst_ref=dest,
        send_sem=send_sem,
        recv_sem=recv_sem,
        device_id=device,
        device_id_type=pl.DeviceIdType.MESH,
    )


def signal(sem, device):
    pl.semaphore_signal(sem, inc=1, device_id=device, device_id_type=pl.DeviceIdType.MESH)


class Scatter:
    def __init__(self, partial, groups, bufs, sems):
        self.partial, self.groups = partial, groups
        self.from_x, self.from_y, self.stay, self.stay_y, self.stay_x, self.for_y, self.for_x, self.low, self.high = bufs
        self.first_send, self.first_recv, self.second_send, self.second_recv, self.load_sem = sems
        self.to_x, self.to_y = neighbours()

    @staticmethod
    def scratch(rows, width):
        dma = pltpu.SemaphoreType.DMA
        whole_rows, half_rows = pltpu.VMEM((rows, width), BF), pltpu.VMEM((rows // 2, width), BF)
        return [whole_rows] * 3 + [half_rows] * 6 + [dma((8,)), dma((8,)), dma((4,)), dma((4,)), dma((6,))]

    def first_copies(self, g):
        base, rows, own = self.groups[g]
        half = rows // 2
        part = lambda number: self.partial.at[pl.ds(base + number * half, half)]
        at = lambda buf, number: buf.at[pl.ds(own + number * half, half)]
        plan = [
            (part(2), at(self.from_x, 0), self.to_x),
            (part(6), at(self.from_x, 1), self.to_x),
            (part(5), at(self.from_y, 0), self.to_y),
            (part(7), at(self.from_y, 1), self.to_y),
        ]
        return [
            remote(source, dest, self.first_send.at[4 * g + k], self.first_recv.at[4 * g + k], device)
            for k, (source, dest, device) in enumerate(plan)
        ]

    def loads(self, g):
        base, rows, own = self.groups[g]
        half = rows // 2
        copy = lambda number, count, dest, k: pltpu.make_async_copy(
            self.partial.at[pl.ds(base + number * half, count)], dest, self.load_sem.at[3 * g + k]
        )
        return [
            copy(0, rows, self.stay.at[pl.ds(own, rows)], 0),
            copy(4, half, self.stay_y.at[pl.ds(own // 2, half)], 1),
            copy(3, half, self.stay_x.at[pl.ds(own // 2, half)], 2),
        ]

    def second_copies(self, g):
        _, rows, own = self.groups[g]
        at = pl.ds(own // 2, rows // 2)
        return [
            remote(self.for_y.at[at], self.low.at[at], self.second_send.at[2 * g], self.second_recv.at[2 * g], self.to_y),
            remote(
                self.for_x.at[at], self.high.at[at], self.second_send.at[2 * g + 1], self.second_recv.at[2 * g + 1], self.to_x
            ),
        ]

    def start(self, g):
        copies = self.first_copies(g)
        for k in (1, 3, 0, 2):
            copies[k].start()
        for copy in self.loads(g):
            copy.start()

    def forward(self, g):
        _, rows, own = self.groups[g]
        half = rows // 2
        copies = self.first_copies(g)
        copies[1].wait_recv()
        copies[3].wait_recv()
        for copy in self.loads(g):
            copy.wait()
        at = pl.ds(own // 2, half)
        self.for_y[at, :] = add_low(self.stay_y[at, :], self.from_x[pl.ds(own + half, half), :])
        self.for_x[at, :] = add_low(self.stay_x[at, :], self.from_y[pl.ds(own + half, half), :])
        for copy in self.second_copies(g):
            copy.start()

    def total(self, g, use):
        _, rows, own = self.groups[g]
        half = rows // 2
        copies, seconds = self.first_copies(g), self.second_copies(g)
        copies[0].wait_recv()
        copies[2].wait_recv()
        for copy in copies:
            copy.wait_send()
        for copy in seconds:
            copy.wait()
        first = pl.ds(own, half)
        rest = pl.ds(own // 2, half)
        for side, (got, more) in enumerate(((self.from_x, self.low), (self.from_y, self.high))):
            at = pl.ds(own + side * half, half)
            use(at, self.stay[at, :].astype(F32) + got[first, :].astype(F32) + more[rest, :].astype(F32))


class Gather:
    def __init__(self, own, out, groups, sems):
        self.own, self.out, self.groups = own, out, groups
        self.first_send, self.first_recv, self.second_send, self.second_recv, self.local_sem = sems
        self.to_x, self.to_y = neighbours()

    @staticmethod
    def scratch():
        dma = pltpu.SemaphoreType.DMA
        return [dma((4,)), dma((4,)), dma((4,)), dma((4,)), dma((2,))]

    def first_copies(self, g):
        base, rows, own = self.groups[g]
        source = self.own.at[pl.ds(own, rows)]
        place = lambda k: self.out.at[pl.ds(base + k * rows, rows)]
        return [
            remote(source, place(1), self.first_send.at[2 * g], self.first_recv.at[2 * g], self.to_x),
            remote(source, place(2), self.first_send.at[2 * g + 1], self.first_recv.at[2 * g + 1], self.to_y),
        ]

    def local(self, g):
        base, rows, own = self.groups[g]
        return pltpu.make_async_copy(self.own.at[pl.ds(own, rows)], self.out.at[pl.ds(base, rows)], self.local_sem.at[g])

    def second_copies(self, g):
        base, rows, _ = self.groups[g]
        half = rows // 2
        part = lambda number: self.out.at[pl.ds(base + number * half, half)]
        return [
            remote(part(4), part(6), self.second_send.at[2 * g], self.second_recv.at[2 * g], self.to_x),
            remote(part(3), part(7), self.second_send.at[2 * g + 1], self.second_recv.at[2 * g + 1], self.to_y),
        ]

    def start(self, g):
        for copy in self.first_copies(g):
            copy.start()
        self.local(g).start()

    def forward(self, g):
        for copy in self.first_copies(g):
            copy.wait_recv()
        for copy in self.second_copies(g):
            copy.start()

    def finish(self, g):
        for copy in self.first_copies(g):
            copy.wait_send()
        for copy in self.second_copies(g):
            copy.wait()
        self.local(g).wait()


ROWS = 128
CORE_SLOTS, HOP_SLOTS = 3, 4


class Ring:
    def __init__(self, slots, send_sem, recv_sem, credit, total):
        self.slots, self.send_sem, self.recv_sem, self.credit, self.total = slots, send_sem, recv_sem, credit, total
        self.count = slots.shape[0]

    def copy(self, source, at, send_at, device):
        slot = lax.rem(at, self.count)
        return pltpu.make_async_remote_copy(
            src_ref=source,
            dst_ref=self.slots.at[slot],
            send_sem=self.send_sem.at[send_at],
            recv_sem=self.recv_sem.at[slot],
            device_id=device,
            device_id_type=pl.DeviceIdType.MESH,
        )

    def send(self, source, at, send_at, device):
        @pl.when(at >= self.count)
        def _():
            pl.semaphore_wait(self.credit, 1)

        self.copy(source, at, send_at, device).start()

    def sent(self, source, at, send_at, device):
        self.copy(source, at, send_at, device).wait_send()

    def arrived(self, source, at, send_at, device):
        self.copy(source, at, send_at, device).wait_recv()
        return self.slots.at[lax.rem(at, self.count)]

    def free(self, at, device):
        @pl.when(at + self.count < self.total)
        def _():
            pl.semaphore_signal(self.credit, inc=1, device_id=device, device_id_type=pl.DeviceIdType.MESH)


def sums_kernel(n_ctx, items, n_right, n_extra, tasks, *refs):
    n_left = len(items)
    left_refs, right_refs = refs[:n_left], refs[n_left : n_left + n_right]
    extra_in, refs = refs[n_left + n_right : n_left + n_right + n_extra[0]], refs[n_left + n_right + n_extra[0] :]
    out_refs, extra_out, refs = refs[:n_left], refs[n_left : n_left + n_extra[1]], refs[n_left + n_extra[1] :]
    extra_scratch, refs = refs[: n_extra[2]], refs[n_extra[2] :]
    (
        left_buf, right_buf, other_buf, ring, core_in, hop_in, hop_mid, hop_out, core_out,
        left_sem, right_sem, core_send, core_recv, in_send, in_recv, mid_send, mid_recv, out_send, out_recv,
        fin_send, fin_recv, store_sem, core_credit, in_credit, mid_credit, out_credit, fin_credit,
    ) = refs
    starts = [0]
    for _, _, chunks in items:
        starts.append(starts[-1] + chunks)
    total = starts[-1]
    n_ring = ring.shape[0]
    chips = n_ctx // 2
    mid = chips // 2
    index = lax.axis_index("ctx")
    rank = lax.axis_index("tp")
    core = lax.rem(index, 2)
    chip = index // 2
    low_side = chip < mid
    place = jnp.where(low_side, chip, chips - 1 - chip)
    toward = jnp.where(low_side, 1, -1)
    partner = (chip * 2 + 1 - core, rank)
    after = ((chip + toward) * 2 + core, rank)
    before = ((chip - toward) * 2 + core, rank)
    is_first = place == 0
    is_last = place == mid - 1
    lag_t = mid
    lag_u = lag_t + 2
    lag_o = lag_u + 2 * (mid - 1)
    lag_f = lag_o + 1
    lag_w = lag_f + 1

    barrier = pltpu.get_barrier_semaphore()
    pl.semaphore_signal(barrier, inc=1, device_id=partner, device_id_type=pl.DeviceIdType.MESH)

    @pl.when(chip > 0)
    def _():
        pl.semaphore_signal(
            barrier, inc=1, device_id=((chip - 1) * 2 + core, rank), device_id_type=pl.DeviceIdType.MESH
        )

    @pl.when(chip < chips - 1)
    def _():
        pl.semaphore_signal(
            barrier, inc=1, device_id=((chip + 1) * 2 + core, rank), device_id_type=pl.DeviceIdType.MESH
        )

    greeted = 1
    if tasks is not None:
        for device in neighbours():
            signal(barrier, device)
        greeted = 3
    pl.semaphore_wait(barrier, greeted + jnp.where(chip > 0, 1, 0) + jnp.where(chip < chips - 1, 1, 0))

    to_core = Ring(core_in, core_send, core_recv, core_credit, total)
    to_after = Ring(hop_in, in_send, in_recv, in_credit, total)
    across = Ring(hop_mid, mid_send, mid_recv, mid_credit, total)
    to_before = Ring(hop_out, out_send, out_recv, out_credit, total)
    to_final = Ring(core_out, fin_send, fin_recv, fin_credit, total)

    rights = [pltpu.make_async_copy(right_refs[k], right_buf.at[k], right_sem.at[k]) for k in range(n_right)]
    for copy in rights:
        copy.start()

    def for_item(at, action):
        for number in range(n_left):
            @pl.when((at >= starts[number]) & (at < starts[number + 1]))
            def _(number=number):
                action(number, at - starts[number])

    def rows_at(number, chunk, side):
        half = items[number][2] * ROWS
        return pl.multiple_of(side * half + chunk * ROWS, ROWS)

    def left_copy(number, chunk, slot, which):
        side = core if which == 0 else 1 - core
        return pltpu.make_async_copy(
            left_refs[number].at[:, pl.ds(rows_at(number, chunk, side), ROWS)],
            left_buf.at[slot, which],
            left_sem.at[slot, which],
        )

    def load_left(at):
        def action(number, chunk):
            for which in range(2):
                left_copy(number, chunk, lax.rem(at, 2), which).start()

        for_item(at, action)

    load_left(0)
    planned = tasks(extra_in, extra_out, extra_scratch) if tasks is not None else {}
    if 0 in planned:
        planned.pop(0)()
    for copy in rights:
        copy.wait()

    def step(i, carry):
        def at_lag(lag):
            at = i - lag
            return at, (at >= 0) & (at < total)

        at, now = at_lag(lag_w)

        @pl.when(now)
        def _():
            slot = lax.rem(at, n_ring)
            source = ring.at[slot]

            def action(number, chunk):
                store(number, chunk, at, 0).wait()
                store(number, chunk, at, 1).wait()

            for_item(at, action)
            to_final.sent(source, at, slot, partner)
            to_final.free(at, partner)

            @pl.when(jnp.logical_not(is_first))
            def _():
                to_before.sent(source, at, slot, before)

        at, now = at_lag(lag_o)

        @pl.when(now & jnp.logical_not(is_last))
        def _():
            slot = lax.rem(at, n_ring)
            source = ring.at[slot]
            to_after.sent(source, at, slot, after)
            got = to_before.arrived(source, at, slot, after)
            ring[slot] = got[...]
            to_before.free(at, after)

            @pl.when(jnp.logical_not(is_first))
            def _():
                to_before.send(source, at, slot, before)

        @pl.when(now)
        def _():
            slot = lax.rem(at, n_ring)
            to_final.send(ring.at[slot], at, slot, partner)

        at, now = at_lag(lag_u)

        @pl.when(now & is_last)
        def _():
            slot = lax.rem(at, n_ring)
            source = ring.at[slot]
            across.sent(source, at, slot, after)
            got = across.arrived(source, at, slot, after)
            ring[slot] = add_low(ring[slot], got[...])
            across.free(at, after)

            @pl.when(jnp.logical_not(is_first))
            def _():
                to_before.send(source, at, slot, before)

        at, now = at_lag(lag_t)

        @pl.when(now)
        def _():
            slot = lax.rem(at, n_ring)
            source = ring.at[slot]

            @pl.when(jnp.logical_not(is_first))
            def _():
                got = to_after.arrived(source, at, slot, before)
                ring[slot] = add_low(ring[slot], got[...])
                to_after.free(at, before)

            @pl.when(is_last)
            def _():
                across.send(source, at, slot, after)

            @pl.when(jnp.logical_not(is_first) & jnp.logical_not(is_last))
            def _():
                to_after.send(source, at, slot, after)

        at, now = at_lag(1)

        @pl.when(now)
        def _():
            slot = lax.rem(at, n_ring)
            source = ring.at[slot]
            own = other_buf.at[lax.rem(at, 2)]
            to_core.sent(own, at, lax.rem(at, 2), partner)
            got = to_core.arrived(own, at, lax.rem(at, 2), partner)
            ring[slot] = add_low(ring[slot], got[...])
            to_core.free(at, partner)

            @pl.when(is_first & jnp.logical_not(is_last))
            def _():
                to_after.send(source, at, slot, after)

        at, now = at_lag(lag_f)

        @pl.when(now)
        def _():
            slot = lax.rem(at, n_ring)
            to_final.arrived(ring.at[slot], at, slot, partner)

            def action(number, chunk):
                store(number, chunk, at, 0).start()
                store(number, chunk, at, 1).start()

            for_item(at, action)

        for when, task in planned.items():
            pl.when(i == when)(task)

        @pl.when(i + 1 < total)
        def _():
            load_left(i + 1)

        @pl.when(i < total)
        def _():
            slot = lax.rem(i, 2)

            def action(number, chunk):
                for which in range(2):
                    left_copy(number, chunk, slot, which).wait()
                right = right_buf.at[items[number][1]]
                other_buf[slot] = contract_rows(left_buf[slot, 1], right[...]).astype(BF)
                to_core.send(other_buf.at[slot], i, slot, partner)
                ring[lax.rem(i, n_ring)] = contract_rows(left_buf[slot, 0], right[...]).astype(BF)

            for_item(i, action)

        return carry

    def store(number, chunk, at, which):
        source = ring.at[lax.rem(at, n_ring)] if which == 0 else core_out.at[lax.rem(at, CORE_SLOTS)]
        side = core if which == 0 else 1 - core
        return pltpu.make_async_copy(
            source,
            out_refs[number].at[pl.ds(rows_at(number, chunk, side), ROWS), :],
            store_sem.at[which, lax.rem(at, 2)],
        )

    lax.fori_loop(0, total + lag_w, step, 0)


def weight_sums(items, rights, n_ctx, collective_id, extra=None):
    tokens, width = rights[0].shape
    shapes = [(k, right, left.shape[1] // 2 // ROWS) for k, (left, right) in enumerate(items)]
    mid = n_ctx // 4
    n_ring = mid + 2 + 2 * (mid - 1) + 3
    any_spec = pl.BlockSpec(memory_space=pl.ANY)
    args, arg_specs, outs, out_specs, scratch, tasks = extra if extra is not None else ([], [], [], [], [], None)
    counts = (len(args), len(outs), len(scratch))
    chunk = (ROWS, width)
    dma = pltpu.SemaphoreType.DMA
    return pl.pallas_call(
        functools.partial(sums_kernel, n_ctx, shapes, len(rights), counts, tasks),
        out_shape=[jax.ShapeDtypeStruct((left.shape[1], width), BF) for left, _ in items] + outs,
        in_specs=[any_spec] * (len(items) + len(rights)) + arg_specs,
        out_specs=[any_spec] * len(items) + out_specs,
        scratch_shapes=scratch
        + [
            pltpu.VMEM((2, 2, tokens, ROWS), BF),
            pltpu.VMEM((len(rights), tokens, width), BF),
            pltpu.VMEM((2,) + chunk, BF),
            pltpu.VMEM((n_ring,) + chunk, BF),
            pltpu.VMEM((CORE_SLOTS,) + chunk, BF),
            pltpu.VMEM((HOP_SLOTS,) + chunk, BF),
            pltpu.VMEM((HOP_SLOTS,) + chunk, BF),
            pltpu.VMEM((HOP_SLOTS,) + chunk, BF),
            pltpu.VMEM((CORE_SLOTS,) + chunk, BF),
            dma((2, 2)),
            dma((len(rights),)),
            dma((2,)),
            dma((CORE_SLOTS,)),
            dma((n_ring,)),
            dma((HOP_SLOTS,)),
            dma((n_ring,)),
            dma((HOP_SLOTS,)),
            dma((n_ring,)),
            dma((HOP_SLOTS,)),
            dma((n_ring,)),
            dma((CORE_SLOTS,)),
            dma((2, 2)),
        ]
        + [pltpu.SemaphoreType.REGULAR] * 5,
        compiler_params=pltpu.CompilerParams(
            vmem_limit_bytes=VMEM_LIMIT, collective_id=collective_id, has_side_effects=True
        ),
        cost_estimate=pl.CostEstimate(
            flops=sum(2 * left.shape[1] * tokens * width for left, _ in items),
            bytes_accessed=sum(2 * left.shape[1] * (tokens + width) for left, _ in items),
            transcendentals=0,
        ),
    )(*[left for left, _ in items], *rights, *args)


VMEM_SPEC = pl.BlockSpec(memory_space=pltpu.VMEM)
ANY_SPEC = pl.BlockSpec(memory_space=pl.ANY)


def norm_back_rows(values, gain, grad):
    inv = inverse_rms(values)
    unit = values * inv
    scaled = grad * gain
    back = (scaled - unit * jnp.mean(scaled * unit, axis=-1, keepdims=True)) * inv
    return back, jnp.sum(grad * unit, axis=0, keepdims=True)


def feed_tasks(groups, extra_in, extra_out, scratch):
    d_ref, y_ref, residual, grads, gain = extra_in
    dr, da_all, gain_grad, output = extra_out
    n = len(Scatter.scratch(16, 128))
    bufs, rest = scratch[:n], scratch[n:]
    da_own, free, gather_sems = rest[0], rest[1], rest[2:]
    first = Scatter(d_ref, groups, bufs[:9], bufs[9:])
    last = Scatter(y_ref, groups, bufs[:9], bufs[9:])
    gather = Gather(da_own, da_all, groups, gather_sems)
    order = list(reversed(range(len(groups))))

    def begin():
        gain_grad[...] = jnp.zeros_like(gain_grad)
        for g in order:
            first.start(g)

    def use(at, total):
        back, more = norm_back_rows(residual[at, :], gain[...], total)
        total_grad = grads[at, :].astype(F32) + back
        dr[at, :] = total_grad
        da_own[at, :] = total_grad.astype(BF)
        gain_grad[...] += more

    def spread(g):
        first.total(g, use)
        gather.start(g)

    def use_out(at, total):
        output[at, :] = (residual[at, :] + total).astype(BF)

    def again():
        for device in neighbours():
            signal(free, device)
        for g in order:
            gather.finish(g)

    def begin_out():
        pl.semaphore_wait(free, 2)
        for g in order:
            last.start(g)

    def forward_all():
        for g in order:
            last.forward(g)

    plan = {
        0: begin,
        2: lambda: first.forward(order[0]),
        4: lambda: first.forward(order[-1]),
        5: lambda: spread(order[0]),
        6: lambda: spread(order[-1]),
        8: lambda: gather.forward(order[0]),
        10: lambda: gather.forward(order[-1]),
        12: again,
        13: begin_out,
        16: forward_all,
        18: lambda: [last.total(g, use_out) for g in order] and None,
    }
    return plan


def feed_extra(groups, d_partial, y_partial, residual, grads, gain):
    rows, width = residual.shape
    outs = [
        jax.ShapeDtypeStruct((rows, width), F32),
        jax.ShapeDtypeStruct(d_partial.shape, BF),
        jax.ShapeDtypeStruct((1, width), F32),
        jax.ShapeDtypeStruct((rows, width), BF),
    ]
    scratch = (
        Scatter.scratch(rows, width)
        + [pltpu.VMEM((rows, width), BF), pltpu.SemaphoreType.REGULAR]
        + Gather.scratch()
    )
    return (
        [d_partial, y_partial, residual, grads, gain],
        [ANY_SPEC, ANY_SPEC, VMEM_SPEC, VMEM_SPEC, VMEM_SPEC],
        outs,
        [VMEM_SPEC, ANY_SPEC, VMEM_SPEC, VMEM_SPEC],
        scratch,
        functools.partial(feed_tasks, groups),
    )


def input_tasks(groups, extra_in, extra_out, scratch):
    i_ref, rows_in, dr, gain = extra_in
    input_grad, gain_grad = extra_out
    scatter = Scatter(i_ref, groups, scratch[:9], scratch[9:])
    order = list(reversed(range(len(groups))))

    def begin():
        gain_grad[...] = jnp.zeros_like(gain_grad)
        for g in order:
            scatter.start(g)

    def use(at, total):
        back, more = norm_back_rows(rows_in[at, :], gain[...], total)
        input_grad[at, :] = (dr[at, :] + back).astype(BF)
        gain_grad[...] += more

    return {
        0: begin,
        2: lambda: scatter.forward(order[0]),
        4: lambda: scatter.forward(order[-1]),
        5: lambda: scatter.total(order[0], use),
        6: lambda: scatter.total(order[-1], use),
    }


def input_extra(groups, partial, rows_in, dr, gain):
    rows, width = rows_in.shape
    outs = [jax.ShapeDtypeStruct((rows, width), BF), jax.ShapeDtypeStruct((1, width), F32)]
    return (
        [partial, rows_in, dr, gain],
        [ANY_SPEC, VMEM_SPEC, VMEM_SPEC, VMEM_SPEC],
        outs,
        [VMEM_SPEC, VMEM_SPEC],
        Scatter.scratch(rows, width),
        functools.partial(input_tasks, groups),
    )


def body(
    tokens,
    counts,
    norm_gain,
    w_query,
    w_key,
    w_value,
    w_output,
    mlp_gain,
    w_gate,
    w_up,
    w_down,
    cotangent,
):
    n_ctx = lax.axis_size("ctx")
    me = lax.axis_index("ctx")
    rank = lax.axis_index("tp")
    odd = rank & 1
    core = me & 1
    length = 2 * BLOCK * n_ctx
    heads = w_query.shape[1] // HD
    gain_one = norm_gain.astype(F32)
    gain_two = mlp_gain.astype(F32)

    inverse = THETA ** (-(jnp.arange(HD // 2, dtype=F32) * (2.0 / HD)))
    angles = jnp.arange(length, dtype=jnp.int32).astype(F32)[:, None] * inverse[None, :]
    cos_half, sin_half = jnp.cos(angles), jnp.sin(angles)
    cos_full = jnp.concatenate([cos_half, cos_half], axis=1)
    sin_full = jnp.concatenate([-sin_half, sin_half], axis=1)

    def own_blocks(table):
        front = lax.dynamic_slice_in_dim(table, me * BLOCK, BLOCK, 0)
        back = lax.dynamic_slice_in_dim(table, (2 * n_ctx - 1 - me) * BLOCK, BLOCK, 0)
        return front, back

    cos_front, cos_back = own_blocks(cos_full)
    sin_front, sin_back = own_blocks(sin_full)
    own_counts = lax.dynamic_index_in_dim(counts, me, 0, keepdims=False)
    offsets = jnp.arange(BLOCK, dtype=jnp.int32)

    def valid_of(sequence, half):
        return (offsets < own_counts[sequence, half]).astype(F32)

    cos_own = jnp.concatenate([cos_front, cos_back])
    sin_own = jnp.concatenate([sin_front, sin_back])
    sequences = counts.shape[1]
    paired = lax.axis_size("tp") == 4 and sequences == 6
    if paired:
        ranks = [rank ^ k for k in range(4)]
        seq_a = [3 * (r >> 1) + 2 * (r & 1) for r in ranks]
        seq_b = [1 + 3 * (r >> 1) for r in ranks]
        valids = {
            "b": jnp.concatenate([valid_of(s, r & 1) for s, r in zip(seq_b, ranks)]),
            "a": jnp.concatenate([valid_of(s, half) for s in seq_a for half in range(2)]),
        }
        flip_back = lambda own: jnp.where(odd == 1, jnp.roll(own, BLOCK, axis=0), own)
        tables = {
            "b": (jnp.tile(flip_back(cos_own), (2, 1)), jnp.tile(flip_back(sin_own), (2, 1))),
            "a": (jnp.tile(cos_own, (4, 1)), jnp.tile(sin_own, (4, 1))),
        }
        scalars = {"b": jnp.stack([me, odd]).astype(jnp.int32), "a": jnp.stack([me, 0]).astype(jnp.int32)}
        n_pairs = {"b": 2 * heads, "a": 4 * heads}
    else:
        valids = {"a": jnp.concatenate([valid_of(s, half) for s in range(sequences) for half in range(2)])}
        tables = {"a": (jnp.tile(cos_own, (sequences, 1)), jnp.tile(sin_own, (sequences, 1)))}
        scalars = {"a": jnp.stack([me, 0]).astype(jnp.int32)}
        n_pairs = {"a": sequences * heads}
    names = tuple(n_pairs)

    def own_rows(array):
        if not paired:
            return {"a": array}
        return {
            "b": lax.dynamic_slice_in_dim(array, (1 - odd) * PAIR, BLOCK, 0),
            "a": lax.dynamic_slice_in_dim(array, odd * BLOCK, PAIR, 0),
        }

    def whole_rows(part):
        if not paired:
            return part["a"]
        return jnp.where(odd == 1, jnp.concatenate([part["b"], part["a"]]), jnp.concatenate([part["a"], part["b"]]))

    x_own = {name: rows.astype(F32) for name, rows in own_rows(tokens[0]).items()}
    g_own = own_rows(cotangent[0])

    split = by_four()
    rows_of = {name: valids[name].shape[0] for name in names}
    total_rows = sum(rows_of.values())
    first_row = {"a": 0, "b": rows_of["a"]}
    valid_head = {name: jnp.broadcast_to(valids[name][:, None], (rows_of[name], HD)) for name in names}
    valid_wide = {name: jnp.broadcast_to(valids[name][:, None].astype(BF), (rows_of[name], heads * HD)) for name in names}
    near = [k for k in range(n_ctx) if k < 6]
    far = [k for k in range(n_ctx) if k >= 6]
    state = {}

    def fence():
        names_held = list(state)
        values = lax.optimization_barrier([state[name] for name in names_held])
        state.update(zip(names_held, values))

    def only_b(step):
        if "b" in names:
            step("b")

    def norm_one(n):
        state["n1", n] = (x_own[n] * inverse_rms(x_own[n]) * gain_one).astype(BF)

    def gather_a(key):
        def step(n):
            state[key, n] = gather_first(state[key, n])

        return step

    def gather_b(key):
        def step(n):
            state[key, n] = gather_second(state[key, n])

        return step

    def query(n):
        state["n1", n] = gathered(state["n1", n])
        cos_tab, sin_tab = tables[n]
        state["qkv", n] = project_qkv(
            scalars[n], state["n1", n], w_query, w_key, w_value, cos_tab, sin_tab, valid_head[n], n_ctx
        )

    def swap_part(key, places, to):
        def step(n):
            got = dict(state.get((to, n), {}))
            got.update(exchange(state[key, n], places, n_ctx))
            state[to, n] = got
            if len(got) == n_ctx:
                state[to, n] = [got[k] for k in range(n_ctx)]
                del state[key, n]

        return step

    def attend(n):
        state["mixed", n] = attention_forward(scalars[n], state["got", n], n_ctx)

    def project(n):
        heads_out, *parts = project_out(
            scalars[n], state.pop(("back", n)), w_output, valid_wide[n], n_pairs[n], n_ctx, split
        )
        state["heads", n], state["r", n] = heads_out, tuple(parts)

    def scatter_a(key):
        def step(n):
            state[key, n] = scatter_first(state[key, n])

        return step

    def scatter_b(key):
        def step(n):
            state[key, n] = scatter_second(state[key, n])

        return step

    def norm_two(n):
        residual = x_own[n] + scattered(state.pop(("r", n)))
        state["residual", n] = residual
        state["n2", n] = (residual * inverse_rms(residual) * gain_two).astype(BF)

    def core_mlp(n):
        state["n2", n] = gathered(state["n2", n])
        state["cot", n] = gathered(state["cot", n])
        held = state.get("mlp", ())
        state["mlp"] = mlp_core(
            state["n2", n], state["cot", n], w_gate, w_up, w_down, total_rows, first_row[n], held
        )

    def attend_back(n):
        state["dqkv", n] = attention_backward(
            scalars[n], state.pop(("got", n)), state.pop(("gdo", n)), cos_full, sin_full, n_ctx
        )

    def query_back(n):
        dq, dk, dv, *parts = project_in(
            scalars[n], state.pop(("gdqkv", n)), (w_query, w_key, w_value), valid_wide[n], n_pairs[n], n_ctx, False
        )
        state["dq", n], state["dk", n], state["dv", n], state["i", n] = dq, dk, dv, parts[0]

    def joined(key):
        parts = [state[key, n] for n in ("a", "b") if n in names]
        return jnp.concatenate(parts) if len(parts) > 1 else parts[0]

    only_b(norm_one)
    only_b(gather_a("n1"))
    norm_one("a")
    for n in names:
        state["cot", n] = g_own[n]
    fence()
    only_b(gather_b("n1"))
    fence()
    gather_a("n1")("a")
    only_b(query)
    fence()
    gather_b("n1")("a")
    only_b(swap_part("qkv", near, "got"))
    fence()
    only_b(swap_part("qkv", far, "got"))
    only_b(gather_a("cot"))
    query("a")
    fence()
    swap_part("qkv", near, "got")("a")
    only_b(attend)
    only_b(gather_b("cot"))
    gather_a("cot")("a")
    fence()
    swap_part("qkv", far, "got")("a")
    only_b(swap_part("mixed", range(n_ctx), "back"))
    gather_b("cot")("a")
    fence()
    attend("a")
    only_b(project)
    only_b(scatter_a("r"))
    fence()
    swap_part("mixed", range(n_ctx), "back")("a")
    only_b(scatter_b("r"))
    only_b(norm_two)
    only_b(gather_a("n2"))
    fence()
    project("a")
    only_b(gather_b("n2"))
    fence()
    scatter_a("r")("a")
    only_b(core_mlp)
    fence()
    scatter_b("r")("a")
    fence()
    norm_two("a")
    gather_a("n2")("a")
    fence()
    gather_b("n2")("a")
    fence()
    core_mlp("a")
    fence()
    groups = tuple((first_row[n], rows_of[n] // 4, first_row[n] // 4) for n in ("a", "b") if n in names)
    in_order = [n for n in ("a", "b") if n in names]

    def own_joined(parts):
        return jnp.concatenate([parts[n] for n in in_order]) if len(in_order) > 1 else parts[in_order[0]]

    def by_group(array, scale=1):
        return {n: array[first_row[n] // scale : (first_row[n] + rows_of[n]) // scale] for n in in_order}

    h, dgp, dup = state["mlp"]
    all_n1, all_n2, all_cot, heads_out = (joined(key) for key in ("n1", "n2", "cot", "heads"))
    d_partial = (times_transposed(dgp, w_gate) + times_transposed(dup, w_up)).astype(BF)
    y_partial = dot(h, w_down).astype(BF)
    own_residual, own_grads, own_x = (
        own_joined(part) for part in ({n: state["residual", n] for n in names}, g_own, x_own)
    )
    feed_items, feed_rights = [(h, 0), (dgp, 1), (dup, 1)], [all_cot, all_n2]
    if split:
        extra = feed_extra(groups, d_partial, y_partial, own_residual, own_grads, gain_two[None])
        sum_down, sum_gate, sum_up, dr, da, gain_two_grad, output = weight_sums(feed_items, feed_rights, n_ctx, 1, extra)
    else:
        sum_down, sum_gate, sum_up = weight_sums(feed_items, feed_rights, n_ctx, 1)
        back, gain_two_grad = norm_back_rows(own_residual, gain_two, scattered(scatter_first((d_partial,))))
        dr = own_grads.astype(F32) + back
        da = gathered(gather_first(dr.astype(BF)))
        output = (own_residual + scattered(scatter_first((y_partial,)))).astype(BF)
    for n, rows in by_group(da).items():
        state["da", n] = rows
        state["do", n] = heads_back(scalars[n], rows, w_output, valid_wide[n], n_ctx)
    for n in names:
        swap_part("do", range(n_ctx), "gdo")(n)
    for n in names:
        attend_back(n)
        swap_part("dqkv", range(n_ctx), "gdqkv")(n)
    for n in names:
        query_back(n)
    i_partial = joined("i")
    input_items = [(heads_out, 0), (joined("dq"), 1), (joined("dk"), 1), (joined("dv"), 1)]
    if split:
        extra = input_extra(groups, i_partial, own_x, dr, gain_one[None])
        sum_out, sum_q, sum_k, sum_v, input_grad, gain_one_grad = weight_sums(
            input_items, [da, all_n1], n_ctx, 2, extra
        )
    else:
        sum_out, sum_q, sum_k, sum_v = weight_sums(input_items, [da, all_n1], n_ctx, 2)
        back, gain_one_grad = norm_back_rows(own_x, gain_one, scattered(scatter_first((i_partial,))))
        input_grad = (dr + back).astype(BF)
    gains = jnp.concatenate([gain_one_grad, gain_two_grad])
    for axis in ("tp", "ctx"):
        size = lax.axis_size(axis)
        for bit in range(size.bit_length() - 1):
            gains = gains + lax.ppermute(gains, axis, [(i, i ^ (1 << bit)) for i in range(size)])
    return (
        whole_rows(by_group(output, 4))[None] if split else output[None],
        whole_rows(by_group(input_grad, 4))[None] if split else input_grad[None],
        gains[0],
        sum_q.T.astype(F32),
        sum_k.T.astype(F32),
        sum_v.T.astype(F32),
        sum_out.astype(F32),
        gains[1],
        sum_gate.T.astype(F32),
        sum_up.T.astype(F32),
        sum_down.astype(F32),
    )


def solution(mesh):
    placed = (
        P("ctx", "tp", None),
        P(),
        P(),
        P(None, "tp"),
        P(None, "tp"),
        P(None, "tp"),
        P("tp", None),
        P(),
        P(None, "tp"),
        P(None, "tp"),
        P("tp", None),
        P("ctx", "tp", None),
    )
    return jax.shard_map(
        body,
        mesh=mesh,
        in_specs=placed,
        out_specs=(
            P("ctx", "tp", None),
            P("ctx", "tp", None),
            P(),
            P(None, "tp"),
            P(None, "tp"),
            P(None, "tp"),
            P("tp", None),
            P(),
            P(None, "tp"),
            P(None, "tp"),
            P("tp", None),
        ),
        check_vma=False,
    )
```

time: 1690 us -> 1300 us (0.77)
  Pallas kernels: 136 us -> 671 us
  waiting for transfers between devices: 647 us -> 220 us
  starting transfers between devices: 254 us -> 112 us
  matrix products: 192 us -> 58.3 us
  blocking collectives: 81.8 us -> 0 us
  other arithmetic: 194 us -> 114 us
  local copies, waits for them, and re-layouts: 169 us -> 119 us
    pallas_call x2 -> x10, Pallas kernels: 19.5 us -> 551 us  [the longest x2 482 us: weight_sums(): pl.pallas_call(functools.partial(sums_kernel, n_ctx, shapes, len(rights),...]
    ppermute x44 -> x5, waiting for transfers between devices: 295 us -> 0.01 us  [body(): lax.ppermute(gains, axis, [(i, i ^ 1 << bit) for i in range(size)])]
    dot_general x14 -> x0, matrix products: 101 us -> none  [contract_rows(): lax.dot_general(left, right, (((0,), (0,)), ((), ())), preferred_element_...]
    ppermute x32 -> x16, waiting for transfers between devices: 118 us -> 24.9 us  [send_y(): return lax.ppermute(values, 'tp', Y_SWAP)]
    ppermute x44 -> x5, starting transfers between devices: 93 us -> 3.68 us  [body(): lax.ppermute(gains, axis, [(i, i ^ 1 << bit) for i in range(size)])]
    psum x1 -> x0, blocking collectives: 81.8 us -> none  [body(): lax.psum(jnp.stack([sum(gain_one_grad.values()), sum(gain_two_grad.values...]
    ppermute x56, waiting for transfers between devices: 189 us -> 137 us  [exchange(): lax.ppermute(pieces[k], 'ctx', [(i, i ^ k) for i in range(n_ctx)])]
    select_n x28 -> x0, other arithmetic: 40.4 us -> none  [the longest x7 20.9 us: join(): low = jnp.where(core == 0, mine, other).astype(F32)]
  transfers between devices with their start and end apart: 164 -> 93, of which waited for: 61 -> 30; matrix products, arithmetic and copies ran while one was open for 29% -> 13% of each run, Pallas kernels for 6% -> 10%
where the time goes in v2:
time: 1300 us
  Pallas kernels  671 us (52%)
  waiting for transfers between devices  220 us (17%)
  local copies, waits for them, and re-layouts  119 us (9%)
  other arithmetic  114 us (9%)
  starting transfers between devices  112 us (9%)
  matrix products  58.3 us (4%)
    pallas_call x2, Pallas kernels, weight_sums(): pl.pallas_call(functools.partial(sums_kernel, n_ctx, shapes, len(rights),...  482 us
    ppermute x56, waiting for transfers between devices, exchange(): lax.ppermute(pieces[k], 'ctx', [(i, i ^ k) for i in range(n_ctx)])  137 us
    unnamed x260, local copies, waits for them, and re-layouts  85 us
    ppermute x56, starting transfers between devices, exchange(): lax.ppermute(pieces[k], 'ctx', [(i, i ^ k) for i in range(n_ctx)])  83.4 us
    ppermute x16, waiting for transfers between devices, send_x(): return lax.ppermute(values, 'tp', X_SWAP)  57.9 us
    pallas_call x2, Pallas kernels, mlp_core(): pl.pallas_call(mlp_kernel, out_shape=(out, out, out), grid=(hidden // til...  57.3 us
    pallas_call x2, Pallas kernels, attention_backward(): pl.pallas_call(functools.partial(attention_back_kernel, n_ctx, tile), out...  41.3 us
    dot_general x2, matrix products, times_transposed(): lax.dot_general(left, right, (((1,), (1,)), ((), ())), preferred_element_...  40.7 us
  transfers between devices with their start and end apart: 93, of which 30 were waited for; matrix products, arithmetic and copies ran while one was open for 13% of the time, Pallas kernels for 10%

profile of v2, /device:TPU:1, one launch (start us, length us, event | category | flops | bytes accessed | tf_op | source)
XLA Modules:
  0.0 1296.1 jit_solution(11646866317698348663)
XLA Ops:
  41.8 9.0 shard_map.203
  111.3 13.3 %shard_map.204 = (bf16[2,3,256,128]{3,2,1,0:T(8,128)(2,1)}, bf16[2,3,256,128]{3,2,1,0:T(8,128)(2,1)}, bf16[2,3,256,128]{3,2,1,0:T(8,128)(2,1)}, bf16[2,3,256,128...) custom-call(s32[2]{0:T(128)} %get-tuple-element.1116.scalar_ref, ...), custom_call_target="tpu_custom_call" | custom-call | flops 6442450944 | bytes 10485760 | tf_op jit(solution)/shard_map/pallas_call | solution.py:196
  128.8 27.4 %collective-permute-done.17 = bf16[64,2048]{1,0:T(8,128)(2,1)S(1)} collective-permute-done((bf16[64,2048]{1,0:T(8,128)(2,1)S(1)}, bf16[64,2048]{1,0:T(8,128)(2,1)S(1)}, u32[]{:S(2)}, u32[]{:S(2)}) %collective-permute-start.17) | collective-permute-done | bytes 262176 | tf_op jit(solution)/shard_map/ppermute | solution.py:38
  156.5 7.2 collective-permute-done.18
  167.6 8.0 shard_map.205
  182.2 11.9 collective-permute-done.24.refs_4_
  194.1 8.4 collective-permute-done.25.refs_5_
  209.8 18.3 %collective-permute-done.32.refs_3_ = bf16[1,256,128]{2,1,0:T(8,128)(2,1)S(1)} collective-permute-done((bf16[1,256,128]{2,1,0:T(8,128)(2,1)}, bf16[1,256,128]{2,1,0:T(8,128)(2,1)S(1)}, u32[]{:S(2)}, u32[]{:S(2)}) %collective-permute-start.32) | collective-permute-done | bytes 65568 | tf_op jit(solution)/shard_map/ppermute | solution.py:113
  228.3 16.6 %collective-permute-done.33.refs_4_ = bf16[1,256,128]{2,1,0:T(8,128)(2,1)S(1)} collective-permute-done((bf16[1,256,128]{2,1,0:T(8,128)(2,1)}, bf16[1,256,128]{2,1,0:T(8,128)(2,1)S(1)}, u32[]{:S(2)}, u32[]{:S(2)}) %collective-permute-start.33) | collective-permute-done | bytes 65568 | tf_op jit(solution)/shard_map/ppermute | solution.py:113
  270.4 12.9 shard_map.206
  311.5 8.3 collective-permute-done.43.refs_5_
  339.2 20.3 %shard_map.209 = (bf16[1536,2048]{1,0:T(8,128)(2,1)}, bf16[1536,2048]{1,0:T(8,128)(2,1)}, bf16[1536,2048]{1,0:T(8,128)(2,1)}) custom-call(bf16[512,2048]{1,0:T(8,128)(2,1)} %copy-done.14, bf16[512,2048]{1,0:T(8,128)(2,1)} %constant_dynamic-update-slice_fusion.10.g_ref, bf16[2048,2048]{1,0:T(8,128)(2,1)} %wg_ref.3, bf16[2048,2048]{1,0:T(8,128)(2,1)} %wu_ref.3, ...), custom_call_target="tpu_custom_call" | custom-call | flops 12884901888 | bytes 35651584 | tf_op jit(solution)/shard_map/pallas_call | solution.py:546
  362.0 10.9 collective-permute-done.54
  381.0 16.7 %collective-permute-done.56 = bf16[256,2048]{1,0:T(8,128)(2,1)S(1)} collective-permute-done((bf16[256,2048]{1,0:T(8,128)(2,1)S(1)}, bf16[256,2048]{1,0:T(8,128)(2,1)S(1)}, u32[]{:S(2)}, u32[]{:S(2)}) %collective-permute-start.56) | collective-permute-done | bytes 1048608 | tf_op jit(solution)/shard_map/ppermute | solution.py:38
  419.9 37.0 %shard_map.210 = (bf16[1536,2048]{1,0:T(8,128)(2,1)}, bf16[1536,2048]{1,0:T(8,128)(2,1)}, bf16[1536,2048]{1,0:T(8,128)(2,1)}) custom-call(bf16[1024,2048]{1,0:T(8,128)(2,1)} %constant_dynamic-update-slice_fusion.25.n_ref, bf16[1024,2048]{1,0:T(8,128)(2,1)} %constant_dynamic-update-slice_fusion.20.g_ref, ...), custom_call_target="tpu_custom_call", output_to_operand_aliasing={{0}: (5, {}), {1}: (6, {}), {2}: (7, {})} | custom-call | flops 25769803776 | bytes 46137344 | tf_op jit(solution)/shard_map/pallas_call | solution.py:546
  456.9 19.4 %fusion.14 = f32[1536,2048]{1,0:T(8,128)} fusion(bf16[1536,2048]{1,0:T(8,128)(2,1)} %get-tuple-element.982.refs_1_, bf16[2048,2048]{1,0:T(8,128)(2,1)} %wg_ref.3), kind=kOutput, calls=%fused_computation.133 | convolution fusion | flops 12884901888 | bytes 27262976 | tf_op jit(solution)/shard_map/dot_general | solution.py:34
  476.3 17.6 %convolution_convert_fusion.refs_6_ = bf16[1536,2048]{1,0:T(8,128)(2,1)} fusion(bf16[1536,2048]{1,0:T(8,128)(2,1)S(1)} %copy-done.111, bf16[2048,2048]{1,0:T(8,128)(2,1)} %wd_ref.3), kind=kOutput, calls=%fused_computation.3 | convolution fusion | flops 12888047616 | bytes 20971520 | tf_op jit(solution)/shard_map/dot_general | solution.py:26
  495.8 21.4 %add_convert_fusion.refs_5_ = bf16[1536,2048]{1,0:T(8,128)(2,1)} fusion(f32[1536,2048]{1,0:T(8,128)} %fusion.14, bf16[1536,2048]{1,0:T(8,128)(2,1)} %get-tuple-element.983.refs_2_, bf16[2048,2048]{1,0:T(8,128)(2,1)} %wu_ref.3), kind=kOutput, calls=%fused_computation.2 | convolution fusion | flops 12891193344 | bytes 33554432 | tf_op jit(solution)/shard_map/dot_general | solution.py:34
  530.4 327.8 %shard_map.211 = (bf16[2048,2048]{1,0:T(8,128)(2,1)}, bf16[2048,2048]{1,0:T(8,128)(2,1)}, bf16[2048,2048]{1,0:T(8,128)(2,1)}, f32[384,2048]{1,0:T(8,128)}, bf16[...) custom-call(bf16[1536,2048]{1,0:T(8,128)(2,1)} %get-tuple-element.981.refs_0_, ...), custom_call_target="tpu_custom_call" | custom-call | flops 38654705664 | bytes 44040192 | tf_op jit(solution)/shard_map/pallas_call | solution.py:1028
  866.2 7.2 shard_map.212
  880.7 11.7 convert_bitcast_fusion.1
  898.9 11.3 convert_bitcast_fusion
  916.9 15.0 %shard_map.216 = (bf16[1,3,256,128]{3,2,1,0:T(8,128)(2,1)}, bf16[1,3,256,128]{3,2,1,0:T(8,128)(2,1)}, bf16[1,3,256,128]{3,2,1,0:T(8,128)(2,1)}, bf16[1,3,256,128...) custom-call(s32[2]{0:T(128)} %get-tuple-element.1115.scalar_ref, ...), custom_call_target="tpu_custom_call" | custom-call | flops 6442450944 | bytes 3670016 | tf_op jit(solution)/shard_map/pallas_call | solution.py:505
  937.3 26.2 %shard_map.213 = (bf16[2,3,256,128]{3,2,1,0:T(8,128)(2,1)}, bf16[2,3,256,128]{3,2,1,0:T(8,128)(2,1)}, bf16[2,3,256,128]{3,2,1,0:T(8,128)(2,1)}, bf16[2,3,256,128...) custom-call(s32[2]{0:T(128)} %get-tuple-element.1116.scalar_ref, ...), custom_call_target="tpu_custom_call" | custom-call | flops 12884901888 | bytes 7340032 | tf_op jit(solution)/shard_map/pallas_call | solution.py:505
  986.4 9.3 collective-permute-done.68.refs_2_
  998.3 9.1 shard_map.217
  1007.5 26.3 %collective-permute-done.71.refs_5_ = bf16[2,3,256,128]{3,2,1,0:T(8,128)(2,1)} collective-permute-done((bf16[2,3,256,128]{3,2,1,0:T(8,128)(2,1)S(1)}, bf16[2,3,256,128]{3,2,1,0:T(8,128)(2,1)}, u32[]{:S(2)}, u32[]{:S(2)}) %collective-permute-start.71) | collective-permute-done | bytes 393248 | tf_op jit(solution)/shard_map/ppermute | solution.py:113
  1033.8 13.8 %shard_map.214 = (bf16[1024,512]{1,0:T(8,128)(2,1)}, bf16[1024,512]{1,0:T(8,128)(2,1)}, bf16[1024,512]{1,0:T(8,128)(2,1)}, bf16[1024,2048]{1,0:T(8,128)(2,1)}) custom-call(s32[2]{0:T(128)} %get-tuple-element.1116.scalar_ref, bf16[2,3,256,128]{3,2,1,0:T(8,128)(2,1)} %get-tuple-element.1010.refs_0_, bf16[2,3,256,128]{3,2,1,0:T(8,128)(2,1)} %copy-done.53, ...), custom_call_target="tpu_custom_call" | custom-call | flops 6442450944 | bytes 10485760 | tf_op jit(solution)/shard_map/pallas_call | solution.py:354
  1058.1 153.8 %shard_map.218 = (bf16[512,2048]{1,0:T(8,128)(2,1)}, bf16[512,2048]{1,0:T(8,128)(2,1)}, bf16[512,2048]{1,0:T(8,128)(2,1)}, bf16[512,2048]{1,0:T(8,128)(2,1)}, bf...) custom-call(bf16[1536,512]{1,0:T(8,128)(2,1)} %pad_maximum_fusion.7.refs_0_, bf16[1536,512]{1,0:T(8,128)(2,1)} %pad_maximum_fusion.8.refs_1_, ...), custom_call_target="tpu_custom_call" | custom-call | flops 12884901888 | bytes 14680064 | tf_op jit(solution)/shard_map/pallas_call | solution.py:1028
  1215.3 17.8 %copy.29 = f32[2048,2048]{1,0:T(8,128)} copy(f32[2048,2048]{0,1:T(8,128)} %convert_bitcast_fusion.1) | data formatting | bytes 33554432
  1233.1 17.6 %copy.30 = f32[2048,2048]{1,0:T(8,128)} copy(f32[2048,2048]{0,1:T(8,128)} %convert_bitcast_fusion) | data formatting | bytes 33554432
  1250.7 11.8 convert_element_type.239
  (539 shorter events, 350.2 us)
Async XLA Ops:
  58.1 33.0 %collective-permute-start.6 = (bf16[128,2048]{1,0:T(8,128)(2,1)}, bf16[128,2048]{1,0:T(8,128)(2,1)}, u32[]{:S(2)}, u32[]{:S(2)}) collective-permute-start(bf16[128,2048]{1,0:T(8,128)(2,1)} %slice.130), channel_id=1, source_target_pairs={{0,1},{1,0},{2,3},{3,2},{4,5},{5,4},{6,7},{7,6},{8,9},{9,8},{10,11... | collective-permute-start | bytes 1572872 | tf_op jit(solution)/shard_map/ppermute | solution.py:38
  60.3 30.8 %collective-permute-start.7 = (bf16[128,2048]{1,0:T(8,128)(2,1)}, bf16[128,2048]{1,0:T(8,128)(2,1)}, u32[]{:S(2)}, u32[]{:S(2)}) collective-permute-start(bf16[128,2048]{1,0:T(8,128)(2,1)} %slice.131), channel_id=1, source_target_pairs={{0,2},{1,3},{2,0},{3,1},{4,6},{5,7},{6,4},{7,5},{8,10},{9,11},{10,... | collective-permute-start | bytes 1572872 | tf_op jit(solution)/shard_map/ppermute | solution.py:42
  91.1 33.6 %collective-permute-start.13 = (bf16[128,2048]{1,0:T(8,128)(2,1)S(1)}, bf16[128,2048]{1,0:T(8,128)(2,1)S(1)}, u32[]{:S(2)}, u32[]{:S(2)}) collective-permute-start(bf16[128,2048]{1,0:T(8,128)(2,1)S(1)} %dynamic-slice_bitcast_fusion.1), channel_id=1, source_target_pairs={{0,1},{1,0},{2,3},{3,2},{4,5},{5,4},{6,7},{7,6},{8,9},{9,8},{10,11... | collective-permute-start | bytes 1572872 | tf_op jit(solution)/shard_map/ppermute | solution.py:38
  92.3 32.4 %collective-permute-start.14 = (bf16[128,2048]{1,0:T(8,128)(2,1)S(1)}, bf16[128,2048]{1,0:T(8,128)(2,1)S(1)}, u32[]{:S(2)}, u32[]{:S(2)}) collective-permute-start(bf16[128,2048]{1,0:T(8,128)(2,1)S(1)} %dynamic-slice_bitcast_fusion.1), channel_id=1, source_target_pairs={{0,2},{1,3},{2,0},{3,1},{4,6},{5,7},{6,4},{7,5},{8,10},{9,11},{10,... | collective-permute-start | bytes 1572872 | tf_op jit(solution)/shard_map/ppermute | solution.py:42
  95.8 28.8 %collective-permute-start.15 = (bf16[1,3,256,128]{3,2,1,0:T(8,128)(2,1)}, bf16[1,3,256,128]{3,2,1,0:T(8,128)(2,1)S(1)}, u32[]{:S(2)}, u32[]{:S(2)}) collective-permute-start(bf16[1,3,256,128]{3,2,1,0:T(8,128)(2,1)} %get-tuple-element.587), channel_id=1, source_target_pairs={{0,24},{4,28},{8,16},{12,20},{16,8},{20,12},{24,0},{28,4},{1,25},{... | collective-permute-start | bytes 589832 | tf_op jit(solution)/shard_map/ppermute | solution.py:113
  125.6 77.0 %collective-permute-start.19 = (bf16[256,2048]{1,0:T(8,128)(2,1)S(1)}, bf16[256,2048]{1,0:T(8,128)(2,1)S(1)}, u32[]{:S(2)}, u32[]{:S(2)}) collective-permute-start(bf16[256,2048]{1,0:T(8,128)(2,1)S(1)} %dynamic-slice_bitcast_fusion), channel_id=1, source_target_pairs={{0,1},{1,0},{2,3},{3,2},{4,5},{5,4},{6,7},{7,6},{8,9},{9,8},{10,11... | collective-permute-start | bytes 3145736 | tf_op jit(solution)/shard_map/ppermute | solution.py:38
  125.9 76.7 %collective-permute-start.20 = (bf16[256,2048]{1,0:T(8,128)(2,1)S(1)}, bf16[256,2048]{1,0:T(8,128)(2,1)S(1)}, u32[]{:S(2)}, u32[]{:S(2)}) collective-permute-start(bf16[256,2048]{1,0:T(8,128)(2,1)S(1)} %dynamic-slice_bitcast_fusion), channel_id=1, source_target_pairs={{0,2},{1,3},{2,0},{3,1},{4,6},{5,7},{6,4},{7,5},{8,10},{9,11},{10,... | collective-permute-start | bytes 3145736 | tf_op jit(solution)/shard_map/ppermute | solution.py:42
  127.1 29.2 %collective-permute-start.17 = (bf16[64,2048]{1,0:T(8,128)(2,1)S(1)}, bf16[64,2048]{1,0:T(8,128)(2,1)S(1)}, u32[]{:S(2)}, u32[]{:S(2)}) collective-permute-start(bf16[64,2048]{1,0:T(8,128)(2,1)S(1)} %slice.132), channel_id=1, source_target_pairs={{0,1},{1,0},{2,3},{3,2},{4,5},{5,4},{6,7},{7,6},{8,9},{9,8},{10,11... | collective-permute-start | bytes 786440 | tf_op jit(solution)/shard_map/ppermute | solution.py:38
  128.3 35.4 %collective-permute-start.21 = (bf16[2,3,256,128]{3,2,1,0:T(8,128)(2,1)}, bf16[2,3,256,128]{3,2,1,0:T(8,128)(2,1)}, u32[]{:S(2)}, u32[]{:S(2)}) collective-permute-start(bf16[2,3,256,128]{3,2,1,0:T(8,128)(2,1)} %get-tuple-element.611), channel_id=1, source_target_pairs={{0,4},{4,0},{8,12},{12,8},{16,20},{20,16},{24,28},{28,24},{1,5},{5... | collective-permute-start | bytes 1179656 | tf_op jit(solution)/shard_map/ppermute | solution.py:113
  128.8 38.7 %collective-permute-start.22 = (bf16[2,3,256,128]{3,2,1,0:T(8,128)(2,1)}, bf16[2,3,256,128]{3,2,1,0:T(8,128)(2,1)}, u32[]{:S(2)}, u32[]{:S(2)}) collective-permute-start(bf16[2,3,256,128]{3,2,1,0:T(8,128)(2,1)} %get-tuple-element.612), channel_id=1, source_target_pairs={{0,8},{4,12},{8,0},{12,4},{16,24},{20,28},{24,16},{28,20},{1,9},{5... | collective-permute-start | bytes 1179656 | tf_op jit(solution)/shard_map/ppermute | solution.py:113
  163.7 30.4 %collective-permute-start.24 = (bf16[2,3,256,128]{3,2,1,0:T(8,128)(2,1)}, bf16[2,3,256,128]{3,2,1,0:T(8,128)(2,1)}, u32[]{:S(2)}, u32[]{:S(2)}) collective-permute-start(bf16[2,3,256,128]{3,2,1,0:T(8,128)(2,1)} %get-tuple-element.614), channel_id=1, source_target_pairs={{0,16},{4,20},{8,24},{12,28},{16,0},{20,4},{24,8},{28,12},{1,17},{... | collective-permute-start | bytes 1179656 | tf_op jit(solution)/shard_map/ppermute | solution.py:113
  167.5 35.0 %collective-permute-start.25 = (bf16[2,3,256,128]{3,2,1,0:T(8,128)(2,1)}, bf16[2,3,256,128]{3,2,1,0:T(8,128)(2,1)}, u32[]{:S(2)}, u32[]{:S(2)}) collective-permute-start(bf16[2,3,256,128]{3,2,1,0:T(8,128)(2,1)} %get-tuple-element.615), channel_id=1, source_target_pairs={{0,20},{4,16},{8,28},{12,24},{16,4},{20,0},{24,12},{28,8},{1,21},{... | collective-permute-start | bytes 1179656 | tf_op jit(solution)/shard_map/ppermute | solution.py:113
  202.6 58.9 %collective-permute-start.26 = (bf16[128,2048]{1,0:T(8,128)(2,1)S(1)}, bf16[128,2048]{1,0:T(8,128)(2,1)}, u32[]{:S(2)}, u32[]{:S(2)}) collective-permute-start(bf16[128,2048]{1,0:T(8,128)(2,1)S(1)} %slice.134), channel_id=1, source_target_pairs={{0,1},{1,0},{2,3},{3,2},{4,5},{5,4},{6,7},{7,6},{8,9},{9,8},{10,11... | collective-permute-start | bytes 1572872 | tf_op jit(solution)/shard_map/ppermute | solution.py:38
  203.6 57.9 %collective-permute-start.27 = (bf16[128,2048]{1,0:T(8,128)(2,1)S(1)}, bf16[128,2048]{1,0:T(8,128)(2,1)}, u32[]{:S(2)}, u32[]{:S(2)}) collective-permute-start(bf16[128,2048]{1,0:T(8,128)(2,1)S(1)} %slice.135), channel_id=1, source_target_pairs={{0,2},{1,3},{2,0},{3,1},{4,6},{5,7},{6,4},{7,5},{8,10},{9,11},{10,... | collective-permute-start | bytes 1572872 | tf_op jit(solution)/shard_map/ppermute | solution.py:42
  205.0 56.5 %collective-permute-start.28 = (bf16[2,3,256,128]{3,2,1,0:T(8,128)(2,1)}, bf16[2,3,256,128]{3,2,1,0:T(8,128)(2,1)S(1)}, u32[]{:S(2)}, u32[]{:S(2)}) collective-permute-start(bf16[2,3,256,128]{3,2,1,0:T(8,128)(2,1)} %get-tuple-element.651), channel_id=1, source_target_pairs={{0,24},{4,28},{8,16},{12,20},{16,8},{20,12},{24,0},{28,4},{1,25},{... | collective-permute-start | bytes 1179656 | tf_op jit(solution)/shard_map/ppermute | solution.py:113
  206.1 55.4 %collective-permute-start.29 = (bf16[2,3,256,128]{3,2,1,0:T(8,128)(2,1)}, bf16[2,3,256,128]{3,2,1,0:T(8,128)(2,1)S(1)}, u32[]{:S(2)}, u32[]{:S(2)}) collective-permute-start(bf16[2,3,256,128]{3,2,1,0:T(8,128)(2,1)} %get-tuple-element.652), channel_id=1, source_target_pairs={{0,28},{4,24},{8,20},{12,16},{16,12},{20,8},{24,4},{28,0},{1,29},{... | collective-permute-start | bytes 1179656 | tf_op jit(solution)/shard_map/ppermute | solution.py:113
  290.9 28.9 %collective-permute-start.48 = (bf16[128,2048]{1,0:T(8,128)(2,1)S(1)}, bf16[128,2048]{1,0:T(8,128)(2,1)S(1)}, u32[]{:S(2)}, u32[]{:S(2)}) collective-permute-start(bf16[128,2048]{1,0:T(8,128)(2,1)S(1)} %multiply_convert_fusion.2), channel_id=1, source_target_pairs={{0,1},{1,0},{2,3},{3,2},{4,5},{5,4},{6,7},{7,6},{8,9},{9,8},{10,11... | collective-permute-start | bytes 1572872 | tf_op jit(solution)/shard_map/ppermute | solution.py:38
  292.0 28.5 %collective-permute-start.49 = (bf16[128,2048]{1,0:T(8,128)(2,1)S(1)}, bf16[128,2048]{1,0:T(8,128)(2,1)S(1)}, u32[]{:S(2)}, u32[]{:S(2)}) collective-permute-start(bf16[128,2048]{1,0:T(8,128)(2,1)S(1)} %multiply_convert_fusion.2), channel_id=1, source_target_pairs={{0,2},{1,3},{2,0},{3,1},{4,6},{5,7},{6,4},{7,5},{8,10},{9,11},{10,... | collective-permute-start | bytes 1572872 | tf_op jit(solution)/shard_map/ppermute | solution.py:42
  332.7 26.9 %collective-permute-start.52 = (bf16[256,2048]{1,0:T(8,128)(2,1)}, bf16[256,2048]{1,0:T(8,128)(2,1)}, u32[]{:S(2)}, u32[]{:S(2)}) collective-permute-start(bf16[256,2048]{1,0:T(8,128)(2,1)} %get-tuple-element.830), channel_id=1, source_target_pairs={{0,1},{1,0},{2,3},{3,2},{4,5},{5,4},{6,7},{7,6},{8,9},{9,8},{10,11... | collective-permute-start | bytes 3145736 | tf_op jit(solution)/shard_map/ppermute | solution.py:38
  873.4 40.1 %collective-permute-start.60 = (bf16[2,256,128]{2,1,0:T(8,128)(2,1)}, bf16[2,256,128]{2,1,0:T(8,128)(2,1)S(1)}, u32[]{:S(2)}, u32[]{:S(2)}) collective-permute-start(bf16[2,256,128]{2,1,0:T(8,128)(2,1)} %get-tuple-element.1003), channel_id=1, source_target_pairs={{0,4},{4,0},{8,12},{12,8},{16,20},{20,16},{24,28},{28,24},{1,5},{5... | collective-permute-start | bytes 393224 | tf_op jit(solution)/shard_map/ppermute | solution.py:113
  932.0 31.6 %collective-permute-start.81 = (bf16[1,3,256,128]{3,2,1,0:T(8,128)(2,1)}, bf16[1,3,256,128]{3,2,1,0:T(8,128)(2,1)S(1)}, u32[]{:S(2)}, u32[]{:S(2)}) collective-permute-start(bf16[1,3,256,128]{3,2,1,0:T(8,128)(2,1)} %get-tuple-element.1036), channel_id=1, source_target_pairs={{0,4},{4,0},{8,12},{12,8},{16,20},{20,16},{24,28},{28,24},{1,5},{5... | collective-permute-start | bytes 589832 | tf_op jit(solution)/shard_map/ppermute | solution.py:113
  932.5 32.3 %collective-permute-start.82 = (bf16[1,3,256,128]{3,2,1,0:T(8,128)(2,1)}, bf16[1,3,256,128]{3,2,1,0:T(8,128)(2,1)S(1)}, u32[]{:S(2)}, u32[]{:S(2)}) collective-permute-start(bf16[1,3,256,128]{3,2,1,0:T(8,128)(2,1)} %get-tuple-element.1037), channel_id=1, source_target_pairs={{0,8},{4,12},{8,0},{12,4},{16,24},{20,28},{24,16},{28,20},{1,9},{5... | collective-permute-start | bytes 589832 | tf_op jit(solution)/shard_map/ppermute | solution.py:113
  932.5 34.9 %collective-permute-start.83 = (bf16[1,3,256,128]{3,2,1,0:T(8,128)(2,1)}, bf16[1,3,256,128]{3,2,1,0:T(8,128)(2,1)S(1)}, u32[]{:S(2)}, u32[]{:S(2)}) collective-permute-start(bf16[1,3,256,128]{3,2,1,0:T(8,128)(2,1)} %get-tuple-element.1038), channel_id=1, source_target_pairs={{0,12},{4,8},{8,4},{12,0},{16,28},{20,24},{24,20},{28,16},{1,13},{... | collective-permute-start | bytes 589832 | tf_op jit(solution)/shard_map/ppermute | solution.py:113
  934.2 33.2 %collective-permute-start.84 = (bf16[1,3,256,128]{3,2,1,0:T(8,128)(2,1)}, bf16[1,3,256,128]{3,2,1,0:T(8,128)(2,1)S(1)}, u32[]{:S(2)}, u32[]{:S(2)}) collective-permute-start(bf16[1,3,256,128]{3,2,1,0:T(8,128)(2,1)} %get-tuple-element.1039), channel_id=1, source_target_pairs={{0,16},{4,20},{8,24},{12,28},{16,0},{20,4},{24,8},{28,12},{1,17},{... | collective-permute-start | bytes 589832 | tf_op jit(solution)/shard_map/ppermute | solution.py:113
  934.4 40.3 %collective-permute-start.85 = (bf16[1,3,256,128]{3,2,1,0:T(8,128)(2,1)}, bf16[1,3,256,128]{3,2,1,0:T(8,128)(2,1)}, u32[]{:S(2)}, u32[]{:S(2)}) collective-permute-start(bf16[1,3,256,128]{3,2,1,0:T(8,128)(2,1)} %get-tuple-element.1040), channel_id=1, source_target_pairs={{0,20},{4,16},{8,28},{12,24},{16,4},{20,0},{24,12},{28,8},{1,21},{... | collective-permute-start | bytes 589832 | tf_op jit(solution)/shard_map/ppermute | solution.py:113
  967.6 28.2 %collective-permute-start.68 = (bf16[2,3,256,128]{3,2,1,0:T(8,128)(2,1)}, bf16[2,3,256,128]{3,2,1,0:T(8,128)(2,1)S(1)}, u32[]{:S(2)}, u32[]{:S(2)}) collective-permute-start(bf16[2,3,256,128]{3,2,1,0:T(8,128)(2,1)} %get-tuple-element.1012), channel_id=1, source_target_pairs={{0,8},{4,12},{8,0},{12,4},{16,24},{20,28},{24,16},{28,20},{1,9},{5... | collective-permute-start | bytes 1179656 | tf_op jit(solution)/shard_map/ppermute | solution.py:113
  974.7 32.7 %collective-permute-start.69 = (bf16[2,3,256,128]{3,2,1,0:T(8,128)(2,1)S(1)}, bf16[2,3,256,128]{3,2,1,0:T(8,128)(2,1)S(1)}, u32[]{:S(2)}, u32[]{:S(2)}) collective-permute-start(bf16[2,3,256,128]{3,2,1,0:T(8,128)(2,1)S(1)} %copy-done.52), channel_id=1, source_target_pairs={{0,12},{4,8},{8,4},{12,0},{16,28},{20,24},{24,20},{28,16},{1,13},{... | collective-permute-start | bytes 1179656 | tf_op jit(solution)/shard_map/ppermute | solution.py:113
  975.9 31.6 %collective-permute-start.70 = (bf16[2,3,256,128]{3,2,1,0:T(8,128)(2,1)S(1)}, bf16[2,3,256,128]{3,2,1,0:T(8,128)(2,1)}, u32[]{:S(2)}, u32[]{:S(2)}) collective-permute-start(bf16[2,3,256,128]{3,2,1,0:T(8,128)(2,1)S(1)} %copy-done.51), channel_id=1, source_target_pairs={{0,16},{4,20},{8,24},{12,28},{16,0},{20,4},{24,8},{28,12},{1,17},{... | collective-permute-start | bytes 1179656 | tf_op jit(solution)/shard_map/ppermute | solution.py:113
  979.2 54.5 %collective-permute-start.71 = (bf16[2,3,256,128]{3,2,1,0:T(8,128)(2,1)S(1)}, bf16[2,3,256,128]{3,2,1,0:T(8,128)(2,1)}, u32[]{:S(2)}, u32[]{:S(2)}) collective-permute-start(bf16[2,3,256,128]{3,2,1,0:T(8,128)(2,1)S(1)} %copy-done.50), channel_id=1, source_target_pairs={{0,20},{4,16},{8,28},{12,24},{16,4},{20,0},{24,12},{28,8},{1,21},{... | collective-permute-start | bytes 1179656 | tf_op jit(solution)/shard_map/ppermute | solution.py:113
  983.7 50.0 %collective-permute-start.72 = (bf16[2,3,256,128]{3,2,1,0:T(8,128)(2,1)S(1)}, bf16[2,3,256,128]{3,2,1,0:T(8,128)(2,1)}, u32[]{:S(2)}, u32[]{:S(2)}) collective-permute-start(bf16[2,3,256,128]{3,2,1,0:T(8,128)(2,1)S(1)} %copy-done.49), channel_id=1, source_target_pairs={{0,24},{4,28},{8,16},{12,20},{16,8},{20,12},{24,0},{28,4},{1,25},{... | collective-permute-start | bytes 1179656 | tf_op jit(solution)/shard_map/ppermute | solution.py:113
  995.8 38.0 %collective-permute-start.73 = (bf16[2,3,256,128]{3,2,1,0:T(8,128)(2,1)S(1)}, bf16[2,3,256,128]{3,2,1,0:T(8,128)(2,1)}, u32[]{:S(2)}, u32[]{:S(2)}) collective-permute-start(bf16[2,3,256,128]{3,2,1,0:T(8,128)(2,1)S(1)} %copy-done.48), channel_id=1, source_target_pairs={{0,28},{4,24},{8,20},{12,16},{16,12},{20,8},{24,4},{28,0},{1,29},{... | collective-permute-start | bytes 1179656 | tf_op jit(solution)/shard_map/ppermute | solution.py:113
  1212.7 49.8 %collective-permute-start.88 = (f32[2,2048]{1,0:T(2,128)S(1)}, f32[2,2048]{1,0:T(2,128)S(1)}, u32[]{:S(2)}, u32[]{:S(2)}) collective-permute-start(f32[2,2048]{1,0:T(2,128)S(1)} %pad_maximum_fusion.15), channel_id=1, source_target_pairs={{0,1},{1,0},{2,3},{3,2},{4,5},{5,4},{6,7},{7,6},{8,9},{9,8},{10,11... | collective-permute-start | bytes 49160 | tf_op jit(solution)/shard_map/ppermute | solution.py:1492
  (173 other events, 2356.9 us)

commit v3 on v2

--- a/solution.py
+++ b/solution.py
@@ -591,17 +591,29 @@
 
 
 class Scatter:
-    def __init__(self, partial, groups, bufs, sems):
-        self.partial, self.groups = partial, groups
-        self.from_x, self.from_y, self.stay, self.stay_y, self.stay_x, self.for_y, self.for_x, self.low, self.high = bufs
+    def __init__(self, partial, groups, bufs, sems, loaded=True):
+        self.partial, self.groups, self.loaded = partial, groups, loaded
+        self.from_x, self.from_y, self.for_y, self.for_x, self.low, self.high = bufs[:6]
+        if loaded:
+            self.stay, self.stay_y, self.stay_x = bufs[6:]
         self.first_send, self.first_recv, self.second_send, self.second_recv, self.load_sem = sems
         self.to_x, self.to_y = neighbours()
 
     @staticmethod
-    def scratch(rows, width):
+    def scratch(rows, width, loaded=True):
         dma = pltpu.SemaphoreType.DMA
         whole_rows, half_rows = pltpu.VMEM((rows, width), BF), pltpu.VMEM((rows // 2, width), BF)
-        return [whole_rows] * 3 + [half_rows] * 6 + [dma((8,)), dma((8,)), dma((4,)), dma((4,)), dma((6,))]
+        bufs = [whole_rows] * 2 + [half_rows] * 4 + ([whole_rows] + [half_rows] * 2 if loaded else [])
+        return bufs + [dma((8,)), dma((8,)), dma((4,)), dma((4,)), dma((6,))]
+
+    def piece(self, g, number):
+        base, rows, own = self.groups[g]
+        half = rows // 2
+        if not self.loaded:
+            return self.partial[pl.ds(base + number * half, half), :]
+        if number < 2:
+            return self.stay[pl.ds(own + number * half, half), :]
+        return (self.stay_x if number == 3 else self.stay_y)[pl.ds(own // 2, half), :]
 
     def first_copies(self, g):
         base, rows, own = self.groups[g]
@@ -641,12 +653,13 @@
             ),
         ]
 
-    def start(self, g):
+    def start(self, g, which=(1, 3, 0, 2), loads=True):
         copies = self.first_copies(g)
-        for k in (1, 3, 0, 2):
+        for k in which:
             copies[k].start()
-        for copy in self.loads(g):
-            copy.start()
+        if loads:
+            for copy in self.loads(g):
+                copy.start()
 
     def forward(self, g):
         _, rows, own = self.groups[g]
@@ -654,11 +667,12 @@
         copies = self.first_copies(g)
         copies[1].wait_recv()
         copies[3].wait_recv()
-        for copy in self.loads(g):
-            copy.wait()
+        if self.loaded:
+            for copy in self.loads(g):
+                copy.wait()
         at = pl.ds(own // 2, half)
-        self.for_y[at, :] = add_low(self.stay_y[at, :], self.from_x[pl.ds(own + half, half), :])
-        self.for_x[at, :] = add_low(self.stay_x[at, :], self.from_y[pl.ds(own + half, half), :])
+        self.for_y[at, :] = add_low(self.piece(g, 4), self.from_x[pl.ds(own + half, half), :])
+        self.for_x[at, :] = add_low(self.piece(g, 3), self.from_y[pl.ds(own + half, half), :])
         for copy in self.second_copies(g):
             copy.start()
 
@@ -676,7 +690,7 @@
         rest = pl.ds(own // 2, half)
         for side, (got, more) in enumerate(((self.from_x, self.low), (self.from_y, self.high))):
             at = pl.ds(own + side * half, half)
-            use(at, self.stay[at, :].astype(F32) + got[first, :].astype(F32) + more[rest, :].astype(F32))
+            use(at, self.piece(g, side).astype(F32) + got[first, :].astype(F32) + more[rest, :].astype(F32))
 
 
 class Gather:
@@ -722,13 +736,15 @@
             copy.wait_recv()
         for copy in self.second_copies(g):
             copy.start()
+        self.local(g).wait()
 
     def finish(self, g):
-        for copy in self.first_copies(g):
+        for copy in self.second_copies(g):
+            copy.wait_recv()
+
+    def sent(self, g):
+        for copy in self.first_copies(g) + self.second_copies(g):
             copy.wait_send()
-        for copy in self.second_copies(g):
-            copy.wait()
-        self.local(g).wait()
 
 
 ROWS = 128
@@ -1114,6 +1130,7 @@
             signal(free, device)
         for g in order:
             gather.finish(g)
+            gather.sent(g)
 
     def begin_out():
         pl.semaphore_wait(free, 2)
@@ -1199,6 +1216,436 @@
         Scatter.scratch(rows, width),
         functools.partial(input_tasks, groups),
     )
+
+
+class Exchange:
+    def __init__(self, dest, sems, by_device):
+        self.dest, self.by_device = dest, by_device
+        self.send_sem, self.recv_sem, self.own_sem = sems
+        self.n_ctx = dest.shape[1]
+        self.me, self.rank = lax.axis_index("ctx"), lax.axis_index("tp")
+
+    @staticmethod
+    def scratch(units, n_ctx):
+        dma = pltpu.SemaphoreType.DMA
+        return [dma((units, n_ctx)), dma((units, n_ctx)), dma((units,))]
+
+    def copy(self, source, unit, k):
+        other = jnp.bitwise_xor(self.me, k)
+        place = other if self.by_device else k
+        return remote(
+            source.at[unit, place],
+            self.dest.at[unit, k],
+            self.send_sem.at[unit, k],
+            self.recv_sem.at[unit, k],
+            (other, self.rank),
+        )
+
+    def own(self, source, unit):
+        place = self.me if self.by_device else 0
+        return pltpu.make_async_copy(source.at[unit, place], self.dest.at[unit, 0], self.own_sem.at[unit])
+
+    def start(self, source, unit):
+        for k in reversed(range(1, self.n_ctx)):
+            self.copy(source, unit, k).start()
+        self.own(source, unit).start()
+
+    def arrived(self, source, unit):
+        for k in range(1, self.n_ctx):
+            self.copy(source, unit, k).wait_recv()
+        self.own(source, unit).wait()
+
+    def sent(self, source, unit):
+        for k in range(1, self.n_ctx):
+            self.copy(source, unit, k).wait_send()
+
+
+def greet(n_ctx, tp_too):
+    index, rank = lax.axis_index("ctx"), lax.axis_index("tp")
+    barrier = pltpu.get_barrier_semaphore()
+    for k in range(1, n_ctx):
+        signal(barrier, (jnp.bitwise_xor(index, k), rank))
+    if tp_too:
+        for device in neighbours():
+            signal(barrier, device)
+    pl.semaphore_wait(barrier, n_ctx - 1 + (2 if tp_too else 0))
+
+
+def in_turn(count):
+    return [count - 1] + list(range(count - 1))
+
+
+def attend_rows(qs, ks, vs, os, tile):
+    length = qs.shape[0]
+    factor = -(HD ** (-0.5)) * LOG2E
+    shift = math.log(length) * LOG2E
+    row_at = lax.broadcasted_iota(jnp.int32, (tile, tile), 0)
+    col_at = lax.broadcasted_iota(jnp.int32, (tile, tile), 1)
+    for i in range(length // tile):
+        query = qs[i * tile : (i + 1) * tile, :]
+
+        def part(j, masked):
+            at = pl.ds(pl.multiple_of(j * tile, tile), tile)
+            raw = times_transposed(query, ks[at, :])
+            prob = 1.0 / (1.0 + jnp.exp2(raw * factor + shift))
+            if masked:
+                prob = jnp.where(row_at >= col_at, prob, 0.0)
+            return dot(prob.astype(BF), vs[at, :])
+
+        total = part(i, True)
+        if i > 0:
+            total = lax.fori_loop(0, i, lambda j, acc: acc + part(j, False), total)
+        os[i * tile : (i + 1) * tile, :] = total.astype(BF)
+
+
+def forward_kernel(n_ctx, groups, units, tile, *refs):
+    x_ref, cot_ref, gain_one, gain_two, wq_ref, wk_ref, wv_ref, wo_ref, cos_ref, sin_ref, valid_ref = refs[:11]
+    n1_out, got_out, heads_out, residual, n2_out, cot_out = refs[11:17]
+    rows_buf, own_buf, send, got, o_send, o_got, qs, ks, vs, os = refs[17:27]
+    rest = refs[27:]
+    n_gather, n_exchange = len(Gather.scratch()), len(Exchange.scratch(1, 2))
+    n1_sems, rest = rest[:n_gather], rest[n_gather:]
+    n2_sems, rest = rest[:n_gather], rest[n_gather:]
+    cot_sems, rest = rest[:n_gather], rest[n_gather:]
+    x_sems, rest = rest[:n_exchange], rest[n_exchange:]
+    o_sems, rest = rest[:n_exchange], rest[n_exchange:]
+    (n1_sem, got_sem), rest = rest[:2], rest[2:]
+    me, rank = lax.axis_index("ctx"), lax.axis_index("tp")
+    odd = lax.rem(rank, 2)
+    heads = wq_ref.shape[1] // HD
+    per_unit = n_ctx // heads
+    unit_rows = per_unit * PAIR
+
+    greet(n_ctx, True)
+    gather_one = Gather(own_buf, rows_buf, groups, n1_sems)
+    gather_two = Gather(own_buf, n2_out, groups, n2_sems)
+    gather_cot = Gather(cot_ref, cot_out, groups, cot_sems)
+    scatter = Scatter(rows_buf, groups, rest[:6], rest[6:], loaded=False)
+    trade = Exchange(got, x_sems, True)
+    trade_back = Exchange(o_got, o_sems, False)
+    order = list(reversed(range(len(groups))))
+    last_u, mid_u, end_u = in_turn(len(units))
+
+    def halves_of(u):
+        return halves_at(odd if units[u][1] else 0)
+
+    def normed(source, gain, at):
+        values = source[at, :].astype(F32)
+        return (values * inverse_rms(values) * gain[...]).astype(BF)
+
+    for g in order:
+        _, rows, own = groups[g]
+        at = pl.ds(own, rows)
+        own_buf[at, :] = normed(x_ref, gain_one, at)
+        gather_one.start(g)
+
+    def query(u, block):
+        base, flipped = units[u]
+        first, second = halves_of(u)
+        at = pl.ds(base + block * PAIR, PAIR)
+        rows = rows_buf[at, :]
+        table = 1 if flipped else 0
+        for which, w_ref in enumerate((wq_ref, wk_ref, wv_ref)):
+            product = dot(rows, w_ref[...])
+            for head in range(heads):
+                part = product[:, head * HD : (head + 1) * HD]
+                if which < 2:
+                    part = part * cos_ref[table] + pltpu.roll(part, HD // 2, 1) * sin_ref[table]
+                else:
+                    part = part * valid_ref[at, :]
+                part = part.astype(BF)
+                send[u, block * heads + head, which, first, :] = part[:BLOCK]
+                send[u, block * heads + head, which, second, :] = part[BLOCK:]
+
+    def query_unit(u):
+        for block in range(per_unit):
+            query(u, block)
+        trade.start(send, u)
+
+    store_n1 = pltpu.make_async_copy(rows_buf, n1_out, n1_sem)
+    store_got = [pltpu.make_async_copy(got.at[u], got_out.at[u], got_sem.at[u]) for u in range(len(units))]
+
+    gather_one.forward(order[0])
+    gather_one.finish(order[0])
+    query_unit(last_u)
+    gather_one.forward(order[1])
+    query_unit(mid_u)
+    gather_one.finish(order[1])
+    for g in order:
+        gather_cot.start(g)
+    query_unit(end_u)
+    store_n1.start()
+
+    def attend(u):
+        trade.arrived(send, u)
+        store_got[u].start()
+        for k in range(n_ctx):
+            front, back = both_places(me, k, n_ctx)
+            for which, dest in enumerate((qs, ks, vs)):
+                dest[front, :] = got[u, k, which, :BLOCK, :]
+                dest[back, :] = got[u, k, which, BLOCK:, :]
+        attend_rows(qs, ks, vs, os, tile)
+        for k in range(n_ctx):
+            front, back = both_places(me, k, n_ctx)
+            o_send[u, k, :BLOCK, :] = os[front, :]
+            o_send[u, k, BLOCK:, :] = os[back, :]
+        trade_back.start(o_send, u)
+
+    def project(u):
+        trade_back.arrived(o_send, u)
+        base, _ = units[u]
+        first, second = halves_of(u)
+        for block in range(per_unit):
+            at = pl.ds(base + block * PAIR, PAIR)
+            low = valid_ref[at, :].astype(BF)
+            for head in range(heads):
+                place = jnp.bitwise_xor(me, block * heads + head)
+                part = jnp.concatenate([o_got[u, place, first, :], o_got[u, place, second, :]], axis=0)
+                heads_out[at, head * HD : (head + 1) * HD] = part * low
+            rows_buf[at, :] = dot(heads_out[at, :], wo_ref[...]).astype(BF)
+
+    def use(at, total):
+        residual[at, :] = x_ref[at, :].astype(F32) + total
+        own_buf[at, :] = normed(residual, gain_two, at)
+
+    def finish_group(g):
+        scatter.total(g, use)
+        gather_two.start(g)
+
+    attend(last_u)
+    for g in order:
+        gather_one.sent(g)
+    store_n1.wait()
+    project(last_u)
+    scatter.start(order[0], loads=False)
+    for g in order:
+        gather_cot.forward(g)
+    scatter.forward(order[0])
+    finish_group(order[0])
+    attend(mid_u)
+    gather_two.forward(order[0])
+    project(mid_u)
+    scatter.start(order[1], (0,), loads=False)
+    attend(end_u)
+    project(end_u)
+    scatter.start(order[1], (1, 3, 2), loads=False)
+    scatter.forward(order[1])
+    finish_group(order[1])
+    gather_two.forward(order[1])
+    for u in range(len(units)):
+        trade.sent(send, u)
+        trade_back.sent(o_send, u)
+        store_got[u].wait()
+    for g in order:
+        gather_cot.finish(g)
+        gather_two.finish(g)
+        gather_two.sent(g)
+        gather_cot.sent(g)
+
+
+def forward_layer(x_own, cot_own, gain_one, gain_two, wq, wk, wv, wo, cos_tab, sin_tab, valid, n_ctx, groups, units):
+    rows, depth = x_own.shape
+    width = wq.shape[1]
+    tokens = valid.shape[0]
+    length = 2 * n_ctx * BLOCK
+    n_units = len(units)
+    vmem = lambda shape, dtype=BF: pltpu.VMEM(shape, dtype)
+    outs = [
+        jax.ShapeDtypeStruct((tokens, depth), BF),
+        jax.ShapeDtypeStruct((n_units, n_ctx, 3, PAIR, HD), BF),
+        jax.ShapeDtypeStruct((tokens, width), BF),
+        jax.ShapeDtypeStruct((rows, depth), F32),
+        jax.ShapeDtypeStruct((tokens, depth), BF),
+        jax.ShapeDtypeStruct((tokens, depth), BF),
+    ]
+    return pl.pallas_call(
+        functools.partial(forward_kernel, n_ctx, groups, units, min(512, length)),
+        out_shape=outs,
+        in_specs=[VMEM_SPEC, ANY_SPEC] + [VMEM_SPEC] * 9,
+        out_specs=[ANY_SPEC, ANY_SPEC, VMEM_SPEC, VMEM_SPEC, ANY_SPEC, ANY_SPEC],
+        scratch_shapes=[
+            vmem((tokens, depth)),
+            vmem((rows, depth)),
+            vmem((n_units, n_ctx, 3, PAIR, HD)),
+            vmem((n_units, n_ctx, 3, PAIR, HD)),
+            vmem((n_units, n_ctx, PAIR, HD)),
+            vmem((n_units, n_ctx, PAIR, HD)),
+        ]
+        + [vmem((length, HD))] * 4
+        + Gather.scratch() * 3
+        + Exchange.scratch(n_units, n_ctx) * 2
+        + [pltpu.SemaphoreType.DMA, pltpu.SemaphoreType.DMA((n_units,))]
+        + Scatter.scratch(rows, depth, loaded=False),
+        compiler_params=pltpu.CompilerParams(vmem_limit_bytes=VMEM_LIMIT, collective_id=3, has_side_effects=True),
+        cost_estimate=pl.CostEstimate(
+            flops=8 * tokens * depth * width, bytes_accessed=8 * tokens * depth, transcendentals=0
+        ),
+    )(x_own, cot_own, gain_one, gain_two, wq, wk, wv, wo, cos_tab, sin_tab, valid)
+
+
+def attend_rows_back(qs, ks, vs, gs, os, dqs, cos_ref, sin_ref, tile):
+    length = qs.shape[0]
+    scale = HD ** (-0.5)
+    factor = -scale * LOG2E
+    shift = math.log(length) * LOG2E
+    count = length // tile
+    key_at = lax.broadcasted_iota(jnp.int32, (tile, tile), 0)
+    query_at = lax.broadcasted_iota(jnp.int32, (tile, tile), 1)
+    dqs[...] = jnp.zeros_like(dqs)
+
+    def unrotate(values, at):
+        return (values * cos_ref[at, :] - pltpu.roll(values, HD // 2, 1) * sin_ref[at, :]).astype(BF)
+
+    for j in range(count):
+        own = slice(j * tile, (j + 1) * tile)
+        keys = ks[own, :]
+        values = vs[own, :]
+
+        def part(i, masked):
+            at = pl.ds(pl.multiple_of(i * tile, tile), tile)
+            query = qs[at, :]
+            grad = gs[at, :]
+            raw = times_transposed(keys, query)
+            prob = 1.0 / (1.0 + jnp.exp2(raw * factor + shift))
+            if masked:
+                prob = jnp.where(query_at >= key_at, prob, 0.0)
+            prob_grad = times_transposed(values, grad)
+            score_grad = (prob_grad * prob * (1.0 - prob)).astype(BF)
+            dqs[at, :] += contract_rows(score_grad, keys)
+            return dot(score_grad, query), dot(prob.astype(BF), grad)
+
+        total = part(j, True)
+        if j + 1 < count:
+
+            def step(i, acc):
+                more = part(i, False)
+                return acc[0] + more[0], acc[1] + more[1]
+
+            total = lax.fori_loop(j + 1, count, step, total)
+        os[1, own, :] = unrotate(total[0] * scale, own)
+        os[2, own, :] = total[1].astype(BF)
+    for i in range(count):
+        at = slice(i * tile, (i + 1) * tile)
+        os[0, at, :] = unrotate(dqs[at, :] * scale, at)
+
+
+def middle_kernel(n_ctx, units, tile, *refs):
+    da_ref, got_ref, wq_ref, wk_ref, wv_ref, wo_ref, cos_ref, sin_ref, valid_ref = refs[:9]
+    dq_ref, dk_ref, dv_ref, partial_out = refs[9:13]
+    rows_buf, got, do_send, do_got, back_send, back_got, qs, ks, vs, gs, os, dqs = refs[13:25]
+    rest = refs[25:]
+    n_exchange = len(Exchange.scratch(1, 2))
+    do_sems, back_sems, rest = rest[:n_exchange], rest[n_exchange : 2 * n_exchange], rest[2 * n_exchange :]
+    da_sem, got_sem, out_sem = rest
+    me, rank = lax.axis_index("ctx"), lax.axis_index("tp")
+    odd = lax.rem(rank, 2)
+    heads = wq_ref.shape[1] // HD
+    per_unit = n_ctx // heads
+    unit_rows = per_unit * PAIR
+    count = len(units)
+    order = in_turn(count)
+
+    def rows_of(u):
+        return pl.ds(units[u][0], unit_rows)
+
+    load_da = [pltpu.make_async_copy(da_ref.at[rows_of(u)], rows_buf.at[rows_of(u)], da_sem.at[u]) for u in range(count)]
+    load_got = [pltpu.make_async_copy(got_ref.at[u], got.at[u], got_sem.at[u]) for u in range(count)]
+    store = [
+        pltpu.make_async_copy(rows_buf.at[rows_of(u)], partial_out.at[rows_of(u)], out_sem.at[u]) for u in range(count)
+    ]
+    for u in order:
+        load_da[u].start()
+    for u in order:
+        load_got[u].start()
+    greet(n_ctx, False)
+    trade = Exchange(do_got, do_sems, True)
+    trade_back = Exchange(back_got, back_sems, False)
+
+    for u in order:
+        load_da[u].wait()
+        base, flipped = units[u]
+        first, second = halves_at(odd if flipped else 0)
+        for block in range(per_unit):
+            at = pl.ds(base + block * PAIR, PAIR)
+            grad = times_transposed(rows_buf[at, :], wo_ref[...]).astype(BF)
+            low = valid_ref[at, :].astype(BF)
+            for head in range(heads):
+                part = grad[:, head * HD : (head + 1) * HD] * low
+                do_send[u, block * heads + head, first, :] = part[:BLOCK]
+                do_send[u, block * heads + head, second, :] = part[BLOCK:]
+        trade.start(do_send, u)
+    for u in order:
+        load_got[u].wait()
+
+    def attend(turn, carry):
+        u = lax.rem(turn + count - 1, count)
+        trade.arrived(do_send, u)
+        for k in range(n_ctx):
+            front, back = both_places(me, k, n_ctx)
+            for which, dest in enumerate((qs, ks, vs)):
+                dest[front, :] = got[u, k, which, :BLOCK, :]
+                dest[back, :] = got[u, k, which, BLOCK:, :]
+            gs[front, :] = do_got[u, k, :BLOCK, :]
+            gs[back, :] = do_got[u, k, BLOCK:, :]
+        attend_rows_back(qs, ks, vs, gs, os, dqs, cos_ref, sin_ref, tile)
+        for k in range(n_ctx):
+            front, back = both_places(me, k, n_ctx)
+            for which in range(3):
+                back_send[u, k, which, :BLOCK, :] = os[which, front, :]
+                back_send[u, k, which, BLOCK:, :] = os[which, back, :]
+        trade_back.start(back_send, u)
+        return carry
+
+    lax.fori_loop(0, count, attend, 0)
+
+    for u in order:
+        trade_back.arrived(back_send, u)
+        base, flipped = units[u]
+        first, second = halves_at(odd if flipped else 0)
+        for block in range(per_unit):
+            at = pl.ds(base + block * PAIR, PAIR)
+            low = valid_ref[at, :].astype(BF)
+            total = None
+            for which, (grad_ref, w_ref) in enumerate(((dq_ref, wq_ref), (dk_ref, wk_ref), (dv_ref, wv_ref))):
+                for head in range(heads):
+                    place = jnp.bitwise_xor(me, block * heads + head)
+                    part = jnp.concatenate(
+                        [back_got[u, place, which, first, :], back_got[u, place, which, second, :]], axis=0
+                    )
+                    grad_ref[at, head * HD : (head + 1) * HD] = part * low if which == 2 else part
+                product = times_transposed(grad_ref[at, :], w_ref[...])
+                total = product if total is None else total + product
+            rows_buf[at, :] = total.astype(BF)
+        store[u].start()
+    for u in order:
+        trade.sent(do_send, u)
+        trade_back.sent(back_send, u)
+        store[u].wait()
+
+
+def middle_layer(da, got, wq, wk, wv, wo, cos_full, sin_full, valid, n_ctx, units):
+    tokens, depth = da.shape
+    width = wq.shape[1]
+    length = 2 * n_ctx * BLOCK
+    count = len(units)
+    vmem = lambda shape, dtype=BF: pltpu.VMEM(shape, dtype)
+    dma = pltpu.SemaphoreType.DMA
+    three, one = (count, n_ctx, 3, PAIR, HD), (count, n_ctx, PAIR, HD)
+    return pl.pallas_call(
+        functools.partial(middle_kernel, n_ctx, units, min(512, length)),
+        out_shape=[jax.ShapeDtypeStruct((tokens, width), BF)] * 3 + [jax.ShapeDtypeStruct((tokens, depth), BF)],
+        in_specs=[ANY_SPEC, ANY_SPEC] + [VMEM_SPEC] * 7,
+        out_specs=[VMEM_SPEC] * 3 + [ANY_SPEC],
+        scratch_shapes=[vmem((tokens, depth)), vmem(three), vmem(one), vmem(one), vmem(three), vmem(three)]
+        + [vmem((length, HD))] * 4
+        + [vmem((3, length, HD)), vmem((length, HD), F32)]
+        + Exchange.scratch(count, n_ctx) * 2
+        + [dma((count,))] * 3,
+        compiler_params=pltpu.CompilerParams(vmem_limit_bytes=VMEM_LIMIT, collective_id=4, has_side_effects=True),
+        cost_estimate=pl.CostEstimate(
+            flops=8 * tokens * depth * width, bytes_accessed=8 * tokens * depth, transcendentals=0
+        ),
+    )(da, got, wq, wk, wv, wo, cos_full, sin_full, valid)
 
 
 def body(
@@ -1247,7 +1694,7 @@
     cos_own = jnp.concatenate([cos_front, cos_back])
     sin_own = jnp.concatenate([sin_front, sin_back])
     sequences = counts.shape[1]
-    paired = lax.axis_size("tp") == 4 and sequences == 6
+    paired = by_four() and sequences == 6 and n_ctx == 2 * heads
     if paired:
         ranks = [rank ^ k for k in range(4)]
         seq_a = [3 * (r >> 1) + 2 * (r & 1) for r in ranks]
@@ -1387,57 +1834,6 @@
         parts = [state[key, n] for n in ("a", "b") if n in names]
         return jnp.concatenate(parts) if len(parts) > 1 else parts[0]
 
-    only_b(norm_one)
-    only_b(gather_a("n1"))
-    norm_one("a")
-    for n in names:
-        state["cot", n] = g_own[n]
-    fence()
-    only_b(gather_b("n1"))
-    fence()
-    gather_a("n1")("a")
-    only_b(query)
-    fence()
-    gather_b("n1")("a")
-    only_b(swap_part("qkv", near, "got"))
-    fence()
-    only_b(swap_part("qkv", far, "got"))
-    only_b(gather_a("cot"))
-    query("a")
-    fence()
-    swap_part("qkv", near, "got")("a")
-    only_b(attend)
-    only_b(gather_b("cot"))
-    gather_a("cot")("a")
-    fence()
-    swap_part("qkv", far, "got")("a")
-    only_b(swap_part("mixed", range(n_ctx), "back"))
-    gather_b("cot")("a")
-    fence()
-    attend("a")
-    only_b(project)
-    only_b(scatter_a("r"))
-    fence()
-    swap_part("mixed", range(n_ctx), "back")("a")
-    only_b(scatter_b("r"))
-    only_b(norm_two)
-    only_b(gather_a("n2"))
-    fence()
-    project("a")
-    only_b(gather_b("n2"))
-    fence()
-    scatter_a("r")("a")
-    only_b(core_mlp)
-    fence()
-    scatter_b("r")("a")
-    fence()
-    norm_two("a")
-    gather_a("n2")("a")
-    fence()
-    gather_b("n2")("a")
-    fence()
-    core_mlp("a")
-    fence()
     groups = tuple((first_row[n], rows_of[n] // 4, first_row[n] // 4) for n in ("a", "b") if n in names)
     in_order = [n for n in ("a", "b") if n in names]
 
@@ -1447,15 +1843,35 @@
     def by_group(array, scale=1):
         return {n: array[first_row[n] // scale : (first_row[n] + rows_of[n]) // scale] for n in in_order}
 
-    h, dgp, dup = state["mlp"]
-    all_n1, all_n2, all_cot, heads_out = (joined(key) for key in ("n1", "n2", "cot", "heads"))
+    own_grads, own_x = own_joined(g_own), own_joined(x_own)
+    if paired:
+        units = ((0, False), (2 * PAIR, False), (4 * PAIR, True))
+        flat_valid = jnp.concatenate([valid_head["a"], valid_head["b"]])
+        tabs = [jnp.stack([tab, flip_back(tab)]) for tab in (cos_own, sin_own)]
+        all_n1, got, heads_out, own_residual, all_n2, all_cot = forward_layer(
+            own_joined(own_rows(tokens[0])), own_grads, gain_one[None], gain_two[None], w_query, w_key, w_value, w_output,
+            *tabs, flat_valid, n_ctx, groups, units,
+        )
+    else:
+        norm_one("a")
+        state["cot", "a"] = g_own["a"]
+        gather_a("n1")("a")
+        query("a")
+        swap_part("qkv", range(n_ctx), "got")("a")
+        attend("a")
+        swap_part("mixed", range(n_ctx), "back")("a")
+        project("a")
+        scatter_a("r")("a")
+        norm_two("a")
+        gather_a("n2")("a")
+        gather_a("cot")("a")
+        all_n1, all_n2, all_cot = state["n1", "a"], gathered(state["n2", "a"]), gathered(state["cot", "a"])
+        heads_out, own_residual = state["heads", "a"], state["residual", "a"]
+    h, dgp, dup = mlp_core(all_n2, all_cot, w_gate, w_up, w_down, total_rows, 0)
     d_partial = (times_transposed(dgp, w_gate) + times_transposed(dup, w_up)).astype(BF)
     y_partial = dot(h, w_down).astype(BF)
-    own_residual, own_grads, own_x = (
-        own_joined(part) for part in ({n: state["residual", n] for n in names}, g_own, x_own)
-    )
     feed_items, feed_rights = [(h, 0), (dgp, 1), (dup, 1)], [all_cot, all_n2]
-    if split:
+    if paired:
         extra = feed_extra(groups, d_partial, y_partial, own_residual, own_grads, gain_two[None])
         sum_down, sum_gate, sum_up, dr, da, gain_two_grad, output = weight_sums(feed_items, feed_rights, n_ctx, 1, extra)
     else:
@@ -1464,19 +1880,19 @@
         dr = own_grads.astype(F32) + back
         da = gathered(gather_first(dr.astype(BF)))
         output = (own_residual + scattered(scatter_first((y_partial,)))).astype(BF)
-    for n, rows in by_group(da).items():
-        state["da", n] = rows
-        state["do", n] = heads_back(scalars[n], rows, w_output, valid_wide[n], n_ctx)
-    for n in names:
-        swap_part("do", range(n_ctx), "gdo")(n)
-    for n in names:
-        attend_back(n)
-        swap_part("dqkv", range(n_ctx), "gdqkv")(n)
-    for n in names:
-        query_back(n)
-    i_partial = joined("i")
-    input_items = [(heads_out, 0), (joined("dq"), 1), (joined("dk"), 1), (joined("dv"), 1)]
-    if split:
+    if paired:
+        dq, dk, dv, i_partial = middle_layer(
+            da, got, w_query, w_key, w_value, w_output, cos_full, sin_full, flat_valid, n_ctx, units
+        )
+    else:
+        state["do", "a"] = heads_back(scalars["a"], da, w_output, valid_wide["a"], n_ctx)
+        swap_part("do", range(n_ctx), "gdo")("a")
+        attend_back("a")
+        swap_part("dqkv", range(n_ctx), "gdqkv")("a")
+        query_back("a")
+        dq, dk, dv, i_partial = (state[key, "a"] for key in ("dq", "dk", "dv", "i"))
+    input_items = [(heads_out, 0), (dq, 1), (dk, 1), (dv, 1)]
+    if paired:
         extra = input_extra(groups, i_partial, own_x, dr, gain_one[None])
         sum_out, sum_q, sum_k, sum_v, input_grad, gain_one_grad = weight_sums(
             input_items, [da, all_n1], n_ctx, 2, extra
@@ -1491,8 +1907,8 @@
         for bit in range(size.bit_length() - 1):
             gains = gains + lax.ppermute(gains, axis, [(i, i ^ (1 << bit)) for i in range(size)])
     return (
-        whole_rows(by_group(output, 4))[None] if split else output[None],
-        whole_rows(by_group(input_grad, 4))[None] if split else input_grad[None],
+        whole_rows(by_group(output, 4))[None] if paired else output[None],
+        whole_rows(by_group(input_grad, 4))[None] if paired else input_grad[None],
         gains[0],
         sum_q.T.astype(F32),
         sum_k.T.astype(F32),

time: 1300 us -> 1180 us (0.908)
  Pallas kernels: 671 us -> 974 us
  waiting for transfers between devices: 220 us -> 0.66 us
  starting transfers between devices: 112 us -> 3.74 us
  local copies, waits for them, and re-layouts: 119 us -> 59.5 us
  other arithmetic: 114 us -> 70.8 us
    pallas_call x12 -> x2, Pallas kernels: 132 us -> 464 us  [the longest x1 312 us: forward_layer(): pl.pallas_call(functools.partial(forward_kernel, n_ctx, groups, units, mi...]
    ppermute x88 -> x0, waiting for transfers between devices: 220 us -> none  [the longest x56 137 us: exchange(): lax.ppermute(pieces[k], 'ctx', [(i, i ^ k) for i in range(n_ctx)])]
    ppermute x88 -> x0, starting transfers between devices: 108 us -> none  [the longest x56 83.4 us: exchange(): lax.ppermute(pieces[k], 'ctx', [(i, i ^ k) for i in range(n_ctx)])]
    unnamed x260 -> x30, local copies, waits for them, and re-layouts: 85 us -> 52.8 us
    concatenate x10 -> x3, other arithmetic: 30.9 us -> 0.02 us  [the longest x1 0.01 us: body(): jnp.concatenate([valid_of(s, r & 1) for s, r in zip(seq_b, ranks)])]
    pallas_call x2, Pallas kernels: 482 us -> 459 us  [weight_sums(): pl.pallas_call(functools.partial(sums_kernel, n_ctx, shapes, len(rights),...]
    pallas_call x2 -> x1, Pallas kernels: 57.3 us -> 51.2 us  [mlp_core(): pl.pallas_call(mlp_kernel, out_shape=(out, out, out), grid=(hidden // til...]
  transfers between devices with their start and end apart: 93 -> 5, of which waited for: 30 -> 1; matrix products, arithmetic and copies ran while one was open for 13% -> 9% of each run, Pallas kernels for 10% -> 0%
where the time goes in v3:
time: 1180 us; the launch traced here: 1170 us
  Pallas kernels  974 us (83%)
  other arithmetic  70.8 us (6%)
  local copies, waits for them, and re-layouts  59.5 us (5%)
  matrix products  57.8 us (5%)
    pallas_call x2, Pallas kernels, weight_sums(): pl.pallas_call(functools.partial(sums_kernel, n_ctx, shapes, len(rights),...  459 us
    pallas_call x1, Pallas kernels, forward_layer(): pl.pallas_call(functools.partial(forward_kernel, n_ctx, groups, units, mi...  312 us
    pallas_call x1, Pallas kernels, middle_layer(): pl.pallas_call(functools.partial(middle_kernel, n_ctx, units, min(512, le...  152 us
    unnamed x30, local copies, waits for them, and re-layouts  52.8 us
    pallas_call x1, Pallas kernels, mlp_core(): pl.pallas_call(mlp_kernel, out_shape=(out, out, out), grid=(hidden // til...  51.2 us
    dot_general x2, matrix products, times_transposed(): lax.dot_general(left, right, (((1,), (1,)), ((), ())), preferred_element_...  38.7 us
  transfers between devices with their start and end apart: 5, of which 1 were waited for; matrix products, arithmetic and copies ran while one was open for 9% of the time, Pallas kernels for 0%

profile of v3, /device:TPU:1, one launch (start us, length us, event | category | flops | bytes accessed | tf_op | source)
XLA Modules:
  0.0 1167.8 jit_solution(5910232642351766890)
XLA Ops:
  0.8 1.6 constant_dynamic-slice_fusion.4
  9.2 1.3 broadcast_in_dim.40
  10.5 1.3 broadcast_in_dim.41
  13.1 1.7 dynamic-slice_bitcast_fusion
  14.7 1.3 iota_compare_fusion.2
  16.1 1.3 iota_compare_fusion
  18.7 3.7 multiply_sine_fusion
  22.4 1.9 pad_maximum_fusion.2
  26.0 2.6 fusion.8
  29.8 311.5 %shard_map.203 = (bf16[1536,2048]{1,0:T(8,128)(2,1)}, bf16[3,8,3,256,128]{4,3,2,1,0:T(8,128)(2,1)}, bf16[1536,512]{1,0:T(8,128)(2,1)}, f32[384,2048]{1,0:T(8,128...) custom-call(bf16[384,2048]{1,0:T(8,128)(2,1)} %get-tuple-element.77.refs_0_, ...), custom_call_target="tpu_custom_call" | custom-call | flops 12884901888 | bytes 25165824 | tf_op jit(solution)/shard_map/pallas_call | solution.py:1461
  341.3 51.2 %shard_map.204 = (bf16[1536,2048]{1,0:T(8,128)(2,1)}, bf16[1536,2048]{1,0:T(8,128)(2,1)}, bf16[1536,2048]{1,0:T(8,128)(2,1)}) custom-call(bf16[1536,2048]{1,0:T(8,128)(2,1)} %get-tuple-element.37.n_ref.refs_4_, bf16[1536,2048]{1,0:T(8,128)(2,1)} %get-tuple-element.38.g_ref.refs_3_, bf16[2048,2048]{1,0:T(8,128)(2,1)} %wg_ref.1, bf16[2048,2048]{1,0:T(8,128)(2,1)} %wu_ref.1, ...), custom_call_target="tpu_custom_call" | custom-call | flops 38654705664 | bytes 56623104 | tf_op jit(solution)/shard_map/pallas_call | solution.py:546
  392.5 19.2 %convolution_convert_fusion.refs_6_ = bf16[1536,2048]{1,0:T(8,128)(2,1)} fusion(bf16[1536,2048]{1,0:T(8,128)(2,1)} %get-tuple-element.39.refs_0_, bf16[2048,2048]{1,0:T(8,128)(2,1)} %wd_ref.1), kind=kOutput, calls=%fused_computation.3 | convolution fusion | flops 12888047616 | bytes 20971520 | tf_op jit(solution)/shard_map/dot_general | solution.py:26
  411.7 17.5 %fusion.10 = f32[1536,2048]{1,0:T(8,128)} fusion(bf16[1536,2048]{1,0:T(8,128)(2,1)S(1)} %copy-done.8, bf16[2048,2048]{1,0:T(8,128)(2,1)} %wg_ref.1), kind=kOutput, calls=%fused_computation.68 | convolution fusion | flops 12884901888 | bytes 27262976 | tf_op jit(solution)/shard_map/dot_general | solution.py:34
  429.2 21.2 %add_convert_fusion.refs_5_ = bf16[1536,2048]{1,0:T(8,128)(2,1)} fusion(f32[1536,2048]{1,0:T(8,128)} %fusion.10, bf16[1536,2048]{1,0:T(8,128)(2,1)} %get-tuple-element.41.refs_2_, bf16[2048,2048]{1,0:T(8,128)(2,1)} %wu_ref.1), kind=kOutput, calls=%fused_computation.2 | convolution fusion | flops 12891193344 | bytes 33554432 | tf_op jit(solution)/shard_map/dot_general | solution.py:34
  450.4 320.5 %shard_map.205 = (bf16[2048,2048]{1,0:T(8,128)(2,1)}, bf16[2048,2048]{1,0:T(8,128)(2,1)}, bf16[2048,2048]{1,0:T(8,128)(2,1)}, f32[384,2048]{1,0:T(8,128)}, bf16[...) custom-call(bf16[1536,2048]{1,0:T(8,128)(2,1)} %get-tuple-element.39.refs_0_, ...), custom_call_target="tpu_custom_call" | custom-call | flops 38654705664 | bytes 44040192 | tf_op jit(solution)/shard_map/pallas_call | solution.py:1044
  770.9 152.3 %shard_map.206 = (bf16[1536,512]{1,0:T(8,128)(2,1)}, bf16[1536,512]{1,0:T(8,128)(2,1)}, bf16[1536,512]{1,0:T(8,128)(2,1)}, bf16[1536,2048]{1,0:T(8,128)(2,1)}) custom-call(bf16[1536,2048]{1,0:T(8,128)(2,1)} %get-tuple-element.45.refs_0_.refs_4_, bf16[3,8,3,256,128]{4,3,2,1,0:T(8,128)(2,1)} %get-tuple-element.46.refs_1_, bf16[2048,512]{1,0:T(8,128)(2,1)} %refs_2_.1, ...), custom_call_target="tpu_custom_call" | custom-call | flops 12884901888 | bytes 25165824 | tf_op jit(solution)/shard_map/pallas_call | solution.py:1634
  923.2 138.2 %shard_map.207 = (bf16[512,2048]{1,0:T(8,128)(2,1)}, bf16[512,2048]{1,0:T(8,128)(2,1)}, bf16[512,2048]{1,0:T(8,128)(2,1)}, bf16[512,2048]{1,0:T(8,128)(2,1)}, bf...) custom-call(bf16[1536,512]{1,0:T(8,128)(2,1)} %get-tuple-element.44.refs_0_, bf16[1536,512]{1,0:T(8,128)(2,1)} %get-tuple-element.47.refs_1_, ...), custom_call_target="tpu_custom_call" | custom-call | flops 12884901888 | bytes 14680064 | tf_op jit(solution)/shard_map/pallas_call | solution.py:1044
  1062.8 11.7 convert_bitcast_fusion.1
  1074.4 11.4 convert_bitcast_fusion
  1085.8 2.5 convert_bitcast_fusion.4
  1089.4 2.5 convert_bitcast_fusion.3
  1092.2 2.5 convert_bitcast_fusion.2
  1095.0 1.8 fusion
  1097.6 1.8 collective-permute-start.4
  1099.4 1.8 fusion.1
  1101.2 5.3 copy.23
  1106.5 5.3 copy.24
  1111.8 5.5 copy.25
  1117.3 2.5 convert_element_type.80
  1119.9 17.6 %copy.26 = f32[2048,2048]{1,0:T(8,128)} copy(f32[2048,2048]{0,1:T(8,128)} %convert_bitcast_fusion.1) | data formatting | bytes 33554432
  1137.5 17.6 %copy.27 = f32[2048,2048]{1,0:T(8,128)} copy(f32[2048,2048]{0,1:T(8,128)} %convert_bitcast_fusion) | data formatting | bytes 33554432
  1155.1 11.7 convert_element_type.85
  (70 shorter events, 16.5 us)
Async XLA Ops:
  392.5 19.2 %copy-start.8 = (bf16[1536,2048]{1,0:T(8,128)(2,1)S(1)}, bf16[1536,2048]{1,0:T(8,128)(2,1)}, u32[]{:S(2)}) copy-start(bf16[1536,2048]{1,0:T(8,128)(2,1)} %get-tuple-element.40.refs_1_) | copy-start | bytes 18874372
  923.2 138.2 %copy-start.6 = (f32[1,2048]{1,0:T(1,128)S(1)}, f32[1,2048]{1,0:T(1,128)}, u32[]{:S(2)}) copy-start(f32[1,2048]{1,0:T(1,128)} %get-tuple-element.55) | copy-start | bytes 24580
  1062.1 26.3 %collective-permute-start = (f32[2,2048]{1,0:T(2,128)S(1)}, f32[2,2048]{1,0:T(2,128)S(1)}, u32[]{:S(2)}, u32[]{:S(2)}) collective-permute-start(f32[2,2048]{1,0:T(2,128)S(1)} %pad_maximum_fusion.6), channel_id=1, source_target_pairs={{0,1},{1,0},{2,3},{3,2},{4,5},{5,4},{6,7},{7,6},{8,9},{9,8},{10,11... | collective-permute-start | bytes 49160 | tf_op jit(solution)/shard_map/ppermute | solution.py:1908
  1074.4 11.4 copy-start.5
  1085.8 2.6 copy-start.7
  1085.8 3.5 copy-start.4
  1088.4 3.8 copy-start.3
  1088.4 3.5 collective-permute-start.1
  1091.9 2.9 copy-start
  1091.9 3.0 collective-permute-start.2
  1094.8 2.0 copy-start.1
  1095.0 2.7 collective-permute-start.3
  1097.6 69.1 %collective-permute-start.4 = (f32[2,2048]{1,0:T(2,128)S(1)}, f32[2,2048]{1,0:T(2,128)S(1)}, u32[]{:S(2)}, u32[]{:S(2)}) collective-permute-start(f32[2,2048]{1,0:T(2,128)S(1)} %add.177), channel_id=1, source_target_pairs={{0,16},{4,20},{8,24},{12,28},{16,0},{20,4},{24,8},{28,12},{1,17},{... | collective-permute-start | bytes 49160 | tf_op jit(solution)/shard_map/ppermute | solution.py:1908
  1111.8 5.5 copy-start.2

commit v4 on v3

--- a/solution.py
+++ b/solution.py
@@ -16,7 +16,7 @@
 LOG2E = 1.4426950408889634
 BF = jnp.bfloat16
 F32 = jnp.float32
-VMEM_LIMIT = 58 * 1024 * 1024
+VMEM_LIMIT = 60 * 1024 * 1024
 
 X_SWAP = [(i, i ^ 1) for i in range(4)]
 Y_SWAP = [(i, i ^ 2) for i in range(4)]
@@ -747,8 +747,8 @@
             copy.wait_send()
 
 
-ROWS = 128
-CORE_SLOTS, HOP_SLOTS = 3, 4
+TILE, ROWS = 128, 64
+CORE_SLOTS, HOP_SLOTS = 4, 4
 
 
 class Ring:
@@ -787,12 +787,14 @@
             pl.semaphore_signal(self.credit, inc=1, device_id=device, device_id_type=pl.DeviceIdType.MESH)
 
 
-def sums_kernel(n_ctx, items, n_right, n_extra, tasks, *refs):
+def sums_kernel(n_ctx, items, n_right, n_extra, tasks, late, *refs):
     n_left = len(items)
     left_refs, right_refs = refs[:n_left], refs[n_left : n_left + n_right]
     extra_in, refs = refs[n_left + n_right : n_left + n_right + n_extra[0]], refs[n_left + n_right + n_extra[0] :]
     out_refs, extra_out, refs = refs[:n_left], refs[n_left : n_left + n_extra[1]], refs[n_left + n_extra[1] :]
     extra_scratch, refs = refs[: n_extra[2]], refs[n_extra[2] :]
+    right_refs = list(right_refs) + [extra_out[k] for k in late]
+    n_right += len(late)
     (
         left_buf, right_buf, other_buf, ring, core_in, hop_in, hop_mid, hop_out, core_out,
         left_sem, right_sem, core_send, core_recv, in_send, in_recv, mid_send, mid_recv, out_send, out_recv,
@@ -851,9 +853,10 @@
     to_before = Ring(hop_out, out_send, out_recv, out_credit, total)
     to_final = Ring(core_out, fin_send, fin_recv, fin_credit, total)
 
-    rights = [pltpu.make_async_copy(right_refs[k], right_buf.at[k], right_sem.at[k]) for k in range(n_right)]
-    for copy in rights:
-        copy.start()
+    def right_copy(k):
+        return pltpu.make_async_copy(right_refs[k], right_buf.at[k % 2], right_sem.at[k % 2])
+
+    right_copy(0).start()
 
     def for_item(at, action):
         for number in range(n_left):
@@ -867,8 +870,9 @@
 
     def left_copy(number, chunk, slot, which):
         side = core if which == 0 else 1 - core
+        half = items[number][2] * ROWS
         return pltpu.make_async_copy(
-            left_refs[number].at[:, pl.ds(rows_at(number, chunk, side), ROWS)],
+            left_refs[number].at[:, pl.ds(pl.multiple_of(side * half + chunk // 2 * TILE, TILE), TILE)],
             left_buf.at[slot, which],
             left_sem.at[slot, which],
         )
@@ -876,16 +880,17 @@
     def load_left(at):
         def action(number, chunk):
             for which in range(2):
-                left_copy(number, chunk, lax.rem(at, 2), which).start()
+                left_copy(number, chunk, lax.rem(at // 2, 2), which).start()
 
         for_item(at, action)
 
     load_left(0)
-    planned = tasks(extra_in, extra_out, extra_scratch) if tasks is not None else {}
+    planned, each = tasks(extra_in, extra_out, extra_scratch) if tasks is not None else ({}, None)
     if 0 in planned:
         planned.pop(0)()
-    for copy in rights:
-        copy.wait()
+    if n_right > 1:
+        right_copy(1).start()
+    right_copy(0).wait()
 
     def step(i, carry):
         def at_lag(lag):
@@ -973,9 +978,9 @@
         def _():
             slot = lax.rem(at, n_ring)
             source = ring.at[slot]
-            own = other_buf.at[lax.rem(at, 2)]
-            to_core.sent(own, at, lax.rem(at, 2), partner)
-            got = to_core.arrived(own, at, lax.rem(at, 2), partner)
+            own = other_buf.at[lax.rem(at, 4)]
+            to_core.sent(own, at, lax.rem(at, 4), partner)
+            got = to_core.arrived(own, at, lax.rem(at, 4), partner)
             ring[slot] = add_low(ring[slot], got[...])
             to_core.free(at, partner)
 
@@ -999,21 +1004,42 @@
         for when, task in planned.items():
             pl.when(i == when)(task)
 
-        @pl.when(i + 1 < total)
+        if each is not None:
+            each(i)
+
+        @pl.when((i + 2 < total) & (lax.rem(i, 2) == 0))
         def _():
-            load_left(i + 1)
-
-        @pl.when(i < total)
+            load_left(i + 2)
+
+        @pl.when((i < total) & (lax.rem(i, 2) == 0))
         def _():
-            slot = lax.rem(i, 2)
+            slot = lax.rem(i // 2, 2)
 
             def action(number, chunk):
+                which_right = items[number][1]
+                if which_right > 0 and items[number - 1][1] != which_right:
+
+                    @pl.when(chunk == 0)
+                    def _():
+                        right_copy(which_right).wait()
+
+                if which_right > 0 and which_right + 1 < n_right:
+
+                    @pl.when(chunk == items[number][2] // 2)
+                    def _():
+                        right_copy(which_right + 1).start()
+
                 for which in range(2):
                     left_copy(number, chunk, slot, which).wait()
-                right = right_buf.at[items[number][1]]
-                other_buf[slot] = contract_rows(left_buf[slot, 1], right[...]).astype(BF)
-                to_core.send(other_buf.at[slot], i, slot, partner)
-                ring[lax.rem(i, n_ring)] = contract_rows(left_buf[slot, 0], right[...]).astype(BF)
+                right = right_buf.at[which_right % 2]
+                product = contract_rows(left_buf[slot, 1], right[...]).astype(BF)
+                for part in range(2):
+                    place = lax.rem(i + part, 4)
+                    other_buf[place] = product[part * ROWS : (part + 1) * ROWS]
+                    to_core.send(other_buf.at[place], i + part, place, partner)
+                product = contract_rows(left_buf[slot, 0], right[...]).astype(BF)
+                for part in range(2):
+                    ring[lax.rem(i + part, n_ring)] = product[part * ROWS : (part + 1) * ROWS]
 
             for_item(i, action)
 
@@ -1031,26 +1057,26 @@
     lax.fori_loop(0, total + lag_w, step, 0)
 
 
-def weight_sums(items, rights, n_ctx, collective_id, extra=None):
+def weight_sums(items, rights, n_ctx, collective_id, extra=None, late=()):
     tokens, width = rights[0].shape
     shapes = [(k, right, left.shape[1] // 2 // ROWS) for k, (left, right) in enumerate(items)]
     mid = n_ctx // 4
-    n_ring = mid + 2 + 2 * (mid - 1) + 3
+    n_ring = mid + 2 + 2 * (mid - 1) + 4
     any_spec = pl.BlockSpec(memory_space=pl.ANY)
     args, arg_specs, outs, out_specs, scratch, tasks = extra if extra is not None else ([], [], [], [], [], None)
     counts = (len(args), len(outs), len(scratch))
     chunk = (ROWS, width)
     dma = pltpu.SemaphoreType.DMA
     return pl.pallas_call(
-        functools.partial(sums_kernel, n_ctx, shapes, len(rights), counts, tasks),
+        functools.partial(sums_kernel, n_ctx, shapes, len(rights), counts, tasks, late),
         out_shape=[jax.ShapeDtypeStruct((left.shape[1], width), BF) for left, _ in items] + outs,
         in_specs=[any_spec] * (len(items) + len(rights)) + arg_specs,
         out_specs=[any_spec] * len(items) + out_specs,
         scratch_shapes=scratch
         + [
-            pltpu.VMEM((2, 2, tokens, ROWS), BF),
-            pltpu.VMEM((len(rights), tokens, width), BF),
-            pltpu.VMEM((2,) + chunk, BF),
+            pltpu.VMEM((2, 2, tokens, TILE), BF),
+            pltpu.VMEM((min(2, len(rights) + len(late)), tokens, width), BF),
+            pltpu.VMEM((4,) + chunk, BF),
             pltpu.VMEM((n_ring,) + chunk, BF),
             pltpu.VMEM((CORE_SLOTS,) + chunk, BF),
             pltpu.VMEM((HOP_SLOTS,) + chunk, BF),
@@ -1058,8 +1084,8 @@
             pltpu.VMEM((HOP_SLOTS,) + chunk, BF),
             pltpu.VMEM((CORE_SLOTS,) + chunk, BF),
             dma((2, 2)),
-            dma((len(rights),)),
             dma((2,)),
+            dma((4,)),
             dma((CORE_SLOTS,)),
             dma((n_ring,)),
             dma((HOP_SLOTS,)),
@@ -1096,20 +1122,85 @@
 
 
 def feed_tasks(groups, extra_in, extra_out, scratch):
-    d_ref, y_ref, residual, grads, gain = extra_in
-    dr, da_all, gain_grad, output = extra_out
+    dgp_ref, dup_ref, wg_ref, wu_ref, residual, grads, gain = extra_in
+    dr, da_all, gain_grad, d_ref = extra_out
     n = len(Scatter.scratch(16, 128))
     bufs, rest = scratch[:n], scratch[n:]
-    da_own, free, gather_sems = rest[0], rest[1], rest[2:]
-    first = Scatter(d_ref, groups, bufs[:9], bufs[9:])
-    last = Scatter(y_ref, groups, bufs[:9], bufs[9:])
-    gather = Gather(da_own, da_all, groups, gather_sems)
+    weights, lefts, tile_out, weight_sem, left_sem, out_sem = rest[:6]
+    da_own = bufs[0]
+    scatter = Scatter(d_ref, groups, bufs[:9], bufs[9:])
+    gather = Gather(da_own, da_all, groups, rest[6:])
     order = list(reversed(range(len(groups))))
+    rows, columns = lefts.shape[2], weights.shape[1]
+    row_tiles = dgp_ref.shape[0] // rows
+    tiles = row_tiles * (d_ref.shape[1] // columns)
+
+    def weight_copies(part):
+        at = pl.ds(pl.multiple_of(part * columns, columns), columns)
+        return [
+            pltpu.make_async_copy(ref.at[at], weights.at[k], weight_sem.at[k]) for k, ref in enumerate((wg_ref, wu_ref))
+        ]
+
+    def left_copies(tile):
+        at = pl.ds(pl.multiple_of(lax.rem(tile, row_tiles) * rows, rows), rows)
+        slot = lax.rem(tile, 2)
+        return [
+            pltpu.make_async_copy(ref.at[at], lefts.at[slot, k], left_sem.at[slot, k])
+            for k, ref in enumerate((dgp_ref, dup_ref))
+        ]
+
+    def out_copy(tile):
+        slot = lax.rem(tile, 2)
+        return pltpu.make_async_copy(
+            tile_out.at[slot],
+            d_ref.at[
+                pl.ds(pl.multiple_of(lax.rem(tile, row_tiles) * rows, rows), rows),
+                pl.ds(pl.multiple_of(tile // row_tiles * columns, columns), columns),
+            ],
+            out_sem.at[slot],
+        )
 
     def begin():
         gain_grad[...] = jnp.zeros_like(gain_grad)
+        for copy in weight_copies(0) + left_copies(0):
+            copy.start()
+
+    def each(i):
+        @pl.when(i < tiles)
+        def _():
+            slot = lax.rem(i, 2)
+
+            @pl.when(i + 1 < tiles)
+            def _():
+                for copy in left_copies(i + 1):
+                    copy.start()
+
+            @pl.when(lax.rem(i, row_tiles) == 0)
+            def _():
+                @pl.when(i > 0)
+                def _():
+                    for copy in weight_copies(i // row_tiles):
+                        copy.start()
+
+                for copy in weight_copies(i // row_tiles):
+                    copy.wait()
+
+            for copy in left_copies(i):
+                copy.wait()
+            total = times_transposed(lefts[slot, 0], weights[0]) + times_transposed(lefts[slot, 1], weights[1])
+
+            @pl.when(i >= 2)
+            def _():
+                out_copy(i - 2).wait()
+
+            tile_out[slot] = total.astype(BF)
+            out_copy(i).start()
+
+    def start():
+        out_copy(tiles - 2).wait()
+        out_copy(tiles - 1).wait()
         for g in order:
-            first.start(g)
+            scatter.start(g)
 
     def use(at, total):
         back, more = norm_back_rows(residual[at, :], gain[...], total)
@@ -1119,101 +1210,118 @@
         gain_grad[...] += more
 
     def spread(g):
-        first.total(g, use)
+        scatter.total(g, use)
         gather.start(g)
 
-    def use_out(at, total):
-        output[at, :] = (residual[at, :] + total).astype(BF)
-
-    def again():
-        for device in neighbours():
-            signal(free, device)
+    def finish():
         for g in order:
             gather.finish(g)
             gather.sent(g)
 
-    def begin_out():
+    plan = {
+        0: begin,
+        tiles: start,
+        tiles + 4: lambda: scatter.forward(order[0]),
+        tiles + 7: lambda: scatter.forward(order[-1]),
+        tiles + 8: lambda: spread(order[0]),
+        tiles + 10: lambda: spread(order[-1]),
+        tiles + 13: lambda: gather.forward(order[0]),
+        tiles + 17: lambda: gather.forward(order[-1]),
+        tiles + 23: finish,
+    }
+    return plan, each
+
+
+def feed_extra(groups, dgp, dup, wg, wu, residual, grads, gain):
+    rows, width = residual.shape
+    tokens, hidden = dgp.shape
+    dma = pltpu.SemaphoreType.DMA
+    outs = [
+        jax.ShapeDtypeStruct((rows, width), F32),
+        jax.ShapeDtypeStruct((tokens, width), BF),
+        jax.ShapeDtypeStruct((1, width), F32),
+        jax.ShapeDtypeStruct((tokens, width), BF),
+    ]
+    scratch = (
+        Scatter.scratch(rows, width)
+        + [
+            pltpu.VMEM((2, width // 2, hidden), BF),
+            pltpu.VMEM((2, 2, PAIR, hidden), BF),
+            pltpu.VMEM((2, PAIR, width // 2), BF),
+            dma((2,)),
+            dma((2, 2)),
+            dma((2,)),
+        ]
+        + Gather.scratch()
+    )
+    return (
+        [dgp, dup, wg, wu, residual, grads, gain],
+        [ANY_SPEC] * 4 + [VMEM_SPEC] * 3,
+        outs,
+        [VMEM_SPEC, ANY_SPEC, VMEM_SPEC, ANY_SPEC],
+        scratch,
+        functools.partial(feed_tasks, groups),
+    )
+
+
+def input_tasks(groups, extra_in, extra_out, scratch):
+    i_ref, y_ref, rows_in, dr, gain, residual = extra_in
+    input_grad, gain_grad, output = extra_out
+    bufs, free = scratch[:-1], scratch[-1]
+    first = Scatter(i_ref, groups, bufs[:9], bufs[9:])
+    last = Scatter(y_ref, groups, bufs[:9], bufs[9:])
+    order = list(reversed(range(len(groups))))
+
+    def begin():
+        gain_grad[...] = jnp.zeros_like(gain_grad)
+        for g in order:
+            first.start(g)
+
+    def use(at, total):
+        back, more = norm_back_rows(rows_in[at, :].astype(F32), gain[...], total)
+        input_grad[at, :] = (dr[at, :] + back).astype(BF)
+        gain_grad[...] += more
+
+    def again():
+        first.total(order[-1], use)
+        for device in neighbours():
+            signal(free, device)
         pl.semaphore_wait(free, 2)
         for g in order:
             last.start(g)
 
-    def forward_all():
+    def use_out(at, total):
+        output[at, :] = (residual[at, :] + total).astype(BF)
+
+    def finish():
         for g in order:
-            last.forward(g)
-
-    plan = {
+            last.total(g, use_out)
+
+    return {
         0: begin,
-        2: lambda: first.forward(order[0]),
-        4: lambda: first.forward(order[-1]),
-        5: lambda: spread(order[0]),
-        6: lambda: spread(order[-1]),
-        8: lambda: gather.forward(order[0]),
-        10: lambda: gather.forward(order[-1]),
-        12: again,
-        13: begin_out,
-        16: forward_all,
-        18: lambda: [last.total(g, use_out) for g in order] and None,
-    }
-    return plan
-
-
-def feed_extra(groups, d_partial, y_partial, residual, grads, gain):
-    rows, width = residual.shape
+        3: lambda: first.forward(order[0]),
+        8: lambda: first.forward(order[-1]),
+        9: lambda: first.total(order[0], use),
+        11: again,
+        15: lambda: last.forward(order[0]),
+        20: lambda: last.forward(order[-1]),
+        23: finish,
+    }, None
+
+
+def input_extra(groups, i_partial, y_partial, rows_in, dr, gain, residual):
+    rows, width = rows_in.shape
     outs = [
-        jax.ShapeDtypeStruct((rows, width), F32),
-        jax.ShapeDtypeStruct(d_partial.shape, BF),
+        jax.ShapeDtypeStruct((rows, width), BF),
         jax.ShapeDtypeStruct((1, width), F32),
         jax.ShapeDtypeStruct((rows, width), BF),
     ]
-    scratch = (
-        Scatter.scratch(rows, width)
-        + [pltpu.VMEM((rows, width), BF), pltpu.SemaphoreType.REGULAR]
-        + Gather.scratch()
-    )
     return (
-        [d_partial, y_partial, residual, grads, gain],
-        [ANY_SPEC, ANY_SPEC, VMEM_SPEC, VMEM_SPEC, VMEM_SPEC],
+        [i_partial, y_partial, rows_in, dr, gain, residual],
+        [ANY_SPEC, ANY_SPEC] + [VMEM_SPEC] * 4,
         outs,
-        [VMEM_SPEC, ANY_SPEC, VMEM_SPEC, VMEM_SPEC],
-        scratch,
-        functools.partial(feed_tasks, groups),
-    )
-
-
-def input_tasks(groups, extra_in, extra_out, scratch):
-    i_ref, rows_in, dr, gain = extra_in
-    input_grad, gain_grad = extra_out
-    scatter = Scatter(i_ref, groups, scratch[:9], scratch[9:])
-    order = list(reversed(range(len(groups))))
-
-    def begin():
-        gain_grad[...] = jnp.zeros_like(gain_grad)
-        for g in order:
-            scatter.start(g)
-
-    def use(at, total):
-        back, more = norm_back_rows(rows_in[at, :], gain[...], total)
-        input_grad[at, :] = (dr[at, :] + back).astype(BF)
-        gain_grad[...] += more
-
-    return {
-        0: begin,
-        2: lambda: scatter.forward(order[0]),
-        4: lambda: scatter.forward(order[-1]),
-        5: lambda: scatter.total(order[0], use),
-        6: lambda: scatter.total(order[-1], use),
-    }
-
-
-def input_extra(groups, partial, rows_in, dr, gain):
-    rows, width = rows_in.shape
-    outs = [jax.ShapeDtypeStruct((rows, width), BF), jax.ShapeDtypeStruct((1, width), F32)]
-    return (
-        [partial, rows_in, dr, gain],
-        [ANY_SPEC, VMEM_SPEC, VMEM_SPEC, VMEM_SPEC],
-        outs,
-        [VMEM_SPEC, VMEM_SPEC],
-        Scatter.scratch(rows, width),
+        [VMEM_SPEC] * 3,
+        Scatter.scratch(rows, width) + [pltpu.SemaphoreType.REGULAR],
         functools.partial(input_tasks, groups),
     )
 
@@ -1530,13 +1638,13 @@
 
 
 def middle_kernel(n_ctx, units, tile, *refs):
-    da_ref, got_ref, wq_ref, wk_ref, wv_ref, wo_ref, cos_ref, sin_ref, valid_ref = refs[:9]
-    dq_ref, dk_ref, dv_ref, partial_out = refs[9:13]
-    rows_buf, got, do_send, do_got, back_send, back_got, qs, ks, vs, gs, os, dqs = refs[13:25]
-    rest = refs[25:]
+    da_ref, got_ref, h_ref, wq_ref, wk_ref, wv_ref, wo_ref, wd_ref, cos_ref, sin_ref, valid_ref = refs[:11]
+    grad_ref, partial_out, y_out = refs[11:14]
+    rows_buf, got, do_send, do_got, back_send, back_got, h_buf, qs, ks, vs, gs, os, dqs = refs[14:27]
+    rest = refs[27:]
     n_exchange = len(Exchange.scratch(1, 2))
     do_sems, back_sems, rest = rest[:n_exchange], rest[n_exchange : 2 * n_exchange], rest[2 * n_exchange :]
-    da_sem, got_sem, out_sem = rest
+    da_sem, got_sem, out_sem, h_sem, y_sem = rest
     me, rank = lax.axis_index("ctx"), lax.axis_index("tp")
     odd = lax.rem(rank, 2)
     heads = wq_ref.shape[1] // HD
@@ -1598,6 +1706,31 @@
 
     lax.fori_loop(0, count, attend, 0)
 
+    tiles = rows_buf.shape[0] // PAIR
+
+    def tile_rows(tile):
+        return pl.ds(pl.multiple_of(tile * PAIR, PAIR), PAIR)
+
+    def load_h(tile):
+        slot = lax.rem(tile, 2)
+        return pltpu.make_async_copy(h_ref.at[tile_rows(tile)], h_buf.at[slot], h_sem.at[slot])
+
+    load_h(0).start()
+
+    def down(tile, carry):
+        @pl.when(tile + 1 < tiles)
+        def _():
+            load_h(tile + 1).start()
+
+        load_h(tile).wait()
+        rows_buf[tile_rows(tile), :] = dot(h_buf[lax.rem(tile, 2)], wd_ref[...]).astype(BF)
+        return carry
+
+    lax.fori_loop(0, tiles, down, 0)
+    store_y = pltpu.make_async_copy(rows_buf, y_out, y_sem)
+    store_y.start()
+    store_y.wait()
+
     for u in order:
         trade_back.arrived(back_send, u)
         base, flipped = units[u]
@@ -1606,14 +1739,16 @@
             at = pl.ds(base + block * PAIR, PAIR)
             low = valid_ref[at, :].astype(BF)
             total = None
-            for which, (grad_ref, w_ref) in enumerate(((dq_ref, wq_ref), (dk_ref, wk_ref), (dv_ref, wv_ref))):
+            for which, w_ref in enumerate((wq_ref, wk_ref, wv_ref)):
+                width = heads * HD
                 for head in range(heads):
                     place = jnp.bitwise_xor(me, block * heads + head)
                     part = jnp.concatenate(
                         [back_got[u, place, which, first, :], back_got[u, place, which, second, :]], axis=0
                     )
-                    grad_ref[at, head * HD : (head + 1) * HD] = part * low if which == 2 else part
-                product = times_transposed(grad_ref[at, :], w_ref[...])
+                    columns = slice(which * width + head * HD, which * width + (head + 1) * HD)
+                    grad_ref[at, columns] = part * low if which == 2 else part
+                product = times_transposed(grad_ref[at, which * width : (which + 1) * width], w_ref[...])
                 total = product if total is None else total + product
             rows_buf[at, :] = total.astype(BF)
         store[u].start()
@@ -1623,7 +1758,7 @@
         store[u].wait()
 
 
-def middle_layer(da, got, wq, wk, wv, wo, cos_full, sin_full, valid, n_ctx, units):
+def middle_layer(da, got, h, wq, wk, wv, wo, wd, cos_full, sin_full, valid, n_ctx, units):
     tokens, depth = da.shape
     width = wq.shape[1]
     length = 2 * n_ctx * BLOCK
@@ -1633,19 +1768,23 @@
     three, one = (count, n_ctx, 3, PAIR, HD), (count, n_ctx, PAIR, HD)
     return pl.pallas_call(
         functools.partial(middle_kernel, n_ctx, units, min(512, length)),
-        out_shape=[jax.ShapeDtypeStruct((tokens, width), BF)] * 3 + [jax.ShapeDtypeStruct((tokens, depth), BF)],
-        in_specs=[ANY_SPEC, ANY_SPEC] + [VMEM_SPEC] * 7,
-        out_specs=[VMEM_SPEC] * 3 + [ANY_SPEC],
+        out_shape=[jax.ShapeDtypeStruct((tokens, 3 * width), BF)] + [jax.ShapeDtypeStruct((tokens, depth), BF)] * 2,
+        in_specs=[ANY_SPEC] * 3 + [VMEM_SPEC] * 8,
+        out_specs=[VMEM_SPEC] + [ANY_SPEC] * 2,
         scratch_shapes=[vmem((tokens, depth)), vmem(three), vmem(one), vmem(one), vmem(three), vmem(three)]
+        + [vmem((2, PAIR, h.shape[1]))]
         + [vmem((length, HD))] * 4
         + [vmem((3, length, HD)), vmem((length, HD), F32)]
         + Exchange.scratch(count, n_ctx) * 2
-        + [dma((count,))] * 3,
+        + [dma((count,))] * 3
+        + [dma((2,)), dma],
         compiler_params=pltpu.CompilerParams(vmem_limit_bytes=VMEM_LIMIT, collective_id=4, has_side_effects=True),
         cost_estimate=pl.CostEstimate(
-            flops=8 * tokens * depth * width, bytes_accessed=8 * tokens * depth, transcendentals=0
+            flops=8 * tokens * depth * width + 2 * tokens * depth * h.shape[1],
+            bytes_accessed=8 * tokens * depth,
+            transcendentals=0,
         ),
-    )(da, got, wq, wk, wv, wo, cos_full, sin_full, valid)
+    )(da, got, h, wq, wk, wv, wo, wd, cos_full, sin_full, valid)
 
 
 def body(
@@ -1688,8 +1827,9 @@
     own_counts = lax.dynamic_index_in_dim(counts, me, 0, keepdims=False)
     offsets = jnp.arange(BLOCK, dtype=jnp.int32)
 
-    def valid_of(sequence, half):
-        return (offsets < own_counts[sequence, half]).astype(F32)
+    def valid_of(sequence_list, half_list):
+        held = own_counts[jnp.stack(sequence_list), jnp.stack(half_list)]
+        return (offsets[None, :] < held[:, None]).astype(F32).reshape(-1)
 
     cos_own = jnp.concatenate([cos_front, cos_back])
     sin_own = jnp.concatenate([sin_front, sin_back])
@@ -1697,12 +1837,10 @@
     paired = by_four() and sequences == 6 and n_ctx == 2 * heads
     if paired:
         ranks = [rank ^ k for k in range(4)]
-        seq_a = [3 * (r >> 1) + 2 * (r & 1) for r in ranks]
-        seq_b = [1 + 3 * (r >> 1) for r in ranks]
-        valids = {
-            "b": jnp.concatenate([valid_of(s, r & 1) for s, r in zip(seq_b, ranks)]),
-            "a": jnp.concatenate([valid_of(s, half) for s in seq_a for half in range(2)]),
-        }
+        blocks_a = [(3 * (r >> 1) + 2 * (r & 1), jnp.int32(half)) for r in ranks for half in range(2)]
+        blocks_b = [(1 + 3 * (r >> 1), r & 1) for r in ranks]
+        flat_valid = valid_of(*zip(*(blocks_a + blocks_b)))
+        valids = {"b": flat_valid[len(blocks_a) * BLOCK :], "a": flat_valid[: len(blocks_a) * BLOCK]}
         flip_back = lambda own: jnp.where(odd == 1, jnp.roll(own, BLOCK, axis=0), own)
         tables = {
             "b": (jnp.tile(flip_back(cos_own), (2, 1)), jnp.tile(flip_back(sin_own), (2, 1))),
@@ -1711,7 +1849,8 @@
         scalars = {"b": jnp.stack([me, odd]).astype(jnp.int32), "a": jnp.stack([me, 0]).astype(jnp.int32)}
         n_pairs = {"b": 2 * heads, "a": 4 * heads}
     else:
-        valids = {"a": jnp.concatenate([valid_of(s, half) for s in range(sequences) for half in range(2)])}
+        flat_valid = (offsets[None, None, :] < own_counts[:, :, None]).astype(F32).reshape(-1)
+        valids = {"a": flat_valid}
         tables = {"a": (jnp.tile(cos_own, (sequences, 1)), jnp.tile(sin_own, (sequences, 1)))}
         scalars = {"a": jnp.stack([me, 0]).astype(jnp.int32)}
         n_pairs = {"a": sequences * heads}
@@ -1725,10 +1864,8 @@
             "a": lax.dynamic_slice_in_dim(array, odd * BLOCK, PAIR, 0),
         }
 
-    def whole_rows(part):
-        if not paired:
-            return part["a"]
-        return jnp.where(odd == 1, jnp.concatenate([part["b"], part["a"]]), jnp.concatenate([part["a"], part["b"]]))
+    def whole_rows(array):
+        return jnp.where(odd == 1, jnp.roll(array, BLOCK, axis=0), array) if paired else array
 
     x_own = {name: rows.astype(F32) for name, rows in own_rows(tokens[0]).items()}
     g_own = own_rows(cotangent[0])
@@ -1835,22 +1972,18 @@
         return jnp.concatenate(parts) if len(parts) > 1 else parts[0]
 
     groups = tuple((first_row[n], rows_of[n] // 4, first_row[n] // 4) for n in ("a", "b") if n in names)
-    in_order = [n for n in ("a", "b") if n in names]
-
-    def own_joined(parts):
-        return jnp.concatenate([parts[n] for n in in_order]) if len(in_order) > 1 else parts[in_order[0]]
-
-    def by_group(array, scale=1):
-        return {n: array[first_row[n] // scale : (first_row[n] + rows_of[n]) // scale] for n in in_order}
-
-    own_grads, own_x = own_joined(g_own), own_joined(x_own)
+
+    def own_order(array):
+        return jnp.where(odd == 1, jnp.roll(array, -BLOCK, axis=0), array) if paired else array
+
+    own_grads, own_rows_in = own_order(cotangent[0]), own_order(tokens[0])
     if paired:
         units = ((0, False), (2 * PAIR, False), (4 * PAIR, True))
-        flat_valid = jnp.concatenate([valid_head["a"], valid_head["b"]])
+        wide_valid = jnp.broadcast_to(flat_valid[:, None], (total_rows, HD))
         tabs = [jnp.stack([tab, flip_back(tab)]) for tab in (cos_own, sin_own)]
         all_n1, got, heads_out, own_residual, all_n2, all_cot = forward_layer(
-            own_joined(own_rows(tokens[0])), own_grads, gain_one[None], gain_two[None], w_query, w_key, w_value, w_output,
-            *tabs, flat_valid, n_ctx, groups, units,
+            own_rows_in, own_grads, gain_one[None], gain_two[None], w_query, w_key, w_value, w_output,
+            *tabs, wide_valid, n_ctx, groups, units,
         )
     else:
         norm_one("a")
@@ -1868,55 +2001,53 @@
         all_n1, all_n2, all_cot = state["n1", "a"], gathered(state["n2", "a"]), gathered(state["cot", "a"])
         heads_out, own_residual = state["heads", "a"], state["residual", "a"]
     h, dgp, dup = mlp_core(all_n2, all_cot, w_gate, w_up, w_down, total_rows, 0)
-    d_partial = (times_transposed(dgp, w_gate) + times_transposed(dup, w_up)).astype(BF)
-    y_partial = dot(h, w_down).astype(BF)
-    feed_items, feed_rights = [(h, 0), (dgp, 1), (dup, 1)], [all_cot, all_n2]
     if paired:
-        extra = feed_extra(groups, d_partial, y_partial, own_residual, own_grads, gain_two[None])
-        sum_down, sum_gate, sum_up, dr, da, gain_two_grad, output = weight_sums(feed_items, feed_rights, n_ctx, 1, extra)
+        extra = feed_extra(groups, dgp, dup, w_gate, w_up, own_residual, own_grads, gain_two[None])
+        sum_down, sum_gate, sum_up, sum_out, dr, da, gain_two_grad, _ = weight_sums(
+            [(h, 0), (all_n2, 1), (all_n2, 2), (heads_out, 3)], [all_cot, dgp, dup], n_ctx, 1, extra, late=(1,)
+        )
+        dqkv, i_partial, y_partial = middle_layer(
+            da, got, h, w_query, w_key, w_value, w_output, w_down, cos_full, sin_full, wide_valid, n_ctx, units
+        )
+        extra = input_extra(groups, i_partial, y_partial, own_rows_in, dr, gain_one[None], own_residual)
+        sum_qkv, input_grad, gain_one_grad, output = weight_sums([(all_n1, 0)], [dqkv], n_ctx, 2, extra)
     else:
-        sum_down, sum_gate, sum_up = weight_sums(feed_items, feed_rights, n_ctx, 1)
+        d_partial = (times_transposed(dgp, w_gate) + times_transposed(dup, w_up)).astype(BF)
+        y_partial = dot(h, w_down).astype(BF)
+        (sum_down,) = weight_sums([(h, 0)], [all_cot], n_ctx, 1)
+        sum_gate, sum_up = weight_sums([(all_n2, 0), (all_n2, 1)], [dgp, dup], n_ctx, 2)
         back, gain_two_grad = norm_back_rows(own_residual, gain_two, scattered(scatter_first((d_partial,))))
         dr = own_grads.astype(F32) + back
         da = gathered(gather_first(dr.astype(BF)))
         output = (own_residual + scattered(scatter_first((y_partial,)))).astype(BF)
-    if paired:
-        dq, dk, dv, i_partial = middle_layer(
-            da, got, w_query, w_key, w_value, w_output, cos_full, sin_full, flat_valid, n_ctx, units
-        )
-    else:
         state["do", "a"] = heads_back(scalars["a"], da, w_output, valid_wide["a"], n_ctx)
         swap_part("do", range(n_ctx), "gdo")("a")
         attend_back("a")
         swap_part("dqkv", range(n_ctx), "gdqkv")("a")
         query_back("a")
-        dq, dk, dv, i_partial = (state[key, "a"] for key in ("dq", "dk", "dv", "i"))
-    input_items = [(heads_out, 0), (dq, 1), (dk, 1), (dv, 1)]
-    if paired:
-        extra = input_extra(groups, i_partial, own_x, dr, gain_one[None])
-        sum_out, sum_q, sum_k, sum_v, input_grad, gain_one_grad = weight_sums(
-            input_items, [da, all_n1], n_ctx, 2, extra
+        (sum_out,) = weight_sums([(heads_out, 0)], [da], n_ctx, 3)
+        (sum_qkv,) = weight_sums(
+            [(all_n1, 0)], [jnp.concatenate([state[key, "a"] for key in ("dq", "dk", "dv")], axis=1)], n_ctx, 4
         )
-    else:
-        sum_out, sum_q, sum_k, sum_v = weight_sums(input_items, [da, all_n1], n_ctx, 2)
-        back, gain_one_grad = norm_back_rows(own_x, gain_one, scattered(scatter_first((i_partial,))))
+        back, gain_one_grad = norm_back_rows(x_own["a"], gain_one, scattered(scatter_first((state["i", "a"],))))
         input_grad = (dr + back).astype(BF)
+    grad_query, grad_key, grad_value = (part.astype(F32) for part in jnp.split(sum_qkv, 3, axis=1))
     gains = jnp.concatenate([gain_one_grad, gain_two_grad])
     for axis in ("tp", "ctx"):
         size = lax.axis_size(axis)
         for bit in range(size.bit_length() - 1):
             gains = gains + lax.ppermute(gains, axis, [(i, i ^ (1 << bit)) for i in range(size)])
     return (
-        whole_rows(by_group(output, 4))[None] if paired else output[None],
-        whole_rows(by_group(input_grad, 4))[None] if paired else input_grad[None],
+        whole_rows(output)[None],
+        whole_rows(input_grad)[None],
         gains[0],
-        sum_q.T.astype(F32),
-        sum_k.T.astype(F32),
-        sum_v.T.astype(F32),
+        grad_query,
+        grad_key,
+        grad_value,
         sum_out.astype(F32),
         gains[1],
-        sum_gate.T.astype(F32),
-        sum_up.T.astype(F32),
+        sum_gate.astype(F32),
+        sum_up.astype(F32),
         sum_down.astype(F32),
     )
 

time: 1180 us -> 1060 us (0.90)
  matrix products: 57.8 us -> 0 us
  local copies, waits for them, and re-layouts: 59.5 us -> 9.36 us
    dot_general x3 -> x0, matrix products: 57.8 us -> none  [the longest x2 38.7 us: times_transposed(): lax.dot_general(left, right, (((1,), (1,)), ((), ())), preferred_element_...]
    unnamed x30 -> x20, local copies, waits for them, and re-layouts: 52.8 us -> 0.05 us
    convert_element_type x5 -> x4, other arithmetic: 30.7 us -> 31.7 us  [the longest x1 11.7 us: body(): sum_gate.astype(F32)]
  transfers between devices with their start and end apart: 5 -> 5, of which waited for: 1 -> 3; matrix products, arithmetic and copies ran while one was open for 9% -> 5% of each run, Pallas kernels for 0% -> 0%
where the time goes in v4:
time: 1060 us
  Pallas kernels  969 us (91%)
  other arithmetic  65.1 us (6%)
    pallas_call x2, Pallas kernels, weight_sums(): pl.pallas_call(functools.partial(sums_kernel, n_ctx, shapes, len(rights),...  452 us
    pallas_call x1, Pallas kernels, forward_layer(): pl.pallas_call(functools.partial(forward_kernel, n_ctx, groups, units, mi...  311 us
    pallas_call x1, Pallas kernels, middle_layer(): pl.pallas_call(functools.partial(middle_kernel, n_ctx, units, min(512, le...  155 us
    pallas_call x1, Pallas kernels, mlp_core(): pl.pallas_call(mlp_kernel, out_shape=(out, out, out), grid=(hidden // til...  51.1 us
  transfers between devices with their start and end apart: 5, of which 3 were waited for; matrix products, arithmetic and copies ran while one was open for 5% of the time, Pallas kernels for 0%

profile of v4, /device:TPU:1, one launch (start us, length us, event | category | flops | bytes accessed | tf_op | source)
XLA Modules:
  0.0 1057.0 jit_solution(14031881500896794159)
XLA Ops:
  0.7 2.0 slice_bitcast_fusion.3
  2.7 2.3 slice_bitcast_fusion.1
  5.0 0.8 slice_bitcast_fusion.2
  5.8 1.0 slice_bitcast_fusion
  6.9 3.7 multiply_sine_fusion
  10.6 1.9 pad_maximum_fusion
  13.2 0.7 gather_fusion
  15.3 0.7 pad_maximum_fusion.2.refs_8_
  16.0 0.7 pad_maximum_fusion.3.refs_9_
  16.7 4.9 maximum_select_fusion
  21.7 1.1 broadcast_in_dim.33.refs_10_
  22.8 311.1 %shard_map.203 = (bf16[1536,2048]{1,0:T(8,128)(2,1)}, bf16[3,8,3,256,128]{4,3,2,1,0:T(8,128)(2,1)}, bf16[1536,512]{1,0:T(8,128)(2,1)}, f32[384,2048]{1,0:T(8,128...) custom-call(bf16[384,2048]{1,0:T(8,128)(2,1)} %get-tuple-element.69.refs_0_.refs_4_, ...), custom_call_target="tpu_custom_call" | custom-call | flops 12884901888 | bytes 25165824 | tf_op jit(solution)/shard_map/pallas_call | solution.py:1569
  334.0 51.1 %shard_map.204 = (bf16[1536,2048]{1,0:T(8,128)(2,1)}, bf16[1536,2048]{1,0:T(8,128)(2,1)}, bf16[1536,2048]{1,0:T(8,128)(2,1)}) custom-call(bf16[1536,2048]{1,0:T(8,128)(2,1)} %get-tuple-element.35.n_ref.refs_1_.refs_2_, bf16[1536,2048]{1,0:T(8,128)(2,1)} %get-tuple-element.36.g_ref.refs_4_, bf16[2048,2048]{1,0:T(8,128)(2,1)} %refs_9_.1, ...), custom_call_target="tpu_custom_call" | custom-call | flops 38654705664 | bytes 56623104 | tf_op jit(solution)/shard_map/pallas_call | solution.py:546
  385.1 338.3 %shard_map.205 = (bf16[2048,2048]{1,0:T(8,128)(2,1)}, bf16[2048,2048]{1,0:T(8,128)(2,1)}, bf16[2048,2048]{1,0:T(8,128)(2,1)}, bf16[512,2048]{1,0:T(8,128)(2,1)},...) custom-call(bf16[1536,2048]{1,0:T(8,128)(2,1)} %get-tuple-element.37.refs_0_., ...), custom_call_target="tpu_custom_call" | custom-call | flops 41875931136 | bytes 47710208 | tf_op jit(solution)/shard_map/pallas_call | solution.py:1070
  723.4 154.8 %shard_map.206 = (bf16[1536,1536]{1,0:T(8,128)(2,1)}, bf16[1536,2048]{1,0:T(8,128)(2,1)}, bf16[1536,2048]{1,0:T(8,128)(2,1)}) custom-call(bf16[1536,2048]{1,0:T(8,128)(2,1)} %get-tuple-element.42.refs_0_, bf16[3,8,3,256,128]{4,3,2,1,0:T(8,128)(2,1)} %get-tuple-element.43.refs_1_, bf16[1536,2048]{1,0:T(8,128)(2,1)} %get-tuple-element.37.refs_0_.refs_2_, ...), custom_call_target="tpu_custom_call" | custom-call | flops 25769803776 | bytes 25165824 | tf_op jit(solution)/shard_map/pallas_call | solution.py:1769
  878.2 113.9 %shard_map.207 = (bf16[2048,1536]{1,0:T(8,128)(2,1)}, bf16[384,2048]{1,0:T(8,128)(2,1)}, f32[1,2048]{1,0:T(1,128)}, bf16[384,2048]{1,0:T(8,128)(2,1)}) custom-call(bf16[1536,2048]{1,0:T(8,128)(2,1)} %get-tuple-element.34.refs_0_, bf16[1536,1536]{1,0:T(8,128)(2,1)} %get-tuple-element.44.refs_1_, bf16[1536,2048]{1,0:T(8,128)(2,1)} %get-tuple-element.45.refs_2_, ...), custom_call_target="tpu_custom_call" | custom-call | flops 9663676416 | bytes 12582912 | tf_op jit(solution)/shard_map/pallas_call | solution.py:1070
  992.1 0.7 pad_maximum_fusion.4
  992.9 2.6 collective-permute-done
  995.5 0.7 fusion.13
  996.3 2.6 collective-permute-done.1
  998.9 0.7 fusion.15
  999.6 4.4 collective-permute-start.2
  1004.0 8.3 slice_convert_fusion
  1012.5 1.7 fusion
  1014.4 0.7 collective-permute-done.3
  1015.1 1.8 collective-permute-start.4
  1016.8 1.8 fusion.1
  1018.6 2.5 convert_element_type.52
  1021.1 11.7 %convert_element_type.53 = f32[2048,2048]{1,0:T(8,128)} convert(bf16[2048,2048]{1,0:T(8,128)(2,1)} %get-tuple-element.54) | non-fusion elementwise | flops 4194304 | bytes 25165824 | tf_op jit(solution)/shard_map/convert_element_type | solution.py:2049
  1032.8 11.7 %convert_element_type.54 = f32[2048,2048]{1,0:T(8,128)} convert(bf16[2048,2048]{1,0:T(8,128)(2,1)} %get-tuple-element.55) | non-fusion elementwise | flops 4194304 | bytes 25165824 | tf_op jit(solution)/shard_map/convert_element_type | solution.py:2050
  1044.5 11.7 %convert_element_type.55 = f32[2048,2048]{1,0:T(8,128)} convert(bf16[2048,2048]{1,0:T(8,128)(2,1)} %get-tuple-element.56) | non-fusion elementwise | flops 4194304 | bytes 25165824 | tf_op jit(solution)/shard_map/convert_element_type | solution.py:2051
  1056.2 0.6 fusion.14
  (47 shorter events, 2.5 us)
Async XLA Ops:
  0.6 12.2 %copy-start = (s32[8,6,2]{0,2,1:T(2,128)S(1)}, s32[8,6,2]{0,2,1:T(2,128)}, u32[]{:S(2)}) copy-start(s32[8,6,2]{0,2,1:T(2,128)} %param.13) | copy-start | bytes 1156
  0.7 4.4 copy-start.3
  12.5 1.5 copy-start.8
  12.5 2.1 copy-start.9
  12.5 4.2 copy-start.2
  878.2 113.9 %copy-start.7 = (f32[1,2048]{1,0:T(1,128)S(1)}, f32[1,2048]{1,0:T(1,128)}, u32[]{:S(2)}) copy-start(f32[1,2048]{1,0:T(1,128)} %get-tuple-element.51) | copy-start | bytes 24580
  992.8 2.7 collective-permute-start
  996.2 2.7 collective-permute-start.1
  999.6 12.8 %collective-permute-start.2 = (f32[2,2048]{1,0:T(2,128)S(1)}, f32[2,2048]{1,0:T(2,128)S(1)}, u32[]{:S(2)}, u32[]{:S(2)}) collective-permute-start(f32[2,2048]{1,0:T(2,128)S(1)} %fusion.15), channel_id=1, source_target_pairs={{0,4},{4,0},{8,12},{12,8},{16,20},{20,16},{24,28},{28,24},{1,5},{5... | collective-permute-start | bytes 49160 | tf_op jit(solution)/shard_map/ppermute | solution.py:2039
  1004.0 8.3 copy-start.5
  1012.3 1.9 copy-start.4
  1012.4 2.7 collective-permute-start.3
  1014.3 4.3 copy-start.6
  1015.1 41.1 %collective-permute-start.4 = (f32[2,2048]{1,0:T(2,128)S(1)}, f32[2,2048]{1,0:T(2,128)S(1)}, u32[]{:S(2)}, u32[]{:S(2)}) collective-permute-start(f32[2,2048]{1,0:T(2,128)S(1)} %add.91), channel_id=1, source_target_pairs={{0,16},{4,20},{8,24},{12,28},{16,0},{20,4},{24,8},{28,12},{1,17},{... | collective-permute-start | bytes 49160 | tf_op jit(solution)/shard_map/ppermute | solution.py:2039
  1044.5 12.3 %copy-start.1 = (s32[8,6,2]{0,2,1:T(2,128)S(1)}, s32[8,6,2]{0,2,1:T(2,128)}, u32[]{:S(2)}) copy-start(s32[8,6,2]{0,2,1:T(2,128)} %param.13) | copy-start | bytes 1156

commit v5 on v4

--- a/solution.py
+++ b/solution.py
@@ -694,8 +694,9 @@
 
 
 class Gather:
-    def __init__(self, own, out, groups, sems):
-        self.own, self.out, self.groups = own, out, groups
+    def __init__(self, own, out, groups, sems, own_at=None, local=True):
+        self.own, self.out, self.groups, self.has_local = own, out, groups, local
+        self.own_at = own_at if own_at is not None else [group[2] for group in groups]
         self.first_send, self.first_recv, self.second_send, self.second_recv, self.local_sem = sems
         self.to_x, self.to_y = neighbours()
 
@@ -705,8 +706,8 @@
         return [dma((4,)), dma((4,)), dma((4,)), dma((4,)), dma((2,))]
 
     def first_copies(self, g):
-        base, rows, own = self.groups[g]
-        source = self.own.at[pl.ds(own, rows)]
+        base, rows, _ = self.groups[g]
+        source = self.own.at[pl.ds(self.own_at[g], rows)]
         place = lambda k: self.out.at[pl.ds(base + k * rows, rows)]
         return [
             remote(source, place(1), self.first_send.at[2 * g], self.first_recv.at[2 * g], self.to_x),
@@ -714,8 +715,8 @@
         ]
 
     def local(self, g):
-        base, rows, own = self.groups[g]
-        return pltpu.make_async_copy(self.own.at[pl.ds(own, rows)], self.out.at[pl.ds(base, rows)], self.local_sem.at[g])
+        base, rows, _ = self.groups[g]
+        return pltpu.make_async_copy(self.own.at[pl.ds(self.own_at[g], rows)], self.out.at[pl.ds(base, rows)], self.local_sem.at[g])
 
     def second_copies(self, g):
         base, rows, _ = self.groups[g]
@@ -729,14 +730,22 @@
     def start(self, g):
         for copy in self.first_copies(g):
             copy.start()
-        self.local(g).start()
+        if self.has_local:
+            self.local(g).start()
+
+    def forward_x(self, g):
+        self.first_copies(g)[0].wait_recv()
+        self.second_copies(g)[1].start()
+
+    def forward_y(self, g):
+        self.first_copies(g)[1].wait_recv()
+        self.second_copies(g)[0].start()
 
     def forward(self, g):
-        for copy in self.first_copies(g):
-            copy.wait_recv()
-        for copy in self.second_copies(g):
-            copy.start()
-        self.local(g).wait()
+        self.forward_x(g)
+        self.forward_y(g)
+        if self.has_local:
+            self.local(g).wait()
 
     def finish(self, g):
         for copy in self.second_copies(g):
@@ -825,27 +834,25 @@
     lag_f = lag_o + 1
     lag_w = lag_f + 1
 
-    barrier = pltpu.get_barrier_semaphore()
-    pl.semaphore_signal(barrier, inc=1, device_id=partner, device_id_type=pl.DeviceIdType.MESH)
-
-    @pl.when(chip > 0)
-    def _():
-        pl.semaphore_signal(
-            barrier, inc=1, device_id=((chip - 1) * 2 + core, rank), device_id_type=pl.DeviceIdType.MESH
-        )
-
-    @pl.when(chip < chips - 1)
-    def _():
-        pl.semaphore_signal(
-            barrier, inc=1, device_id=((chip + 1) * 2 + core, rank), device_id_type=pl.DeviceIdType.MESH
-        )
-
-    greeted = 1
     if tasks is not None:
-        for device in neighbours():
-            signal(barrier, device)
-        greeted = 3
-    pl.semaphore_wait(barrier, greeted + jnp.where(chip > 0, 1, 0) + jnp.where(chip < chips - 1, 1, 0))
+        greet(n_ctx, True)
+    else:
+        barrier = pltpu.get_barrier_semaphore()
+        pl.semaphore_signal(barrier, inc=1, device_id=partner, device_id_type=pl.DeviceIdType.MESH)
+
+        @pl.when(chip > 0)
+        def _():
+            pl.semaphore_signal(
+                barrier, inc=1, device_id=((chip - 1) * 2 + core, rank), device_id_type=pl.DeviceIdType.MESH
+            )
+
+        @pl.when(chip < chips - 1)
+        def _():
+            pl.semaphore_signal(
+                barrier, inc=1, device_id=((chip + 1) * 2 + core, rank), device_id_type=pl.DeviceIdType.MESH
+            )
+
+        pl.semaphore_wait(barrier, 1 + jnp.where(chip > 0, 1, 0) + jnp.where(chip < chips - 1, 1, 0))
 
     to_core = Ring(core_in, core_send, core_recv, core_credit, total)
     to_after = Ring(hop_in, in_send, in_recv, in_credit, total)
@@ -1264,65 +1271,89 @@
     )
 
 
-def input_tasks(groups, extra_in, extra_out, scratch):
-    i_ref, y_ref, rows_in, dr, gain, residual = extra_in
-    input_grad, gain_grad, output = extra_out
-    bufs, free = scratch[:-1], scratch[-1]
-    first = Scatter(i_ref, groups, bufs[:9], bufs[9:])
-    last = Scatter(y_ref, groups, bufs[:9], bufs[9:])
+def input_tasks(n_ctx, groups, extra_in, extra_out, scratch):
+    i_ref, rows_in, dr, gain, gain_two_grad = extra_in
+    input_grad, gain_sums = extra_out
+    n = len(Scatter.scratch(16, 128))
+    scatter = Scatter(i_ref, groups, scratch[:9], scratch[9:n])
+    gains, got_tp, got_ctx, send_tp, recv_tp, send_ctx, recv_ctx = scratch[n:]
     order = list(reversed(range(len(groups))))
+    me, rank = lax.axis_index("ctx"), lax.axis_index("tp")
+
+    def tp_hop(k):
+        return remote(gains.at[k], got_tp.at[k], send_tp.at[k], recv_tp.at[k], neighbours()[k])
+
+    def ctx_hop(k):
+        place = gains.at[2]
+        return remote(place, got_ctx.at[k], send_ctx.at[k], recv_ctx.at[k], (jnp.bitwise_xor(me, k), rank))
 
     def begin():
-        gain_grad[...] = jnp.zeros_like(gain_grad)
+        gains[0] = jnp.zeros(gains.shape[1:], F32)
+        gains[0, 8:9, :] = gain_two_grad[...]
         for g in order:
-            first.start(g)
+            scatter.start(g)
 
     def use(at, total):
         back, more = norm_back_rows(rows_in[at, :].astype(F32), gain[...], total)
         input_grad[at, :] = (dr[at, :] + back).astype(BF)
-        gain_grad[...] += more
-
-    def again():
-        first.total(order[-1], use)
-        for device in neighbours():
-            signal(free, device)
-        pl.semaphore_wait(free, 2)
-        for g in order:
-            last.start(g)
-
-    def use_out(at, total):
-        output[at, :] = (residual[at, :] + total).astype(BF)
+        gains[0, 0:1, :] += more
+
+    def rest():
+        scatter.total(order[-1], use)
+        tp_hop(0).start()
+
+    def second():
+        tp_hop(0).wait()
+        gains[1] = gains[0] + got_tp[0]
+        tp_hop(1).start()
+
+    def third():
+        tp_hop(1).wait()
+        gains[2] = gains[1] + got_tp[1]
+        for k in range(1, n_ctx):
+            ctx_hop(k).start()
 
     def finish():
-        for g in order:
-            last.total(g, use_out)
+        for k in range(1, n_ctx):
+            ctx_hop(k).wait()
+        got_ctx[0] = gains[2]
+        total = got_ctx[jnp.bitwise_xor(me, 0)]
+        for index in range(1, n_ctx):
+            total = total + got_ctx[jnp.bitwise_xor(me, index)]
+        gain_sums[...] = total
 
     return {
         0: begin,
-        3: lambda: first.forward(order[0]),
-        8: lambda: first.forward(order[-1]),
-        9: lambda: first.total(order[0], use),
-        11: again,
-        15: lambda: last.forward(order[0]),
-        20: lambda: last.forward(order[-1]),
-        23: finish,
+        4: lambda: scatter.forward(order[0]),
+        9: lambda: scatter.forward(order[-1]),
+        10: lambda: scatter.total(order[0], use),
+        13: rest,
+        15: second,
+        17: third,
+        20: finish,
     }, None
 
 
-def input_extra(groups, i_partial, y_partial, rows_in, dr, gain, residual):
+def input_extra(n_ctx, groups, i_partial, rows_in, dr, gain, gain_two_grad):
     rows, width = rows_in.shape
-    outs = [
-        jax.ShapeDtypeStruct((rows, width), BF),
-        jax.ShapeDtypeStruct((1, width), F32),
-        jax.ShapeDtypeStruct((rows, width), BF),
-    ]
+    dma = pltpu.SemaphoreType.DMA
+    outs = [jax.ShapeDtypeStruct((rows, width), BF), jax.ShapeDtypeStruct((16, width), F32)]
     return (
-        [i_partial, y_partial, rows_in, dr, gain, residual],
-        [ANY_SPEC, ANY_SPEC] + [VMEM_SPEC] * 4,
+        [i_partial, rows_in, dr, gain, gain_two_grad],
+        [ANY_SPEC] + [VMEM_SPEC] * 4,
         outs,
-        [VMEM_SPEC] * 3,
-        Scatter.scratch(rows, width) + [pltpu.SemaphoreType.REGULAR],
-        functools.partial(input_tasks, groups),
+        [VMEM_SPEC] * 2,
+        Scatter.scratch(rows, width)
+        + [
+            pltpu.VMEM((3, 16, width), F32),
+            pltpu.VMEM((2, 16, width), F32),
+            pltpu.VMEM((n_ctx, 16, width), F32),
+            dma((2,)),
+            dma((2,)),
+            dma((n_ctx,)),
+            dma((n_ctx,)),
+        ],
+        functools.partial(input_tasks, n_ctx, groups),
     )
 
 
@@ -1358,6 +1389,17 @@
             self.copy(source, unit, k).start()
         self.own(source, unit).start()
 
+    def start_some(self, source, unit, first, count):
+        for k in reversed(range(self.n_ctx)):
+            other = jnp.bitwise_xor(self.me, k)
+
+            @pl.when((other >= first) & (other < first + count))
+            def _(k=k):
+                if k == 0:
+                    self.own(source, unit).start()
+                else:
+                    self.copy(source, unit, k).start()
+
     def arrived(self, source, unit):
         for k in range(1, self.n_ctx):
             self.copy(source, unit, k).wait_recv()
@@ -1379,6 +1421,11 @@
     pl.semaphore_wait(barrier, n_ctx - 1 + (2 if tp_too else 0))
 
 
+def rotation(cos_tab, sin_tab, block_cos, block_sin):
+    sign = jnp.where(lax.broadcasted_iota(jnp.int32, cos_tab.shape, 1) < HD // 2, -1.0, 1.0)
+    return cos_tab * block_cos - sin_tab * block_sin, (sin_tab * block_cos + cos_tab * block_sin) * sign
+
+
 def in_turn(count):
     return [count - 1] + list(range(count - 1))
 
@@ -1407,32 +1454,38 @@
 
 
 def forward_kernel(n_ctx, groups, units, tile, *refs):
-    x_ref, cot_ref, gain_one, gain_two, wq_ref, wk_ref, wv_ref, wo_ref, cos_ref, sin_ref, valid_ref = refs[:11]
-    n1_out, got_out, heads_out, residual, n2_out, cot_out = refs[11:17]
-    rows_buf, own_buf, send, got, o_send, o_got, qs, ks, vs, os = refs[17:27]
-    rest = refs[27:]
+    tokens_ref, cot_ref, gain_one, gain_two, wq_ref, wk_ref, wv_ref, wo_ref, cos_ref, sin_ref, bcos_ref, bsin_ref, valid_ref = refs[:13]
+    n1_out, got_out, heads_out, residual, n2_out, cot_out = refs[13:19]
+    x_ref, rows_buf, own_buf, send, got, o_send, o_got, tabs, qs, ks, vs, os = refs[19:31]
+    rest = refs[31:]
     n_gather, n_exchange = len(Gather.scratch()), len(Exchange.scratch(1, 2))
     n1_sems, rest = rest[:n_gather], rest[n_gather:]
     n2_sems, rest = rest[:n_gather], rest[n_gather:]
     cot_sems, rest = rest[:n_gather], rest[n_gather:]
     x_sems, rest = rest[:n_exchange], rest[n_exchange:]
     o_sems, rest = rest[:n_exchange], rest[n_exchange:]
-    (n1_sem, got_sem), rest = rest[:2], rest[2:]
+    (n1_sem, got_sem, load_sem), rest = rest[:3], rest[3:]
     me, rank = lax.axis_index("ctx"), lax.axis_index("tp")
     odd = lax.rem(rank, 2)
     heads = wq_ref.shape[1] // HD
     per_unit = n_ctx // heads
-    unit_rows = per_unit * PAIR
-
+    own_at = [pl.multiple_of(odd * BLOCK, BLOCK), pl.multiple_of((1 - odd) * PAIR, BLOCK)]
+
+    def load_x(g):
+        _, rows, own = groups[g]
+        return pltpu.make_async_copy(
+            tokens_ref.at[pl.ds(own_at[g], rows)], x_ref.at[pl.ds(own, rows)], load_sem.at[g]
+        )
+
+    for g in range(2):
+        load_x(g).start()
     greet(n_ctx, True)
-    gather_one = Gather(own_buf, rows_buf, groups, n1_sems)
+    gather_one = Gather(own_buf, rows_buf, groups, n1_sems, local=False)
     gather_two = Gather(own_buf, n2_out, groups, n2_sems)
-    gather_cot = Gather(cot_ref, cot_out, groups, cot_sems)
+    gather_cot = Gather(cot_ref, cot_out, groups, cot_sems, own_at=own_at)
     scatter = Scatter(rows_buf, groups, rest[:6], rest[6:], loaded=False)
     trade = Exchange(got, x_sems, True)
     trade_back = Exchange(o_got, o_sems, False)
-    order = list(reversed(range(len(groups))))
-    last_u, mid_u, end_u = in_turn(len(units))
 
     def halves_of(u):
         return halves_at(odd if units[u][1] else 0)
@@ -1441,47 +1494,58 @@
         values = source[at, :].astype(F32)
         return (values * inverse_rms(values) * gain[...]).astype(BF)
 
-    for g in order:
-        _, rows, own = groups[g]
-        at = pl.ds(own, rows)
-        own_buf[at, :] = normed(x_ref, gain_one, at)
+    def begin(g):
+        base, rows, own = groups[g]
+        load_x(g).wait()
+        low = normed(x_ref, gain_one, pl.ds(own, rows))
+        own_buf[pl.ds(own, rows), :] = low
         gather_one.start(g)
+        rows_buf[pl.ds(base, rows), :] = low
+
+    begin(0)
+    for half, block in enumerate((me, 2 * n_ctx - 1 - me)):
+        cos_part, sin_part = rotation(
+            cos_ref[...], sin_ref[...], bcos_ref[pl.ds(block, 1), :], bsin_ref[pl.ds(block, 1), :]
+        )
+        tabs[0, half * BLOCK : (half + 1) * BLOCK, :] = cos_part
+        tabs[1, half * BLOCK : (half + 1) * BLOCK, :] = sin_part
 
     def query(u, block):
         base, flipped = units[u]
         first, second = halves_of(u)
         at = pl.ds(base + block * PAIR, PAIR)
         rows = rows_buf[at, :]
-        table = 1 if flipped else 0
         for which, w_ref in enumerate((wq_ref, wk_ref, wv_ref)):
             product = dot(rows, w_ref[...])
             for head in range(heads):
                 part = product[:, head * HD : (head + 1) * HD]
-                if which < 2:
-                    part = part * cos_ref[table] + pltpu.roll(part, HD // 2, 1) * sin_ref[table]
-                else:
-                    part = part * valid_ref[at, :]
-                part = part.astype(BF)
-                send[u, block * heads + head, which, first, :] = part[:BLOCK]
-                send[u, block * heads + head, which, second, :] = part[BLOCK:]
-
-    def query_unit(u):
-        for block in range(per_unit):
-            query(u, block)
-        trade.start(send, u)
+                pair = block * heads + head
+                for half, to in ((0, first), (1, second)):
+                    piece = part[half * BLOCK : (half + 1) * BLOCK]
+                    if which < 2:
+                        piece = piece * tabs[0, to, :] + pltpu.roll(piece, HD // 2, 1) * tabs[1, to, :]
+                    else:
+                        piece = piece * valid_ref[pl.ds(base + block * PAIR + half * BLOCK, BLOCK), :]
+                    send[u, pair, which, to, :] = piece.astype(BF)
+        trade.start_some(send, u, block * heads, heads)
 
     store_n1 = pltpu.make_async_copy(rows_buf, n1_out, n1_sem)
     store_got = [pltpu.make_async_copy(got.at[u], got_out.at[u], got_sem.at[u]) for u in range(len(units))]
 
-    gather_one.forward(order[0])
-    gather_one.finish(order[0])
-    query_unit(last_u)
-    gather_one.forward(order[1])
-    query_unit(mid_u)
-    gather_one.finish(order[1])
-    for g in order:
+    query(0, 0)
+    gather_one.forward_x(0)
+    gather_one.forward_y(0)
+    begin(1)
+    query(0, 1)
+    query(1, 0)
+    gather_one.finish(0)
+    query(1, 1)
+    gather_one.forward(1)
+    gather_one.finish(1)
+    for g in range(2):
         gather_cot.start(g)
-    query_unit(end_u)
+    query(2, 0)
+    query(2, 1)
     store_n1.start()
 
     def attend(u):
@@ -1520,39 +1584,39 @@
         scatter.total(g, use)
         gather_two.start(g)
 
-    attend(last_u)
-    for g in order:
+    attend(0)
+    for g in range(2):
         gather_one.sent(g)
     store_n1.wait()
-    project(last_u)
-    scatter.start(order[0], loads=False)
-    for g in order:
+    attend(1)
+    for g in range(2):
         gather_cot.forward(g)
-    scatter.forward(order[0])
-    finish_group(order[0])
-    attend(mid_u)
-    gather_two.forward(order[0])
-    project(mid_u)
-    scatter.start(order[1], (0,), loads=False)
-    attend(end_u)
-    project(end_u)
-    scatter.start(order[1], (1, 3, 2), loads=False)
-    scatter.forward(order[1])
-    finish_group(order[1])
-    gather_two.forward(order[1])
+    project(0)
+    scatter.start(0, (0,), loads=False)
+    project(1)
+    scatter.start(0, (1, 3, 2), loads=False)
+    attend(2)
+    scatter.forward(0)
+    project(2)
+    scatter.start(1, loads=False)
+    finish_group(0)
+    scatter.forward(1)
+    finish_group(1)
+    gather_two.forward(0)
+    gather_two.forward(1)
     for u in range(len(units)):
         trade.sent(send, u)
         trade_back.sent(o_send, u)
         store_got[u].wait()
-    for g in order:
+    for g in range(2):
         gather_cot.finish(g)
         gather_two.finish(g)
         gather_two.sent(g)
         gather_cot.sent(g)
 
 
-def forward_layer(x_own, cot_own, gain_one, gain_two, wq, wk, wv, wo, cos_tab, sin_tab, valid, n_ctx, groups, units):
-    rows, depth = x_own.shape
+def forward_layer(tokens_in, cot_in, gain_one, gain_two, wq, wk, wv, wo, tables, valid, n_ctx, groups, units):
+    rows, depth = tokens_in.shape
     width = wq.shape[1]
     tokens = valid.shape[0]
     length = 2 * n_ctx * BLOCK
@@ -1569,26 +1633,28 @@
     return pl.pallas_call(
         functools.partial(forward_kernel, n_ctx, groups, units, min(512, length)),
         out_shape=outs,
-        in_specs=[VMEM_SPEC, ANY_SPEC] + [VMEM_SPEC] * 9,
+        in_specs=[ANY_SPEC, ANY_SPEC] + [VMEM_SPEC] * 11,
         out_specs=[ANY_SPEC, ANY_SPEC, VMEM_SPEC, VMEM_SPEC, ANY_SPEC, ANY_SPEC],
         scratch_shapes=[
+            vmem((rows, depth)),
             vmem((tokens, depth)),
             vmem((rows, depth)),
             vmem((n_units, n_ctx, 3, PAIR, HD)),
             vmem((n_units, n_ctx, 3, PAIR, HD)),
             vmem((n_units, n_ctx, PAIR, HD)),
             vmem((n_units, n_ctx, PAIR, HD)),
+            vmem((2, PAIR, HD), F32),
         ]
         + [vmem((length, HD))] * 4
         + Gather.scratch() * 3
         + Exchange.scratch(n_units, n_ctx) * 2
-        + [pltpu.SemaphoreType.DMA, pltpu.SemaphoreType.DMA((n_units,))]
+        + [pltpu.SemaphoreType.DMA, pltpu.SemaphoreType.DMA((n_units,)), pltpu.SemaphoreType.DMA((2,))]
         + Scatter.scratch(rows, depth, loaded=False),
         compiler_params=pltpu.CompilerParams(vmem_limit_bytes=VMEM_LIMIT, collective_id=3, has_side_effects=True),
         cost_estimate=pl.CostEstimate(
             flops=8 * tokens * depth * width, bytes_accessed=8 * tokens * depth, transcendentals=0
         ),
-    )(x_own, cot_own, gain_one, gain_two, wq, wk, wv, wo, cos_tab, sin_tab, valid)
+    )(tokens_in, cot_in, gain_one, gain_two, wq, wk, wv, wo, *tables, valid)
 
 
 def attend_rows_back(qs, ks, vs, gs, os, dqs, cos_ref, sin_ref, tile):
@@ -1637,14 +1703,17 @@
         os[0, at, :] = unrotate(dqs[at, :] * scale, at)
 
 
-def middle_kernel(n_ctx, units, tile, *refs):
-    da_ref, got_ref, h_ref, wq_ref, wk_ref, wv_ref, wo_ref, wd_ref, cos_ref, sin_ref, valid_ref = refs[:11]
-    grad_ref, partial_out, y_out = refs[11:14]
-    rows_buf, got, do_send, do_got, back_send, back_got, h_buf, qs, ks, vs, gs, os, dqs = refs[14:27]
-    rest = refs[27:]
+def middle_kernel(n_ctx, groups, units, tile, *refs):
+    da_ref, got_ref, h_ref, residual_ref, wd_ref, wq_ref, wk_ref, wv_ref, wo_ref = refs[:9]
+    cos_ref, sin_ref, bcos_ref, bsin_ref, valid_ref = refs[9:14]
+    grad_ref, partial_out, output = refs[14:17]
+    rows_buf, got, do_send, do_got, back_got, h_buf, wd_buf, res_buf, cos_full, sin_full = refs[17:27]
+    qs, ks, vs, gs, os, dqs = refs[27:33]
+    rest = refs[33:]
+    back_send = got
     n_exchange = len(Exchange.scratch(1, 2))
     do_sems, back_sems, rest = rest[:n_exchange], rest[n_exchange : 2 * n_exchange], rest[2 * n_exchange :]
-    da_sem, got_sem, out_sem, h_sem, y_sem = rest
+    (da_sem, got_sem, out_sem, h_sem, wd_sem, res_sem, y_sem), rest = rest[:7], rest[7:]
     me, rank = lax.axis_index("ctx"), lax.axis_index("tp")
     odd = lax.rem(rank, 2)
     heads = wq_ref.shape[1] // HD
@@ -1658,14 +1727,14 @@
 
     load_da = [pltpu.make_async_copy(da_ref.at[rows_of(u)], rows_buf.at[rows_of(u)], da_sem.at[u]) for u in range(count)]
     load_got = [pltpu.make_async_copy(got_ref.at[u], got.at[u], got_sem.at[u]) for u in range(count)]
-    store = [
-        pltpu.make_async_copy(rows_buf.at[rows_of(u)], partial_out.at[rows_of(u)], out_sem.at[u]) for u in range(count)
-    ]
     for u in order:
         load_da[u].start()
     for u in order:
         load_got[u].start()
-    greet(n_ctx, False)
+    first_wd = pltpu.make_async_copy(wd_ref.at[:, pl.ds(0, wd_buf.shape[1])], wd_buf, wd_sem)
+    first_wd.start()
+    greet(n_ctx, True)
+    scatter = Scatter(rows_buf, groups, rest[:6], rest[6:], loaded=False)
     trade = Exchange(do_got, do_sems, True)
     trade_back = Exchange(back_got, back_sems, False)
 
@@ -1682,6 +1751,11 @@
                 do_send[u, block * heads + head, first, :] = part[:BLOCK]
                 do_send[u, block * heads + head, second, :] = part[BLOCK:]
         trade.start(do_send, u)
+    for block in range(2 * n_ctx):
+        at = slice(block * BLOCK, (block + 1) * BLOCK)
+        cos_full[at, :], sin_full[at, :] = rotation(
+            cos_ref[...], sin_ref[...], bcos_ref[block : block + 1, :], bsin_ref[block : block + 1, :]
+        )
     for u in order:
         load_got[u].wait()
 
@@ -1695,7 +1769,7 @@
                 dest[back, :] = got[u, k, which, BLOCK:, :]
             gs[front, :] = do_got[u, k, :BLOCK, :]
             gs[back, :] = do_got[u, k, BLOCK:, :]
-        attend_rows_back(qs, ks, vs, gs, os, dqs, cos_ref, sin_ref, tile)
+        attend_rows_back(qs, ks, vs, gs, os, dqs, cos_full, sin_full, tile)
         for k in range(n_ctx):
             front, back = both_places(me, k, n_ctx)
             for which in range(3):
@@ -1711,27 +1785,60 @@
     def tile_rows(tile):
         return pl.ds(pl.multiple_of(tile * PAIR, PAIR), PAIR)
 
-    def load_h(tile):
-        slot = lax.rem(tile, 2)
-        return pltpu.make_async_copy(h_ref.at[tile_rows(tile)], h_buf.at[slot], h_sem.at[slot])
+    def load_h(step):
+        slot = lax.rem(step, 2)
+        return pltpu.make_async_copy(h_ref.at[tile_rows(lax.rem(step, tiles))], h_buf.at[slot], h_sem.at[slot])
+
+    columns = wd_buf.shape[1]
+    parts = rows_buf.shape[1] // columns
+
+    def part_columns(part):
+        return pl.ds(pl.multiple_of(part * columns, columns), columns)
+
+    def load_wd(part):
+        return pltpu.make_async_copy(wd_ref.at[:, part_columns(part)], wd_buf, wd_sem)
 
     load_h(0).start()
 
-    def down(tile, carry):
-        @pl.when(tile + 1 < tiles)
+    def down(step, carry):
+        part, tile = step // tiles, lax.rem(step, tiles)
+
+        @pl.when(step + 1 < tiles * parts)
         def _():
-            load_h(tile + 1).start()
-
-        load_h(tile).wait()
-        rows_buf[tile_rows(tile), :] = dot(h_buf[lax.rem(tile, 2)], wd_ref[...]).astype(BF)
+            load_h(step + 1).start()
+
+        @pl.when(tile == 0)
+        def _():
+            @pl.when(part > 0)
+            def _():
+                load_wd(part).start()
+
+            load_wd(part).wait()
+
+        load_h(step).wait()
+        rows_buf[tile_rows(tile), part_columns(part)] = dot(h_buf[lax.rem(step, 2)], wd_buf[...]).astype(BF)
         return carry
 
-    lax.fori_loop(0, tiles, down, 0)
-    store_y = pltpu.make_async_copy(rows_buf, y_out, y_sem)
-    store_y.start()
-    store_y.wait()
-
-    for u in order:
+    lax.fori_loop(0, tiles * parts, down, 0)
+    last_group = len(groups) - 1
+    out_rows = rest[0]
+    for g in (last_group, 0):
+        scatter.start(g, loads=False)
+
+    def use(at, total):
+        size = total.shape[0]
+        load = pltpu.make_async_copy(residual_ref.at[at], res_buf.at[pl.ds(0, size)], res_sem)
+        load.start()
+        load.wait()
+        low = (res_buf[:size, :] + total).astype(BF)
+        out_rows[at, :] = low
+
+    def store(number, first):
+        slot = number % 2
+        return pltpu.make_async_copy(h_buf.at[slot], partial_out.at[pl.ds(first, PAIR)], out_sem.at[slot])
+
+    stored = []
+    for turn, u in enumerate(order):
         trade_back.arrived(back_send, u)
         base, flipped = units[u]
         first, second = halves_at(odd if flipped else 0)
@@ -1750,15 +1857,29 @@
                     grad_ref[at, columns] = part * low if which == 2 else part
                 product = times_transposed(grad_ref[at, which * width : (which + 1) * width], w_ref[...])
                 total = product if total is None else total + product
-            rows_buf[at, :] = total.astype(BF)
-        store[u].start()
+            number = len(stored)
+            if number >= 2:
+                stored[number - 2].wait()
+            h_buf[number % 2] = total.astype(BF)
+            stored.append(store(number, base + block * PAIR))
+            stored[-1].start()
+        if turn == 0:
+            scatter.forward(last_group)
+            scatter.forward(0)
+        if turn == 1:
+            for g in (last_group, 0):
+                scatter.total(g, use)
+            store_y = pltpu.make_async_copy(out_rows, output, y_sem)
+            store_y.start()
+    store_y.wait()
+    for copy in stored[-2:]:
+        copy.wait()
     for u in order:
         trade.sent(do_send, u)
         trade_back.sent(back_send, u)
-        store[u].wait()
-
-
-def middle_layer(da, got, h, wq, wk, wv, wo, wd, cos_full, sin_full, valid, n_ctx, units):
+
+
+def middle_layer(da, got, h, residual, wq, wk, wv, wo, wd, tables, valid, n_ctx, groups, units):
     tokens, depth = da.shape
     width = wq.shape[1]
     length = 2 * n_ctx * BLOCK
@@ -1766,25 +1887,31 @@
     vmem = lambda shape, dtype=BF: pltpu.VMEM(shape, dtype)
     dma = pltpu.SemaphoreType.DMA
     three, one = (count, n_ctx, 3, PAIR, HD), (count, n_ctx, PAIR, HD)
+    most_rows = max(rows for _, rows, _ in groups) // 2
     return pl.pallas_call(
-        functools.partial(middle_kernel, n_ctx, units, min(512, length)),
-        out_shape=[jax.ShapeDtypeStruct((tokens, 3 * width), BF)] + [jax.ShapeDtypeStruct((tokens, depth), BF)] * 2,
-        in_specs=[ANY_SPEC] * 3 + [VMEM_SPEC] * 8,
-        out_specs=[VMEM_SPEC] + [ANY_SPEC] * 2,
-        scratch_shapes=[vmem((tokens, depth)), vmem(three), vmem(one), vmem(one), vmem(three), vmem(three)]
-        + [vmem((2, PAIR, h.shape[1]))]
+        functools.partial(middle_kernel, n_ctx, groups, units, min(512, length)),
+        out_shape=[
+            jax.ShapeDtypeStruct((tokens, 3 * width), BF),
+            jax.ShapeDtypeStruct((tokens, depth), BF),
+            jax.ShapeDtypeStruct(residual.shape, BF),
+        ],
+        in_specs=[ANY_SPEC] * 5 + [VMEM_SPEC] * 9,
+        out_specs=[VMEM_SPEC, ANY_SPEC, ANY_SPEC],
+        scratch_shapes=[vmem((tokens, depth)), vmem(three), vmem(one), vmem(one), vmem(three)]
+        + [vmem((2, PAIR, depth)), vmem((h.shape[1], depth // 2)), vmem((most_rows, depth), F32)]
+        + [vmem((length, HD), F32)] * 2
         + [vmem((length, HD))] * 4
         + [vmem((3, length, HD)), vmem((length, HD), F32)]
         + Exchange.scratch(count, n_ctx) * 2
-        + [dma((count,))] * 3
-        + [dma((2,)), dma],
+        + [dma((count,)), dma((count,)), dma((2,)), dma((2,)), dma, dma, dma]
+        + Scatter.scratch(residual.shape[0], depth, loaded=False),
         compiler_params=pltpu.CompilerParams(vmem_limit_bytes=VMEM_LIMIT, collective_id=4, has_side_effects=True),
         cost_estimate=pl.CostEstimate(
             flops=8 * tokens * depth * width + 2 * tokens * depth * h.shape[1],
             bytes_accessed=8 * tokens * depth,
             transcendentals=0,
         ),
-    )(da, got, h, wq, wk, wv, wo, wd, cos_full, sin_full, valid)
+    )(da, got, h, residual, wd, wq, wk, wv, wo, *tables, valid)
 
 
 def body(
@@ -1980,10 +2107,13 @@
     if paired:
         units = ((0, False), (2 * PAIR, False), (4 * PAIR, True))
         wide_valid = jnp.broadcast_to(flat_valid[:, None], (total_rows, HD))
-        tabs = [jnp.stack([tab, flip_back(tab)]) for tab in (cos_own, sin_own)]
+        twice = lambda table: jnp.concatenate([table, table], axis=1)
+        starts = BLOCK * jnp.arange(2 * n_ctx, dtype=jnp.int32)
+        spans = [at.astype(F32)[:, None] * inverse[None, :] for at in (offsets, starts)]
+        turns = [twice(part(angle)) for angle in spans for part in (jnp.cos, jnp.sin)]
         all_n1, got, heads_out, own_residual, all_n2, all_cot = forward_layer(
-            own_rows_in, own_grads, gain_one[None], gain_two[None], w_query, w_key, w_value, w_output,
-            *tabs, wide_valid, n_ctx, groups, units,
+            tokens[0], cotangent[0], gain_one[None], gain_two[None], w_query, w_key, w_value, w_output,
+            turns, wide_valid, n_ctx, groups, units,
         )
     else:
         norm_one("a")
@@ -2006,11 +2136,12 @@
         sum_down, sum_gate, sum_up, sum_out, dr, da, gain_two_grad, _ = weight_sums(
             [(h, 0), (all_n2, 1), (all_n2, 2), (heads_out, 3)], [all_cot, dgp, dup], n_ctx, 1, extra, late=(1,)
         )
-        dqkv, i_partial, y_partial = middle_layer(
-            da, got, h, w_query, w_key, w_value, w_output, w_down, cos_full, sin_full, wide_valid, n_ctx, units
+        dqkv, i_partial, output = middle_layer(
+            da, got, h, own_residual, w_query, w_key, w_value, w_output, w_down, turns, wide_valid, n_ctx, groups, units
         )
-        extra = input_extra(groups, i_partial, y_partial, own_rows_in, dr, gain_one[None], own_residual)
-        sum_qkv, input_grad, gain_one_grad, output = weight_sums([(all_n1, 0)], [dqkv], n_ctx, 2, extra)
+        extra = input_extra(n_ctx, groups, i_partial, own_rows_in, dr, gain_one[None], gain_two_grad)
+        sum_qkv, input_grad, gain_sums = weight_sums([(all_n1, 0)], [dqkv], n_ctx, 2, extra)
+        gains = gain_sums[::8]
     else:
         d_partial = (times_transposed(dgp, w_gate) + times_transposed(dup, w_up)).astype(BF)
         y_partial = dot(h, w_down).astype(BF)
@@ -2032,11 +2163,8 @@
         back, gain_one_grad = norm_back_rows(x_own["a"], gain_one, scattered(scatter_first((state["i", "a"],))))
         input_grad = (dr + back).astype(BF)
     grad_query, grad_key, grad_value = (part.astype(F32) for part in jnp.split(sum_qkv, 3, axis=1))
-    gains = jnp.concatenate([gain_one_grad, gain_two_grad])
-    for axis in ("tp", "ctx"):
-        size = lax.axis_size(axis)
-        for bit in range(size.bit_length() - 1):
-            gains = gains + lax.ppermute(gains, axis, [(i, i ^ (1 << bit)) for i in range(size)])
+    if not paired:
+        gains = lax.psum(jnp.concatenate([gain_one_grad, gain_two_grad]), ("ctx", "tp"))
     return (
         whole_rows(output)[None],
         whole_rows(input_grad)[None],

time: 1060 us -> 1010 us (0.953)
  Pallas kernels: 969 us -> 935 us
  other arithmetic: 65.1 us -> 54.1 us
    pallas_call x1, Pallas kernels: 311 us -> 255 us  [forward_layer(): pl.pallas_call(functools.partial(forward_kernel, n_ctx, groups, units, mi...]
    pallas_call x2, Pallas kernels: 452 us -> 477 us  [weight_sums(): pl.pallas_call(functools.partial(sums_kernel, n_ctx, shapes, len(rights),...]
  transfers between devices with their start and end apart: 5 -> 0, of which waited for: 3 -> 0; matrix products, arithmetic and copies ran while one was open for 5% -> 0% of each run, Pallas kernels for 0% -> 0%
where the time goes in v5:
time: 1010 us; the launch traced here: 1000 us
  Pallas kernels  935 us (93%)
  other arithmetic  54.1 us (5%)
  local copies, waits for them, and re-layouts  10.2 us (1%)
    pallas_call x2, Pallas kernels, weight_sums(): pl.pallas_call(functools.partial(sums_kernel, n_ctx, shapes, len(rights),...  477 us
    pallas_call x1, Pallas kernels, forward_layer(): pl.pallas_call(functools.partial(forward_kernel, n_ctx, groups, units, mi...  255 us
    pallas_call x1, Pallas kernels, middle_layer(): pl.pallas_call(functools.partial(middle_kernel, n_ctx, groups, units, min...  152 us
    pallas_call x1, Pallas kernels, mlp_core(): pl.pallas_call(mlp_kernel, out_shape=(out, out, out), grid=(hidden // til...  51.1 us

profile of v5, /device:TPU:1, one launch (start us, length us, event | category | flops | bytes accessed | tf_op | source)
XLA Modules:
  0.0 1000.5 jit_solution(4563353788434096346)
XLA Ops:
  0.7 0.1 stack.54
  0.8 0.1 stack.59
  1.0 0.4 copy-done
  1.4 0.1 copy.24
  1.5 0.7 gather_fusion
  2.3 1.3 broadcast_in_dim.38
  3.6 1.3 broadcast_in_dim.39
  4.9 0.1 multiply_sine_fusion.1
  5.0 0.7 pad_maximum_fusion.2
  5.7 0.3 multiply_sine_fusion
  6.0 0.8 pad_maximum_fusion
  6.8 1.1 slice_bitcast_fusion.2
  7.9 1.1 slice_bitcast_fusion.3
  9.0 1.1 broadcast_in_dim.35.refs_12_.refs_13_
  10.3 3.1 maximum_select_fusion
  13.4 255.2 %shard_map.203 = (bf16[1536,2048]{1,0:T(8,128)(2,1)}, bf16[3,8,3,256,128]{4,3,2,1,0:T(8,128)(2,1)}, bf16[1536,512]{1,0:T(8,128)(2,1)}, f32[384,2048]{1,0:T(8,128...) custom-call(bf16[384,2048]{1,0:T(8,128)(2,1)} %bitcast.38, bf16[384,2048]{1,0:T(8,128)(2,1)} %bitcast.39, ...), custom_call_target="tpu_custom_call" | custom-call | flops 12884901888 | bytes 25165824 | tf_op jit(solution)/shard_map/pallas_call | solution.py:1633
  268.6 51.1 %shard_map.204 = (bf16[1536,2048]{1,0:T(8,128)(2,1)}, bf16[1536,2048]{1,0:T(8,128)(2,1)}, bf16[1536,2048]{1,0:T(8,128)(2,1)}) custom-call(bf16[1536,2048]{1,0:T(8,128)(2,1)} %get-tuple-element.33.n_ref.refs_1_.refs_2_, bf16[1536,2048]{1,0:T(8,128)(2,1)} %get-tuple-element.34.g_ref.refs_4_, bf16[2048,2048]{1,0:T(8,128)(2,1)} %refs_9_.1, ...), custom_call_target="tpu_custom_call" | custom-call | flops 38654705664 | bytes 56623104 | tf_op jit(solution)/shard_map/pallas_call | solution.py:546
  319.7 362.6 %shard_map.205 = (bf16[2048,2048]{1,0:T(8,128)(2,1)}, bf16[2048,2048]{1,0:T(8,128)(2,1)}, bf16[2048,2048]{1,0:T(8,128)(2,1)}, bf16[512,2048]{1,0:T(8,128)(2,1)},...) custom-call(bf16[1536,2048]{1,0:T(8,128)(2,1)} %get-tuple-element.35.refs_0_., ...), custom_call_target="tpu_custom_call" | custom-call | flops 41875931136 | bytes 47710208 | tf_op jit(solution)/shard_map/pallas_call | solution.py:1077
  682.2 152.0 %shard_map.206 = (bf16[1536,1536]{1,0:T(8,128)(2,1)}, bf16[1536,2048]{1,0:T(8,128)(2,1)}, bf16[384,2048]{1,0:T(8,128)(2,1)}) custom-call(bf16[1536,2048]{1,0:T(8,128)(2,1)} %get-tuple-element.40.refs_0_, bf16[3,8,3,256,128]{4,3,2,1,0:T(8,128)(2,1)} %get-tuple-element.41.refs_1_, bf16[1536,2048]{1,0:T(8,128)(2,1)} %get-tuple-element.35.refs_0_.refs_2_, ...), custom_call_target="tpu_custom_call" | custom-call | flops 25769803776 | bytes 25165824 | tf_op jit(solution)/shard_map/pallas_call | solution.py:1891
  834.3 114.3 %shard_map.207 = (bf16[2048,1536]{1,0:T(8,128)(2,1)}, bf16[384,2048]{1,0:T(8,128)(2,1)}, f32[16,2048]{1,0:T(8,128)}) custom-call(bf16[1536,2048]{1,0:T(8,128)(2,1)} %get-tuple-element.43.refs_0_, bf16[1536,1536]{1,0:T(8,128)(2,1)} %get-tuple-element.44.refs_1_, bf16[1536,2048]{1,0:T(8,128)(2,1)} %get-tuple-element.45.refs_2_, ...), custom_call_target="tpu_custom_call" | custom-call | flops 9663676416 | bytes 12582912 | tf_op jit(solution)/shard_map/pallas_call | solution.py:1077
  948.6 1.0 slice.61
  949.7 0.6 fusion.8
  950.3 1.1 slice.59
  951.4 1.3 slice.60
  952.7 1.7 fusion.1
  954.6 1.7 fusion
  956.3 2.7 convert_element_type.66
  959.0 1.0 slice-done.1
  960.0 5.2 slice_convert_fusion
  965.3 11.7 %convert_element_type.67 = f32[2048,2048]{1,0:T(8,128)} convert(bf16[2048,2048]{1,0:T(8,128)(2,1)} %get-tuple-element.52) | non-fusion elementwise | flops 4194304 | bytes 25165824 | tf_op jit(solution)/shard_map/convert_element_type | solution.py:2177
  976.9 11.7 %convert_element_type.68 = f32[2048,2048]{1,0:T(8,128)} convert(bf16[2048,2048]{1,0:T(8,128)(2,1)} %get-tuple-element.53) | non-fusion elementwise | flops 4194304 | bytes 25165824 | tf_op jit(solution)/shard_map/convert_element_type | solution.py:2178
  988.6 11.7 %convert_element_type.69 = f32[2048,2048]{1,0:T(8,128)} convert(bf16[2048,2048]{1,0:T(8,128)(2,1)} %get-tuple-element.54) | non-fusion elementwise | flops 4194304 | bytes 25165824 | tf_op jit(solution)/shard_map/convert_element_type | solution.py:2179
  (27 shorter events, 0.5 us)
Async XLA Ops:
  0.6 0.7 copy-start
  0.7 9.5 copy-start.3
  0.7 9.4 copy-start.2
  834.3 117.1 %copy-start.4 = (bf16[384,2048]{1,0:T(8,128)(2,1)S(1)}, bf16[384,2048]{1,0:T(8,128)(2,1)}, u32[]{:S(2)}) copy-start(bf16[384,2048]{1,0:T(8,128)(2,1)} %get-tuple-element.42) | copy-start | bytes 4718596
  948.6 4.1 copy-start.5
  954.5 1.8 copy-start.6
  954.5 4.5 slice-start
  954.6 5.5 slice-start.1
  988.6 11.7 %copy-start.1 = (s32[8,6,2]{0,2,1:T(2,128)S(1)}, s32[8,6,2]{0,2,1:T(2,128)}, u32[]{:S(2)}) copy-start(s32[8,6,2]{0,2,1:T(2,128)} %param.13) | copy-start | bytes 1156

commit v6 on v5

--- a/solution.py
+++ b/solution.py
@@ -528,11 +528,7 @@
     gate_pre = dot(rows, wg_ref[...])
     up_pre = dot(rows, wu_ref[...])
     hidden_grad = times_transposed(g_ref[...], wd_ref[...])
-    gate_sig = 1.0 / (1.0 + jnp.exp2(gate_pre * (-LOG2E)))
-    gate_act = gate_pre * gate_sig
-    h_ref[...] = (gate_act * up_pre).astype(BF)
-    dup_ref[...] = (hidden_grad * gate_act).astype(BF)
-    dgp_ref[...] = (hidden_grad * up_pre * (gate_sig * (1.0 + gate_pre * (1.0 - gate_sig)))).astype(BF)
+    h_ref[...], dgp_ref[...], dup_ref[...] = feed_values(gate_pre, up_pre, hidden_grad)
 
 
 def mlp_core(normed, grads, wg, wu, wd, total, first, held=()):
@@ -798,8 +794,12 @@
 
 def sums_kernel(n_ctx, items, n_right, n_extra, tasks, late, *refs):
     n_left = len(items)
-    left_refs, right_refs = refs[:n_left], refs[n_left : n_left + n_right]
-    extra_in, refs = refs[n_left + n_right : n_left + n_right + n_extra[0]], refs[n_left + n_right + n_extra[0] :]
+    made = items[0][3]
+    n_held = n_left - (1 if made else 0)
+    left_refs, right_refs = refs[:n_held], refs[n_held : n_held + n_right]
+    left_refs = ((None,) if made else ()) + tuple(left_refs)
+    refs = refs[n_held + n_right :]
+    extra_in, refs = refs[: n_extra[0]], refs[n_extra[0] :]
     out_refs, extra_out, refs = refs[:n_left], refs[n_left : n_left + n_extra[1]], refs[n_left + n_extra[1] :]
     extra_scratch, refs = refs[: n_extra[2]], refs[n_extra[2] :]
     right_refs = list(right_refs) + [extra_out[k] for k in late]
@@ -810,7 +810,7 @@
         fin_send, fin_recv, store_sem, core_credit, in_credit, mid_credit, out_credit, fin_credit,
     ) = refs
     starts = [0]
-    for _, _, chunks in items:
+    for _, _, chunks, _ in items:
         starts.append(starts[-1] + chunks)
     total = starts[-1]
     n_ring = ring.shape[0]
@@ -886,16 +886,27 @@
 
     def load_left(at):
         def action(number, chunk):
+            if number == 0 and made:
+                maker.load(chunk // 2)
+                return
+            if number == 1 and made:
+
+                @pl.when(chunk == 0)
+                def _():
+                    maker.release()
+
             for which in range(2):
                 left_copy(number, chunk, lax.rem(at // 2, 2), which).start()
 
         for_item(at, action)
 
-    load_left(0)
-    planned, each = tasks(extra_in, extra_out, extra_scratch) if tasks is not None else ({}, None)
+    planned, each, maker = tasks(extra_in, extra_out, extra_scratch) if tasks is not None else ({}, None, None)
     if 0 in planned:
         planned.pop(0)()
-    if n_right > 1:
+    if made:
+        maker.begin(left_buf, right_buf)
+    load_left(0)
+    if n_right > 1 and not made:
         right_copy(1).start()
     right_copy(0).wait()
 
@@ -1028,16 +1039,21 @@
 
                     @pl.when(chunk == 0)
                     def _():
+                        if made and which_right in (1, n_right - 1):
+                            right_copy(which_right).start()
                         right_copy(which_right).wait()
 
-                if which_right > 0 and which_right + 1 < n_right:
+                if which_right > 0 and which_right + 1 < n_right - (1 if made else 0):
 
                     @pl.when(chunk == items[number][2] // 2)
                     def _():
                         right_copy(which_right + 1).start()
 
-                for which in range(2):
-                    left_copy(number, chunk, slot, which).wait()
+                if number == 0 and made:
+                    maker.make(chunk // 2)
+                else:
+                    for which in range(2):
+                        left_copy(number, chunk, slot, which).wait()
                 right = right_buf.at[which_right % 2]
                 product = contract_rows(left_buf[slot, 1], right[...]).astype(BF)
                 for part in range(2):
@@ -1064,9 +1080,13 @@
     lax.fori_loop(0, total + lag_w, step, 0)
 
 
-def weight_sums(items, rights, n_ctx, collective_id, extra=None, late=()):
+def weight_sums(items, rights, n_ctx, collective_id, extra=None, late=(), limit=VMEM_LIMIT):
     tokens, width = rights[0].shape
-    shapes = [(k, right, left.shape[1] // 2 // ROWS) for k, (left, right) in enumerate(items)]
+    columns = [left if isinstance(left, int) else left.shape[1] for left, _ in items]
+    held = [left for left, _ in items if not isinstance(left, int)]
+    shapes = [
+        (k, right, columns[k] // 2 // ROWS, isinstance(left, int)) for k, (left, right) in enumerate(items)
+    ]
     mid = n_ctx // 4
     n_ring = mid + 2 + 2 * (mid - 1) + 4
     any_spec = pl.BlockSpec(memory_space=pl.ANY)
@@ -1076,8 +1096,8 @@
     dma = pltpu.SemaphoreType.DMA
     return pl.pallas_call(
         functools.partial(sums_kernel, n_ctx, shapes, len(rights), counts, tasks, late),
-        out_shape=[jax.ShapeDtypeStruct((left.shape[1], width), BF) for left, _ in items] + outs,
-        in_specs=[any_spec] * (len(items) + len(rights)) + arg_specs,
+        out_shape=[jax.ShapeDtypeStruct((count, width), BF) for count in columns] + outs,
+        in_specs=[any_spec] * (len(held) + len(rights)) + arg_specs,
         out_specs=[any_spec] * len(items) + out_specs,
         scratch_shapes=scratch
         + [
@@ -1106,14 +1126,14 @@
         ]
         + [pltpu.SemaphoreType.REGULAR] * 5,
         compiler_params=pltpu.CompilerParams(
-            vmem_limit_bytes=VMEM_LIMIT, collective_id=collective_id, has_side_effects=True
+            vmem_limit_bytes=limit, collective_id=collective_id, has_side_effects=True
         ),
         cost_estimate=pl.CostEstimate(
-            flops=sum(2 * left.shape[1] * tokens * width for left, _ in items),
-            bytes_accessed=sum(2 * left.shape[1] * (tokens + width) for left, _ in items),
+            flops=sum(2 * count * tokens * width for count in columns),
+            bytes_accessed=sum(2 * count * (tokens + width) for count in columns),
             transcendentals=0,
         ),
-    )(*[left for left, _ in items], *rights, *args)
+    )(*held, *rights, *args)
 
 
 VMEM_SPEC = pl.BlockSpec(memory_space=pltpu.VMEM)
@@ -1128,19 +1148,160 @@
     return back, jnp.sum(grad * unit, axis=0, keepdims=True)
 
 
+def own_copies(ref, buf, groups, sem):
+    odd = lax.rem(lax.axis_index("tp"), 2)
+    starts = [pl.multiple_of(odd * BLOCK, BLOCK), pl.multiple_of((1 - odd) * PAIR, BLOCK)]
+    return [
+        pltpu.make_async_copy(ref.at[pl.ds(start, rows)], buf.at[pl.ds(own, rows)], sem.at[g])
+        for g, (start, (_, rows, own)) in enumerate(zip(starts, groups))
+    ]
+
+
+class Maker:
+    def __init__(self, refs, outs, weights, downs, stage, sems):
+        self.n2_ref, self.wg_ref, self.wu_ref, self.wd_ref = refs
+        self.h_out, self.dgp_out, self.dup_out = outs
+        self.weights, self.downs, self.stage = weights, downs, stage
+        self.n2_sem, self.weight_sem, self.h_sem, self.grad_sem = sems
+        self.core = lax.rem(lax.axis_index("ctx"), 2)
+        self.half = self.h_out.shape[1] // 2
+        self.tiles = self.half // TILE
+
+    def first(self, tile, which):
+        side = self.core if which == 0 else 1 - self.core
+        return pl.multiple_of(side * self.half + tile * TILE, TILE)
+
+    def copies(self, tile):
+        slot = lax.rem(tile, 2)
+        deep = self.weights.shape[1]
+        made = []
+        for which in range(2):
+            at = pl.ds(self.first(tile, which), TILE)
+            for kind, ref in enumerate((self.wg_ref, self.wu_ref)):
+                to = pl.multiple_of((slot * 2 + kind) * 2 * TILE + which * TILE, TILE)
+                for part in range(2):
+                    made.append((ref.at[pl.ds(part * deep, deep), at], self.weights.at[part, :, pl.ds(to, TILE)]))
+            made.append((self.wd_ref.at[at], self.downs.at[slot, 0, pl.ds(which * TILE, TILE)]))
+        return [
+            pltpu.make_async_copy(source, dest, self.weight_sem.at[slot, k]) for k, (source, dest) in enumerate(made)
+        ]
+
+    def load(self, tile):
+        for copy in self.copies(tile):
+            copy.start()
+
+    def begin(self, left_buf, right_buf):
+        self.left_buf, self.right_buf = left_buf, right_buf
+        self.n2_copy().start()
+
+    def n2_copy(self):
+        return pltpu.make_async_copy(self.n2_ref, self.right_buf.at[1], self.n2_sem)
+
+    def h_stores(self, tile):
+        slot = lax.rem(tile, 2)
+        return [
+            pltpu.make_async_copy(
+                self.left_buf.at[slot, which],
+                self.h_out.at[:, pl.ds(self.first(tile, which), TILE)],
+                self.h_sem.at[slot, which],
+            )
+            for which in range(2)
+        ]
+
+    def grad_stores(self, tile):
+        return [
+            pltpu.make_async_copy(
+                self.stage.at[kind, which], out.at[:, pl.ds(self.first(tile, which), TILE)], self.grad_sem.at[kind, which]
+            )
+            for kind, out in enumerate((self.dgp_out, self.dup_out))
+            for which in range(2)
+        ]
+
+    def make(self, tile):
+        slot = lax.rem(tile, 2)
+        deep = self.weights.shape[1]
+
+        @pl.when(tile == 0)
+        def _():
+            self.n2_copy().wait()
+
+        @pl.when(tile > 0)
+        def _():
+            for copy in self.grad_stores(tile - 1):
+                copy.wait()
+
+        @pl.when(tile > 1)
+        def _():
+            for copy in self.h_stores(tile - 2):
+                copy.wait()
+
+        for copy in self.copies(tile):
+            copy.wait()
+        at_gate = pl.ds(pl.multiple_of(slot * 4 * TILE, TILE), 2 * TILE)
+        at_up = pl.ds(pl.multiple_of((slot * 4 + 2) * TILE, TILE), 2 * TILE)
+        count = 512
+
+        def rows_step(step, carry):
+            rows = pl.ds(pl.multiple_of(step * count, count), count)
+            low, high = self.right_buf[1, rows, :deep], self.right_buf[1, rows, deep:]
+            gate_pre = dot(low, self.weights[0, :, at_gate]) + dot(high, self.weights[1, :, at_gate])
+            up_pre = dot(low, self.weights[0, :, at_up]) + dot(high, self.weights[1, :, at_up])
+            hidden_grad = times_transposed(self.right_buf[0, rows, :], self.downs[slot, 0])
+            h, dgp, dup = feed_values(gate_pre, up_pre, hidden_grad)
+            for which in range(2):
+                part = slice(which * TILE, (which + 1) * TILE)
+                self.left_buf[slot, which, rows, :] = h[:, part]
+                self.stage[0, which, rows, :] = dgp[:, part]
+                self.stage[1, which, rows, :] = dup[:, part]
+            return carry
+
+        lax.fori_loop(0, self.right_buf.shape[1] // count, rows_step, 0)
+        for copy in self.h_stores(tile) + self.grad_stores(tile):
+            copy.start()
+
+    def release(self):
+        for copy in self.h_stores(self.tiles - 2):
+            copy.wait()
+
+    def finish(self):
+        for copy in self.h_stores(self.tiles - 1) + self.grad_stores(self.tiles - 1):
+            copy.wait()
+
+
+def feed_values(gate_pre, up_pre, hidden_grad):
+    gate_sig = 1.0 / (1.0 + jnp.exp2(gate_pre * (-LOG2E)))
+    gate_act = gate_pre * gate_sig
+    return (
+        (gate_act * up_pre).astype(BF),
+        (hidden_grad * up_pre * (gate_sig * (1.0 + gate_pre * (1.0 - gate_sig)))).astype(BF),
+        (hidden_grad * gate_act).astype(BF),
+    )
+
+
 def feed_tasks(groups, extra_in, extra_out, scratch):
-    dgp_ref, dup_ref, wg_ref, wu_ref, residual, grads, gain = extra_in
-    dr, da_all, gain_grad, d_ref = extra_out
+    n2_ref, wg_ref, wu_ref, wd_ref, residual, cot_ref, gain = extra_in
+    dr, da_all, gain_grad, d_ref, h_ref, dgp_ref, dup_ref = extra_out
     n = len(Scatter.scratch(16, 128))
     bufs, rest = scratch[:n], scratch[n:]
     weights, lefts, tile_out, weight_sem, left_sem, out_sem = rest[:6]
+    grads, stage, own_sem, n2_sem, make_sem, h_sem, grad_sem = rest[6:13]
     da_own = bufs[0]
     scatter = Scatter(d_ref, groups, bufs[:9], bufs[9:])
-    gather = Gather(da_own, da_all, groups, rest[6:])
+    gather = Gather(da_own, da_all, groups, rest[13:])
+    maker = Maker(
+        (n2_ref, wg_ref, wu_ref, wd_ref),
+        (h_ref, dgp_ref, dup_ref),
+        weights,
+        lefts,
+        stage,
+        (n2_sem, make_sem, h_sem, grad_sem),
+    )
     order = list(reversed(range(len(groups))))
     rows, columns = lefts.shape[2], weights.shape[1]
     row_tiles = dgp_ref.shape[0] // rows
     tiles = row_tiles * (d_ref.shape[1] // columns)
+    after = maker.half // ROWS
+    shift = after + 1
 
     def weight_copies(part):
         at = pl.ds(pl.multiple_of(part * columns, columns), columns)
@@ -1169,11 +1330,18 @@
 
     def begin():
         gain_grad[...] = jnp.zeros_like(gain_grad)
+        for copy in own_copies(cot_ref, grads, groups, own_sem):
+            copy.start()
+
+    def whole_hidden():
+        maker.finish()
         for copy in weight_copies(0) + left_copies(0):
             copy.start()
 
-    def each(i):
-        @pl.when(i < tiles)
+    def each(step):
+        i = step - shift
+
+        @pl.when((i >= 0) & (i < tiles))
         def _():
             slot = lax.rem(i, 2)
 
@@ -1206,6 +1374,8 @@
     def start():
         out_copy(tiles - 2).wait()
         out_copy(tiles - 1).wait()
+        for copy in own_copies(cot_ref, grads, groups, own_sem):
+            copy.wait()
         for g in order:
             scatter.start(g)
 
@@ -1225,30 +1395,32 @@
             gather.finish(g)
             gather.sent(g)
 
+    first = shift + tiles
     plan = {
         0: begin,
-        tiles: start,
-        tiles + 4: lambda: scatter.forward(order[0]),
-        tiles + 7: lambda: scatter.forward(order[-1]),
-        tiles + 8: lambda: spread(order[0]),
-        tiles + 10: lambda: spread(order[-1]),
-        tiles + 13: lambda: gather.forward(order[0]),
-        tiles + 17: lambda: gather.forward(order[-1]),
-        tiles + 23: finish,
+        after: whole_hidden,
+        first: start,
+        first + 3: lambda: scatter.forward(order[0]),
+        first + 6: lambda: scatter.forward(order[-1]),
+        first + 7: lambda: spread(order[0]),
+        first + 9: lambda: spread(order[-1]),
+        first + 11: lambda: gather.forward(order[0]),
+        first + 15: lambda: gather.forward(order[-1]),
+        first + 18: finish,
     }
-    return plan, each
-
-
-def feed_extra(groups, dgp, dup, wg, wu, residual, grads, gain):
+    return plan, each, maker
+
+
+def feed_extra(groups, n2, wg, wu, wd, residual, cot, gain):
     rows, width = residual.shape
-    tokens, hidden = dgp.shape
+    tokens, hidden = n2.shape[0], wg.shape[1]
     dma = pltpu.SemaphoreType.DMA
     outs = [
         jax.ShapeDtypeStruct((rows, width), F32),
         jax.ShapeDtypeStruct((tokens, width), BF),
         jax.ShapeDtypeStruct((1, width), F32),
         jax.ShapeDtypeStruct((tokens, width), BF),
-    ]
+    ] + [jax.ShapeDtypeStruct((tokens, hidden), BF)] * 3
     scratch = (
         Scatter.scratch(rows, width)
         + [
@@ -1258,25 +1430,32 @@
             dma((2,)),
             dma((2, 2)),
             dma((2,)),
+            pltpu.VMEM((rows, width), BF),
+            pltpu.VMEM((2, 2, tokens, TILE), BF),
+            dma((2,)),
+            dma,
+            dma((2, 10)),
+            dma((2, 2)),
+            dma((2, 2)),
         ]
         + Gather.scratch()
     )
     return (
-        [dgp, dup, wg, wu, residual, grads, gain],
-        [ANY_SPEC] * 4 + [VMEM_SPEC] * 3,
+        [n2, wg, wu, wd, residual, cot, gain],
+        [ANY_SPEC] * 4 + [VMEM_SPEC, ANY_SPEC, VMEM_SPEC],
         outs,
-        [VMEM_SPEC, ANY_SPEC, VMEM_SPEC, ANY_SPEC],
+        [VMEM_SPEC, ANY_SPEC, VMEM_SPEC] + [ANY_SPEC] * 4,
         scratch,
         functools.partial(feed_tasks, groups),
     )
 
 
 def input_tasks(n_ctx, groups, extra_in, extra_out, scratch):
-    i_ref, rows_in, dr, gain, gain_two_grad = extra_in
+    i_ref, tokens_ref, dr, gain, gain_two_grad = extra_in
     input_grad, gain_sums = extra_out
     n = len(Scatter.scratch(16, 128))
     scatter = Scatter(i_ref, groups, scratch[:9], scratch[9:n])
-    gains, got_tp, got_ctx, send_tp, recv_tp, send_ctx, recv_ctx = scratch[n:]
+    gains, got_tp, got_ctx, send_tp, recv_tp, send_ctx, recv_ctx, rows_in, own_sem = scratch[n:]
     order = list(reversed(range(len(groups))))
     me, rank = lax.axis_index("ctx"), lax.axis_index("tp")
 
@@ -1290,8 +1469,12 @@
     def begin():
         gains[0] = jnp.zeros(gains.shape[1:], F32)
         gains[0, 8:9, :] = gain_two_grad[...]
+        for copy in own_copies(tokens_ref, rows_in, groups, own_sem):
+            copy.start()
         for g in order:
             scatter.start(g)
+        for copy in own_copies(tokens_ref, rows_in, groups, own_sem):
+            copy.wait()
 
     def use(at, total):
         back, more = norm_back_rows(rows_in[at, :].astype(F32), gain[...], total)
@@ -1331,16 +1514,16 @@
         15: second,
         17: third,
         20: finish,
-    }, None
-
-
-def input_extra(n_ctx, groups, i_partial, rows_in, dr, gain, gain_two_grad):
-    rows, width = rows_in.shape
+    }, None, None
+
+
+def input_extra(n_ctx, groups, i_partial, tokens_in, dr, gain, gain_two_grad):
+    rows, width = tokens_in.shape
     dma = pltpu.SemaphoreType.DMA
     outs = [jax.ShapeDtypeStruct((rows, width), BF), jax.ShapeDtypeStruct((16, width), F32)]
     return (
-        [i_partial, rows_in, dr, gain, gain_two_grad],
-        [ANY_SPEC] + [VMEM_SPEC] * 4,
+        [i_partial, tokens_in, dr, gain, gain_two_grad],
+        [ANY_SPEC] * 2 + [VMEM_SPEC] * 3,
         outs,
         [VMEM_SPEC] * 2,
         Scatter.scratch(rows, width)
@@ -1352,6 +1535,8 @@
             dma((2,)),
             dma((n_ctx,)),
             dma((n_ctx,)),
+            pltpu.VMEM((rows, width), BF),
+            dma((2,)),
         ],
         functools.partial(input_tasks, n_ctx, groups),
     )
@@ -2100,10 +2285,6 @@
 
     groups = tuple((first_row[n], rows_of[n] // 4, first_row[n] // 4) for n in ("a", "b") if n in names)
 
-    def own_order(array):
-        return jnp.where(odd == 1, jnp.roll(array, -BLOCK, axis=0), array) if paired else array
-
-    own_grads, own_rows_in = own_order(cotangent[0]), own_order(tokens[0])
     if paired:
         units = ((0, False), (2 * PAIR, False), (4 * PAIR, True))
         wide_valid = jnp.broadcast_to(flat_valid[:, None], (total_rows, HD))
@@ -2130,19 +2311,23 @@
         gather_a("cot")("a")
         all_n1, all_n2, all_cot = state["n1", "a"], gathered(state["n2", "a"]), gathered(state["cot", "a"])
         heads_out, own_residual = state["heads", "a"], state["residual", "a"]
-    h, dgp, dup = mlp_core(all_n2, all_cot, w_gate, w_up, w_down, total_rows, 0)
     if paired:
-        extra = feed_extra(groups, dgp, dup, w_gate, w_up, own_residual, own_grads, gain_two[None])
-        sum_down, sum_gate, sum_up, sum_out, dr, da, gain_two_grad, _ = weight_sums(
-            [(h, 0), (all_n2, 1), (all_n2, 2), (heads_out, 3)], [all_cot, dgp, dup], n_ctx, 1, extra, late=(1,)
+        extra = feed_extra(groups, all_n2, w_gate, w_up, w_down, own_residual, cotangent[0], gain_two[None])
+        sum_down, sum_gate, sum_up, sum_out, dr, da, gain_two_grad, _, h, _, _ = weight_sums(
+            [(w_down.shape[0], 0), (all_n2, 1), (all_n2, 2), (heads_out, 3)],
+            [all_cot], n_ctx, 1, extra, late=(5, 6, 1), limit=62 * 1024 * 1024,
         )
         dqkv, i_partial, output = middle_layer(
             da, got, h, own_residual, w_query, w_key, w_value, w_output, w_down, turns, wide_valid, n_ctx, groups, units
         )
-        extra = input_extra(n_ctx, groups, i_partial, own_rows_in, dr, gain_one[None], gain_two_grad)
-        sum_qkv, input_grad, gain_sums = weight_sums([(all_n1, 0)], [dqkv], n_ctx, 2, extra)
+        extra = input_extra(n_ctx, groups, i_partial, tokens[0], dr, gain_one[None], gain_two_grad)
+        sum_qkv, input_grad, gain_sums = weight_sums(
+            [(all_n1, 0)], [dqkv], n_ctx, 2, extra, limit=36 * 1024 * 1024
+        )
         gains = gain_sums[::8]
     else:
+        own_grads = cotangent[0]
+        h, dgp, dup = mlp_core(all_n2, all_cot, w_gate, w_up, w_down, total_rows, 0)
         d_partial = (times_transposed(dgp, w_gate) + times_transposed(dup, w_up)).astype(BF)
         y_partial = dot(h, w_down).astype(BF)
         (sum_down,) = weight_sums([(h, 0)], [all_cot], n_ctx, 1)

time: 1010 us -> 963 us (0.953)
  Pallas kernels: 935 us -> 894 us
    pallas_call x1 -> x0, Pallas kernels: 51.1 us -> none  [mlp_core(): pl.pallas_call(mlp_kernel, out_shape=(out, out, out), grid=(hidden // til...]
    pallas_call x2, Pallas kernels: 477 us -> 487 us  [weight_sums(): pl.pallas_call(functools.partial(sums_kernel, n_ctx, shapes, len(rights),...]
where the time goes in v6:
time: 963 us; the launch traced here: 959 us
  Pallas kernels  894 us (93%)
  other arithmetic  50.9 us (5%)
  local copies, waits for them, and re-layouts  12.6 us (1%)
    pallas_call x2, Pallas kernels, weight_sums(): pl.pallas_call(functools.partial(sums_kernel, n_ctx, shapes, len(rights),...  487 us
    pallas_call x1, Pallas kernels, forward_layer(): pl.pallas_call(functools.partial(forward_kernel, n_ctx, groups, units, mi...  255 us
    pallas_call x1, Pallas kernels, middle_layer(): pl.pallas_call(functools.partial(middle_kernel, n_ctx, groups, units, min...  152 us

profile of v6, /device:TPU:1, one launch (start us, length us, event | category | flops | bytes accessed | tf_op | source)
XLA Modules:
  0.0 958.7 jit_solution(10894395296906803683)
XLA Ops:
  0.7 0.1 stack.54
  0.8 0.1 stack.59
  0.9 0.4 copy-done
  1.3 0.1 constant_dynamic-slice_fusion
  1.4 0.1 copy.24
  1.5 0.7 gather_fusion
  2.3 0.1 convert_bitcast_fusion
  2.3 1.3 broadcast_in_dim.38
  3.6 1.3 broadcast_in_dim.39
  4.9 0.1 multiply_sine_fusion.1
  5.0 0.7 pad_maximum_fusion.2
  5.7 0.3 multiply_sine_fusion
  6.0 0.8 pad_maximum_fusion
  6.8 1.1 broadcast_in_dim.35.refs_12_.refs_13_
  7.9 255.2 %shard_map.203 = (bf16[1536,2048]{1,0:T(8,128)(2,1)}, bf16[3,8,3,256,128]{4,3,2,1,0:T(8,128)(2,1)}, bf16[1536,512]{1,0:T(8,128)(2,1)}, f32[384,2048]{1,0:T(8,128...) custom-call(bf16[384,2048]{1,0:T(8,128)(2,1)} %bitcast.31, bf16[384,2048]{1,0:T(8,128)(2,1)} %bitcast.38, ...), custom_call_target="tpu_custom_call" | custom-call | flops 12884901888 | bytes 25165824 | tf_op jit(solution)/shard_map/pallas_call | solution.py:1818
  263.1 376.3 %shard_map.204 = (bf16[2048,2048]{1,0:T(8,128)(2,1)}, bf16[2048,2048]{1,0:T(8,128)(2,1)}, bf16[2048,2048]{1,0:T(8,128)(2,1)}, bf16[512,2048]{1,0:T(8,128)(2,1)},...) custom-call(bf16[1536,2048]{1,0:T(8,128)(2,1)} %get-tuple-element.31, ...), custom_call_target="tpu_custom_call" | custom-call | flops 41875931136 | bytes 47710208 | tf_op jit(solution)/shard_map/pallas_call | solution.py:1097
  639.4 151.7 %shard_map.205 = (bf16[1536,1536]{1,0:T(8,128)(2,1)}, bf16[1536,2048]{1,0:T(8,128)(2,1)}, bf16[384,2048]{1,0:T(8,128)(2,1)}) custom-call(bf16[1536,2048]{1,0:T(8,128)(2,1)} %get-tuple-element.35.refs_0_, bf16[3,8,3,256,128]{4,3,2,1,0:T(8,128)(2,1)} %get-tuple-element.36.refs_1_, bf16[1536,2048]{1,0:T(8,128)(2,1)} %get-tuple-element.37.refs_2_, ...), custom_call_target="tpu_custom_call" | custom-call | flops 25769803776 | bytes 25165824 | tf_op jit(solution)/shard_map/pallas_call | solution.py:2076
  791.2 2.3 copy-done.5
  793.5 1.9 copy-done.6
  795.4 111.0 %shard_map.206 = (bf16[2048,1536]{1,0:T(8,128)(2,1)S(1)}, bf16[384,2048]{1,0:T(8,128)(2,1)S(1)}, f32[16,2048]{1,0:T(8,128)S(1)}) custom-call(bf16[1536,2048]{1,0:T(8,128)(2,1)} %get-tuple-element.39.refs_0_, bf16[1536,1536]{1,0:T(8,128)(2,1)S(1)} %copy-done.5, bf16[1536,2048]{1,0:T(8,128)(2,1)} %get-tuple-element.41.refs_2_, bf16[384,2048]{1,0:T(8,128)(2,1)S(1)} %bitcast.32, ...), custom_call_target="tpu_custom_call" | custom-call | flops 9663676416 | bytes 12582912 | tf_op jit(solution)/shard_map/pallas_call | solution.py:1097
  906.4 2.7 copy-done.2
  909.1 0.6 fusion.8
  909.8 1.1 slice.23
  910.9 0.1 slice.26
  910.9 1.7 fusion.1
  912.8 1.7 fusion
  914.5 2.7 convert_element_type.66
  917.2 1.0 slice-done.1
  918.2 5.2 slice_convert_fusion
  923.5 11.7 %convert_element_type.67 = f32[2048,2048]{1,0:T(8,128)} convert(bf16[2048,2048]{1,0:T(8,128)(2,1)} %get-tuple-element.48) | non-fusion elementwise | flops 4194304 | bytes 25165824 | tf_op jit(solution)/shard_map/convert_element_type | solution.py:2362
  935.1 11.7 %convert_element_type.68 = f32[2048,2048]{1,0:T(8,128)} convert(bf16[2048,2048]{1,0:T(8,128)(2,1)} %get-tuple-element.49) | non-fusion elementwise | flops 4194304 | bytes 25165824 | tf_op jit(solution)/shard_map/convert_element_type | solution.py:2363
  946.8 11.7 %convert_element_type.69 = f32[2048,2048]{1,0:T(8,128)} convert(bf16[2048,2048]{1,0:T(8,128)(2,1)} %get-tuple-element.50) | non-fusion elementwise | flops 4194304 | bytes 25165824 | tf_op jit(solution)/shard_map/convert_element_type | solution.py:2364
  (27 shorter events, 0.2 us)
Async XLA Ops:
  0.6 0.7 copy-start
  639.4 151.8 %copy-start.3 = (f32[2048]{0:T(1024)S(1)}, f32[2048]{0:T(1024)}, u32[]{:S(2)}) copy-start(f32[2048]{0:T(1024)} %broadcast_in_dim.38) | copy-start | bytes 24580
  639.4 151.8 %copy-start.4 = (bf16[1,384,2048]{2,1,0:T(8,128)(2,1)S(1)}, bf16[1,384,2048]{2,1,0:T(8,128)(2,1)}, u32[]{:S(2)}) copy-start(bf16[1,384,2048]{2,1,0:T(8,128)(2,1)} %param.12) | copy-start | bytes 4718596
  639.4 151.8 %copy-start.7 = (f32[1,2048]{1,0:T(1,128)S(1)}, f32[1,2048]{1,0:T(1,128)}, u32[]{:S(2)}) copy-start(f32[1,2048]{1,0:T(1,128)} %get-tuple-element.43.refs_6_) | copy-start | bytes 24580
  791.2 2.3 copy-start.5
  793.5 1.9 copy-start.6
  906.4 2.7 copy-start.2
  910.9 1.8 copy-start.8
  912.7 1.8 copy-start.9
  912.7 4.5 slice-start
  912.8 5.5 slice-start.1
  946.8 11.7 %copy-start.1 = (s32[8,6,2]{0,2,1:T(2,128)S(1)}, s32[8,6,2]{0,2,1:T(2,128)}, u32[]{:S(2)}) copy-start(s32[8,6,2]{0,2,1:T(2,128)} %param.13) | copy-start | bytes 1156

commit v7 on v6

--- a/solution.py
+++ b/solution.py
@@ -834,26 +834,6 @@
     lag_f = lag_o + 1
     lag_w = lag_f + 1
 
-    if tasks is not None:
-        greet(n_ctx, True)
-    else:
-        barrier = pltpu.get_barrier_semaphore()
-        pl.semaphore_signal(barrier, inc=1, device_id=partner, device_id_type=pl.DeviceIdType.MESH)
-
-        @pl.when(chip > 0)
-        def _():
-            pl.semaphore_signal(
-                barrier, inc=1, device_id=((chip - 1) * 2 + core, rank), device_id_type=pl.DeviceIdType.MESH
-            )
-
-        @pl.when(chip < chips - 1)
-        def _():
-            pl.semaphore_signal(
-                barrier, inc=1, device_id=((chip + 1) * 2 + core, rank), device_id_type=pl.DeviceIdType.MESH
-            )
-
-        pl.semaphore_wait(barrier, 1 + jnp.where(chip > 0, 1, 0) + jnp.where(chip < chips - 1, 1, 0))
-
     to_core = Ring(core_in, core_send, core_recv, core_credit, total)
     to_after = Ring(hop_in, in_send, in_recv, in_credit, total)
     across = Ring(hop_mid, mid_send, mid_recv, mid_credit, total)
@@ -880,7 +860,7 @@
         half = items[number][2] * ROWS
         return pltpu.make_async_copy(
             left_refs[number].at[:, pl.ds(pl.multiple_of(side * half + chunk // 2 * TILE, TILE), TILE)],
-            left_buf.at[slot, which],
+            left_buf.at[slot, :, pl.ds(which * TILE, TILE)],
             left_sem.at[slot, which],
         )
 
@@ -901,13 +881,32 @@
         for_item(at, action)
 
     planned, each, maker = tasks(extra_in, extra_out, extra_scratch) if tasks is not None else ({}, None, None)
-    if 0 in planned:
-        planned.pop(0)()
     if made:
         maker.begin(left_buf, right_buf)
     load_left(0)
     if n_right > 1 and not made:
         right_copy(1).start()
+    if tasks is not None:
+        greet(n_ctx, True)
+    else:
+        barrier = pltpu.get_barrier_semaphore()
+        pl.semaphore_signal(barrier, inc=1, device_id=partner, device_id_type=pl.DeviceIdType.MESH)
+
+        @pl.when(chip > 0)
+        def _():
+            pl.semaphore_signal(
+                barrier, inc=1, device_id=((chip - 1) * 2 + core, rank), device_id_type=pl.DeviceIdType.MESH
+            )
+
+        @pl.when(chip < chips - 1)
+        def _():
+            pl.semaphore_signal(
+                barrier, inc=1, device_id=((chip + 1) * 2 + core, rank), device_id_type=pl.DeviceIdType.MESH
+            )
+
+        pl.semaphore_wait(barrier, 1 + jnp.where(chip > 0, 1, 0) + jnp.where(chip < chips - 1, 1, 0))
+    if 0 in planned:
+        planned.pop(0)()
     right_copy(0).wait()
 
     def step(i, carry):
@@ -1055,13 +1054,11 @@
                     for which in range(2):
                         left_copy(number, chunk, slot, which).wait()
                 right = right_buf.at[which_right % 2]
-                product = contract_rows(left_buf[slot, 1], right[...]).astype(BF)
+                product = contract_rows(left_buf[slot], right[...]).astype(BF)
                 for part in range(2):
                     place = lax.rem(i + part, 4)
-                    other_buf[place] = product[part * ROWS : (part + 1) * ROWS]
+                    other_buf[place] = product[TILE + part * ROWS : TILE + (part + 1) * ROWS]
                     to_core.send(other_buf.at[place], i + part, place, partner)
-                product = contract_rows(left_buf[slot, 0], right[...]).astype(BF)
-                for part in range(2):
                     ring[lax.rem(i + part, n_ring)] = product[part * ROWS : (part + 1) * ROWS]
 
             for_item(i, action)
@@ -1101,7 +1098,7 @@
         out_specs=[any_spec] * len(items) + out_specs,
         scratch_shapes=scratch
         + [
-            pltpu.VMEM((2, 2, tokens, TILE), BF),
+            pltpu.VMEM((2, tokens, 2 * TILE), BF),
             pltpu.VMEM((min(2, len(rights) + len(late)), tokens, width), BF),
             pltpu.VMEM((4,) + chunk, BF),
             pltpu.VMEM((n_ring,) + chunk, BF),
@@ -1201,7 +1198,7 @@
         slot = lax.rem(tile, 2)
         return [
             pltpu.make_async_copy(
-                self.left_buf.at[slot, which],
+                self.left_buf.at[slot, :, pl.ds(which * TILE, TILE)],
                 self.h_out.at[:, pl.ds(self.first(tile, which), TILE)],
                 self.h_sem.at[slot, which],
             )
@@ -1211,7 +1208,9 @@
     def grad_stores(self, tile):
         return [
             pltpu.make_async_copy(
-                self.stage.at[kind, which], out.at[:, pl.ds(self.first(tile, which), TILE)], self.grad_sem.at[kind, which]
+                self.stage.at[kind, :, pl.ds(which * TILE, TILE)],
+                out.at[:, pl.ds(self.first(tile, which), TILE)],
+                self.grad_sem.at[kind, which],
             )
             for kind, out in enumerate((self.dgp_out, self.dup_out))
             for which in range(2)
@@ -1248,11 +1247,9 @@
             up_pre = dot(low, self.weights[0, :, at_up]) + dot(high, self.weights[1, :, at_up])
             hidden_grad = times_transposed(self.right_buf[0, rows, :], self.downs[slot, 0])
             h, dgp, dup = feed_values(gate_pre, up_pre, hidden_grad)
-            for which in range(2):
-                part = slice(which * TILE, (which + 1) * TILE)
-                self.left_buf[slot, which, rows, :] = h[:, part]
-                self.stage[0, which, rows, :] = dgp[:, part]
-                self.stage[1, which, rows, :] = dup[:, part]
+            self.left_buf[slot, rows, :] = h
+            self.stage[0, rows, :] = dgp
+            self.stage[1, rows, :] = dup
             return carry
 
         lax.fori_loop(0, self.right_buf.shape[1] // count, rows_step, 0)
@@ -1431,7 +1428,7 @@
             dma((2, 2)),
             dma((2,)),
             pltpu.VMEM((rows, width), BF),
-            pltpu.VMEM((2, 2, tokens, TILE), BF),
+            pltpu.VMEM((2, tokens, 2 * TILE), BF),
             dma((2,)),
             dma,
             dma((2, 10)),
@@ -1540,6 +1537,32 @@
         ],
         functools.partial(input_tasks, n_ctx, groups),
     )
+
+
+def cast_kernel(out_in, gate_in, up_in, down_in, qkv_in, out_ref, gate_ref, up_ref, down_ref, *qkv_refs):
+    for source, dest in ((out_in, out_ref), (gate_in, gate_ref), (up_in, up_ref), (down_in, down_ref)):
+        dest[...] = source[...].astype(F32)
+    width = qkv_refs[0].shape[1]
+    for k, dest in enumerate(qkv_refs):
+        dest[...] = qkv_in[:, k * width : (k + 1) * width].astype(F32)
+
+
+def cast_sums(*sums):
+    steps = 16
+    block = lambda array: pl.BlockSpec((array.shape[0] // steps, array.shape[1]), lambda i: (i, 0))
+    outs = [jax.ShapeDtypeStruct(array.shape, F32) for array in sums[:-1]]
+    outs += [jax.ShapeDtypeStruct((sums[-1].shape[0], sums[-1].shape[1] // 3), F32)] * 3
+    return pl.pallas_call(
+        cast_kernel,
+        out_shape=outs,
+        grid=(steps,),
+        in_specs=[block(array) for array in sums],
+        out_specs=[block(array) for array in outs],
+        compiler_params=params(),
+        cost_estimate=pl.CostEstimate(
+            flops=0, bytes_accessed=sum(6 * array.shape[0] * array.shape[1] for array in sums), transcendentals=0
+        ),
+    )(*sums)
 
 
 class Exchange:
@@ -2322,7 +2345,7 @@
         )
         extra = input_extra(n_ctx, groups, i_partial, tokens[0], dr, gain_one[None], gain_two_grad)
         sum_qkv, input_grad, gain_sums = weight_sums(
-            [(all_n1, 0)], [dqkv], n_ctx, 2, extra, limit=36 * 1024 * 1024
+            [(all_n1, 0)], [dqkv], n_ctx, 2, extra
         )
         gains = gain_sums[::8]
     else:
@@ -2347,7 +2370,9 @@
         )
         back, gain_one_grad = norm_back_rows(x_own["a"], gain_one, scattered(scatter_first((state["i", "a"],))))
         input_grad = (dr + back).astype(BF)
-    grad_query, grad_key, grad_value = (part.astype(F32) for part in jnp.split(sum_qkv, 3, axis=1))
+    grad_out, grad_gate, grad_up, grad_down, grad_query, grad_key, grad_value = cast_sums(
+        sum_out, sum_gate, sum_up, sum_down, sum_qkv
+    )
     if not paired:
         gains = lax.psum(jnp.concatenate([gain_one_grad, gain_two_grad]), ("ctx", "tp"))
     return (
@@ -2357,11 +2382,11 @@
         grad_query,
         grad_key,
         grad_value,
-        sum_out.astype(F32),
+        grad_out,
         gains[1],
-        sum_gate.astype(F32),
-        sum_up.astype(F32),
-        sum_down.astype(F32),
+        grad_gate,
+        grad_up,
+        grad_down,
     )
 
 

time: 963 us -> 948 us (0.984)
  other arithmetic: 50.9 us -> 8.01 us
  Pallas kernels: 894 us -> 924 us
    convert_element_type x5 -> x0, other arithmetic: 42.9 us -> none  [the longest x1 11.7 us: body(): sum_down.astype(F32)]
    pallas_call x0 -> x1, Pallas kernels: none -> 35.3 us  [cast_sums(): pl.pallas_call(cast_kernel, out_shape=outs, grid=(steps,), in_specs=[bloc...]
where the time goes in v7:
time: 948 us; the launch traced here: 940 us
  Pallas kernels  924 us (97%)
    pallas_call x2, Pallas kernels, weight_sums(): pl.pallas_call(functools.partial(sums_kernel, n_ctx, shapes, len(rights),...  480 us
    pallas_call x1, Pallas kernels, forward_layer(): pl.pallas_call(functools.partial(forward_kernel, n_ctx, groups, units, mi...  255 us
    pallas_call x1, Pallas kernels, middle_layer(): pl.pallas_call(functools.partial(middle_kernel, n_ctx, groups, units, min...  154 us
    pallas_call x1, Pallas kernels, cast_sums(): pl.pallas_call(cast_kernel, out_shape=outs, grid=(steps,), in_specs=[bloc...  35.3 us

profile of v7, /device:TPU:1, one launch (start us, length us, event | category | flops | bytes accessed | tf_op | source)
XLA Modules:
  0.0 940.0 jit_solution(6641737153266840084)
XLA Ops:
  0.6 0.0 copy-start
  0.7 0.1 stack.54
  0.8 0.1 stack.59
  0.9 0.4 copy-done
  1.3 0.1 constant_dynamic-slice_fusion
  1.4 0.1 copy.24
  1.5 0.7 gather_fusion
  2.3 0.1 convert_bitcast_fusion
  2.3 1.3 broadcast_in_dim.38
  3.6 1.3 broadcast_in_dim.39
  4.9 0.1 multiply_sine_fusion.1
  5.0 0.7 pad_maximum_fusion.2
  5.7 0.3 multiply_sine_fusion
  6.0 0.8 pad_maximum_fusion
  6.8 1.1 broadcast_in_dim.35.refs_12_.refs_13_
  7.9 255.1 %shard_map.203 = (bf16[1536,2048]{1,0:T(8,128)(2,1)}, bf16[3,8,3,256,128]{4,3,2,1,0:T(8,128)(2,1)}, bf16[1536,512]{1,0:T(8,128)(2,1)}, f32[384,2048]{1,0:T(8,128...) custom-call(bf16[384,2048]{1,0:T(8,128)(2,1)} %bitcast.36, bf16[384,2048]{1,0:T(8,128)(2,1)} %bitcast.34, ...), custom_call_target="tpu_custom_call" | custom-call | flops 12884901888 | bytes 25165824 | tf_op jit(solution)/shard_map/pallas_call | solution.py:1841
  263.1 365.9 %shard_map.204 = (bf16[2048,2048]{1,0:T(8,128)(2,1)}, bf16[2048,2048]{1,0:T(8,128)(2,1)}, bf16[2048,2048]{1,0:T(8,128)(2,1)}, bf16[512,2048]{1,0:T(8,128)(2,1)},...) custom-call(bf16[1536,2048]{1,0:T(8,128)(2,1)} %get-tuple-element.38, ...), custom_call_target="tpu_custom_call" | custom-call | flops 41875931136 | bytes 47710208 | tf_op jit(solution)/shard_map/pallas_call | solution.py:1094
  629.0 153.7 %shard_map.205 = (bf16[1536,1536]{1,0:T(8,128)(2,1)}, bf16[1536,2048]{1,0:T(8,128)(2,1)}, bf16[384,2048]{1,0:T(8,128)(2,1)}) custom-call(bf16[1536,2048]{1,0:T(8,128)(2,1)} %get-tuple-element.42.refs_0_, bf16[3,8,3,256,128]{4,3,2,1,0:T(8,128)(2,1)} %get-tuple-element.43.refs_1_, bf16[1536,2048]{1,0:T(8,128)(2,1)} %get-tuple-element.44.refs_2_, ...), custom_call_target="tpu_custom_call" | custom-call | flops 25769803776 | bytes 25165824 | tf_op jit(solution)/shard_map/pallas_call | solution.py:2099
  782.7 0.0 copy-start.2
  782.7 114.1 %shard_map.206 = (bf16[2048,1536]{1,0:T(8,128)(2,1)}, bf16[384,2048]{1,0:T(8,128)(2,1)}, f32[16,2048]{1,0:T(8,128)}) custom-call(bf16[1536,2048]{1,0:T(8,128)(2,1)} %get-tuple-element.46.refs_0_, bf16[1536,1536]{1,0:T(8,128)(2,1)} %get-tuple-element.47.refs_1_, bf16[1536,2048]{1,0:T(8,128)(2,1)} %get-tuple-element.48.refs_2_, bf16[384,2048]{1,0:T(8,128)(2,1)} %bitcast.37, ...), custom_call_target="tpu_custom_call" | custom-call | flops 9663676416 | bytes 12582912 | tf_op jit(solution)/shard_map/pallas_call | solution.py:1094
  896.8 0.0 copy-start.3
  896.8 1.0 slice.27
  897.9 0.6 fusion.8
  898.5 1.1 slice.25
  899.6 0.0 copy-done.2
  899.6 1.3 slice.26
  900.9 0.0 copy-done.3
  900.9 1.7 fusion.1
  902.7 0.1 slice.24
  902.8 1.7 fusion
  904.5 35.3 %shard_map.207 = (f32[512,2048]{1,0:T(8,128)}, f32[2048,2048]{1,0:T(8,128)}, f32[2048,2048]{1,0:T(8,128)}, f32[2048,2048]{1,0:T(8,128)}, f32[2048,512]{1,0:T(8,1...) custom-call(bf16[512,2048]{1,0:T(8,128)(2,1)} %get-tuple-element.53.out_in, bf16[2048,2048]{1,0:T(8,128)(2,1)} %get-tuple-element.54.gate_in, ...), custom_call_target="tpu_custom_call" | custom-call | bytes 100663296 | tf_op jit(solution)/shard_map/pallas_call | solution.py:1555
  939.8 0.0 copy-done.1
  (6 shorter events, 0.1 us)
Async XLA Ops:
  0.6 0.7 copy-start
  782.7 116.9 %copy-start.2 = (bf16[384,2048]{1,0:T(8,128)(2,1)S(1)}, bf16[384,2048]{1,0:T(8,128)(2,1)}, u32[]{:S(2)}) copy-start(bf16[384,2048]{1,0:T(8,128)(2,1)} %get-tuple-element.45) | copy-start | bytes 4718596
  896.8 4.1 copy-start.3
  904.5 35.3 %copy-start.1 = (s32[8,6,2]{0,2,1:T(2,128)S(1)}, s32[8,6,2]{0,2,1:T(2,128)}, u32[]{:S(2)}) copy-start(s32[8,6,2]{0,2,1:T(2,128)} %param.13) | copy-start | bytes 1156

commit v8 on v7

--- a/solution.py
+++ b/solution.py
@@ -1377,7 +1377,7 @@
             scatter.start(g)
 
     def use(at, total):
-        back, more = norm_back_rows(residual[at, :], gain[...], total)
+        back, more = norm_back_rows(residual[at, :], gain[...].astype(F32), total)
         total_grad = grads[at, :].astype(F32) + back
         dr[at, :] = total_grad
         da_own[at, :] = total_grad.astype(BF)
@@ -1470,11 +1470,14 @@
             copy.start()
         for g in order:
             scatter.start(g)
+
+    def forward_first():
         for copy in own_copies(tokens_ref, rows_in, groups, own_sem):
             copy.wait()
+        scatter.forward(order[0])
 
     def use(at, total):
-        back, more = norm_back_rows(rows_in[at, :].astype(F32), gain[...], total)
+        back, more = norm_back_rows(rows_in[at, :].astype(F32), gain[...].astype(F32), total)
         input_grad[at, :] = (dr[at, :] + back).astype(BF)
         gains[0, 0:1, :] += more
 
@@ -1504,7 +1507,7 @@
 
     return {
         0: begin,
-        4: lambda: scatter.forward(order[0]),
+        4: forward_first,
         9: lambda: scatter.forward(order[-1]),
         10: lambda: scatter.total(order[0], use),
         13: rest,
@@ -1539,30 +1542,68 @@
     )
 
 
-def cast_kernel(out_in, gate_in, up_in, down_in, qkv_in, out_ref, gate_ref, up_ref, down_ref, *qkv_refs):
-    for source, dest in ((out_in, out_ref), (gate_in, gate_ref), (up_in, up_ref), (down_in, down_ref)):
+def cast_kernel(groups, *refs):
+    out_in, gate_in, up_in, down_in, qkv_in = refs[:5]
+    n_more = 3 if groups else 0
+    more_in, refs = refs[5 : 5 + n_more], refs[5 + n_more :]
+    for source, dest in zip((out_in, gate_in, up_in, down_in), refs[:4]):
         dest[...] = source[...].astype(F32)
-    width = qkv_refs[0].shape[1]
-    for k, dest in enumerate(qkv_refs):
+    width = refs[4].shape[1]
+    for k, dest in enumerate(refs[4:7]):
         dest[...] = qkv_in[:, k * width : (k + 1) * width].astype(F32)
-
-
-def cast_sums(*sums):
+    if not groups:
+        return
+    row_outs, gain_outs, sem = refs[7:9], refs[9:11], refs[11]
+    gains = more_in[2]
+    gain_outs[0][...] = gains[0:1, :]
+    gain_outs[1][...] = gains[8:9, :]
+    odd = lax.rem(lax.axis_index("tp"), 2)
+    starts = (pl.multiple_of(odd * BLOCK, BLOCK), pl.multiple_of((1 - odd) * PAIR, BLOCK))
+
+    def copies():
+        return [
+            pltpu.make_async_copy(source.at[pl.ds(own, rows)], dest.at[pl.ds(start, rows)], sem.at[k, g])
+            for k, (source, dest) in enumerate(zip(more_in[:2], row_outs))
+            for g, (start, (_, rows, own)) in enumerate(zip(starts, groups))
+        ]
+
+    @pl.when(pl.program_id(0) == 0)
+    def _():
+        for copy in copies():
+            copy.start()
+
+    @pl.when(pl.program_id(0) == pl.num_programs(0) - 1)
+    def _():
+        for copy in copies():
+            copy.wait()
+
+
+def cast_sums(sums, groups=(), rows=(), gains=None):
     steps = 16
     block = lambda array: pl.BlockSpec((array.shape[0] // steps, array.shape[1]), lambda i: (i, 0))
     outs = [jax.ShapeDtypeStruct(array.shape, F32) for array in sums[:-1]]
     outs += [jax.ShapeDtypeStruct((sums[-1].shape[0], sums[-1].shape[1] // 3), F32)] * 3
+    in_specs, out_specs, scratch = [block(array) for array in sums], [block(array) for array in outs], []
+    args = list(sums)
+    if groups:
+        args += list(rows) + [gains]
+        in_specs += [ANY_SPEC, ANY_SPEC, whole(gains.shape)]
+        outs += [jax.ShapeDtypeStruct(array.shape, array.dtype) for array in rows]
+        outs += [jax.ShapeDtypeStruct((1, gains.shape[1]), F32)] * 2
+        out_specs += [ANY_SPEC, ANY_SPEC] + [whole((1, gains.shape[1]))] * 2
+        scratch = [pltpu.SemaphoreType.DMA((2, len(groups)))]
     return pl.pallas_call(
-        cast_kernel,
+        functools.partial(cast_kernel, groups),
         out_shape=outs,
         grid=(steps,),
-        in_specs=[block(array) for array in sums],
-        out_specs=[block(array) for array in outs],
+        in_specs=in_specs,
+        out_specs=out_specs,
+        scratch_shapes=scratch,
         compiler_params=params(),
         cost_estimate=pl.CostEstimate(
             flops=0, bytes_accessed=sum(6 * array.shape[0] * array.shape[1] for array in sums), transcendentals=0
         ),
-    )(*sums)
+    )(*args)
 
 
 class Exchange:
@@ -1662,10 +1703,11 @@
 
 
 def forward_kernel(n_ctx, groups, units, tile, *refs):
-    tokens_ref, cot_ref, gain_one, gain_two, wq_ref, wk_ref, wv_ref, wo_ref, cos_ref, sin_ref, bcos_ref, bsin_ref, valid_ref = refs[:13]
+    tokens_ref, cot_ref, wq_in, wk_in, wv_in, wo_in, gain_one, gain_two = refs[:8]
+    cos_ref, sin_ref, bcos_ref, bsin_ref, valid_ref = refs[8:13]
     n1_out, got_out, heads_out, residual, n2_out, cot_out = refs[13:19]
     x_ref, rows_buf, own_buf, send, got, o_send, o_got, tabs, qs, ks, vs, os = refs[19:31]
-    rest = refs[31:]
+    (wq_ref, wk_ref, wv_ref, wo_ref, weight_sem), rest = refs[31:36], refs[36:]
     n_gather, n_exchange = len(Gather.scratch()), len(Exchange.scratch(1, 2))
     n1_sems, rest = rest[:n_gather], rest[n_gather:]
     n2_sems, rest = rest[:n_gather], rest[n_gather:]
@@ -1685,8 +1727,14 @@
             tokens_ref.at[pl.ds(own_at[g], rows)], x_ref.at[pl.ds(own, rows)], load_sem.at[g]
         )
 
+    load_weights = [
+        pltpu.make_async_copy(source, dest, weight_sem.at[k])
+        for k, (source, dest) in enumerate(((wq_in, wq_ref), (wk_in, wk_ref), (wv_in, wv_ref), (wo_in, wo_ref)))
+    ]
     for g in range(2):
         load_x(g).start()
+    for copy in load_weights:
+        copy.start()
     greet(n_ctx, True)
     gather_one = Gather(own_buf, rows_buf, groups, n1_sems, local=False)
     gather_two = Gather(own_buf, n2_out, groups, n2_sems)
@@ -1700,7 +1748,7 @@
 
     def normed(source, gain, at):
         values = source[at, :].astype(F32)
-        return (values * inverse_rms(values) * gain[...]).astype(BF)
+        return (values * inverse_rms(values) * gain[...].astype(F32)).astype(BF)
 
     def begin(g):
         base, rows, own = groups[g]
@@ -1740,6 +1788,8 @@
     store_n1 = pltpu.make_async_copy(rows_buf, n1_out, n1_sem)
     store_got = [pltpu.make_async_copy(got.at[u], got_out.at[u], got_sem.at[u]) for u in range(len(units))]
 
+    for copy in load_weights:
+        copy.wait()
     query(0, 0)
     gather_one.forward_x(0)
     gather_one.forward_y(0)
@@ -1841,7 +1891,7 @@
     return pl.pallas_call(
         functools.partial(forward_kernel, n_ctx, groups, units, min(512, length)),
         out_shape=outs,
-        in_specs=[ANY_SPEC, ANY_SPEC] + [VMEM_SPEC] * 11,
+        in_specs=[ANY_SPEC] * 6 + [VMEM_SPEC] * 7,
         out_specs=[ANY_SPEC, ANY_SPEC, VMEM_SPEC, VMEM_SPEC, ANY_SPEC, ANY_SPEC],
         scratch_shapes=[
             vmem((rows, depth)),
@@ -1854,6 +1904,8 @@
             vmem((2, PAIR, HD), F32),
         ]
         + [vmem((length, HD))] * 4
+        + [vmem(wq.shape)] * 3
+        + [vmem(wo.shape), pltpu.SemaphoreType.DMA((4,))]
         + Gather.scratch() * 3
         + Exchange.scratch(n_units, n_ctx) * 2
         + [pltpu.SemaphoreType.DMA, pltpu.SemaphoreType.DMA((n_units,)), pltpu.SemaphoreType.DMA((2,))]
@@ -1862,7 +1914,7 @@
         cost_estimate=pl.CostEstimate(
             flops=8 * tokens * depth * width, bytes_accessed=8 * tokens * depth, transcendentals=0
         ),
-    )(tokens_in, cot_in, gain_one, gain_two, wq, wk, wv, wo, *tables, valid)
+    )(tokens_in, cot_in, wq, wk, wv, wo, gain_one, gain_two, *tables, valid)
 
 
 def attend_rows_back(qs, ks, vs, gs, os, dqs, cos_ref, sin_ref, tile):
@@ -1912,12 +1964,17 @@
 
 
 def middle_kernel(n_ctx, groups, units, tile, *refs):
-    da_ref, got_ref, h_ref, residual_ref, wd_ref, wq_ref, wk_ref, wv_ref, wo_ref = refs[:9]
+    da_ref, got_ref, h_ref, residual_ref, wd_ref, wq_in, wk_in, wv_in, wo_in = refs[:9]
     cos_ref, sin_ref, bcos_ref, bsin_ref, valid_ref = refs[9:14]
     grad_ref, partial_out, output = refs[14:17]
     rows_buf, got, do_send, do_got, back_got, h_buf, wd_buf, res_buf, cos_full, sin_full = refs[17:27]
     qs, ks, vs, gs, os, dqs = refs[27:33]
-    rest = refs[33:]
+    (wq_ref, wk_ref, wv_ref, wo_ref, weight_sem), rest = refs[33:38], refs[38:]
+    load_weights = [
+        pltpu.make_async_copy(source, dest, weight_sem.at[k])
+        for k, (source, dest) in enumerate(((wo_in, wo_ref), (wq_in, wq_ref), (wk_in, wk_ref), (wv_in, wv_ref)))
+    ]
+    load_weights[0].start()
     back_send = got
     n_exchange = len(Exchange.scratch(1, 2))
     do_sems, back_sems, rest = rest[:n_exchange], rest[n_exchange : 2 * n_exchange], rest[2 * n_exchange :]
@@ -1941,11 +1998,14 @@
         load_got[u].start()
     first_wd = pltpu.make_async_copy(wd_ref.at[:, pl.ds(0, wd_buf.shape[1])], wd_buf, wd_sem)
     first_wd.start()
+    for copy in load_weights[1:]:
+        copy.start()
     greet(n_ctx, True)
     scatter = Scatter(rows_buf, groups, rest[:6], rest[6:], loaded=False)
     trade = Exchange(do_got, do_sems, True)
     trade_back = Exchange(back_got, back_sems, False)
 
+    load_weights[0].wait()
     for u in order:
         load_da[u].wait()
         base, flipped = units[u]
@@ -1964,6 +2024,8 @@
         cos_full[at, :], sin_full[at, :] = rotation(
             cos_ref[...], sin_ref[...], bcos_ref[block : block + 1, :], bsin_ref[block : block + 1, :]
         )
+    for copy in load_weights[1:]:
+        copy.wait()
     for u in order:
         load_got[u].wait()
 
@@ -2103,13 +2165,15 @@
             jax.ShapeDtypeStruct((tokens, depth), BF),
             jax.ShapeDtypeStruct(residual.shape, BF),
         ],
-        in_specs=[ANY_SPEC] * 5 + [VMEM_SPEC] * 9,
+        in_specs=[ANY_SPEC] * 9 + [VMEM_SPEC] * 5,
         out_specs=[VMEM_SPEC, ANY_SPEC, ANY_SPEC],
         scratch_shapes=[vmem((tokens, depth)), vmem(three), vmem(one), vmem(one), vmem(three)]
         + [vmem((2, PAIR, depth)), vmem((h.shape[1], depth // 2)), vmem((most_rows, depth), F32)]
         + [vmem((length, HD), F32)] * 2
         + [vmem((length, HD))] * 4
         + [vmem((3, length, HD)), vmem((length, HD), F32)]
+        + [vmem(wq.shape)] * 3
+        + [vmem(wo.shape), dma((4,))]
         + Exchange.scratch(count, n_ctx) * 2
         + [dma((count,)), dma((count,)), dma((2,)), dma((2,)), dma, dma, dma]
         + Scatter.scratch(residual.shape[0], depth, loaded=False),
@@ -2199,9 +2263,6 @@
             "a": lax.dynamic_slice_in_dim(array, odd * BLOCK, PAIR, 0),
         }
 
-    def whole_rows(array):
-        return jnp.where(odd == 1, jnp.roll(array, BLOCK, axis=0), array) if paired else array
-
     x_own = {name: rows.astype(F32) for name, rows in own_rows(tokens[0]).items()}
     g_own = own_rows(cotangent[0])
 
@@ -2316,7 +2377,7 @@
         spans = [at.astype(F32)[:, None] * inverse[None, :] for at in (offsets, starts)]
         turns = [twice(part(angle)) for angle in spans for part in (jnp.cos, jnp.sin)]
         all_n1, got, heads_out, own_residual, all_n2, all_cot = forward_layer(
-            tokens[0], cotangent[0], gain_one[None], gain_two[None], w_query, w_key, w_value, w_output,
+            tokens[0], cotangent[0], norm_gain[None], mlp_gain[None], w_query, w_key, w_value, w_output,
             turns, wide_valid, n_ctx, groups, units,
         )
     else:
@@ -2335,7 +2396,7 @@
         all_n1, all_n2, all_cot = state["n1", "a"], gathered(state["n2", "a"]), gathered(state["cot", "a"])
         heads_out, own_residual = state["heads", "a"], state["residual", "a"]
     if paired:
-        extra = feed_extra(groups, all_n2, w_gate, w_up, w_down, own_residual, cotangent[0], gain_two[None])
+        extra = feed_extra(groups, all_n2, w_gate, w_up, w_down, own_residual, cotangent[0], mlp_gain[None])
         sum_down, sum_gate, sum_up, sum_out, dr, da, gain_two_grad, _, h, _, _ = weight_sums(
             [(w_down.shape[0], 0), (all_n2, 1), (all_n2, 2), (heads_out, 3)],
             [all_cot], n_ctx, 1, extra, late=(5, 6, 1), limit=62 * 1024 * 1024,
@@ -2343,11 +2404,10 @@
         dqkv, i_partial, output = middle_layer(
             da, got, h, own_residual, w_query, w_key, w_value, w_output, w_down, turns, wide_valid, n_ctx, groups, units
         )
-        extra = input_extra(n_ctx, groups, i_partial, tokens[0], dr, gain_one[None], gain_two_grad)
+        extra = input_extra(n_ctx, groups, i_partial, tokens[0], dr, norm_gain[None], gain_two_grad)
         sum_qkv, input_grad, gain_sums = weight_sums(
             [(all_n1, 0)], [dqkv], n_ctx, 2, extra
         )
-        gains = gain_sums[::8]
     else:
         own_grads = cotangent[0]
         h, dgp, dup = mlp_core(all_n2, all_cot, w_gate, w_up, w_down, total_rows, 0)
@@ -2370,14 +2430,17 @@
         )
         back, gain_one_grad = norm_back_rows(x_own["a"], gain_one, scattered(scatter_first((state["i", "a"],))))
         input_grad = (dr + back).astype(BF)
-    grad_out, grad_gate, grad_up, grad_down, grad_query, grad_key, grad_value = cast_sums(
-        sum_out, sum_gate, sum_up, sum_down, sum_qkv
-    )
-    if not paired:
+    sums = (sum_out, sum_gate, sum_up, sum_down, sum_qkv)
+    if paired:
+        *grads, output, input_grad, grad_norm_gain, grad_mlp_gain = cast_sums(sums, groups, (output, input_grad), gain_sums)
+        gains = grad_norm_gain[0], grad_mlp_gain[0]
+    else:
+        grads = cast_sums(sums)
         gains = lax.psum(jnp.concatenate([gain_one_grad, gain_two_grad]), ("ctx", "tp"))
+    grad_out, grad_gate, grad_up, grad_down, grad_query, grad_key, grad_value = grads
     return (
-        whole_rows(output)[None],
-        whole_rows(input_grad)[None],
+        output[None],
+        input_grad[None],
         gains[0],
         grad_query,
         grad_key,

time: 948 us -> 1000 us (1.055)
  Pallas kernels: 924 us -> 983 us
    pallas_call x1, Pallas kernels: 35.3 us -> 101 us  [cast_sums(): pl.pallas_call(functools.partial(cast_kernel, groups), out_shape=outs, gr...]
where the time goes in v8:
time: 1000 us; the launch traced here: 992 us
  Pallas kernels  983 us (98%)
    pallas_call x2, Pallas kernels, weight_sums(): pl.pallas_call(functools.partial(sums_kernel, n_ctx, shapes, len(rights),...  479 us
    pallas_call x1, Pallas kernels, forward_layer(): pl.pallas_call(functools.partial(forward_kernel, n_ctx, groups, units, mi...  253 us
    pallas_call x1, Pallas kernels, middle_layer(): pl.pallas_call(functools.partial(middle_kernel, n_ctx, groups, units, min...  151 us
    pallas_call x1, Pallas kernels, cast_sums(): pl.pallas_call(functools.partial(cast_kernel, groups), out_shape=outs, gr...  101 us

profile of v8, /device:TPU:1, one launch (start us, length us, event | category | flops | bytes accessed | tf_op | source)
XLA Modules:
  0.0 991.6 jit_solution(17652286902629538378)
XLA Ops:
  0.6 0.0 copy-start
  0.7 0.1 stack.54
  0.8 0.1 stack.59
  1.0 0.4 copy-done
  1.3 0.1 constant_dynamic-slice_fusion
  1.4 0.1 copy.24
  1.5 0.7 gather_fusion
  2.3 0.1 convert_bitcast_fusion
  2.3 1.3 broadcast_in_dim.10.refs_6_.refs_5_
  3.6 1.3 broadcast_in_dim.11.refs_7_.refs_10_
  4.9 0.1 multiply_sine_fusion.1
  5.0 0.7 pad_maximum_fusion.2
  5.7 0.3 multiply_sine_fusion
  6.0 0.8 pad_maximum_fusion
  6.8 1.1 broadcast_in_dim.12.refs_12_.refs_13_
  7.9 252.8 %shard_map.203 = (bf16[1536,2048]{1,0:T(8,128)(2,1)}, bf16[3,8,3,256,128]{4,3,2,1,0:T(8,128)(2,1)}, bf16[1536,512]{1,0:T(8,128)(2,1)}, f32[384,2048]{1,0:T(8,128...) custom-call(bf16[384,2048]{1,0:T(8,128)(2,1)} %bitcast.26, bf16[384,2048]{1,0:T(8,128)(2,1)} %bitcast.24, ...), custom_call_target="tpu_custom_call" | custom-call | flops 12884901888 | bytes 25165824 | tf_op jit(solution)/shard_map/pallas_call | solution.py:1891
  260.7 365.9 %shard_map.204 = (bf16[2048,2048]{1,0:T(8,128)(2,1)}, bf16[2048,2048]{1,0:T(8,128)(2,1)}, bf16[2048,2048]{1,0:T(8,128)(2,1)}, bf16[512,2048]{1,0:T(8,128)(2,1)},...) custom-call(bf16[1536,2048]{1,0:T(8,128)(2,1)} %get-tuple-element.42, ...), custom_call_target="tpu_custom_call" | custom-call | flops 41875931136 | bytes 47710208 | tf_op jit(solution)/shard_map/pallas_call | solution.py:1094
  626.6 151.3 %shard_map.205 = (bf16[1536,1536]{1,0:T(8,128)(2,1)}, bf16[1536,2048]{1,0:T(8,128)(2,1)}, bf16[384,2048]{1,0:T(8,128)(2,1)}) custom-call(bf16[1536,2048]{1,0:T(8,128)(2,1)} %get-tuple-element.51.refs_0_, bf16[3,8,3,256,128]{4,3,2,1,0:T(8,128)(2,1)} %get-tuple-element.52.refs_1_, bf16[1536,2048]{1,0:T(8,128)(2,1)} %get-tuple-element.53.refs_2_, ...), custom_call_target="tpu_custom_call" | custom-call | flops 25769803776 | bytes 25165824 | tf_op jit(solution)/shard_map/pallas_call | solution.py:2161
  778.0 112.8 %shard_map.206 = (bf16[2048,1536]{1,0:T(8,128)(2,1)}, bf16[384,2048]{1,0:T(8,128)(2,1)}, f32[16,2048]{1,0:T(8,128)}) custom-call(bf16[1536,2048]{1,0:T(8,128)(2,1)} %get-tuple-element.50.refs_0_, bf16[1536,1536]{1,0:T(8,128)(2,1)} %get-tuple-element.54.refs_1_, bf16[1536,2048]{1,0:T(8,128)(2,1)} %get-tuple-element.55.refs_2_, bf16[384,2048]{1,0:T(8,128)(2,1)} %bitcast.27, ...), custom_call_target="tpu_custom_call" | custom-call | flops 9663676416 | bytes 12582912 | tf_op jit(solution)/shard_map/pallas_call | solution.py:1094
  890.8 0.0 copy-start.1
  890.8 100.6 %shard_map.207 = (f32[512,2048]{1,0:T(8,128)}, f32[2048,2048]{1,0:T(8,128)}, f32[2048,2048]{1,0:T(8,128)}, f32[2048,2048]{1,0:T(8,128)}, f32[2048,512]{1,0:T(8,1...) custom-call(bf16[512,2048]{1,0:T(8,128)(2,1)} %get-tuple-element.46., ...), custom_call_target="tpu_custom_call" | custom-call | bytes 100663296 | tf_op jit(solution)/shard_map/pallas_call | solution.py:1595
  991.4 0.0 copy-done.1
  (4 shorter events, 0.0 us)
Async XLA Ops:
  0.6 0.7 copy-start
  890.8 100.7 %copy-start.1 = (s32[8,6,2]{0,2,1:T(2,128)S(1)}, s32[8,6,2]{0,2,1:T(2,128)}, u32[]{:S(2)}) copy-start(s32[8,6,2]{0,2,1:T(2,128)} %param.13) | copy-start | bytes 1156

commit v9 on v8

--- a/solution.py
+++ b/solution.py
@@ -690,20 +690,19 @@
 
 
 class Gather:
-    def __init__(self, own, out, groups, sems, own_at=None, local=True):
-        self.own, self.out, self.groups, self.has_local = own, out, groups, local
-        self.own_at = own_at if own_at is not None else [group[2] for group in groups]
-        self.first_send, self.first_recv, self.second_send, self.second_recv, self.local_sem = sems
+    def __init__(self, own, out, groups, sems, local=True, via=None):
+        self.own, self.out, self.groups, self.has_local, self.via = own, out, groups, local, via
+        self.first_send, self.first_recv, self.second_send, self.second_recv, self.local_sem, self.via_sem = sems
         self.to_x, self.to_y = neighbours()
 
     @staticmethod
     def scratch():
         dma = pltpu.SemaphoreType.DMA
-        return [dma((4,)), dma((4,)), dma((4,)), dma((4,)), dma((2,))]
+        return [dma((4,)), dma((4,)), dma((4,)), dma((4,)), dma((2,)), dma((4,))]
 
     def first_copies(self, g):
-        base, rows, _ = self.groups[g]
-        source = self.own.at[pl.ds(self.own_at[g], rows)]
+        base, rows, own = self.groups[g]
+        source = self.own.at[pl.ds(own, rows)]
         place = lambda k: self.out.at[pl.ds(base + k * rows, rows)]
         return [
             remote(source, place(1), self.first_send.at[2 * g], self.first_recv.at[2 * g], self.to_x),
@@ -711,17 +710,34 @@
         ]
 
     def local(self, g):
-        base, rows, _ = self.groups[g]
-        return pltpu.make_async_copy(self.own.at[pl.ds(self.own_at[g], rows)], self.out.at[pl.ds(base, rows)], self.local_sem.at[g])
+        base, rows, own = self.groups[g]
+        return pltpu.make_async_copy(self.own.at[pl.ds(own, rows)], self.out.at[pl.ds(base, rows)], self.local_sem.at[g])
 
     def second_copies(self, g):
-        base, rows, _ = self.groups[g]
+        base, rows, own = self.groups[g]
         half = rows // 2
         part = lambda number: self.out.at[pl.ds(base + number * half, half)]
+        if self.via is None:
+            low, high = part(4), part(3)
+        else:
+            low, high = (self.via.at[pl.ds(own + k * half, half)] for k in range(2))
         return [
-            remote(part(4), part(6), self.second_send.at[2 * g], self.second_recv.at[2 * g], self.to_x),
-            remote(part(3), part(7), self.second_send.at[2 * g + 1], self.second_recv.at[2 * g + 1], self.to_y),
+            remote(low, part(6), self.second_send.at[2 * g], self.second_recv.at[2 * g], self.to_x),
+            remote(high, part(7), self.second_send.at[2 * g + 1], self.second_recv.at[2 * g + 1], self.to_y),
         ]
+
+    def pass_on(self, g, which):
+        if self.via is not None:
+            base, rows, own = self.groups[g]
+            half = rows // 2
+            load = pltpu.make_async_copy(
+                self.out.at[pl.ds(base + (4 - which) * half, half)],
+                self.via.at[pl.ds(own + which * half, half)],
+                self.via_sem.at[2 * g + which],
+            )
+            load.start()
+            load.wait()
+        self.second_copies(g)[which].start()
 
     def start(self, g):
         for copy in self.first_copies(g):
@@ -731,11 +747,11 @@
 
     def forward_x(self, g):
         self.first_copies(g)[0].wait_recv()
-        self.second_copies(g)[1].start()
+        self.pass_on(g, 1)
 
     def forward_y(self, g):
         self.first_copies(g)[1].wait_recv()
-        self.second_copies(g)[0].start()
+        self.pass_on(g, 0)
 
     def forward(self, g):
         self.forward_x(g)
@@ -1284,7 +1300,7 @@
     grads, stage, own_sem, n2_sem, make_sem, h_sem, grad_sem = rest[6:13]
     da_own = bufs[0]
     scatter = Scatter(d_ref, groups, bufs[:9], bufs[9:])
-    gather = Gather(da_own, da_all, groups, rest[13:])
+    gather = Gather(da_own, da_all, groups, rest[13:], via=bufs[1])
     maker = Maker(
         (n2_ref, wg_ref, wu_ref, wd_ref),
         (h_ref, dgp_ref, dup_ref),
@@ -1553,29 +1569,18 @@
         dest[...] = qkv_in[:, k * width : (k + 1) * width].astype(F32)
     if not groups:
         return
-    row_outs, gain_outs, sem = refs[7:9], refs[9:11], refs[11]
+    row_outs, gain_outs = refs[7:9], refs[9:11]
     gains = more_in[2]
-    gain_outs[0][...] = gains[0:1, :]
-    gain_outs[1][...] = gains[8:9, :]
     odd = lax.rem(lax.axis_index("tp"), 2)
     starts = (pl.multiple_of(odd * BLOCK, BLOCK), pl.multiple_of((1 - odd) * PAIR, BLOCK))
 
-    def copies():
-        return [
-            pltpu.make_async_copy(source.at[pl.ds(own, rows)], dest.at[pl.ds(start, rows)], sem.at[k, g])
-            for k, (source, dest) in enumerate(zip(more_in[:2], row_outs))
-            for g, (start, (_, rows, own)) in enumerate(zip(starts, groups))
-        ]
-
     @pl.when(pl.program_id(0) == 0)
     def _():
-        for copy in copies():
-            copy.start()
-
-    @pl.when(pl.program_id(0) == pl.num_programs(0) - 1)
-    def _():
-        for copy in copies():
-            copy.wait()
+        gain_outs[0][...] = gains[0:1, :]
+        gain_outs[1][...] = gains[8:9, :]
+        for source, dest in zip(more_in[:2], row_outs):
+            for start, (_, rows, own) in zip(starts, groups):
+                dest[pl.ds(start, rows), :] = source[pl.ds(own, rows), :]
 
 
 def cast_sums(sums, groups=(), rows=(), gains=None):
@@ -1583,22 +1588,20 @@
     block = lambda array: pl.BlockSpec((array.shape[0] // steps, array.shape[1]), lambda i: (i, 0))
     outs = [jax.ShapeDtypeStruct(array.shape, F32) for array in sums[:-1]]
     outs += [jax.ShapeDtypeStruct((sums[-1].shape[0], sums[-1].shape[1] // 3), F32)] * 3
-    in_specs, out_specs, scratch = [block(array) for array in sums], [block(array) for array in outs], []
+    in_specs, out_specs = [block(array) for array in sums], [block(array) for array in outs]
     args = list(sums)
     if groups:
         args += list(rows) + [gains]
-        in_specs += [ANY_SPEC, ANY_SPEC, whole(gains.shape)]
+        in_specs += [whole(array.shape) for array in (*rows, gains)]
         outs += [jax.ShapeDtypeStruct(array.shape, array.dtype) for array in rows]
         outs += [jax.ShapeDtypeStruct((1, gains.shape[1]), F32)] * 2
-        out_specs += [ANY_SPEC, ANY_SPEC] + [whole((1, gains.shape[1]))] * 2
-        scratch = [pltpu.SemaphoreType.DMA((2, len(groups)))]
+        out_specs += [whole(array.shape) for array in rows] + [whole((1, gains.shape[1]))] * 2
     return pl.pallas_call(
         functools.partial(cast_kernel, groups),
         out_shape=outs,
         grid=(steps,),
         in_specs=in_specs,
         out_specs=out_specs,
-        scratch_shapes=scratch,
         compiler_params=params(),
         cost_estimate=pl.CostEstimate(
             flops=0, bytes_accessed=sum(6 * array.shape[0] * array.shape[1] for array in sums), transcendentals=0
@@ -1707,7 +1710,7 @@
     cos_ref, sin_ref, bcos_ref, bsin_ref, valid_ref = refs[8:13]
     n1_out, got_out, heads_out, residual, n2_out, cot_out = refs[13:19]
     x_ref, rows_buf, own_buf, send, got, o_send, o_got, tabs, qs, ks, vs, os = refs[19:31]
-    (wq_ref, wk_ref, wv_ref, wo_ref, weight_sem), rest = refs[31:36], refs[36:]
+    (wq_ref, wk_ref, wv_ref, wo_ref, weight_sem, cot_buf, cot_via, cot_sem), rest = refs[31:39], refs[39:]
     n_gather, n_exchange = len(Gather.scratch()), len(Exchange.scratch(1, 2))
     n1_sems, rest = rest[:n_gather], rest[n_gather:]
     n2_sems, rest = rest[:n_gather], rest[n_gather:]
@@ -1733,13 +1736,13 @@
     ]
     for g in range(2):
         load_x(g).start()
-    for copy in load_weights:
+    for copy in load_weights + own_copies(cot_ref, cot_buf, groups, cot_sem):
         copy.start()
     greet(n_ctx, True)
     gather_one = Gather(own_buf, rows_buf, groups, n1_sems, local=False)
-    gather_two = Gather(own_buf, n2_out, groups, n2_sems)
-    gather_cot = Gather(cot_ref, cot_out, groups, cot_sems, own_at=own_at)
     scatter = Scatter(rows_buf, groups, rest[:6], rest[6:], loaded=False)
+    gather_two = Gather(own_buf, n2_out, groups, n2_sems, via=scatter.from_y)
+    gather_cot = Gather(cot_buf, cot_out, groups, cot_sems, via=cot_via)
     trade = Exchange(got, x_sems, True)
     trade_back = Exchange(o_got, o_sems, False)
 
@@ -1800,6 +1803,8 @@
     query(1, 1)
     gather_one.forward(1)
     gather_one.finish(1)
+    for copy in own_copies(cot_ref, cot_buf, groups, cot_sem):
+        copy.wait()
     for g in range(2):
         gather_cot.start(g)
     query(2, 0)
@@ -1906,6 +1911,7 @@
         + [vmem((length, HD))] * 4
         + [vmem(wq.shape)] * 3
         + [vmem(wo.shape), pltpu.SemaphoreType.DMA((4,))]
+        + [vmem((rows, depth)), vmem((rows, depth)), pltpu.SemaphoreType.DMA((2,))]
         + Gather.scratch() * 3
         + Exchange.scratch(n_units, n_ctx) * 2
         + [pltpu.SemaphoreType.DMA, pltpu.SemaphoreType.DMA((n_units,)), pltpu.SemaphoreType.DMA((2,))]

time: 1000 us -> 939 us (0.939)
  Pallas kernels: 983 us -> 922 us
    pallas_call x1, Pallas kernels: 101 us -> 38 us  [cast_sums(): pl.pallas_call(functools.partial(cast_kernel, groups), out_shape=outs, gr...]
where the time goes in v9:
time: 939 us; the launch traced here: 930 us
  Pallas kernels  922 us (98%)
    pallas_call x2, Pallas kernels, weight_sums(): pl.pallas_call(functools.partial(sums_kernel, n_ctx, shapes, len(rights),...  481 us
    pallas_call x1, Pallas kernels, forward_layer(): pl.pallas_call(functools.partial(forward_kernel, n_ctx, groups, units, mi...  252 us
    pallas_call x1, Pallas kernels, middle_layer(): pl.pallas_call(functools.partial(middle_kernel, n_ctx, groups, units, min...  151 us
    pallas_call x1, Pallas kernels, cast_sums(): pl.pallas_call(functools.partial(cast_kernel, groups), out_shape=outs, gr...  38 us

profile of v9, /device:TPU:1, one launch (start us, length us, event | category | flops | bytes accessed | tf_op | source)
XLA Modules:
  0.0 930.4 jit_solution(6361583551318051433)
XLA Ops:
  0.6 0.0 copy-start
  0.7 0.1 stack.54
  0.8 0.1 stack.59
  1.0 0.4 copy-done
  1.3 0.1 constant_dynamic-slice_fusion
  1.4 0.1 copy.24
  1.5 0.7 gather_fusion
  2.3 0.1 convert_bitcast_fusion
  2.3 1.3 broadcast_in_dim.10.refs_6_.refs_5_
  3.6 1.3 broadcast_in_dim.11.refs_7_.refs_10_
  4.9 0.1 multiply_sine_fusion.1
  5.0 0.7 pad_maximum_fusion.2
  5.7 0.3 multiply_sine_fusion
  6.0 0.8 pad_maximum_fusion
  6.8 1.1 broadcast_in_dim.12.refs_12_.refs_13_
  7.9 251.9 %shard_map.203 = (bf16[1536,2048]{1,0:T(8,128)(2,1)}, bf16[3,8,3,256,128]{4,3,2,1,0:T(8,128)(2,1)}, bf16[1536,512]{1,0:T(8,128)(2,1)}, f32[384,2048]{1,0:T(8,128...) custom-call(bf16[384,2048]{1,0:T(8,128)(2,1)} %bitcast.26, bf16[384,2048]{1,0:T(8,128)(2,1)} %bitcast.24, ...), custom_call_target="tpu_custom_call" | custom-call | flops 12884901888 | bytes 25165824 | tf_op jit(solution)/shard_map/pallas_call | solution.py:1896
  259.9 368.1 %shard_map.204 = (bf16[2048,2048]{1,0:T(8,128)(2,1)}, bf16[2048,2048]{1,0:T(8,128)(2,1)}, bf16[2048,2048]{1,0:T(8,128)(2,1)}, bf16[512,2048]{1,0:T(8,128)(2,1)},...) custom-call(bf16[1536,2048]{1,0:T(8,128)(2,1)} %get-tuple-element.42, ...), custom_call_target="tpu_custom_call" | custom-call | flops 41875931136 | bytes 47710208 | tf_op jit(solution)/shard_map/pallas_call | solution.py:1110
  628.0 151.3 %shard_map.205 = (bf16[1536,1536]{1,0:T(8,128)(2,1)}, bf16[1536,2048]{1,0:T(8,128)(2,1)}, bf16[384,2048]{1,0:T(8,128)(2,1)}) custom-call(bf16[1536,2048]{1,0:T(8,128)(2,1)} %get-tuple-element.51.refs_0_, bf16[3,8,3,256,128]{4,3,2,1,0:T(8,128)(2,1)} %get-tuple-element.52.refs_1_, bf16[1536,2048]{1,0:T(8,128)(2,1)} %get-tuple-element.53.refs_2_, ...), custom_call_target="tpu_custom_call" | custom-call | flops 25769803776 | bytes 25165824 | tf_op jit(solution)/shard_map/pallas_call | solution.py:2167
  779.3 112.8 %shard_map.206 = (bf16[2048,1536]{1,0:T(8,128)(2,1)}, bf16[384,2048]{1,0:T(8,128)(2,1)}, f32[16,2048]{1,0:T(8,128)}) custom-call(bf16[1536,2048]{1,0:T(8,128)(2,1)} %get-tuple-element.50.refs_0_, bf16[1536,1536]{1,0:T(8,128)(2,1)} %get-tuple-element.54.refs_1_, bf16[1536,2048]{1,0:T(8,128)(2,1)} %get-tuple-element.55.refs_2_, bf16[384,2048]{1,0:T(8,128)(2,1)} %bitcast.27, ...), custom_call_target="tpu_custom_call" | custom-call | flops 9663676416 | bytes 12582912 | tf_op jit(solution)/shard_map/pallas_call | solution.py:1110
  892.1 0.0 copy-start.1
  892.1 38.0 %shard_map.207 = (f32[512,2048]{1,0:T(8,128)}, f32[2048,2048]{1,0:T(8,128)}, f32[2048,2048]{1,0:T(8,128)}, f32[2048,2048]{1,0:T(8,128)}, f32[2048,512]{1,0:T(8,1...) custom-call(bf16[512,2048]{1,0:T(8,128)(2,1)} %get-tuple-element.46., ...), custom_call_target="tpu_custom_call" | custom-call | bytes 100663296 | tf_op jit(solution)/shard_map/pallas_call | solution.py:1599
  930.1 0.0 copy-done.1
  (4 shorter events, 0.0 us)
Async XLA Ops:
  0.6 0.7 copy-start
  892.1 38.0 %copy-start.1 = (s32[8,6,2]{0,2,1:T(2,128)S(1)}, s32[8,6,2]{0,2,1:T(2,128)}, u32[]{:S(2)}) copy-start(s32[8,6,2]{0,2,1:T(2,128)} %param.13) | copy-start | bytes 1156

commit v10 on v9

--- a/solution.py
+++ b/solution.py
@@ -844,10 +844,10 @@
     before = ((chip - toward) * 2 + core, rank)
     is_first = place == 0
     is_last = place == mid - 1
-    lag_t = mid
+    lag_t = mid + 1
     lag_u = lag_t + 2
     lag_o = lag_u + 2 * (mid - 1)
-    lag_f = lag_o + 1
+    lag_f = lag_o + 2
     lag_w = lag_f + 1
 
     to_core = Ring(core_in, core_send, core_recv, core_credit, total)
@@ -1101,7 +1101,7 @@
         (k, right, columns[k] // 2 // ROWS, isinstance(left, int)) for k, (left, right) in enumerate(items)
     ]
     mid = n_ctx // 4
-    n_ring = mid + 2 + 2 * (mid - 1) + 4
+    n_ring = mid + 3 + 2 * (mid - 1) + 5
     any_spec = pl.BlockSpec(memory_space=pl.ANY)
     args, arg_specs, outs, out_specs, scratch, tasks = extra if extra is not None else ([], [], [], [], [], None)
     counts = (len(args), len(outs), len(scratch))
@@ -1584,7 +1584,7 @@
 
 
 def cast_sums(sums, groups=(), rows=(), gains=None):
-    steps = 16
+    steps = 8
     block = lambda array: pl.BlockSpec((array.shape[0] // steps, array.shape[1]), lambda i: (i, 0))
     outs = [jax.ShapeDtypeStruct(array.shape, F32) for array in sums[:-1]]
     outs += [jax.ShapeDtypeStruct((sums[-1].shape[0], sums[-1].shape[1] // 3), F32)] * 3

time: 939 us -> 930 us (level)
  no operation moved by 1% of the time
where the time goes in v10:
time: 930 us; the launch traced here: 921 us
  Pallas kernels  913 us (98%)
    pallas_call x2, Pallas kernels, weight_sums(): pl.pallas_call(functools.partial(sums_kernel, n_ctx, shapes, len(rights),...  475 us
    pallas_call x1, Pallas kernels, forward_layer(): pl.pallas_call(functools.partial(forward_kernel, n_ctx, groups, units, mi...  252 us
    pallas_call x1, Pallas kernels, middle_layer(): pl.pallas_call(functools.partial(middle_kernel, n_ctx, groups, units, min...  151 us
    pallas_call x1, Pallas kernels, cast_sums(): pl.pallas_call(functools.partial(cast_kernel, groups), out_shape=outs, gr...  35.4 us

profile of v10, /device:TPU:1, one launch (start us, length us, event | category | flops | bytes accessed | tf_op | source)
XLA Modules:
  0.0 921.3 jit_solution(14678303490915825865)
XLA Ops:
  0.6 0.0 copy-start
  0.7 0.1 stack.54
  0.8 0.1 stack.59
  1.0 0.4 copy-done
  1.3 0.1 constant_dynamic-slice_fusion
  1.4 0.1 copy.24
  1.5 0.7 gather_fusion
  2.3 0.1 convert_bitcast_fusion
  2.3 1.3 broadcast_in_dim.10.refs_6_.refs_5_
  3.6 1.3 broadcast_in_dim.11.refs_7_.refs_10_
  4.9 0.1 multiply_sine_fusion.1
  5.0 0.7 pad_maximum_fusion.2
  5.7 0.3 multiply_sine_fusion
  6.0 0.8 pad_maximum_fusion
  6.8 1.1 broadcast_in_dim.12.refs_12_.refs_13_
  7.9 251.9 %shard_map.203 = (bf16[1536,2048]{1,0:T(8,128)(2,1)}, bf16[3,8,3,256,128]{4,3,2,1,0:T(8,128)(2,1)}, bf16[1536,512]{1,0:T(8,128)(2,1)}, f32[384,2048]{1,0:T(8,128...) custom-call(bf16[384,2048]{1,0:T(8,128)(2,1)} %bitcast.26, bf16[384,2048]{1,0:T(8,128)(2,1)} %bitcast.24, ...), custom_call_target="tpu_custom_call" | custom-call | flops 12884901888 | bytes 25165824 | tf_op jit(solution)/shard_map/pallas_call | solution.py:1896
  259.9 358.2 %shard_map.204 = (bf16[2048,2048]{1,0:T(8,128)(2,1)}, bf16[2048,2048]{1,0:T(8,128)(2,1)}, bf16[2048,2048]{1,0:T(8,128)(2,1)}, bf16[512,2048]{1,0:T(8,128)(2,1)},...) custom-call(bf16[1536,2048]{1,0:T(8,128)(2,1)} %get-tuple-element.42, ...), custom_call_target="tpu_custom_call" | custom-call | flops 41875931136 | bytes 47710208 | tf_op jit(solution)/shard_map/pallas_call | solution.py:1110
  618.1 150.8 %shard_map.205 = (bf16[1536,1536]{1,0:T(8,128)(2,1)}, bf16[1536,2048]{1,0:T(8,128)(2,1)}, bf16[384,2048]{1,0:T(8,128)(2,1)}) custom-call(bf16[1536,2048]{1,0:T(8,128)(2,1)} %get-tuple-element.51.refs_0_, bf16[3,8,3,256,128]{4,3,2,1,0:T(8,128)(2,1)} %get-tuple-element.52.refs_1_, bf16[1536,2048]{1,0:T(8,128)(2,1)} %get-tuple-element.53.refs_2_, ...), custom_call_target="tpu_custom_call" | custom-call | flops 25769803776 | bytes 25165824 | tf_op jit(solution)/shard_map/pallas_call | solution.py:2167
  768.9 116.8 %shard_map.206 = (bf16[2048,1536]{1,0:T(8,128)(2,1)}, bf16[384,2048]{1,0:T(8,128)(2,1)}, f32[16,2048]{1,0:T(8,128)}) custom-call(bf16[1536,2048]{1,0:T(8,128)(2,1)} %get-tuple-element.50.refs_0_, bf16[1536,1536]{1,0:T(8,128)(2,1)} %get-tuple-element.54.refs_1_, bf16[1536,2048]{1,0:T(8,128)(2,1)} %get-tuple-element.55.refs_2_, bf16[384,2048]{1,0:T(8,128)(2,1)} %bitcast.27, ...), custom_call_target="tpu_custom_call" | custom-call | flops 9663676416 | bytes 12582912 | tf_op jit(solution)/shard_map/pallas_call | solution.py:1110
  885.7 0.0 copy-start.1
  885.7 35.4 %shard_map.207 = (f32[512,2048]{1,0:T(8,128)}, f32[2048,2048]{1,0:T(8,128)}, f32[2048,2048]{1,0:T(8,128)}, f32[2048,2048]{1,0:T(8,128)}, f32[2048,512]{1,0:T(8,1...) custom-call(bf16[512,2048]{1,0:T(8,128)(2,1)} %get-tuple-element.46., ...), custom_call_target="tpu_custom_call" | custom-call | bytes 100663296 | tf_op jit(solution)/shard_map/pallas_call | solution.py:1599
  921.1 0.0 copy-done.1
  (4 shorter events, 0.0 us)
Async XLA Ops:
  0.6 0.7 copy-start
  885.7 35.4 %copy-start.1 = (s32[8,6,2]{0,2,1:T(2,128)S(1)}, s32[8,6,2]{0,2,1:T(2,128)}, u32[]{:S(2)}) copy-start(s32[8,6,2]{0,2,1:T(2,128)} %param.13) | copy-start | bytes 1156

commit v11 on v10

--- a/solution.py
+++ b/solution.py
@@ -806,6 +806,14 @@
         @pl.when(at + self.count < self.total)
         def _():
             pl.semaphore_signal(self.credit, inc=1, device_id=device, device_id_type=pl.DeviceIdType.MESH)
+
+
+def lags(mid, spare):
+    more = 1 if spare else 0
+    lag_t = mid + 2 * more
+    lag_o = lag_t + 2 + 2 * (mid - 1)
+    lag_f = lag_o + 1 + more
+    return 1 + more, lag_t, lag_t + 2, lag_o, lag_f, lag_f + 1
 
 
 def sums_kernel(n_ctx, items, n_right, n_extra, tasks, late, *refs):
@@ -844,11 +852,7 @@
     before = ((chip - toward) * 2 + core, rank)
     is_first = place == 0
     is_last = place == mid - 1
-    lag_t = mid + 1
-    lag_u = lag_t + 2
-    lag_o = lag_u + 2 * (mid - 1)
-    lag_f = lag_o + 2
-    lag_w = lag_f + 1
+    lag_a, lag_t, lag_u, lag_o, lag_f, lag_w = lags(mid, made)
 
     to_core = Ring(core_in, core_send, core_recv, core_credit, total)
     to_after = Ring(hop_in, in_send, in_recv, in_credit, total)
@@ -1005,7 +1009,7 @@
             def _():
                 to_after.send(source, at, slot, after)
 
-        at, now = at_lag(1)
+        at, now = at_lag(lag_a)
 
         @pl.when(now)
         def _():
@@ -1101,7 +1105,7 @@
         (k, right, columns[k] // 2 // ROWS, isinstance(left, int)) for k, (left, right) in enumerate(items)
     ]
     mid = n_ctx // 4
-    n_ring = mid + 3 + 2 * (mid - 1) + 5
+    n_ring = lags(mid, shapes[0][3])[-1] + 2
     any_spec = pl.BlockSpec(memory_space=pl.ANY)
     args, arg_specs, outs, out_specs, scratch, tasks = extra if extra is not None else ([], [], [], [], [], None)
     counts = (len(args), len(outs), len(scratch))

time: 930 us -> 928 us (level)
  no operation moved by 1% of the time
where the time goes in v11:
time: 928 us; the launch traced here: 919 us
  Pallas kernels  911 us (98%)
    pallas_call x2, Pallas kernels, weight_sums(): pl.pallas_call(functools.partial(sums_kernel, n_ctx, shapes, len(rights),...  472 us
    pallas_call x1, Pallas kernels, forward_layer(): pl.pallas_call(functools.partial(forward_kernel, n_ctx, groups, units, mi...  252 us
    pallas_call x1, Pallas kernels, middle_layer(): pl.pallas_call(functools.partial(middle_kernel, n_ctx, groups, units, min...  152 us
    pallas_call x1, Pallas kernels, cast_sums(): pl.pallas_call(functools.partial(cast_kernel, groups), out_shape=outs, gr...  35.4 us

profile of v11, /device:TPU:1, one launch (start us, length us, event | category | flops | bytes accessed | tf_op | source)
XLA Modules:
  0.0 919.4 jit_solution(2017502186037978048)
XLA Ops:
  0.6 0.0 copy-start
  0.7 0.1 stack.54
  0.8 0.1 stack.59
  1.0 0.4 copy-done
  1.3 0.1 constant_dynamic-slice_fusion
  1.4 0.1 copy.24
  1.5 0.7 gather_fusion
  2.3 0.1 convert_bitcast_fusion
  2.3 1.3 broadcast_in_dim.10.refs_6_.refs_5_
  3.6 1.3 broadcast_in_dim.11.refs_7_.refs_10_
  4.9 0.1 multiply_sine_fusion.1
  5.0 0.7 pad_maximum_fusion.2
  5.7 0.3 multiply_sine_fusion
  6.0 0.8 pad_maximum_fusion
  6.8 1.1 broadcast_in_dim.12.refs_12_.refs_13_
  7.9 251.9 %shard_map.203 = (bf16[1536,2048]{1,0:T(8,128)(2,1)}, bf16[3,8,3,256,128]{4,3,2,1,0:T(8,128)(2,1)}, bf16[1536,512]{1,0:T(8,128)(2,1)}, f32[384,2048]{1,0:T(8,128...) custom-call(bf16[384,2048]{1,0:T(8,128)(2,1)} %bitcast.26, bf16[384,2048]{1,0:T(8,128)(2,1)} %bitcast.24, ...), custom_call_target="tpu_custom_call" | custom-call | flops 12884901888 | bytes 25165824 | tf_op jit(solution)/shard_map/pallas_call | solution.py:1900
  259.9 359.2 %shard_map.204 = (bf16[2048,2048]{1,0:T(8,128)(2,1)}, bf16[2048,2048]{1,0:T(8,128)(2,1)}, bf16[2048,2048]{1,0:T(8,128)(2,1)}, bf16[512,2048]{1,0:T(8,128)(2,1)},...) custom-call(bf16[1536,2048]{1,0:T(8,128)(2,1)} %get-tuple-element.42, ...), custom_call_target="tpu_custom_call" | custom-call | flops 41875931136 | bytes 47710208 | tf_op jit(solution)/shard_map/pallas_call | solution.py:1114
  619.0 152.2 %shard_map.205 = (bf16[1536,1536]{1,0:T(8,128)(2,1)}, bf16[1536,2048]{1,0:T(8,128)(2,1)}, bf16[384,2048]{1,0:T(8,128)(2,1)}) custom-call(bf16[1536,2048]{1,0:T(8,128)(2,1)} %get-tuple-element.51.refs_0_, bf16[3,8,3,256,128]{4,3,2,1,0:T(8,128)(2,1)} %get-tuple-element.52.refs_1_, bf16[1536,2048]{1,0:T(8,128)(2,1)} %get-tuple-element.53.refs_2_, ...), custom_call_target="tpu_custom_call" | custom-call | flops 25769803776 | bytes 25165824 | tf_op jit(solution)/shard_map/pallas_call | solution.py:2171
  771.2 112.5 %shard_map.206 = (bf16[2048,1536]{1,0:T(8,128)(2,1)}, bf16[384,2048]{1,0:T(8,128)(2,1)}, f32[16,2048]{1,0:T(8,128)}) custom-call(bf16[1536,2048]{1,0:T(8,128)(2,1)} %get-tuple-element.50.refs_0_, bf16[1536,1536]{1,0:T(8,128)(2,1)} %get-tuple-element.54.refs_1_, bf16[1536,2048]{1,0:T(8,128)(2,1)} %get-tuple-element.55.refs_2_, bf16[384,2048]{1,0:T(8,128)(2,1)} %bitcast.27, ...), custom_call_target="tpu_custom_call" | custom-call | flops 9663676416 | bytes 12582912 | tf_op jit(solution)/shard_map/pallas_call | solution.py:1114
  883.8 0.0 copy-start.1
  883.8 35.4 %shard_map.207 = (f32[512,2048]{1,0:T(8,128)}, f32[2048,2048]{1,0:T(8,128)}, f32[2048,2048]{1,0:T(8,128)}, f32[2048,2048]{1,0:T(8,128)}, f32[2048,512]{1,0:T(8,1...) custom-call(bf16[512,2048]{1,0:T(8,128)(2,1)} %get-tuple-element.46., ...), custom_call_target="tpu_custom_call" | custom-call | bytes 100663296 | tf_op jit(solution)/shard_map/pallas_call | solution.py:1603
  919.2 0.0 copy-done.1
  (4 shorter events, 0.0 us)
Async XLA Ops:
  0.6 0.7 copy-start
  883.8 35.4 %copy-start.1 = (s32[8,6,2]{0,2,1:T(2,128)S(1)}, s32[8,6,2]{0,2,1:T(2,128)}, u32[]{:S(2)}) copy-start(s32[8,6,2]{0,2,1:T(2,128)} %param.13) | copy-start | bytes 1156
